TPU v7x, 32 devices: a whole 2x2x4 slice. The times are simulated.
32 devices in a mesh: seq: 4 (over y, x), dp: 8 (over z, core).
Axes of the slice: x: 2, y: 2, z: 4, core: 2. Of those that a mesh axis runs over, the one named last changes fastest.
Arguments:
- sensors: bfloat16 [16384, 512], P(('seq', 'dp')), may hold values from -6 to 6
- slot_region: int32 [16384], P(('seq', 'dp')), may hold values from -1 to 255, as said below
- w_query: bfloat16 [512, 512], replicated, may hold values from -0.25 to 0.25
- w_key: bfloat16 [512, 128], replicated, may hold values from -0.25 to 0.25
- w_value: bfloat16 [512, 128], replicated, may hold values from -0.25 to 0.25
- w_out: bfloat16 [512, 512], replicated, may hold values from -0.25 to 0.25
- temper: float32 [8], replicated, may hold values from 16 to 48
- gain_attn: float32 [512], replicated, may hold values from 0.25 to 1.75
- w_inner: bfloat16 [512, 2048], replicated, may hold values from -0.25 to 0.25
- w_outer: bfloat16 [2048, 512], replicated, may hold values from -0.125 to 0.125
- gain_mlp: float32 [512], replicated, may hold values from 0.25 to 1.75
- gain_dec: float32 [512], replicated, may hold values from 0.25 to 1.75
- w_dec_in: bfloat16 [512, 512], replicated, may hold values from -0.25 to 0.25
- w_dec_out: bfloat16 [512, 512], replicated, may hold values from -0.25 to 0.25
Outputs:
- recon: bfloat16 [16384, 512], P(('seq', 'dp'))
Inputs may be any that keep to these rules, and one draw needn't show every extreme that they name: `slot_region`: each tile of 16 slots holds 0 to 16 live sensors, live slots first; some tile of every device is full, and one owner receives full tiles from every device.
All inputs are finite; a program needn't handle non-finite values.
Results may differ from a plain program's by a relative error of at most 0.015.
Values may be sent and summed in bfloat16 or wider, within the bound.
No kernel may reach another device: no remote copies, remote signals or barrier semaphores. Data moves between devices by JAX's collectives and lax.ppermute only.
A program may use at most 128 MiB of HBM per device.

v0:
```python
import math

import jax
import jax.numpy as jnp
from jax import lax
from jax.sharding import PartitionSpec as P

HEADS = 8
HEAD_DIM = 64
KV_HEADS = 2
REG_DEV = 256


EPS = 1e-06


def rms_scale(values, gain):
    return values * lax.rsqrt(jnp.mean(values * values, axis=-1, keepdims=True) + EPS) * gain


def unit_heads(values, heads):
    shaped = values.reshape(values.shape[0], heads, -1)
    return shaped * lax.rsqrt(jnp.mean(shaped * shaped, axis=-1, keepdims=True) + EPS)


def local(
    sensors,
    slot_region,
    w_query,
    w_key,
    w_value,
    w_out,
    temper,
    gain_attn,
    w_inner,
    w_outer,
    gain_mlp,
    gain_dec,
    w_dec_in,
    w_dec_out,
):
    devices = lax.axis_size(("seq", "dp"))
    sen_dev, width = sensors.shape
    tile = sen_dev // devices
    feats = sensors.reshape(devices, tile, width)
    labels = slot_region.reshape(devices, tile)
    got_feats, got_labels = (
        lax.all_to_all(feats, ("seq", "dp"), split_axis=0, concat_axis=0, tiled=True),
        lax.all_to_all(labels, ("seq", "dp"), split_axis=0, concat_axis=0, tiled=True),
    )
    flat_labels = got_labels.reshape(-1)
    members = jnp.arange(REG_DEV, dtype=jnp.int32)[:, None] == flat_labels[None, :]
    region_sum = jnp.dot(
        members.astype(jnp.bfloat16),
        got_feats.reshape(-1, width),
        preferred_element_type=jnp.float32,
    )
    count = jnp.sum(members.astype(jnp.float32), axis=1)
    pooled = region_sum / (1.0 + count)[:, None]
    attn_in = rms_scale(pooled, gain_attn).astype(jnp.bfloat16)
    rows_here = attn_in.shape[0]
    group = HEADS // KV_HEADS
    query_unit = unit_heads(
        jnp.dot(attn_in, w_query, preferred_element_type=jnp.float32), HEADS
    ).astype(jnp.bfloat16)
    query_grouped = query_unit.reshape(rows_here, KV_HEADS, group, HEAD_DIM)
    key_unit = (
        unit_heads(jnp.dot(attn_in, w_key, preferred_element_type=jnp.float32), KV_HEADS)
        .astype(jnp.bfloat16)
        .reshape(rows_here, KV_HEADS * HEAD_DIM)
    )
    value = jnp.dot(attn_in, w_value, preferred_element_type=jnp.float32).astype(jnp.bfloat16)
    scale = (temper / HEAD_DIM).reshape(KV_HEADS, group, 1, 1)
    start_acc = (
        jnp.zeros((KV_HEADS, group, rows_here, HEAD_DIM), jnp.float32),
        jnp.zeros((KV_HEADS, group, rows_here), jnp.float32),
    )
    keys_in = lax.all_gather(key_unit, ("seq", "dp"), axis=0, tiled=True)
    values_in = lax.all_gather(value, ("seq", "dp"), axis=0, tiled=True)
    key_count = keys_in.shape[0]
    block = math.gcd(key_count, 2048)
    key_blocks = keys_in.reshape(key_count // block, block, KV_HEADS, HEAD_DIM)
    value_blocks = values_in.reshape(key_count // block, block, KV_HEADS, HEAD_DIM)

    def one_block(acc, pair):
        key_block, value_block = pair
        scores = jnp.einsum(
            "rgjd,kgd->gjrk", query_grouped, key_block, preferred_element_type=jnp.float32
        )
        weight = jnp.exp(scores * scale)
        summed = acc[0] + jnp.einsum(
            "gjrk,kgd->gjrd",
            weight.astype(jnp.bfloat16),
            value_block,
            preferred_element_type=jnp.float32,
        )
        return ((summed, acc[1] + jnp.sum(weight, axis=-1)), None)

    result, _ = lax.scan(one_block, start_acc, (key_blocks, value_blocks))
    summed, total = result
    attended = (
        jnp.transpose(summed / total[..., None], (2, 0, 1, 3))
        .reshape(rows_here, HEADS * HEAD_DIM)
        .astype(jnp.bfloat16)
    )
    hidden_one = pooled + jnp.dot(attended, w_out, preferred_element_type=jnp.float32)
    mlp_in = rms_scale(hidden_one, gain_mlp).astype(jnp.bfloat16)
    inner = jax.nn.gelu(jnp.dot(mlp_in, w_inner, preferred_element_type=jnp.float32)).astype(
        jnp.bfloat16
    )
    region_out = (hidden_one + jnp.dot(inner, w_outer, preferred_element_type=jnp.float32)).astype(
        jnp.bfloat16
    )
    lookup = jnp.clip(flat_labels, 0, REG_DEV - 1)
    back_rows = jnp.take(region_out, lookup, axis=0).reshape(devices, tile, width)
    returned = lax.all_to_all(
        back_rows, ("seq", "dp"), split_axis=0, concat_axis=0, tiled=True
    ).reshape(sen_dev, width)
    dec_in = rms_scale(returned.astype(jnp.float32) + sensors.astype(jnp.float32), gain_dec).astype(
        jnp.bfloat16
    )
    dec_hidden = jax.nn.gelu(jnp.dot(dec_in, w_dec_in, preferred_element_type=jnp.float32)).astype(
        jnp.bfloat16
    )
    result = jnp.dot(dec_hidden, w_dec_out, preferred_element_type=jnp.float32)
    return jnp.where((slot_region >= 0)[:, None], result, 0.0).astype(jnp.bfloat16)


def solution(mesh):
    placed = (
        P(("seq", "dp"), None),
        P(("seq", "dp")),
        P(),
        P(),
        P(),
        P(),
        P(),
        P(),
        P(),
        P(),
        P(),
        P(),
        P(),
        P(),
    )
    return jax.shard_map(
        local, mesh=mesh, in_specs=placed, out_specs=P(("seq", "dp"), None), check_vma=False
    )
```

profile of v0, /device:TPU:1, one launch (start us, length us, event | category | flops | bytes accessed | tf_op | source)
XLA Modules:
  0.0 245.5 jit_solution(11595281010111939513)
XLA Ops:
  6.5 0.0 copy-start
  6.5 0.0 copy-start.4
  6.5 0.9 all_to_all.12
  7.5 13.7 %all_to_all.19 = s32[32,1,16]{2,1,0:T(1,128)S(1)} all-to-all(s32[32,1,16]{2,1,0:T(1,128)S(1)} %bitcast.80), channel_id=1, replica_groups=mesh['seq'=4,'dp'=8] {'seq','dp'}, dimensions={0} | all-to-all | bytes 4096 | tf_op jit(solution)/shard_map/all_to_all | solution.py:49
  21.1 2.8 %all-to-all-start.1 = ((bf16[32,16,512]{2,1,0:T(8,128)(2,1)}), bf16[32,16,512]{2,1,0:T(8,128)(2,1)S(1)}, u32[]{:S(2)}, u32[]{:S(2)}) async-start(bf16[32,16,512]{2,1,0:T(8,128)(2,1)} %bitcast.75), calls=%async_computation.1 | async-start | bytes 1048576 | tf_op jit(solution)/shard_map/all_to_all | solution.py:48
  24.0 0.0 all-gather.3.cloned.1.call-start
  24.0 0.6 broadcast.170
  24.6 1.9 fusion.56
  26.5 0.1 reshape.135
  26.6 0.1 convert_reduce_fusion
  26.8 13.5 %all-to-all-done.1 = bf16[32,16,512]{2,1,0:T(8,128)(2,1)S(1)} async-done(((bf16[32,16,512]{2,1,0:T(8,128)(2,1)}), bf16[32,16,512]{2,1,0:T(8,128)(2,1)S(1)}, u32[]{:S(2)}, u32[]{:S(2)}) %all-to-all-start.1) | async-done | bytes 524320 | tf_op jit(solution)/shard_map/all_to_all | solution.py:48
  40.2 0.0 copy-start.2
  40.2 0.4 multiply_reduce_fusion.2
  40.6 0.0 copy-done.4
  40.6 0.1 multiply_convert_fusion.8
  40.8 1.1 bitcast_reduce_fusion.2
  41.9 0.6 fusion.47
  42.6 0.0 all-gather.3.cloned.1.call-update
  42.6 0.0 all-gather.5.cloned.1.call-start
  42.6 0.0 copy-done.2
  42.7 0.8 convolution_convert_fusion
  43.5 0.0 all-gather.5.cloned.1.call-update
  43.6 0.0 copy-done.7
  43.6 0.1 reshape.140
  43.7 0.8 min.18
  44.5 0.7 compare_and_fusion
  45.2 2.3 fusion.57
  47.5 2.0 copy.35
  49.5 1.1 bitcast_reduce_fusion.1
  50.7 2.0 copy.34
  52.7 1.1 multiply_convert_fusion.7
  53.8 43.4 %all-gather.3.cloned.1.call-done = bf16[8192,128]{0,1:T(8,128)(2,1)} async-done(((bf16[256,128]{0,1:T(8,128)(2,1)}), bf16[8192,128]{0,1:T(8,128)(2,1)}) %all-gather.3.cloned.1.call-update) | async-done | bytes 2097168 | tf_op jit(solution)/shard_map/all_gather | solution.py:78
  97.2 4.5 %reshape.138 = bf16[4,2048,2,64]{1,0,3,2:T(4,128)(2,1)} reshape(bf16[8192,128]{0,1:T(8,128)(2,1)} %all-gather.3.cloned.1.call-done) | data formatting | bytes 4194304 | tf_op jit(solution)/shard_map/reshape | solution.py:82
  101.7 4.0 %copy.37 = bf16[4,2048,2,64]{1,3,2,0:T(8,128)(2,1)} copy(bf16[4,2048,2,64]{1,0,3,2:T(4,128)(2,1)} %reshape.138) | data formatting | bytes 4194304
  105.8 49.8 %all-gather.5.cloned.1.call-done = bf16[8192,128]{1,0:T(8,128)(2,1)} async-done(((bf16[256,128]{1,0:T(8,128)(2,1)}), bf16[8192,128]{1,0:T(8,128)(2,1)}) %all-gather.5.cloned.1.call-update) | async-done | bytes 2097168 | tf_op jit(solution)/shard_map/all_gather | solution.py:79
  155.6 8.2 %reshape.153 = bf16[4,2048,2,64]{3,2,1,0:T(2,128)(2,1)} reshape(bf16[8192,128]{1,0:T(8,128)(2,1)} %all-gather.5.cloned.1.call-done) | data formatting | bytes 4194304 | tf_op jit(solution)/shard_map/reshape | solution.py:83
  163.8 10.7 %copy.38 = bf16[4,2048,2,64]{1,3,2,0:T(8,128)(2,1)} copy(bf16[4,2048,2,64]{3,2,1,0:T(2,128)(2,1)} %reshape.153) | data formatting | bytes 4194304
  174.5 32.7 %while.13 = (s32[]{:T(128)}, f32[2,4,256,64]{2,3,1,0:T(8,128)S(1)}, f32[2,4,256]{2,1,0:T(4,128)S(1)}, bf16[4,2048,2,64]{1,3,2,0:T(8,128)(2,1)}, bf16[256,2,4,64]...) while((s32[]{:T(128)}, f32[2,4,256,64]{2,3,1,0:T(8,128)S(1)}, ...), condition=%wide.region_6.7_spmd.clone, body=%wide.region_4.6_spmd.clone.sunk | while | flops 1090783232 | bytes 35946676 | solution.py:99
  174.5 4.2 %bitcast_reduce_fusion.4 = (f32[2,4,256]{2,1,0:T(4,128)S(1)}, f32[2,2048,256,4]{2,1,3,0:T(8,128)S(1)}) fusion(f32[2,4]{1,0:T(2,128)S(1)} %bitcast.72, bf16[256,2,4,64]{0,3,2,1:T(8,128)(2,1)S(1)} %get-tuple-element.193, bf16[4,2048,2,64]{1,3,2,0:T(8,128)(2,1)} %get-tuple-element.192, s32[]{:T(128)S(6)} %copy.47), kind=kOutput, calls=%fused_computation.1.clone.1 | convolution fusion | flops 545257472 | bytes 17571876 | tf_op jit(solution)/shard_map/while/body/eval_jaxpr/rgjd,kgd->gjrk/dot_general | solution.py:87
  178.7 3.9 %fusion.77 = f32[2,4,256,64]{2,3,1,0:T(8,128)S(1)} fusion(f32[2,2048,256,4]{2,1,3,0:T(8,128)S(1)} %get-tuple-element.169, f32[2,4]{1,0:T(2,128)S(1)} %bitcast.73, f32[2,4,256,64]{2,3,1,0:T(8,128)S(1)} %get-tuple-element.181, bf16[4,2048,2,64]{1,3,2,0:T(8,128)(2,1)} %get-tuple-element.195, s32[]{:T(128)S(6)} %copy.47, pred[]{:T(512)S(6)} %compare.3), kind=kOutput, calls=%fused_computation.6.clone.1 | convolution fusion | flops 545521664 | bytes 18350116 | tf_op jit(solution)/shard_map/while/body/eval_jaxpr/gjrk,kgd->gjrd/dot_general | solution.py:91
  182.7 4.2 %bitcast_reduce_fusion.4 = (f32[2,4,256]{2,1,0:T(4,128)S(1)}, f32[2,2048,256,4]{2,1,3,0:T(8,128)S(1)}) fusion(f32[2,4]{1,0:T(2,128)S(1)} %bitcast.72, bf16[256,2,4,64]{0,3,2,1:T(8,128)(2,1)S(1)} %get-tuple-element.193, bf16[4,2048,2,64]{1,3,2,0:T(8,128)(2,1)} %get-tuple-element.192, s32[]{:T(128)S(6)} %copy.47), kind=kOutput, calls=%fused_computation.1.clone.1 | convolution fusion | flops 545257472 | bytes 17571876 | tf_op jit(solution)/shard_map/while/body/eval_jaxpr/rgjd,kgd->gjrk/dot_general | solution.py:87
  186.9 3.9 %fusion.77 = f32[2,4,256,64]{2,3,1,0:T(8,128)S(1)} fusion(f32[2,2048,256,4]{2,1,3,0:T(8,128)S(1)} %get-tuple-element.169, f32[2,4]{1,0:T(2,128)S(1)} %bitcast.73, f32[2,4,256,64]{2,3,1,0:T(8,128)S(1)} %get-tuple-element.181, bf16[4,2048,2,64]{1,3,2,0:T(8,128)(2,1)} %get-tuple-element.195, s32[]{:T(128)S(6)} %copy.47, pred[]{:T(512)S(6)} %compare.3), kind=kOutput, calls=%fused_computation.6.clone.1 | convolution fusion | flops 545521664 | bytes 18350116 | tf_op jit(solution)/shard_map/while/body/eval_jaxpr/gjrk,kgd->gjrd/dot_general | solution.py:91
  190.9 4.2 %bitcast_reduce_fusion.4 = (f32[2,4,256]{2,1,0:T(4,128)S(1)}, f32[2,2048,256,4]{2,1,3,0:T(8,128)S(1)}) fusion(f32[2,4]{1,0:T(2,128)S(1)} %bitcast.72, bf16[256,2,4,64]{0,3,2,1:T(8,128)(2,1)S(1)} %get-tuple-element.193, bf16[4,2048,2,64]{1,3,2,0:T(8,128)(2,1)} %get-tuple-element.192, s32[]{:T(128)S(6)} %copy.47), kind=kOutput, calls=%fused_computation.1.clone.1 | convolution fusion | flops 545257472 | bytes 17571876 | tf_op jit(solution)/shard_map/while/body/eval_jaxpr/rgjd,kgd->gjrk/dot_general | solution.py:87
  195.1 3.9 %fusion.77 = f32[2,4,256,64]{2,3,1,0:T(8,128)S(1)} fusion(f32[2,2048,256,4]{2,1,3,0:T(8,128)S(1)} %get-tuple-element.169, f32[2,4]{1,0:T(2,128)S(1)} %bitcast.73, f32[2,4,256,64]{2,3,1,0:T(8,128)S(1)} %get-tuple-element.181, bf16[4,2048,2,64]{1,3,2,0:T(8,128)(2,1)} %get-tuple-element.195, s32[]{:T(128)S(6)} %copy.47, pred[]{:T(512)S(6)} %compare.3), kind=kOutput, calls=%fused_computation.6.clone.1 | convolution fusion | flops 545521664 | bytes 18350116 | tf_op jit(solution)/shard_map/while/body/eval_jaxpr/gjrk,kgd->gjrd/dot_general | solution.py:91
  199.0 4.2 %bitcast_reduce_fusion.4 = (f32[2,4,256]{2,1,0:T(4,128)S(1)}, f32[2,2048,256,4]{2,1,3,0:T(8,128)S(1)}) fusion(f32[2,4]{1,0:T(2,128)S(1)} %bitcast.72, bf16[256,2,4,64]{0,3,2,1:T(8,128)(2,1)S(1)} %get-tuple-element.193, bf16[4,2048,2,64]{1,3,2,0:T(8,128)(2,1)} %get-tuple-element.192, s32[]{:T(128)S(6)} %copy.47), kind=kOutput, calls=%fused_computation.1.clone.1 | convolution fusion | flops 545257472 | bytes 17571876 | tf_op jit(solution)/shard_map/while/body/eval_jaxpr/rgjd,kgd->gjrk/dot_general | solution.py:87
  203.2 3.9 %fusion.77 = f32[2,4,256,64]{2,3,1,0:T(8,128)S(1)} fusion(f32[2,2048,256,4]{2,1,3,0:T(8,128)S(1)} %get-tuple-element.169, f32[2,4]{1,0:T(2,128)S(1)} %bitcast.73, f32[2,4,256,64]{2,3,1,0:T(8,128)S(1)} %get-tuple-element.181, bf16[4,2048,2,64]{1,3,2,0:T(8,128)(2,1)} %get-tuple-element.195, s32[]{:T(128)S(6)} %copy.47, pred[]{:T(512)S(6)} %compare.3), kind=kOutput, calls=%fused_computation.6.clone.1 | convolution fusion | flops 545521664 | bytes 18350116 | tf_op jit(solution)/shard_map/while/body/eval_jaxpr/gjrk,kgd->gjrd/dot_general | solution.py:91
  207.2 0.0 copy-start.5
  207.2 0.1 divide_convert_fusion
  207.3 2.2 multiply_reduce_fusion.1
  209.5 0.0 copy-done
  209.5 0.0 copy-done.5
  209.5 3.5 %fusion.19 = bf16[256,512]{1,0:T(8,128)(2,1)S(1)} fusion(f32[256,512]{1,0:T(8,128)} %get-tuple-element.123, bf16[2048,512]{1,0:T(8,128)(2,1)S(1)} %copy-done, bf16[512,2048]{1,0:T(8,128)(2,1)} %param.24, f32[512]{0:T(512)S(1)} %copy-done.5, f32[256]{0:T(256)S(1)} %add_rsqrt_fusion.3), kind=kOutput, calls=%fused_computation.30 | convolution fusion | flops 1079115776 | bytes 4983808 | tf_op jit(solution)/shard_map/dot_general | solution.py:111
  212.9 2.0 gather_fusion
  214.9 0.0 copy-start.3
  214.9 0.0 copy-start.1
  214.9 0.0 copy-start.6
  214.9 0.9 broadcast_select_fusion
  215.9 3.4 %all-to-all-start.2 = ((bf16[32,16,512]{2,1,0:T(8,128)(2,1)}), bf16[32,16,512]{2,1,0:T(8,128)(2,1)S(1)}, u32[]{:S(2)}, u32[]{:S(2)}) async-start(bf16[32,16,512]{2,1,0:T(8,128)(2,1)} %broadcast_select_fusion), calls=%async_computation.2 | async-start | bytes 1048576 | tf_op jit(solution)/shard_map/all_to_all | solution.py:116
  219.3 0.0 copy-done.3
  219.3 16.1 %all-to-all-done.2 = bf16[32,16,512]{2,1,0:T(8,128)(2,1)S(1)} async-done(((bf16[32,16,512]{2,1,0:T(8,128)(2,1)}), bf16[32,16,512]{2,1,0:T(8,128)(2,1)S(1)}, u32[]{:S(2)}, u32[]{:S(2)}) %all-to-all-start.2) | async-done | bytes 524320 | tf_op jit(solution)/shard_map/all_to_all | solution.py:116
  235.4 0.0 copy-done.1
  235.4 0.2 multiply_reduce_fusion
  235.7 0.0 copy-done.6
  235.7 3.0 %fusion.18 = bf16[512,512]{1,0:T(8,128)(2,1)} fusion(bf16[512,512]{1,0:T(8,128)(2,1)} %param.29, bf16[512,512]{1,0:T(8,128)(2,1)} %param.28, bf16[512,512]{1,0:T(8,128)(2,1)S(1)} %copy-done.1, bf16[512,512]{1,0:T(8,128)(2,1)S(1)} %bitcast.76, f32[512]{0:T(512)S(1)} %copy-done.6, f32[512]{0:T(512)S(1)} %add_rsqrt_fusion.1, ...), kind=kOutput, calls=%fused_computation.26 | convolution fusion | flops 541327360 | bytes 2626048 | tf_op jit(solution)/shard_map/dot_general | solution.py:125
  (18 shorter events, 0.1 us)
Async XLA Ops:
  6.5 202.9 %copy-start = (bf16[2048,512]{1,0:T(8,128)(2,1)S(1)}, bf16[2048,512]{1,0:T(8,128)(2,1)}, u32[]{:S(2)}) copy-start(bf16[2048,512]{1,0:T(8,128)(2,1)} %param.25) | copy-start | bytes 6291460
  6.5 34.1 %copy-start.4 = (f32[512]{0:T(512)S(1)}, f32[512]{0:T(512)}, u32[]{:S(2)}) copy-start(f32[512]{0:T(512)} %param.23) | copy-start | bytes 6148
  21.1 19.1 %all-to-all-start.1 = ((bf16[32,16,512]{2,1,0:T(8,128)(2,1)}), bf16[32,16,512]{2,1,0:T(8,128)(2,1)S(1)}, u32[]{:S(2)}, u32[]{:S(2)}) async-start(bf16[32,16,512]{2,1,0:T(8,128)(2,1)} %bitcast.75), calls=%async_computation.1 | async-start | bytes 1048576 | tf_op jit(solution)/shard_map/all_to_all | solution.py:48
  24.0 73.2 %all-gather.3.cloned.1.call-start = ((), (), s32[]{:S(2)}) async-start(), calls=%async_computation.3 | async-start | bytes 2162688 | tf_op jit(solution)/shard_map/all_gather | solution.py:78
  40.2 2.4 copy-start.2
  40.2 3.3 %copy-start.7 = (f32[8]{0:T(128)S(1)}, f32[8]{0:T(128)}, u32[]{:S(2)}) copy-start(f32[8]{0:T(128)} %param.22) | copy-start | bytes 100
  42.6 113.0 %all-gather.5.cloned.1.call-start = ((), (), s32[]{:S(2)}) async-start(), calls=%async_computation.4 | async-start | bytes 2162688 | tf_op jit(solution)/shard_map/all_gather | solution.py:79
  207.2 2.2 copy-start.5
  214.9 4.4 %copy-start.3 = (s32[512]{0:T(512)S(1)}, s32[512]{0:T(512)}, u32[]{:S(2)}) copy-start(s32[512]{0:T(512)} %param.17) | copy-start | bytes 6148
  214.9 20.5 %copy-start.1 = (bf16[512,512]{1,0:T(8,128)(2,1)S(1)}, bf16[512,512]{1,0:T(8,128)(2,1)}, u32[]{:S(2)}) copy-start(bf16[512,512]{1,0:T(8,128)(2,1)} %param.16) | copy-start | bytes 1572868
  214.9 20.8 %copy-start.6 = (f32[512]{0:T(512)S(1)}, f32[512]{0:T(512)}, u32[]{:S(2)}) copy-start(f32[512]{0:T(512)} %param.27) | copy-start | bytes 6148
  215.9 19.6 %all-to-all-start.2 = ((bf16[32,16,512]{2,1,0:T(8,128)(2,1)}), bf16[32,16,512]{2,1,0:T(8,128)(2,1)S(1)}, u32[]{:S(2)}, u32[]{:S(2)}) async-start(bf16[32,16,512]{2,1,0:T(8,128)(2,1)} %broadcast_select_fusion), calls=%async_computation.2 | async-start | bytes 1048576 | tf_op jit(solution)/shard_map/all_to_all | solution.py:116
Sparse Core Ops, SparseCore 0:
  42.7 54.4 all-gather.2
  100.2 55.3 all-gather.4
where the time goes:
time: 247 us; the launch traced here: 246 us
  waiting for transfers between devices  123 us (50%)
  matrix products  45.8 us (19%)
  local copies, waits for them, and re-layouts  36 us (15%)
  blocking collectives  13.7 us (6%)
  between operations  13.6 us (6%)
  other arithmetic  7.07 us (3%)
  starting transfers between devices  6.36 us (3%)
    all_gather x1, waiting for transfers between devices, local(): values_in = lax.all_gather(value, ('seq', 'dp'), axis=0, tiled=True)  49.8 us
    all_gather x1, waiting for transfers between devices, local(): keys_in = lax.all_gather(key_unit, ('seq', 'dp'), axis=0, tiled=True)  43.4 us
    dot_general x4, matrix products, one_block(): jnp.einsum('rgjd,kgd->gjrk', query_grouped, key_block, preferred_element_...  16.7 us
    all_to_all x1, waiting for transfers between devices, local(): lax.all_to_all(back_rows, ('seq', 'dp'), split_axis=0, concat_axis=0, til...  16.1 us
    dot_general x4, matrix products, one_block(): jnp.einsum('gjrk,kgd->gjrd', weight.astype(jnp.bfloat16), value_block, pr...  15.8 us
    unnamed x18, local copies, waits for them, and re-layouts  14.8 us
    all_to_all x1, blocking collectives, local(): lax.all_to_all(labels, ('seq', 'dp'), split_axis=0, concat_axis=0, tiled=...  13.7 us
    all_to_all x1, waiting for transfers between devices, local(): lax.all_to_all(feats, ('seq', 'dp'), split_axis=0, concat_axis=0, tiled=T...  13.5 us
  transfers between devices with their start and end apart: 4, of which 4 were waited for; matrix products, arithmetic and copies ran while one was open for 9% of the time, Pallas kernels for 0%

commit v1 on v0

v1 whole, which is shorter than its diff:
```python
import functools
import math

import jax
import jax.numpy as jnp
from jax import lax
from jax.experimental import pallas as pl
from jax.experimental.pallas import tpu as pltpu
from jax.sharding import PartitionSpec as P

HEADS = 8
HEAD_DIM = 64
KV_HEADS = 2
GROUP = HEADS // KV_HEADS
REG_DEV = 256
LANES = 128
EPS = 1e-06
AXES = ("seq", "dp")
F32 = jnp.float32
BF16 = jnp.bfloat16
NT = (((1,), (1,)), ((), ()))
TN = (((0,), (0,)), ((), ()))

VMEM = pl.BlockSpec(memory_space=pltpu.VMEM)
SMEM = pl.BlockSpec(memory_space=pltpu.SMEM)
PARAMS = pltpu.CompilerParams(vmem_limit_bytes=40 * 1024 * 1024)


def mm(a, b):
    return jnp.dot(a, b, preferred_element_type=F32)


def rms(values):
    return values * lax.rsqrt(jnp.mean(values * values, axis=-1, keepdims=True) + EPS)


def pack_kernel(tile, me_ref, sensors_ref, labels_ref, out_ref):
    per_row = LANES // tile
    blocks = sensors_ref.shape[1] // LANES
    tiles = out_ref.shape[0]
    mine = lax.rem(me_ref[0], per_row)
    labels = (labels_ref[...] + 1).astype(F32)
    lane = lax.broadcasted_iota(jnp.int32, labels.shape, 1)
    own_lanes = (lane // tile) == mine
    for k in range(per_row):
        shift = lax.rem(mine - k + per_row, per_row) * tile
        rolled = jnp.where(own_lanes, pltpu.roll(labels, shift, 1), 0.0)
        for g in range(tiles // per_row):
            t = g * per_row + k
            row = jnp.broadcast_to(rolled[g : g + 1, :], (8, LANES)).astype(BF16)
            rows = sensors_ref[t * tile : (t + 1) * tile, :]
            parts = [rows[:, c * LANES : (c + 1) * LANES] for c in range(blocks)]
            out_ref[t] = jnp.concatenate(parts + [row], axis=0)


def pool_kernel(
    tile, core_ref, got_ref, w_q_ref, w_kv_ref, q_scale_ref, gain_ref, pooled_ref, member_ref, keep_ref, send_ref
):
    tiles, _, _ = got_ref.shape
    per_row = LANES // tile
    width = pooled_ref.shape[1]
    blocks = width // LANES
    slots = tiles * tile
    regions = lax.broadcasted_iota(jnp.int32, (REG_DEV, LANES), 0).astype(F32) + 1.0
    count = jnp.zeros((REG_DEV, 1), F32)
    for g in range(tiles // per_row):
        row = got_ref[g * per_row, tile * blocks : tile * blocks + 8, :].astype(F32)
        for k in range(1, per_row):
            row = row + got_ref[g * per_row + k, tile * blocks : tile * blocks + 8, :].astype(F32)
        hit = jnp.where(regions == row[0:1, :], 1.0, 0.0)
        count = count + jnp.sum(hit, axis=1, keepdims=True)
        member_ref[:, g * LANES : (g + 1) * LANES] = hit.astype(BF16)
    members = member_ref[...]
    sums = [
        mm(members, got_ref[:, c * tile : (c + 1) * tile, :].reshape(slots, LANES))
        for c in range(blocks)
    ]
    pooled = jnp.concatenate(sums, axis=1) * (1.0 / (1.0 + count))
    pooled_ref[...] = pooled
    attn_in = (rms(pooled) * gain_ref[...]).astype(BF16)
    at = lax.broadcasted_iota(jnp.int32, (LANES, LANES), 0) // HEAD_DIM
    to = lax.broadcasted_iota(jnp.int32, (LANES, LANES), 1) // HEAD_DIM
    mean_heads = jnp.where(at == to, 1.0 / HEAD_DIM, 0.0).astype(BF16)
    low = lax.broadcasted_iota(jnp.int32, (REG_DEV, LANES), 1) < HEAD_DIM
    core = core_ref[0]

    def put(g, part, value):
        cols = slice(part * LANES, (part + 1) * LANES)

        @pl.when(core == g)
        def _():
            keep_ref[:, cols] = value

        @pl.when(core != g)
        def _():
            send_ref[:, cols] = value

    query = mm(attn_in, w_q_ref[...])
    for h in range(HEADS):
        values = query[:, h * LANES : (h + 1) * LANES]
        square = mm((values * values).astype(BF16), mean_heads)
        unit = values * lax.rsqrt(square + EPS) * q_scale_ref[:, h * LANES : (h + 1) * LANES]
        put(h // GROUP, h % GROUP, unit.astype(BF16))
    keyval = mm(attn_in, w_kv_ref[...])
    for g in range(KV_HEADS):
        values = keyval[:, g * LANES : (g + 1) * LANES]
        square = mm((values * values).astype(BF16), mean_heads)
        unit = values * jnp.where(low, lax.rsqrt(square + EPS), 1.0)
        put(g, GROUP, unit.astype(BF16))


def attend_kernel(n_kv, first, last, key_block, *refs):
    slabs, kvs = refs[:2], refs[2 : 2 + n_kv]
    rest = refs[2 + n_kv :]
    if first:
        (acc_ref,) = rest
    elif last:
        acc_in, keep_ref, send_ref, acc_ref = rest
    else:
        acc_in, acc_ref = rest
    if first:
        acc_ref[...] = jnp.zeros_like(acc_ref)
    else:
        acc_ref[...] = acc_in[...]
    for kv_ref in kvs:
        block = math.gcd(kv_ref.shape[0], key_block)

        def step(i, _, kv_ref=kv_ref, block=block):
            kv = kv_ref[pl.ds(pl.multiple_of(i * block, block), block), :]
            low = lax.broadcasted_iota(jnp.int32, kv.shape, 1) < HEAD_DIM
            ones_value = jnp.where(low, jnp.ones_like(kv), kv)
            for r in range(2):
                for h in range(GROUP):
                    q = slabs[r][:, h * LANES : (h + 1) * LANES]
                    score = lax.dot_general(q, kv, NT, preferred_element_type=F32)
                    weight = jnp.exp2(score).astype(BF16)
                    acc_ref[r, h] += mm(weight, ones_value)
            return 0

        lax.fori_loop(0, kv_ref.shape[0] // block, step, 0)
    if last:
        low = lax.broadcasted_iota(jnp.int32, (REG_DEV, LANES), 1) < HEAD_DIM
        for r, out_ref in enumerate((keep_ref, send_ref)):
            for j in range(GROUP // 2):
                a, b = acc_ref[r, 2 * j], acc_ref[r, 2 * j + 1]
                num = jnp.where(low, pltpu.roll(a, HEAD_DIM, 1), b)
                den = jnp.where(low, a, pltpu.roll(b, HEAD_DIM, 1))
                out_ref[:, j * LANES : (j + 1) * LANES] = (num / den).astype(BF16)


def post_kernel(
    core_ref, mine_ref, other_ref, pooled_ref, member_ref, w_out_ref, gain_ref, w_inner_ref, w_outer_ref, out_ref
):
    half = mine_ref.shape[1]
    core = core_ref[0]
    own = pl.ds(pl.multiple_of(core * half, half), half)
    far = pl.ds(pl.multiple_of((1 - core) * half, half), half)
    hidden = (
        pooled_ref[...] + mm(mine_ref[...], w_out_ref[own, :]) + mm(other_ref[...], w_out_ref[far, :])
    )
    mlp_in = (rms(hidden) * gain_ref[...]).astype(BF16)
    inner = jax.nn.gelu(mm(mlp_in, w_inner_ref[...])).astype(BF16)
    region_out = (hidden + mm(inner, w_outer_ref[...])).astype(BF16)
    slots = member_ref.shape[1]
    block = math.gcd(slots, 512)
    for i in range(slots // block):
        rows = slice(i * block, (i + 1) * block)
        out_ref[rows, :] = lax.dot_general(
            member_ref[:, rows], region_out, TN, preferred_element_type=F32
        ).astype(BF16)


def decode_kernel(back_ref, sensors_ref, live_ref, gain_ref, w_in_ref, w_out_ref, out_ref):
    total = back_ref[...].astype(F32) + sensors_ref[...].astype(F32)
    dec_in = (rms(total) * gain_ref[...]).astype(BF16)
    hidden = jax.nn.gelu(mm(dec_in, w_in_ref[...])).astype(BF16)
    result = mm(hidden, w_out_ref[...])
    out_ref[...] = jnp.where(live_ref[...] > 0.0, result, 0.0).astype(BF16)


def local(
    sensors,
    slot_region,
    w_query,
    w_key,
    w_value,
    w_out,
    temper,
    gain_attn,
    w_inner,
    w_outer,
    gain_mlp,
    gain_dec,
    w_dec_in,
    w_dec_out,
):
    devices = lax.axis_size(AXES)
    sen_dev, width = sensors.shape
    tile = sen_dev // devices
    me = lax.axis_index(AXES).astype(jnp.int32).reshape(1)
    core = lax.rem(me, 2)
    bits = devices.bit_length() - 1
    pay_rows = tile * (width // LANES) + 8

    def flipped(value, mask):
        return lax.ppermute(value, AXES, [(i, i ^ mask) for i in range(devices)])

    payload = pl.pallas_call(
        functools.partial(pack_kernel, tile),
        out_shape=jax.ShapeDtypeStruct((devices, pay_rows, LANES), BF16),
        in_specs=[SMEM, VMEM, VMEM],
        out_specs=VMEM,
        compiler_params=PARAMS,
        name="pack",
    )(me, sensors, slot_region.reshape(-1, LANES))
    got = lax.all_to_all(payload, AXES, split_axis=0, concat_axis=0, tiled=True)

    w_q = jnp.pad(w_query.reshape(width, HEADS, HEAD_DIM), ((0, 0), (0, 0), (0, LANES - HEAD_DIM)))
    w_q = w_q.reshape(width, HEADS * LANES)
    w_kv = jnp.stack(
        [w_key.reshape(width, KV_HEADS, HEAD_DIM), w_value.reshape(width, KV_HEADS, HEAD_DIM)], axis=2
    ).reshape(width, KV_HEADS * LANES)
    q_scale = jnp.repeat(temper * (math.log2(math.e) / HEAD_DIM), LANES).reshape(1, HEADS * LANES)
    live = (slot_region >= 0).astype(F32).reshape(sen_dev, 1)

    slab = (GROUP + 1) * LANES
    pooled, members, keep, send = pl.pallas_call(
        functools.partial(pool_kernel, tile),
        out_shape=(
            jax.ShapeDtypeStruct((REG_DEV, width), F32),
            jax.ShapeDtypeStruct((REG_DEV, sen_dev), BF16),
            jax.ShapeDtypeStruct((REG_DEV, slab), BF16),
            jax.ShapeDtypeStruct((REG_DEV, slab), BF16),
        ),
        in_specs=[SMEM] + [VMEM] * 5,
        out_specs=(VMEM,) * 4,
        compiler_params=PARAMS,
        name="pool",
    )(core, got, w_q, w_kv, q_scale, gain_attn.reshape(1, width))
    other = flipped(send, 1)

    def attend(kvs, acc=None, last=False):
        keys = sum(kv.shape[0] for kv in kvs)
        acc_shape = (2, GROUP, REG_DEV, LANES)
        half = jax.ShapeDtypeStruct((REG_DEV, GROUP * HEAD_DIM), BF16)
        work = 2 * GROUP * REG_DEV * keys
        return pl.pallas_call(
            functools.partial(attend_kernel, len(kvs), acc is None, last, 512),
            out_shape=(half, half) if last else jax.ShapeDtypeStruct(acc_shape, F32),
            in_specs=[VMEM] * (2 + len(kvs) + (acc is not None)),
            out_specs=(VMEM, VMEM) if last else VMEM,
            scratch_shapes=[pltpu.VMEM(acc_shape, F32)] if last else [],
            compiler_params=PARAMS,
            cost_estimate=pl.CostEstimate(
                flops=work * 4 * 256, bytes_accessed=keys * 2 * LANES, transcendentals=work
            ),
            name="attend",
        )(keep, other, *kvs, *(() if acc is None else (acc,)))

    held = jnp.concatenate([keep[:, GROUP * LANES :], other[:, GROUP * LANES :]], axis=0)
    acc = None
    for bit in range(bits - 3, 0, -1):
        came = flipped(held, 1 << bit)
        acc = attend([held] if acc is None else [newest], acc)
        newest = came
        held = jnp.concatenate([held, came], axis=0)
    one, two = 1 << (bits - 2), 1 << (bits - 1)
    came_one, came_two = flipped(held, one), flipped(held, two)
    acc = attend([newest], acc)
    half = held.shape[0] // 2
    far_one, far_two = flipped(came_two[:half], one), flipped(came_one[half:], two)
    acc = attend([came_one, came_two], acc)
    mine, theirs = attend([far_one, far_two], acc, last=True)
    other_heads = flipped(theirs, 1)

    back = pl.pallas_call(
        post_kernel,
        out_shape=jax.ShapeDtypeStruct((sen_dev, width), BF16),
        in_specs=[SMEM] + [VMEM] * 8,
        out_specs=VMEM,
        compiler_params=PARAMS,
        name="post",
    )(core, mine, other_heads, pooled, members, w_out, gain_mlp.reshape(1, width), w_inner, w_outer)
    returned = lax.all_to_all(
        back.reshape(devices, tile, width), AXES, split_axis=0, concat_axis=0, tiled=True
    ).reshape(sen_dev, width)

    rows = math.gcd(sen_dev, 512)
    by_rows = pl.BlockSpec((rows, width), lambda i: (i, 0))
    whole = lambda shape: pl.BlockSpec(shape, lambda i: (0, 0))
    return pl.pallas_call(
        decode_kernel,
        grid=(sen_dev // rows,),
        out_shape=jax.ShapeDtypeStruct((sen_dev, width), BF16),
        in_specs=[
            by_rows,
            by_rows,
            pl.BlockSpec((rows, 1), lambda i: (i, 0)),
            whole((1, width)),
            whole(w_dec_in.shape),
            whole(w_dec_out.shape),
        ],
        out_specs=by_rows,
        compiler_params=PARAMS,
        name="decode",
    )(returned, sensors, live, gain_dec.reshape(1, width), w_dec_in, w_dec_out)


def solution(mesh):
    placed = (P(AXES, None), P(AXES)) + (P(),) * 12
    return jax.shard_map(
        local, mesh=mesh, in_specs=placed, out_specs=P(AXES, None), check_vma=False
    )
```

time: 247 us -> 113 us (0.46)
  waiting for transfers between devices: 123 us -> 52 us
  matrix products: 45.8 us -> 0 us
  Pallas kernels: 0 us -> 39.5 us
  local copies, waits for them, and re-layouts: 36 us -> 3.5 us
  blocking collectives: 13.7 us -> 0 us
  between operations: 13.6 us -> 0.36 us
  starting transfers between devices: 6.36 us -> 16.9 us
  other arithmetic: 7.07 us -> 0.1 us
    all_gather x2 -> x0, waiting for transfers between devices: 93.2 us -> none  [the longest x1 49.8 us: local(): values_in = lax.all_gather(value, ('seq', 'dp'), axis=0, tiled=True)]
    dot_general x15 -> x0, matrix products: 45.8 us -> none  [the longest x4 16.7 us: one_block(): jnp.einsum('rgjd,kgd->gjrk', query_grouped, key_block, preferred_element_...]
    pallas_call x0 -> x9, Pallas kernels: none -> 39.5 us  [the longest x5 31.2 us: attend(): pl.pallas_call(functools.partial(attend_kernel, len(kvs), acc is None, la...]
    ppermute x0 -> x8, waiting for transfers between devices: none -> 20.3 us  [flipped(): return lax.ppermute(value, AXES, [(i, i ^ mask) for i in range(devices)])]
    all_to_all x1 -> x0, blocking collectives: 13.7 us -> none  [local(): lax.all_to_all(labels, ('seq', 'dp'), split_axis=0, concat_axis=0, tiled=...]
    unnamed x18 -> x35, local copies, waits for them, and re-layouts: 14.8 us -> 2.47 us
    reshape x4 -> x3, local copies, waits for them, and re-layouts: 12.9 us -> 0.81 us  [the longest x1 0.54 us: local(): w_q = w_q.reshape(width, HEADS * LANES)]
    ppermute x0 -> x8, starting transfers between devices: none -> 7 us  [flipped(): return lax.ppermute(value, AXES, [(i, i ^ mask) for i in range(devices)])]
  transfers between devices with their start and end apart: 4 -> 10, of which waited for: 4 -> 7; matrix products, arithmetic and copies ran while one was open for 9% -> 1% of each run, Pallas kernels for 0% -> 21%
where the time goes in v1:
time: 113 us; the launch traced here: 112 us
  waiting for transfers between devices  52 us (46%)
  Pallas kernels  39.5 us (35%)
  starting transfers between devices  16.9 us (15%)
  local copies, waits for them, and re-layouts  3.5 us (3%)
    pallas_call x5, Pallas kernels, attend(): pl.pallas_call(functools.partial(attend_kernel, len(kvs), acc is None, la...  31.2 us
    ppermute x8, waiting for transfers between devices, flipped(): return lax.ppermute(value, AXES, [(i, i ^ mask) for i in range(devices)])  20.3 us
    all_to_all x1, waiting for transfers between devices, local(): lax.all_to_all(back.reshape(devices, tile, width), AXES, split_axis=0, co...  15.9 us
    all_to_all x1, waiting for transfers between devices, local(): got = lax.all_to_all(payload, AXES, split_axis=0, concat_axis=0, tiled=True)  15.8 us
    all_to_all x1, starting transfers between devices, local(): got = lax.all_to_all(payload, AXES, split_axis=0, concat_axis=0, tiled=True)  7.1 us
    ppermute x8, starting transfers between devices, flipped(): return lax.ppermute(value, AXES, [(i, i ^ mask) for i in range(devices)])  7 us
    pallas_call x1, Pallas kernels, local(): pl.pallas_call(functools.partial(pool_kernel, tile), out_shape=(jax.Shape...  2.84 us
    pallas_call x1, Pallas kernels, local(): pl.pallas_call(post_kernel, out_shape=jax.ShapeDtypeStruct((sen_dev, widt...  2.81 us
  transfers between devices with their start and end apart: 10, of which 7 were waited for; matrix products, arithmetic and copies ran while one was open for 1% of the time, Pallas kernels for 21%

profile of v1, /device:TPU:1, one launch (start us, length us, event | category | flops | bytes accessed | tf_op | source)
XLA Modules:
  0.0 112.3 jit_solution(3538588840924483459)
XLA Ops:
  0.0 1.0 copy-done
  1.0 0.7 copy-done.7
  1.7 0.9 pack.1
  2.6 7.1 %all-to-all-start = ((bf16[32,72,128]{2,1,0:T(8,128)(2,1)}), bf16[32,72,128]{2,1,0:T(8,128)(2,1)S(1)}, u32[]{:S(2)}, u32[]{:S(2)}) async-start(bf16[32,72,128]{2,1,0:T(8,128)(2,1)} %pack.1), calls=%async_computation | async-start | bytes 1179648 | tf_op jit(solution)/shard_map/all_to_all | solution.py:216
  9.7 0.0 copy-done.12
  9.8 0.2 copy.17
  10.0 0.0 copy-start.13
  10.0 0.0 copy-start.14
  10.0 0.1 pad.4
  10.1 0.0 copy-start.15
  10.1 0.0 copy-start.9
  10.1 0.5 copy.24.w_q_ref
  10.7 0.2 copy-done.13
  10.9 0.1 copy.19
  11.0 0.0 copy-done.14
  11.0 0.1 copy.20
  11.2 0.1 copy.22.w_kv_ref
  11.3 0.0 copy-done.15
  11.4 15.8 %all-to-all-done.got_ref = bf16[32,72,128]{2,1,0:T(8,128)(2,1)S(1)} async-done(((bf16[32,72,128]{2,1,0:T(8,128)(2,1)}), bf16[32,72,128]{2,1,0:T(8,128)(2,1)S(1)}, u32[]{:S(2)}, u32[]{:S(2)}) %all-to-all-start) | async-done | bytes 589856 | tf_op jit(solution)/shard_map/all_to_all | solution.py:216
  27.1 0.1 broadcast_in_dim.3
  27.2 0.0 copy-done.9
  27.2 2.8 %pool.1 = (f32[256,512]{1,0:T(8,128)S(1)}, bf16[256,512]{1,0:T(8,128)(2,1)S(1)}, bf16[256,640]{1,0:T(8,128)(2,1)S(1)}, bf16[256,640]{1,0:T(8,128)(2,1)S(1)}) custom-call(s32[1]{0:T(128)S(6)} %rem.18.core_ref, bf16[32,72,128]{2,1,0:T(8,128)(2,1)S(1)} %all-to-all-done.got_ref, bf16[512,1024]{1,0:T(8,128)(2,1)S(1)} %copy.24.w_q_ref, ...), custom_call_target="tpu_custom_call" | custom-call | tf_op jit(solution)/shard_map/pool/pallas_call | solution.py:227
  30.1 0.7 collective-permute-start
  30.8 1.2 %collective-permute-done.refs_1_ = bf16[256,640]{1,0:T(8,128)(2,1)S(1)} collective-permute-done((bf16[256,640]{1,0:T(8,128)(2,1)S(1)}, bf16[256,640]{1,0:T(8,128)(2,1)S(1)}, u32[]{:S(2)}, u32[]{:S(2)}) %collective-permute-start) | collective-permute-done | bytes 327712 | tf_op jit(solution)/shard_map/ppermute | solution.py:206
  32.0 0.1 collective-permute-start.1
  32.1 7.9 %collective-permute-done.1.refs_2_ = bf16[512,128]{1,0:T(8,128)(2,1)S(1)} collective-permute-done((bf16[512,128]{1,0:T(8,128)(2,1)S(1)}, bf16[512,128]{1,0:T(8,128)(2,1)S(1)}, u32[]{:S(2)}, u32[]{:S(2)}) %collective-permute-start.1) | collective-permute-done | bytes 131104 | tf_op jit(solution)/shard_map/ppermute | solution.py:206
  40.1 0.1 collective-permute-start.2
  40.2 7.4 %collective-permute-done.2.refs_2_ = bf16[1024,128]{1,0:T(8,128)(2,1)S(1)} collective-permute-done((bf16[1024,128]{1,0:T(8,128)(2,1)S(1)}, bf16[1024,128]{1,0:T(8,128)(2,1)S(1)}, u32[]{:S(2)}, u32[]{:S(2)}) %collective-permute-start.2) | collective-permute-done | bytes 262176 | tf_op jit(solution)/shard_map/ppermute | solution.py:206
  47.6 1.2 %collective-permute-start.3 = (bf16[2048,128]{1,0:T(8,128)(2,1)S(1)}, bf16[2048,128]{1,0:T(8,128)(2,1)S(1)}, u32[]{:S(2)}, u32[]{:S(2)}) collective-permute-start(bf16[2048,128]{1,0:T(8,128)(2,1)S(1)} %pad_maximum_fusion), channel_id=1, source_target_pairs={{0,16},{1,17},{2,18},{3,19},{4,20},{5,21},{6,22},{7,23},{8,24},{9,... | collective-permute-start | bytes 1572872 | tf_op jit(solution)/shard_map/ppermute | solution.py:206
  48.8 0.4 collective-permute-start.5
  49.2 1.9 %attend.5.refs_3_ = f32[2,4,256,128]{3,2,1,0:T(8,128)S(1)} custom-call(bf16[256,640]{1,0:T(8,128)(2,1)S(1)} %get-tuple-element.11.refs_0_, bf16[256,640]{1,0:T(8,128)(2,1)S(1)} %collective-permute-done.refs_1_, bf16[512,128]{1,0:T(8,128)(2,1)S(1)} %pad_maximum_fusion.3.refs_2_), custom_call_target="tpu_custom_call" | custom-call | flops 1073741824 | bytes 131072 | tf_op jit(solution)/shard_map/attend/pallas_call | solution.py:247
  51.1 1.9 %attend.6.refs_3_ = f32[2,4,256,128]{3,2,1,0:T(8,128)S(1)} custom-call(bf16[256,640]{1,0:T(8,128)(2,1)S(1)} %get-tuple-element.11.refs_0_, bf16[256,640]{1,0:T(8,128)(2,1)S(1)} %collective-permute-done.refs_1_, bf16[512,128]{1,0:T(8,128)(2,1)S(1)} %collective-permute-done.1.refs_2_, f32[2,4,256,128]{3,2,1,0:T(8,128)S(1)} %attend.5.refs_3_), custom_call_target="tpu_custom_call" | custom-call | flops 1073741824 | bytes 131072 | tf_op jit(solution)/shard_map/attend/pallas_call | solution.py:247
  53.0 4.1 %attend.7.refs_4_ = f32[2,4,256,128]{3,2,1,0:T(8,128)S(1)} custom-call(bf16[256,640]{1,0:T(8,128)(2,1)S(1)} %get-tuple-element.11.refs_0_, bf16[256,640]{1,0:T(8,128)(2,1)S(1)} %collective-permute-done.refs_1_, bf16[1024,128]{1,0:T(8,128)(2,1)S(1)} %collective-permute-done.2.refs_2_, f32[2,4,256,128]{3,2,1,0:T(8,128)S(1)} %attend.6.refs_3_), custom_call_target="tpu_custom_call" | custom-call | flops 2147483648 | bytes 262144 | tf_op jit(solution)/shard_map/attend/pallas_call | solution.py:247
  57.1 2.7 %collective-permute-done.3.refs_3_ = bf16[2048,128]{1,0:T(8,128)(2,1)S(1)} collective-permute-done((bf16[2048,128]{1,0:T(8,128)(2,1)S(1)}, bf16[2048,128]{1,0:T(8,128)(2,1)S(1)}, u32[]{:S(2)}, u32[]{:S(2)}) %collective-permute-start.3) | collective-permute-done | bytes 524320 | tf_op jit(solution)/shard_map/ppermute | solution.py:206
  59.8 1.2 %collective-permute-start.4 = (bf16[1024,128]{1,0:T(8,128)(2,1)S(1)}, bf16[1024,128]{1,0:T(8,128)(2,1)S(1)}, u32[]{:S(2)}, u32[]{:S(2)}) collective-permute-start(bf16[1024,128]{1,0:T(8,128)(2,1)S(1)} %slice.17), channel_id=1, source_target_pairs={{0,8},{1,9},{2,10},{3,11},{4,12},{5,13},{6,14},{7,15},{8,0},{9,1},... | collective-permute-start | bytes 786440 | tf_op jit(solution)/shard_map/ppermute | solution.py:206
  61.0 0.0 collective-permute-done.5.refs_2_
  61.0 0.5 collective-permute-start.6
  61.5 15.3 %attend.8.refs_4_ = f32[2,4,256,128]{3,2,1,0:T(8,128)S(1)} custom-call(bf16[256,640]{1,0:T(8,128)(2,1)S(1)} %get-tuple-element.11.refs_0_, bf16[256,640]{1,0:T(8,128)(2,1)S(1)} %collective-permute-done.refs_1_, bf16[2048,128]{1,0:T(8,128)(2,1)S(1)} %collective-permute-done.5.refs_2_, bf16[2048,128]{1,0:T(8,128)(2,1)S(1)} %collective-permute-done.3.refs_3_, ...), custom_call_target="tpu_custom_call" | custom-call | flops 8589934592 | bytes 1048576 | tf_op jit(solution)/shard_map/attend/pallas_call | solution.py:247
  76.8 0.0 copy-start.2
  76.8 0.0 copy-start.3
  76.8 0.0 copy-start.4
  76.8 0.0 copy-start.10
  76.8 0.0 collective-permute-done.4.refs_2_
  76.8 0.0 collective-permute-done.6.refs_3_
  76.9 8.0 %attend.9 = (bf16[256,256]{1,0:T(8,128)(2,1)S(1)}, bf16[256,256]{1,0:T(8,128)(2,1)S(1)}) custom-call(bf16[256,640]{1,0:T(8,128)(2,1)S(1)} %get-tuple-element.11.refs_0_, bf16[256,640]{1,0:T(8,128)(2,1)S(1)} %collective-permute-done.refs_1_, bf16[1024,128]{1,0:T(8,128)(2,1)S(1)} %collective-permute-done.4.refs_2_, ...), custom_call_target="tpu_custom_call" | custom-call | flops 4294967296 | bytes 524288 | tf_op jit(solution)/shard_map/attend/pallas_call | solution.py:247
  84.9 2.9 %collective-permute-start.7 = (bf16[256,256]{1,0:T(8,128)(2,1)S(1)}, bf16[256,256]{1,0:T(8,128)(2,1)S(1)}, u32[]{:S(2)}, u32[]{:S(2)}) collective-permute-start(bf16[256,256]{1,0:T(8,128)(2,1)S(1)} %get-tuple-element.14), channel_id=1, source_target_pairs={{0,1},{1,0},{2,3},{3,2},{4,5},{5,4},{6,7},{7,6},{8,9},{9,8},{10,11... | collective-permute-start | bytes 393224 | tf_op jit(solution)/shard_map/ppermute | solution.py:206
  87.7 1.0 collective-permute-done.7.other_ref
  88.7 0.0 copy-done.2
  88.7 0.0 copy-done.3
  88.7 0.0 copy-done.4
  88.7 0.0 copy-done.10
  88.7 0.0 copy-start.8
  88.7 0.0 copy-start.1
  88.7 0.0 copy-start.5
  88.8 0.0 copy-start.6
  88.8 0.0 copy-start.11
  88.8 2.8 %post.1 = bf16[512,512]{1,0:T(8,128)(2,1)} custom-call(s32[1]{0:T(128)S(6)} %rem.18.core_ref, bf16[256,256]{1,0:T(8,128)(2,1)S(1)} %get-tuple-element.13.mine_ref, bf16[256,256]{1,0:T(8,128)(2,1)S(1)} %collective-permute-done.7.other_ref, f32[256,512]{1,0:T(8,128)S(1)} %get-tuple-element.15.pooled_ref, bf16[256,512]{1,0:T(8,128)(2,1)S(1)} %get-tuple-element.16.member_ref, ...), custom_call_target="tpu_custom_call" | custom-call | tf_op jit(solution)/shard_map/post/pallas_call | solution.py:276
  91.6 2.8 %all-to-all-start.1 = ((bf16[32,16,512]{2,1,0:T(8,128)(2,1)}), bf16[32,16,512]{2,1,0:T(8,128)(2,1)S(1)}, u32[]{:S(2)}, u32[]{:S(2)}) async-start(bf16[32,16,512]{2,1,0:T(8,128)(2,1)} %bitcast.10), calls=%async_computation.1 | async-start | bytes 1048576 | tf_op jit(solution)/shard_map/all_to_all | solution.py:284
  94.4 0.0 copy-done.8
  94.4 0.1 copy.23.live_ref
  94.6 15.9 %all-to-all-done.1 = bf16[32,16,512]{2,1,0:T(8,128)(2,1)S(1)} async-done(((bf16[32,16,512]{2,1,0:T(8,128)(2,1)}), bf16[32,16,512]{2,1,0:T(8,128)(2,1)S(1)}, u32[]{:S(2)}, u32[]{:S(2)}) %all-to-all-start.1) | async-done | bytes 524320 | tf_op jit(solution)/shard_map/all_to_all | solution.py:284
  110.5 0.0 copy-done.1
  110.5 0.0 copy-done.11
  110.5 1.8 %decode.1 = bf16[512,512]{1,0:T(8,128)(2,1)} custom-call(bf16[512,512]{1,0:T(8,128)(2,1)S(1)} %bitcast.14, bf16[512,512]{1,0:T(8,128)(2,1)S(1)} %copy-done.1, f32[512,1]{1,0:T(8,128)S(1)} %copy.23.live_ref, f32[1,512]{1,0:T(1,128)S(1)} %bitcast.19, bf16[512,512]{1,0:T(8,128)(2,1)S(1)} %copy-done.5, bf16[512,512]{1,0:T(8,128)(2,1)S(1)} %copy-done.6), custom_call_target="tpu_custom_call" | custom-call | tf_op jit(solution)/shard_map/decode/pallas_call | solution.py:291
  (16 shorter events, 0.2 us)
Async XLA Ops:
  0.0 1.0 copy-start
  1.0 0.7 copy-start.7
  1.7 8.0 %copy-start.12 = (bf16[512,512]{1,0:T(8,128)(2,1)S(1)}, bf16[512,512]{1,0:T(8,128)(2,1)}, u32[]{:S(2)}) copy-start(bf16[512,512]{1,0:T(8,128)(2,1)} %param.16) | copy-start | bytes 1572868
  2.6 24.5 %all-to-all-start = ((bf16[32,72,128]{2,1,0:T(8,128)(2,1)}), bf16[32,72,128]{2,1,0:T(8,128)(2,1)S(1)}, u32[]{:S(2)}, u32[]{:S(2)}) async-start(bf16[32,72,128]{2,1,0:T(8,128)(2,1)} %pack.1), calls=%async_computation | async-start | bytes 1179648 | tf_op jit(solution)/shard_map/all_to_all | solution.py:216
  10.0 0.9 copy-start.13
  10.0 1.0 copy-start.14
  10.1 1.2 %copy-start.15 = (f32[8]{0:T(128)S(1)}, f32[8]{0:T(128)}, u32[]{:S(2)}) copy-start(f32[8]{0:T(128)} %param.20) | copy-start | bytes 100
  10.1 17.1 %copy-start.9 = (f32[512]{0:T(512)S(1)}, f32[512]{0:T(512)}, u32[]{:S(2)}) copy-start(f32[512]{0:T(512)} %param.21) | copy-start | bytes 6148
  30.1 2.0 %collective-permute-start = (bf16[256,640]{1,0:T(8,128)(2,1)S(1)}, bf16[256,640]{1,0:T(8,128)(2,1)S(1)}, u32[]{:S(2)}, u32[]{:S(2)}) collective-permute-start(bf16[256,640]{1,0:T(8,128)(2,1)S(1)} %get-tuple-element.12), channel_id=1, source_target_pairs={{0,1},{1,0},{2,3},{3,2},{4,5},{5,4},{6,7},{7,6},{8,9},{9,8},{10,11... | collective-permute-start | bytes 983048 | tf_op jit(solution)/shard_map/ppermute | solution.py:206
  32.0 8.0 %collective-permute-start.1 = (bf16[512,128]{1,0:T(8,128)(2,1)S(1)}, bf16[512,128]{1,0:T(8,128)(2,1)S(1)}, u32[]{:S(2)}, u32[]{:S(2)}) collective-permute-start(bf16[512,128]{1,0:T(8,128)(2,1)S(1)} %pad_maximum_fusion.3.refs_2_), channel_id=1, source_target_pairs={{0,4},{1,5},{2,6},{3,7},{4,0},{5,1},{6,2},{7,3},{8,12},{9,13},{10,... | collective-permute-start | bytes 393224 | tf_op jit(solution)/shard_map/ppermute | solution.py:206
  40.1 7.5 %collective-permute-start.2 = (bf16[1024,128]{1,0:T(8,128)(2,1)S(1)}, bf16[1024,128]{1,0:T(8,128)(2,1)S(1)}, u32[]{:S(2)}, u32[]{:S(2)}) collective-permute-start(bf16[1024,128]{1,0:T(8,128)(2,1)S(1)} %pad_maximum_fusion.2), channel_id=1, source_target_pairs={{0,2},{1,3},{2,0},{3,1},{4,6},{5,7},{6,4},{7,5},{8,10},{9,11},{10,... | collective-permute-start | bytes 786440 | tf_op jit(solution)/shard_map/ppermute | solution.py:206
  47.6 12.2 %collective-permute-start.3 = (bf16[2048,128]{1,0:T(8,128)(2,1)S(1)}, bf16[2048,128]{1,0:T(8,128)(2,1)S(1)}, u32[]{:S(2)}, u32[]{:S(2)}) collective-permute-start(bf16[2048,128]{1,0:T(8,128)(2,1)S(1)} %pad_maximum_fusion), channel_id=1, source_target_pairs={{0,16},{1,17},{2,18},{3,19},{4,20},{5,21},{6,22},{7,23},{8,24},{9,... | collective-permute-start | bytes 1572872 | tf_op jit(solution)/shard_map/ppermute | solution.py:206
  48.8 12.2 %collective-permute-start.5 = (bf16[2048,128]{1,0:T(8,128)(2,1)S(1)}, bf16[2048,128]{1,0:T(8,128)(2,1)S(1)}, u32[]{:S(2)}, u32[]{:S(2)}) collective-permute-start(bf16[2048,128]{1,0:T(8,128)(2,1)S(1)} %pad_maximum_fusion), channel_id=1, source_target_pairs={{0,8},{1,9},{2,10},{3,11},{4,12},{5,13},{6,14},{7,15},{8,0},{9,1},... | collective-permute-start | bytes 1572872 | tf_op jit(solution)/shard_map/ppermute | solution.py:206
  59.8 17.1 %collective-permute-start.4 = (bf16[1024,128]{1,0:T(8,128)(2,1)S(1)}, bf16[1024,128]{1,0:T(8,128)(2,1)S(1)}, u32[]{:S(2)}, u32[]{:S(2)}) collective-permute-start(bf16[1024,128]{1,0:T(8,128)(2,1)S(1)} %slice.17), channel_id=1, source_target_pairs={{0,8},{1,9},{2,10},{3,11},{4,12},{5,13},{6,14},{7,15},{8,0},{9,1},... | collective-permute-start | bytes 786440 | tf_op jit(solution)/shard_map/ppermute | solution.py:206
  61.0 15.9 %collective-permute-start.6 = (bf16[1024,128]{1,0:T(8,128)(2,1)S(1)}, bf16[1024,128]{1,0:T(8,128)(2,1)S(1)}, u32[]{:S(2)}, u32[]{:S(2)}) collective-permute-start(bf16[1024,128]{1,0:T(8,128)(2,1)S(1)} %slice.18), channel_id=1, source_target_pairs={{0,16},{1,17},{2,18},{3,19},{4,20},{5,21},{6,22},{7,23},{8,24},{9,... | collective-permute-start | bytes 786440 | tf_op jit(solution)/shard_map/ppermute | solution.py:206
  76.8 11.9 %copy-start.2 = (bf16[512,2048]{1,0:T(8,128)(2,1)S(1)}, bf16[512,2048]{1,0:T(8,128)(2,1)}, u32[]{:S(2)}) copy-start(bf16[512,2048]{1,0:T(8,128)(2,1)} %w_inner_ref.1) | copy-start | bytes 6291460
  76.8 11.9 %copy-start.3 = (bf16[2048,512]{1,0:T(8,128)(2,1)S(1)}, bf16[2048,512]{1,0:T(8,128)(2,1)}, u32[]{:S(2)}) copy-start(bf16[2048,512]{1,0:T(8,128)(2,1)} %w_outer_ref.1) | copy-start | bytes 6291460
  76.8 11.9 %copy-start.4 = (bf16[512,512]{1,0:T(8,128)(2,1)S(1)}, bf16[512,512]{1,0:T(8,128)(2,1)}, u32[]{:S(2)}) copy-start(bf16[512,512]{1,0:T(8,128)(2,1)} %w_out_ref.2) | copy-start | bytes 1572868
  76.8 11.9 %copy-start.10 = (f32[512]{0:T(512)S(1)}, f32[512]{0:T(512)}, u32[]{:S(2)}) copy-start(f32[512]{0:T(512)} %param.24) | copy-start | bytes 6148
  84.9 3.8 %collective-permute-start.7 = (bf16[256,256]{1,0:T(8,128)(2,1)S(1)}, bf16[256,256]{1,0:T(8,128)(2,1)S(1)}, u32[]{:S(2)}, u32[]{:S(2)}) collective-permute-start(bf16[256,256]{1,0:T(8,128)(2,1)S(1)} %get-tuple-element.14), channel_id=1, source_target_pairs={{0,1},{1,0},{2,3},{3,2},{4,5},{5,4},{6,7},{7,6},{8,9},{9,8},{10,11... | collective-permute-start | bytes 393224 | tf_op jit(solution)/shard_map/ppermute | solution.py:206
  88.7 5.7 %copy-start.8 = (s32[512]{0:T(512)S(1)}, s32[512]{0:T(512)}, u32[]{:S(2)}) copy-start(s32[512]{0:T(512)} %param.15) | copy-start | bytes 6148
  88.7 21.8 %copy-start.1 = (bf16[512,512]{1,0:T(8,128)(2,1)S(1)}, bf16[512,512]{1,0:T(8,128)(2,1)}, u32[]{:S(2)}) copy-start(bf16[512,512]{1,0:T(8,128)(2,1)} %sensors_ref.3) | copy-start | bytes 1572868
  88.7 21.8 %copy-start.5 = (bf16[512,512]{1,0:T(8,128)(2,1)S(1)}, bf16[512,512]{1,0:T(8,128)(2,1)}, u32[]{:S(2)}) copy-start(bf16[512,512]{1,0:T(8,128)(2,1)} %w_in_ref.1) | copy-start | bytes 1572868
  88.8 21.8 %copy-start.6 = (bf16[512,512]{1,0:T(8,128)(2,1)S(1)}, bf16[512,512]{1,0:T(8,128)(2,1)}, u32[]{:S(2)}) copy-start(bf16[512,512]{1,0:T(8,128)(2,1)} %w_out_ref.3) | copy-start | bytes 1572868
  88.8 21.7 %copy-start.11 = (f32[512]{0:T(512)S(1)}, f32[512]{0:T(512)}, u32[]{:S(2)}) copy-start(f32[512]{0:T(512)} %param.25) | copy-start | bytes 6148
  91.6 18.9 %all-to-all-start.1 = ((bf16[32,16,512]{2,1,0:T(8,128)(2,1)}), bf16[32,16,512]{2,1,0:T(8,128)(2,1)S(1)}, u32[]{:S(2)}, u32[]{:S(2)}) async-start(bf16[32,16,512]{2,1,0:T(8,128)(2,1)} %bitcast.10), calls=%async_computation.1 | async-start | bytes 1048576 | tf_op jit(solution)/shard_map/all_to_all | solution.py:284

commit v2 on v1

--- a/solution.py
+++ b/solution.py
@@ -109,38 +109,42 @@
         put(g, GROUP, unit.astype(BF16))
 
 
-def attend_kernel(n_kv, first, last, key_block, *refs):
-    slabs, kvs = refs[:2], refs[2 : 2 + n_kv]
-    rest = refs[2 + n_kv :]
-    if first:
-        (acc_ref,) = rest
-    elif last:
-        acc_in, keep_ref, send_ref, acc_ref = rest
-    else:
-        acc_in, acc_ref = rest
-    if first:
-        acc_ref[...] = jnp.zeros_like(acc_ref)
-    else:
-        acc_ref[...] = acc_in[...]
+def attend_kernel(parts, first, last, *refs):
+    slabs, kvs = refs[:2], refs[2 : 2 + parts]
+    rest = refs[2 + parts :]
+    key_ref, value_ref = rest[-2:]
+    acc_in = None if first else rest[0]
+    acc_ref = rest[-3]
+    at = 0
     for kv_ref in kvs:
-        block = math.gcd(kv_ref.shape[0], key_block)
-
-        def step(i, _, kv_ref=kv_ref, block=block):
-            kv = kv_ref[pl.ds(pl.multiple_of(i * block, block), block), :]
-            low = lax.broadcasted_iota(jnp.int32, kv.shape, 1) < HEAD_DIM
-            ones_value = jnp.where(low, jnp.ones_like(kv), kv)
-            for r in range(2):
-                for h in range(GROUP):
-                    q = slabs[r][:, h * LANES : (h + 1) * LANES]
-                    score = lax.dot_general(q, kv, NT, preferred_element_type=F32)
-                    weight = jnp.exp2(score).astype(BF16)
-                    acc_ref[r, h] += mm(weight, ones_value)
-            return 0
-
-        lax.fori_loop(0, kv_ref.shape[0] // block, step, 0)
+        kv = kv_ref[...]
+        rows = kv.shape[0]
+        low = lax.broadcasted_iota(jnp.int32, kv.shape, 1) < HEAD_DIM
+        key_ref[at : at + rows, :] = kv
+        value_ref[at : at + rows, :] = jnp.where(low, jnp.ones_like(kv), kv)
+        at += rows
+    block = max(n for n in range(REG_DEV, 2561, REG_DEV) if at % n == 0)
+
+    def step(i, old_ref):
+        keys = pl.ds(pl.multiple_of(i * block, block), block)
+        for r in range(2):
+            for h in range(GROUP):
+                q = slabs[r][:, h * LANES : (h + 1) * LANES]
+                score = lax.dot_general(q, key_ref[keys, :], NT, preferred_element_type=F32)
+                new = mm(jnp.exp2(score).astype(BF16), value_ref[keys, :])
+                acc_ref[r, h] = new if old_ref is None else old_ref[r, h] + new
+
+    step(0, acc_in)
+    if at > block:
+
+        def body(i, carry):
+            step(i, acc_ref)
+            return carry
+
+        lax.fori_loop(1, at // block, body, 0)
     if last:
         low = lax.broadcasted_iota(jnp.int32, (REG_DEV, LANES), 1) < HEAD_DIM
-        for r, out_ref in enumerate((keep_ref, send_ref)):
+        for r, out_ref in enumerate(rest[1:3]):
             for j in range(GROUP // 2):
                 a, b = acc_ref[r, 2 * j], acc_ref[r, 2 * j + 1]
                 num = jnp.where(low, pltpu.roll(a, HEAD_DIM, 1), b)
@@ -239,38 +243,41 @@
     )(core, got, w_q, w_kv, q_scale, gain_attn.reshape(1, width))
     other = flipped(send, 1)
 
-    def attend(kvs, acc=None, last=False):
-        keys = sum(kv.shape[0] for kv in kvs)
+    def attend(parts, acc, last):
+        keys = sum(part.shape[0] for part in parts)
         acc_shape = (2, GROUP, REG_DEV, LANES)
         half = jax.ShapeDtypeStruct((REG_DEV, GROUP * HEAD_DIM), BF16)
         work = 2 * GROUP * REG_DEV * keys
         return pl.pallas_call(
-            functools.partial(attend_kernel, len(kvs), acc is None, last, 512),
+            functools.partial(attend_kernel, len(parts), acc is None, last),
             out_shape=(half, half) if last else jax.ShapeDtypeStruct(acc_shape, F32),
-            in_specs=[VMEM] * (2 + len(kvs) + (acc is not None)),
+            in_specs=[VMEM] * (2 + len(parts) + (acc is not None)),
             out_specs=(VMEM, VMEM) if last else VMEM,
-            scratch_shapes=[pltpu.VMEM(acc_shape, F32)] if last else [],
+            scratch_shapes=([pltpu.VMEM(acc_shape, F32)] if last else [])
+            + [pltpu.VMEM((keys, LANES), BF16)] * 2,
             compiler_params=PARAMS,
             cost_estimate=pl.CostEstimate(
                 flops=work * 4 * 256, bytes_accessed=keys * 2 * LANES, transcendentals=work
             ),
             name="attend",
-        )(keep, other, *kvs, *(() if acc is None else (acc,)))
-
-    held = jnp.concatenate([keep[:, GROUP * LANES :], other[:, GROUP * LANES :]], axis=0)
-    acc = None
-    for bit in range(bits - 3, 0, -1):
-        came = flipped(held, 1 << bit)
-        acc = attend([held] if acc is None else [newest], acc)
-        newest = came
-        held = jnp.concatenate([held, came], axis=0)
+        )(keep, other, *parts, *(() if acc is None else (acc,)))
+
     one, two = 1 << (bits - 2), 1 << (bits - 1)
-    came_one, came_two = flipped(held, one), flipped(held, two)
-    acc = attend([newest], acc)
-    half = held.shape[0] // 2
-    far_one, far_two = flipped(came_two[:half], one), flipped(came_one[half:], two)
-    acc = attend([came_one, came_two], acc)
-    mine, theirs = attend([far_one, far_two], acc, last=True)
+    own = jnp.concatenate([keep[:, GROUP * LANES :], other[:, GROUP * LANES :]], axis=0)
+    line, fresh, sides, ready, acc = [own], [own], [], [own], None
+    steps = list(range(bits - 3, 0, -1))
+    while fresh or sides:
+        along = [flipped(part, 1 << steps[0]) for part in line] if steps else []
+        steps = steps[1:]
+        first = [flipped(part, one) for part in fresh]
+        corner = [flipped(b, one) for i, (a, b) in enumerate(sides) if i % 2 == 0]
+        second = [flipped(part, two) for part in fresh]
+        corner += [flipped(a, two) for i, (a, b) in enumerate(sides) if i % 2 == 1]
+        acc = attend(ready, acc, False)
+        acc, along, first, second = lax.optimization_barrier((acc, along, first, second))
+        ready = along + first + second + corner
+        line, fresh, sides = line + along, along, list(zip(first, second))
+    mine, theirs = attend(ready, acc, True)
     other_heads = flipped(theirs, 1)
 
     back = pl.pallas_call(

time: 113 us -> 95.2 us (0.84)
  waiting for transfers between devices: 52 us -> 37.6 us
  Pallas kernels: 39.5 us -> 27.7 us
  starting transfers between devices: 16.9 us -> 25.1 us
    ppermute x8 -> x17, waiting for transfers between devices: 20.3 us -> 5.93 us  [flipped(): return lax.ppermute(value, AXES, [(i, i ^ mask) for i in range(devices)])]
    pallas_call x5, Pallas kernels: 31.2 us -> 19.2 us  [attend(): pl.pallas_call(functools.partial(attend_kernel, len(parts), acc is None,...]
    ppermute x8 -> x17, starting transfers between devices: 7 us -> 14.4 us  [flipped(): return lax.ppermute(value, AXES, [(i, i ^ mask) for i in range(devices)])]
  transfers between devices with their start and end apart: 10 -> 19, of which waited for: 7 -> 5; matrix products, arithmetic and copies ran while one was open for 1% -> 1% of each run, Pallas kernels for 21% -> 18%
where the time goes in v2:
time: 95.2 us; the launch traced here: 94.5 us
  waiting for transfers between devices  37.6 us (39%)
  Pallas kernels  27.7 us (29%)
  starting transfers between devices  25.1 us (26%)
  local copies, waits for them, and re-layouts  3.46 us (4%)
    pallas_call x5, Pallas kernels, attend(): pl.pallas_call(functools.partial(attend_kernel, len(parts), acc is None,...  19.2 us
    all_to_all x1, waiting for transfers between devices, local(): lax.all_to_all(back.reshape(devices, tile, width), AXES, split_axis=0, co...  15.9 us
    all_to_all x1, waiting for transfers between devices, local(): got = lax.all_to_all(payload, AXES, split_axis=0, concat_axis=0, tiled=True)  15.8 us
    ppermute x17, starting transfers between devices, flipped(): return lax.ppermute(value, AXES, [(i, i ^ mask) for i in range(devices)])  14.4 us
    all_to_all x1, starting transfers between devices, local(): got = lax.all_to_all(payload, AXES, split_axis=0, concat_axis=0, tiled=True)  7.1 us
    ppermute x17, waiting for transfers between devices, flipped(): return lax.ppermute(value, AXES, [(i, i ^ mask) for i in range(devices)])  5.93 us
    all_to_all x1, starting transfers between devices, local(): lax.all_to_all(back.reshape(devices, tile, width), AXES, split_axis=0, co...  3.62 us
    pallas_call x1, Pallas kernels, local(): pl.pallas_call(functools.partial(pool_kernel, tile), out_shape=(jax.Shape...  3.01 us
  transfers between devices with their start and end apart: 19, of which 5 were waited for; matrix products, arithmetic and copies ran while one was open for 1% of the time, Pallas kernels for 18%

profile of v2, /device:TPU:1, one launch (start us, length us, event | category | flops | bytes accessed | tf_op | source)
XLA Modules:
  0.0 94.5 jit_solution(5944254185389401373)
XLA Ops:
  0.0 1.0 %copy-done = bf16[512,512]{1,0:T(8,128)(2,1)S(1)} copy-done((bf16[512,512]{1,0:T(8,128)(2,1)S(1)}, bf16[512,512]{1,0:T(8,128)(2,1)}, u32[]{:S(2)}) %copy-start) | copy-done | bytes 524312
  1.0 0.7 copy-done.7
  1.7 0.9 pack.1
  2.6 7.1 %all-to-all-start = ((bf16[32,72,128]{2,1,0:T(8,128)(2,1)}), bf16[32,72,128]{2,1,0:T(8,128)(2,1)S(1)}, u32[]{:S(2)}, u32[]{:S(2)}) async-start(bf16[32,72,128]{2,1,0:T(8,128)(2,1)} %pack.1), calls=%async_computation | async-start | bytes 1179648 | tf_op jit(solution)/shard_map/all_to_all | solution.py:220
  9.7 0.2 copy.17
  10.0 0.0 copy-start.13
  10.0 0.0 copy-start.14
  10.0 0.1 pad.4
  10.1 0.0 copy-start.15
  10.1 0.0 copy-start.9
  10.1 0.5 copy.24.w_q_ref
  10.6 0.2 copy-done.13
  10.9 0.1 copy.19
  11.0 0.1 copy.20
  11.2 0.1 copy.22.w_kv_ref
  11.3 15.8 %all-to-all-done.got_ref = bf16[32,72,128]{2,1,0:T(8,128)(2,1)S(1)} async-done(((bf16[32,72,128]{2,1,0:T(8,128)(2,1)}), bf16[32,72,128]{2,1,0:T(8,128)(2,1)S(1)}, u32[]{:S(2)}, u32[]{:S(2)}) %all-to-all-start) | async-done | bytes 589856 | tf_op jit(solution)/shard_map/all_to_all | solution.py:220
  27.1 0.1 broadcast_in_dim.3
  27.2 3.0 %pool.1 = (f32[256,512]{1,0:T(8,128)S(1)}, bf16[256,512]{1,0:T(8,128)(2,1)S(1)}, bf16[256,640]{1,0:T(8,128)(2,1)S(1)}, bf16[256,640]{1,0:T(8,128)(2,1)S(1)}) custom-call(s32[1]{0:T(128)S(6)} %rem.18.core_ref, bf16[32,72,128]{2,1,0:T(8,128)(2,1)S(1)} %all-to-all-done.got_ref, bf16[512,1024]{1,0:T(8,128)(2,1)S(1)} %copy.24.w_q_ref, ...), custom_call_target="tpu_custom_call" | custom-call | tf_op jit(solution)/shard_map/pool/pallas_call | solution.py:231
  30.2 0.7 collective-permute-start
  30.9 1.2 %collective-permute-done.refs_1_ = bf16[256,640]{1,0:T(8,128)(2,1)S(1)} collective-permute-done((bf16[256,640]{1,0:T(8,128)(2,1)S(1)}, bf16[256,640]{1,0:T(8,128)(2,1)S(1)}, u32[]{:S(2)}, u32[]{:S(2)}) %collective-permute-start) | collective-permute-done | bytes 327712 | tf_op jit(solution)/shard_map/ppermute | solution.py:210
  32.2 0.1 collective-permute-start.1
  32.3 0.5 collective-permute-start.2
  32.8 0.4 collective-permute-start.3
  33.2 1.5 %collective-permute-start.4 = (bf16[512,128]{1,0:T(8,128)(2,1)S(1)}, bf16[512,128]{1,0:T(8,128)(2,1)S(1)}, u32[]{:S(2)}, u32[]{:S(2)}) collective-permute-start(bf16[512,128]{1,0:T(8,128)(2,1)S(1)} %pad_maximum_fusion.1.refs_2_), channel_id=1, source_target_pairs={{0,2},{1,3},{2,0},{3,1},{4,6},{5,7},{6,4},{7,5},{8,10},{9,11},{10,... | collective-permute-start | bytes 393224 | tf_op jit(solution)/shard_map/ppermute | solution.py:210
  34.7 1.9 %attend.5.refs_5_ = f32[2,4,256,128]{3,2,1,0:T(8,128)S(1)} custom-call(bf16[256,640]{1,0:T(8,128)(2,1)S(1)} %get-tuple-element.25.refs_0_, bf16[256,640]{1,0:T(8,128)(2,1)S(1)} %collective-permute-done.refs_1_, bf16[512,128]{1,0:T(8,128)(2,1)S(1)} %pad_maximum_fusion.1.refs_2_), custom_call_target="tpu_custom_call" | custom-call | flops 1073741824 | bytes 131072 | tf_op jit(solution)/shard_map/attend/pallas_call | solution.py:251
  36.6 3.7 %collective-permute-done.1.refs_2_ = bf16[512,128]{1,0:T(8,128)(2,1)S(1)} collective-permute-done((bf16[512,128]{1,0:T(8,128)(2,1)S(1)}, bf16[512,128]{1,0:T(8,128)(2,1)S(1)}, u32[]{:S(2)}, u32[]{:S(2)}) %collective-permute-start.1) | collective-permute-done | bytes 131104 | tf_op jit(solution)/shard_map/ppermute | solution.py:210
  40.3 0.0 collective-permute-done.2.refs_3_
  40.3 0.0 collective-permute-done.3.refs_4_
  40.3 1.1 %collective-permute-start.6 = (bf16[512,128]{1,0:T(8,128)(2,1)S(1)}, bf16[512,128]{1,0:T(8,128)(2,1)S(1)}, u32[]{:S(2)}, u32[]{:S(2)}) collective-permute-start(bf16[512,128]{1,0:T(8,128)(2,1)S(1)} %collective-permute-done.1.refs_2_), channel_id=1, source_target_pairs={{0,8},{1,9},{2,10},{3,11},{4,12},{5,13},{6,14},{7,15},{8,0},{9,1},... | collective-permute-start | bytes 393224 | tf_op jit(solution)/shard_map/ppermute | solution.py:210
  41.4 0.4 collective-permute-start.7
  41.9 1.0 %collective-permute-start.8 = (bf16[512,128]{1,0:T(8,128)(2,1)S(1)}, bf16[512,128]{1,0:T(8,128)(2,1)S(1)}, u32[]{:S(2)}, u32[]{:S(2)}) collective-permute-start(bf16[512,128]{1,0:T(8,128)(2,1)S(1)} %collective-permute-done.3.refs_4_), channel_id=1, source_target_pairs={{0,8},{1,9},{2,10},{3,11},{4,12},{5,13},{6,14},{7,15},{8,0},{9,1},... | collective-permute-start | bytes 393224 | tf_op jit(solution)/shard_map/ppermute | solution.py:210
  42.9 3.5 %attend.6.refs_7_ = f32[2,4,256,128]{3,2,1,0:T(8,128)S(1)} custom-call(bf16[256,640]{1,0:T(8,128)(2,1)S(1)} %get-tuple-element.25.refs_0_, bf16[256,640]{1,0:T(8,128)(2,1)S(1)} %collective-permute-done.refs_1_, bf16[512,128]{1,0:T(8,128)(2,1)S(1)} %collective-permute-done.1.refs_2_, bf16[512,128]{1,0:T(8,128)(2,1)S(1)} %collective-permute-done.2.refs_3_, ...), custom_call_target="tpu_custom_call" | custom-call | flops 3221225472 | bytes 393216 | tf_op jit(solution)/shard_map/attend/pallas_call | solution.py:251
  46.4 0.0 collective-permute-done.4.refs_2_
  46.4 0.0 collective-permute-done.7.refs_5_
  46.4 0.5 collective-permute-start.10
  46.9 1.0 %collective-permute-start.12 = (bf16[512,128]{1,0:T(8,128)(2,1)S(1)}, bf16[512,128]{1,0:T(8,128)(2,1)S(1)}, u32[]{:S(2)}, u32[]{:S(2)}) collective-permute-start(bf16[512,128]{1,0:T(8,128)(2,1)S(1)} %collective-permute-done.5.refs_3_), channel_id=1, source_target_pairs={{0,16},{1,17},{2,18},{3,19},{4,20},{5,21},{6,22},{7,23},{8,24},{9,... | collective-permute-start | bytes 393224 | tf_op jit(solution)/shard_map/ppermute | solution.py:210
  47.9 0.4 collective-permute-start.11
  48.4 1.0 %collective-permute-start.9 = (bf16[512,128]{1,0:T(8,128)(2,1)S(1)}, bf16[512,128]{1,0:T(8,128)(2,1)S(1)}, u32[]{:S(2)}, u32[]{:S(2)}) collective-permute-start(bf16[512,128]{1,0:T(8,128)(2,1)S(1)} %collective-permute-done.4.refs_2_), channel_id=1, source_target_pairs={{0,8},{1,9},{2,10},{3,11},{4,12},{5,13},{6,14},{7,15},{8,0},{9,1},... | collective-permute-start | bytes 393224 | tf_op jit(solution)/shard_map/ppermute | solution.py:210
  49.4 0.4 collective-permute-start.15
  49.9 5.7 %attend.7.refs_7_ = f32[2,4,256,128]{3,2,1,0:T(8,128)S(1)} custom-call(bf16[256,640]{1,0:T(8,128)(2,1)S(1)} %get-tuple-element.25.refs_0_, bf16[256,640]{1,0:T(8,128)(2,1)S(1)} %collective-permute-done.refs_1_, bf16[512,128]{1,0:T(8,128)(2,1)S(1)} %collective-permute-done.4.refs_2_, bf16[512,128]{1,0:T(8,128)(2,1)S(1)} %collective-permute-done.5.refs_3_, ...), custom_call_target="tpu_custom_call" | custom-call | flops 5368709120 | bytes 655360 | tf_op jit(solution)/shard_map/attend/pallas_call | solution.py:251
  55.5 0.0 collective-permute-done.10.refs_3_
  55.5 0.0 collective-permute-done.11.refs_4_
  55.5 0.0 collective-permute-done.9.refs_2_
  55.6 1.3 %collective-permute-start.13 = (bf16[512,128]{1,0:T(8,128)(2,1)S(1)}, bf16[512,128]{1,0:T(8,128)(2,1)S(1)}, u32[]{:S(2)}, u32[]{:S(2)}) collective-permute-start(bf16[512,128]{1,0:T(8,128)(2,1)S(1)} %collective-permute-done.11.refs_4_), channel_id=1, source_target_pairs={{0,8},{1,9},{2,10},{3,11},{4,12},{5,13},{6,14},{7,15},{8,0},{9,1},... | collective-permute-start | bytes 393224 | tf_op jit(solution)/shard_map/ppermute | solution.py:210
  56.9 0.4 collective-permute-start.14
  57.3 5.7 %attend.8.refs_4_ = f32[2,4,256,128]{3,2,1,0:T(8,128)S(1)} custom-call(bf16[256,640]{1,0:T(8,128)(2,1)S(1)} %get-tuple-element.25.refs_0_, bf16[256,640]{1,0:T(8,128)(2,1)S(1)} %collective-permute-done.refs_1_, bf16[512,128]{1,0:T(8,128)(2,1)S(1)} %collective-permute-done.9.refs_2_, bf16[512,128]{1,0:T(8,128)(2,1)S(1)} %collective-permute-done.10.refs_3_, ...), custom_call_target="tpu_custom_call" | custom-call | flops 5368709120 | bytes 655360 | tf_op jit(solution)/shard_map/attend/pallas_call | solution.py:251
  62.9 0.0 copy-start.2
  62.9 0.0 copy-start.3
  62.9 0.0 copy-start.4
  63.0 0.0 copy-start.10
  63.0 0.0 collective-permute-done.13.refs_2_
  63.0 2.5 %attend.9 = (bf16[256,256]{1,0:T(8,128)(2,1)S(1)}, bf16[256,256]{1,0:T(8,128)(2,1)S(1)}) custom-call(bf16[256,640]{1,0:T(8,128)(2,1)S(1)} %get-tuple-element.25.refs_0_, bf16[256,640]{1,0:T(8,128)(2,1)S(1)} %collective-permute-done.refs_1_, bf16[512,128]{1,0:T(8,128)(2,1)S(1)} %collective-permute-done.13.refs_2_, ...), custom_call_target="tpu_custom_call" | custom-call | flops 2147483648 | bytes 262144 | tf_op jit(solution)/shard_map/attend/pallas_call | solution.py:251
  65.5 3.5 %collective-permute-start.16 = (bf16[256,256]{1,0:T(8,128)(2,1)S(1)}, bf16[256,256]{1,0:T(8,128)(2,1)S(1)}, u32[]{:S(2)}, u32[]{:S(2)}) collective-permute-start(bf16[256,256]{1,0:T(8,128)(2,1)S(1)} %get-tuple-element.42), channel_id=1, source_target_pairs={{0,1},{1,0},{2,3},{3,2},{4,5},{5,4},{6,7},{7,6},{8,9},{9,8},{10,11... | collective-permute-start | bytes 393224 | tf_op jit(solution)/shard_map/ppermute | solution.py:210
  69.0 1.0 %collective-permute-done.16.other_ref = bf16[256,256]{1,0:T(8,128)(2,1)S(1)} collective-permute-done((bf16[256,256]{1,0:T(8,128)(2,1)S(1)}, bf16[256,256]{1,0:T(8,128)(2,1)S(1)}, u32[]{:S(2)}, u32[]{:S(2)}) %collective-permute-start.16) | collective-permute-done | bytes 131104 | tf_op jit(solution)/shard_map/ppermute | solution.py:210
  70.0 0.0 copy-start.8
  70.0 0.0 copy-start.1
  70.0 0.0 copy-start.5
  70.0 0.0 copy-start.6
  70.0 0.0 copy-start.11
  70.1 2.8 %post.1 = bf16[512,512]{1,0:T(8,128)(2,1)} custom-call(s32[1]{0:T(128)S(6)} %rem.18.core_ref, bf16[256,256]{1,0:T(8,128)(2,1)S(1)} %get-tuple-element.41.mine_ref, bf16[256,256]{1,0:T(8,128)(2,1)S(1)} %collective-permute-done.16.other_ref, f32[256,512]{1,0:T(8,128)S(1)} %get-tuple-element.43.pooled_ref, bf16[256,512]{1,0:T(8,128)(2,1)S(1)} %get-tuple-element.44.member_ref, ...), custom_call_target="tpu_custom_call" | custom-call | tf_op jit(solution)/shard_map/post/pallas_call | solution.py:283
  72.9 3.6 %all-to-all-start.1 = ((bf16[32,16,512]{2,1,0:T(8,128)(2,1)}), bf16[32,16,512]{2,1,0:T(8,128)(2,1)S(1)}, u32[]{:S(2)}, u32[]{:S(2)}) async-start(bf16[32,16,512]{2,1,0:T(8,128)(2,1)} %bitcast.10), calls=%async_computation.1 | async-start | bytes 1048576 | tf_op jit(solution)/shard_map/all_to_all | solution.py:291
  76.5 0.1 copy.23.live_ref
  76.7 15.9 %all-to-all-done.1 = bf16[32,16,512]{2,1,0:T(8,128)(2,1)S(1)} async-done(((bf16[32,16,512]{2,1,0:T(8,128)(2,1)}), bf16[32,16,512]{2,1,0:T(8,128)(2,1)S(1)}, u32[]{:S(2)}, u32[]{:S(2)}) %all-to-all-start.1) | async-done | bytes 524320 | tf_op jit(solution)/shard_map/all_to_all | solution.py:291
  92.6 1.8 %decode.1 = bf16[512,512]{1,0:T(8,128)(2,1)} custom-call(bf16[512,512]{1,0:T(8,128)(2,1)S(1)} %bitcast.14, bf16[512,512]{1,0:T(8,128)(2,1)S(1)} %copy-done.1, f32[512,1]{1,0:T(8,128)S(1)} %copy.23.live_ref, f32[1,512]{1,0:T(1,128)S(1)} %bitcast.19, bf16[512,512]{1,0:T(8,128)(2,1)S(1)} %copy-done.5, bf16[512,512]{1,0:T(8,128)(2,1)S(1)} %copy-done.6), custom_call_target="tpu_custom_call" | custom-call | tf_op jit(solution)/shard_map/decode/pallas_call | solution.py:298
  (30 shorter events, 0.1 us)
Async XLA Ops:
  0.0 1.0 %copy-start = (bf16[512,512]{1,0:T(8,128)(2,1)S(1)}, bf16[512,512]{1,0:T(8,128)(2,1)}, u32[]{:S(2)}) copy-start(bf16[512,512]{1,0:T(8,128)(2,1)} %sensors_ref.3) | copy-start | bytes 1572868
  1.0 0.7 copy-start.7
  1.7 8.0 %copy-start.12 = (bf16[512,512]{1,0:T(8,128)(2,1)S(1)}, bf16[512,512]{1,0:T(8,128)(2,1)}, u32[]{:S(2)}) copy-start(bf16[512,512]{1,0:T(8,128)(2,1)} %param.16) | copy-start | bytes 1572868
  2.6 24.5 %all-to-all-start = ((bf16[32,72,128]{2,1,0:T(8,128)(2,1)}), bf16[32,72,128]{2,1,0:T(8,128)(2,1)S(1)}, u32[]{:S(2)}, u32[]{:S(2)}) async-start(bf16[32,72,128]{2,1,0:T(8,128)(2,1)} %pack.1), calls=%async_computation | async-start | bytes 1179648 | tf_op jit(solution)/shard_map/all_to_all | solution.py:220
  10.0 0.9 copy-start.13
  10.0 1.0 %copy-start.14 = (bf16[512,128]{1,0:T(8,128)(2,1)S(1)}, bf16[512,128]{1,0:T(8,128)(2,1)}, u32[]{:S(2)}) copy-start(bf16[512,128]{1,0:T(8,128)(2,1)} %param.18) | copy-start | bytes 393220
  10.1 1.2 %copy-start.15 = (f32[8]{0:T(128)S(1)}, f32[8]{0:T(128)}, u32[]{:S(2)}) copy-start(f32[8]{0:T(128)} %param.20) | copy-start | bytes 100
  10.1 17.1 %copy-start.9 = (f32[512]{0:T(512)S(1)}, f32[512]{0:T(512)}, u32[]{:S(2)}) copy-start(f32[512]{0:T(512)} %param.21) | copy-start | bytes 6148
  30.2 2.0 %collective-permute-start = (bf16[256,640]{1,0:T(8,128)(2,1)S(1)}, bf16[256,640]{1,0:T(8,128)(2,1)S(1)}, u32[]{:S(2)}, u32[]{:S(2)}) collective-permute-start(bf16[256,640]{1,0:T(8,128)(2,1)S(1)} %get-tuple-element.26), channel_id=1, source_target_pairs={{0,1},{1,0},{2,3},{3,2},{4,5},{5,4},{6,7},{7,6},{8,9},{9,8},{10,11... | collective-permute-start | bytes 983048 | tf_op jit(solution)/shard_map/ppermute | solution.py:210
  32.2 8.1 %collective-permute-start.1 = (bf16[512,128]{1,0:T(8,128)(2,1)S(1)}, bf16[512,128]{1,0:T(8,128)(2,1)S(1)}, u32[]{:S(2)}, u32[]{:S(2)}) collective-permute-start(bf16[512,128]{1,0:T(8,128)(2,1)S(1)} %pad_maximum_fusion.1.refs_2_), channel_id=1, source_target_pairs={{0,4},{1,5},{2,6},{3,7},{4,0},{5,1},{6,2},{7,3},{8,12},{9,13},{10,... | collective-permute-start | bytes 393224 | tf_op jit(solution)/shard_map/ppermute | solution.py:210
  32.3 8.0 %collective-permute-start.2 = (bf16[512,128]{1,0:T(8,128)(2,1)S(1)}, bf16[512,128]{1,0:T(8,128)(2,1)S(1)}, u32[]{:S(2)}, u32[]{:S(2)}) collective-permute-start(bf16[512,128]{1,0:T(8,128)(2,1)S(1)} %pad_maximum_fusion.1.refs_2_), channel_id=1, source_target_pairs={{0,8},{1,9},{2,10},{3,11},{4,12},{5,13},{6,14},{7,15},{8,0},{9,1},... | collective-permute-start | bytes 393224 | tf_op jit(solution)/shard_map/ppermute | solution.py:210
  32.8 7.5 %collective-permute-start.3 = (bf16[512,128]{1,0:T(8,128)(2,1)S(1)}, bf16[512,128]{1,0:T(8,128)(2,1)S(1)}, u32[]{:S(2)}, u32[]{:S(2)}) collective-permute-start(bf16[512,128]{1,0:T(8,128)(2,1)S(1)} %pad_maximum_fusion.1.refs_2_), channel_id=1, source_target_pairs={{0,16},{1,17},{2,18},{3,19},{4,20},{5,21},{6,22},{7,23},{8,24},{9,... | collective-permute-start | bytes 393224 | tf_op jit(solution)/shard_map/ppermute | solution.py:210
  33.2 13.2 %collective-permute-start.4 = (bf16[512,128]{1,0:T(8,128)(2,1)S(1)}, bf16[512,128]{1,0:T(8,128)(2,1)S(1)}, u32[]{:S(2)}, u32[]{:S(2)}) collective-permute-start(bf16[512,128]{1,0:T(8,128)(2,1)S(1)} %pad_maximum_fusion.1.refs_2_), channel_id=1, source_target_pairs={{0,2},{1,3},{2,0},{3,1},{4,6},{5,7},{6,4},{7,5},{8,10},{9,11},{10,... | collective-permute-start | bytes 393224 | tf_op jit(solution)/shard_map/ppermute | solution.py:210
  40.3 6.1 %collective-permute-start.5 = (bf16[512,128]{1,0:T(8,128)(2,1)S(1)}, bf16[512,128]{1,0:T(8,128)(2,1)S(1)}, u32[]{:S(2)}, u32[]{:S(2)}) collective-permute-start(bf16[512,128]{1,0:T(8,128)(2,1)S(1)} %collective-permute-done.1.refs_2_), channel_id=1, source_target_pairs={{0,2},{1,3},{2,0},{3,1},{4,6},{5,7},{6,4},{7,5},{8,10},{9,11},{10,... | collective-permute-start | bytes 393224 | tf_op jit(solution)/shard_map/ppermute | solution.py:210
  40.3 6.1 %collective-permute-start.6 = (bf16[512,128]{1,0:T(8,128)(2,1)S(1)}, bf16[512,128]{1,0:T(8,128)(2,1)S(1)}, u32[]{:S(2)}, u32[]{:S(2)}) collective-permute-start(bf16[512,128]{1,0:T(8,128)(2,1)S(1)} %collective-permute-done.1.refs_2_), channel_id=1, source_target_pairs={{0,8},{1,9},{2,10},{3,11},{4,12},{5,13},{6,14},{7,15},{8,0},{9,1},... | collective-permute-start | bytes 393224 | tf_op jit(solution)/shard_map/ppermute | solution.py:210
  41.4 5.0 %collective-permute-start.7 = (bf16[512,128]{1,0:T(8,128)(2,1)S(1)}, bf16[512,128]{1,0:T(8,128)(2,1)S(1)}, u32[]{:S(2)}, u32[]{:S(2)}) collective-permute-start(bf16[512,128]{1,0:T(8,128)(2,1)S(1)} %collective-permute-done.1.refs_2_), channel_id=1, source_target_pairs={{0,16},{1,17},{2,18},{3,19},{4,20},{5,21},{6,22},{7,23},{8,24},{9,... | collective-permute-start | bytes 393224 | tf_op jit(solution)/shard_map/ppermute | solution.py:210
  41.9 7.6 %collective-permute-start.8 = (bf16[512,128]{1,0:T(8,128)(2,1)S(1)}, bf16[512,128]{1,0:T(8,128)(2,1)S(1)}, u32[]{:S(2)}, u32[]{:S(2)}) collective-permute-start(bf16[512,128]{1,0:T(8,128)(2,1)S(1)} %collective-permute-done.3.refs_4_), channel_id=1, source_target_pairs={{0,8},{1,9},{2,10},{3,11},{4,12},{5,13},{6,14},{7,15},{8,0},{9,1},... | collective-permute-start | bytes 393224 | tf_op jit(solution)/shard_map/ppermute | solution.py:210
  46.4 9.1 %collective-permute-start.10 = (bf16[512,128]{1,0:T(8,128)(2,1)S(1)}, bf16[512,128]{1,0:T(8,128)(2,1)S(1)}, u32[]{:S(2)}, u32[]{:S(2)}) collective-permute-start(bf16[512,128]{1,0:T(8,128)(2,1)S(1)} %collective-permute-done.5.refs_3_), channel_id=1, source_target_pairs={{0,8},{1,9},{2,10},{3,11},{4,12},{5,13},{6,14},{7,15},{8,0},{9,1},... | collective-permute-start | bytes 393224 | tf_op jit(solution)/shard_map/ppermute | solution.py:210
  46.9 8.6 %collective-permute-start.12 = (bf16[512,128]{1,0:T(8,128)(2,1)S(1)}, bf16[512,128]{1,0:T(8,128)(2,1)S(1)}, u32[]{:S(2)}, u32[]{:S(2)}) collective-permute-start(bf16[512,128]{1,0:T(8,128)(2,1)S(1)} %collective-permute-done.5.refs_3_), channel_id=1, source_target_pairs={{0,16},{1,17},{2,18},{3,19},{4,20},{5,21},{6,22},{7,23},{8,24},{9,... | collective-permute-start | bytes 393224 | tf_op jit(solution)/shard_map/ppermute | solution.py:210
  47.9 7.6 %collective-permute-start.11 = (bf16[512,128]{1,0:T(8,128)(2,1)S(1)}, bf16[512,128]{1,0:T(8,128)(2,1)S(1)}, u32[]{:S(2)}, u32[]{:S(2)}) collective-permute-start(bf16[512,128]{1,0:T(8,128)(2,1)S(1)} %collective-permute-done.4.refs_2_), channel_id=1, source_target_pairs={{0,16},{1,17},{2,18},{3,19},{4,20},{5,21},{6,22},{7,23},{8,24},{9,... | collective-permute-start | bytes 393224 | tf_op jit(solution)/shard_map/ppermute | solution.py:210
  48.4 7.2 %collective-permute-start.9 = (bf16[512,128]{1,0:T(8,128)(2,1)S(1)}, bf16[512,128]{1,0:T(8,128)(2,1)S(1)}, u32[]{:S(2)}, u32[]{:S(2)}) collective-permute-start(bf16[512,128]{1,0:T(8,128)(2,1)S(1)} %collective-permute-done.4.refs_2_), channel_id=1, source_target_pairs={{0,8},{1,9},{2,10},{3,11},{4,12},{5,13},{6,14},{7,15},{8,0},{9,1},... | collective-permute-start | bytes 393224 | tf_op jit(solution)/shard_map/ppermute | solution.py:210
  49.4 7.8 %collective-permute-start.15 = (bf16[512,128]{1,0:T(8,128)(2,1)S(1)}, bf16[512,128]{1,0:T(8,128)(2,1)S(1)}, u32[]{:S(2)}, u32[]{:S(2)}) collective-permute-start(bf16[512,128]{1,0:T(8,128)(2,1)S(1)} %collective-permute-done.7.refs_5_), channel_id=1, source_target_pairs={{0,8},{1,9},{2,10},{3,11},{4,12},{5,13},{6,14},{7,15},{8,0},{9,1},... | collective-permute-start | bytes 393224 | tf_op jit(solution)/shard_map/ppermute | solution.py:210
  55.6 7.4 %collective-permute-start.13 = (bf16[512,128]{1,0:T(8,128)(2,1)S(1)}, bf16[512,128]{1,0:T(8,128)(2,1)S(1)}, u32[]{:S(2)}, u32[]{:S(2)}) collective-permute-start(bf16[512,128]{1,0:T(8,128)(2,1)S(1)} %collective-permute-done.11.refs_4_), channel_id=1, source_target_pairs={{0,8},{1,9},{2,10},{3,11},{4,12},{5,13},{6,14},{7,15},{8,0},{9,1},... | collective-permute-start | bytes 393224 | tf_op jit(solution)/shard_map/ppermute | solution.py:210
  56.9 6.1 %collective-permute-start.14 = (bf16[512,128]{1,0:T(8,128)(2,1)S(1)}, bf16[512,128]{1,0:T(8,128)(2,1)S(1)}, u32[]{:S(2)}, u32[]{:S(2)}) collective-permute-start(bf16[512,128]{1,0:T(8,128)(2,1)S(1)} %collective-permute-done.10.refs_3_), channel_id=1, source_target_pairs={{0,16},{1,17},{2,18},{3,19},{4,20},{5,21},{6,22},{7,23},{8,24},{9,... | collective-permute-start | bytes 393224 | tf_op jit(solution)/shard_map/ppermute | solution.py:210
  62.9 7.1 %copy-start.2 = (bf16[512,2048]{1,0:T(8,128)(2,1)S(1)}, bf16[512,2048]{1,0:T(8,128)(2,1)}, u32[]{:S(2)}) copy-start(bf16[512,2048]{1,0:T(8,128)(2,1)} %w_inner_ref.1) | copy-start | bytes 6291460
  62.9 7.1 %copy-start.3 = (bf16[2048,512]{1,0:T(8,128)(2,1)S(1)}, bf16[2048,512]{1,0:T(8,128)(2,1)}, u32[]{:S(2)}) copy-start(bf16[2048,512]{1,0:T(8,128)(2,1)} %w_outer_ref.1) | copy-start | bytes 6291460
  62.9 7.0 %copy-start.4 = (bf16[512,512]{1,0:T(8,128)(2,1)S(1)}, bf16[512,512]{1,0:T(8,128)(2,1)}, u32[]{:S(2)}) copy-start(bf16[512,512]{1,0:T(8,128)(2,1)} %w_out_ref.2) | copy-start | bytes 1572868
  63.0 7.0 %copy-start.10 = (f32[512]{0:T(512)S(1)}, f32[512]{0:T(512)}, u32[]{:S(2)}) copy-start(f32[512]{0:T(512)} %param.24) | copy-start | bytes 6148
  65.5 4.5 %collective-permute-start.16 = (bf16[256,256]{1,0:T(8,128)(2,1)S(1)}, bf16[256,256]{1,0:T(8,128)(2,1)S(1)}, u32[]{:S(2)}, u32[]{:S(2)}) collective-permute-start(bf16[256,256]{1,0:T(8,128)(2,1)S(1)} %get-tuple-element.42), channel_id=1, source_target_pairs={{0,1},{1,0},{2,3},{3,2},{4,5},{5,4},{6,7},{7,6},{8,9},{9,8},{10,11... | collective-permute-start | bytes 393224 | tf_op jit(solution)/shard_map/ppermute | solution.py:210
  70.0 6.5 %copy-start.8 = (s32[512]{0:T(512)S(1)}, s32[512]{0:T(512)}, u32[]{:S(2)}) copy-start(s32[512]{0:T(512)} %param.15) | copy-start | bytes 6148
  70.0 22.6 %copy-start.1 = (bf16[512,512]{1,0:T(8,128)(2,1)S(1)}, bf16[512,512]{1,0:T(8,128)(2,1)}, u32[]{:S(2)}) copy-start(bf16[512,512]{1,0:T(8,128)(2,1)} %sensors_ref.3) | copy-start | bytes 1572868
  70.0 22.6 %copy-start.5 = (bf16[512,512]{1,0:T(8,128)(2,1)S(1)}, bf16[512,512]{1,0:T(8,128)(2,1)}, u32[]{:S(2)}) copy-start(bf16[512,512]{1,0:T(8,128)(2,1)} %w_in_ref.1) | copy-start | bytes 1572868
  70.0 22.6 %copy-start.6 = (bf16[512,512]{1,0:T(8,128)(2,1)S(1)}, bf16[512,512]{1,0:T(8,128)(2,1)}, u32[]{:S(2)}) copy-start(bf16[512,512]{1,0:T(8,128)(2,1)} %w_out_ref.3) | copy-start | bytes 1572868
  70.0 22.6 %copy-start.11 = (f32[512]{0:T(512)S(1)}, f32[512]{0:T(512)}, u32[]{:S(2)}) copy-start(f32[512]{0:T(512)} %param.25) | copy-start | bytes 6148
  72.9 19.7 %all-to-all-start.1 = ((bf16[32,16,512]{2,1,0:T(8,128)(2,1)}), bf16[32,16,512]{2,1,0:T(8,128)(2,1)S(1)}, u32[]{:S(2)}, u32[]{:S(2)}) async-start(bf16[32,16,512]{2,1,0:T(8,128)(2,1)} %bitcast.10), calls=%async_computation.1 | async-start | bytes 1048576 | tf_op jit(solution)/shard_map/all_to_all | solution.py:291

commit v3 on v2

v3 whole, which is shorter than its diff:
```python
import functools
import math

import jax
import jax.numpy as jnp
from jax import lax
from jax.experimental import pallas as pl
from jax.experimental.pallas import tpu as pltpu
from jax.sharding import PartitionSpec as P

HEADS = 8
HEAD_DIM = 64
KV_HEADS = 2
GROUP = HEADS // KV_HEADS
REG_DEV = 256
LANES = 128
EPS = 1e-06
AXES = ("seq", "dp")
F32 = jnp.float32
BF16 = jnp.bfloat16
NT = (((1,), (1,)), ((), ()))
TN = (((0,), (0,)), ((), ()))

VMEM = pl.BlockSpec(memory_space=pltpu.VMEM)
SMEM = pl.BlockSpec(memory_space=pltpu.SMEM)
PARAMS = pltpu.CompilerParams(vmem_limit_bytes=40 * 1024 * 1024)


def mm(a, b):
    return jnp.dot(a, b, preferred_element_type=F32)


def rms(values):
    return values * lax.rsqrt(jnp.mean(values * values, axis=-1, keepdims=True) + EPS)


def pack_kernel(tile, me_ref, sensors_ref, labels_ref, out_ref):
    per_row = LANES // tile
    blocks = sensors_ref.shape[1] // LANES
    tiles = out_ref.shape[0]
    mine = lax.rem(me_ref[0], per_row)
    labels = (labels_ref[...] + 1).astype(F32)
    lane = lax.broadcasted_iota(jnp.int32, labels.shape, 1)
    own_lanes = (lane // tile) == mine
    for k in range(per_row):
        shift = lax.rem(mine - k + per_row, per_row) * tile
        rolled = jnp.where(own_lanes, pltpu.roll(labels, shift, 1), 0.0)
        for g in range(tiles // per_row):
            t = g * per_row + k
            row = jnp.broadcast_to(rolled[g : g + 1, :], (8, LANES)).astype(BF16)
            rows = sensors_ref[t * tile : (t + 1) * tile, :]
            parts = [rows[:, c * LANES : (c + 1) * LANES] for c in range(blocks)]
            out_ref[t] = jnp.concatenate(parts + [row], axis=0)


def by_heads():
    at = lax.broadcasted_iota(jnp.int32, (LANES, LANES), 0) // HEAD_DIM
    to = lax.broadcasted_iota(jnp.int32, (LANES, LANES), 1) // HEAD_DIM
    return jnp.where(at == to, 1.0 / HEAD_DIM, 0.0).astype(BF16)


def low_lanes(rows):
    return lax.broadcasted_iota(jnp.int32, (rows, LANES), 1) < HEAD_DIM


def pool_kernel(
    tile, core_ref, got_ref, w_key_ref, w_value_ref, gain_ref, pooled_ref, member_ref, attn_in_ref, keep_ref, send_ref
):
    tiles, _, _ = got_ref.shape
    per_row = LANES // tile
    width = pooled_ref.shape[1]
    blocks = width // LANES
    slots = tiles * tile
    regions = lax.broadcasted_iota(jnp.int32, (REG_DEV, LANES), 0).astype(F32) + 1.0
    hits = jnp.zeros((REG_DEV, LANES), F32)
    for g in range(tiles // per_row):
        row = got_ref[g * per_row, tile * blocks : tile * blocks + 8, :].astype(F32)
        for k in range(1, per_row):
            row = row + got_ref[g * per_row + k, tile * blocks : tile * blocks + 8, :].astype(F32)
        hit = jnp.where(regions == row[0:1, :], 1.0, 0.0)
        hits = hits + hit
        member_ref[:, g * LANES : (g + 1) * LANES] = hit.astype(BF16)
    count = jnp.sum(hits, axis=1, keepdims=True)
    members = member_ref[...]
    sums = [
        mm(members, got_ref[:, c * tile : (c + 1) * tile, :].reshape(slots, LANES))
        for c in range(blocks)
    ]
    pooled = jnp.concatenate(sums, axis=1) * (1.0 / (1.0 + count))
    pooled_ref[...] = pooled
    attn_in = (rms(pooled) * gain_ref[...]).astype(BF16)
    attn_in_ref[...] = attn_in
    low = low_lanes(REG_DEV)
    key = mm(attn_in, w_key_ref[...])
    key = key * lax.rsqrt(mm((key * key).astype(BF16), by_heads()) + EPS)
    value = mm(attn_in, w_value_ref[...])
    zero = jnp.where(low, key, pltpu.roll(value, HEAD_DIM, 1)).astype(BF16)
    one = jnp.where(low, pltpu.roll(key, HEAD_DIM, 1), value).astype(BF16)
    first = core_ref[0] == 0
    keep_ref[...] = jnp.where(first, zero, one)
    send_ref[...] = jnp.where(first, one, zero)


def query_kernel(core_ref, attn_in_ref, w_query_ref, scale_ref, keep_ref, send_ref):
    core = core_ref[0]
    half = GROUP * HEAD_DIM
    low = low_lanes(REG_DEV)
    for out_ref, group in ((send_ref, 1 - core), (keep_ref, core)):
        cols = pl.ds(pl.multiple_of(group * half, half), half)
        query = mm(attn_in_ref[...], w_query_ref[:, cols])
        scale = scale_ref[:, cols]
        for j in range(half // LANES):
            pair = slice(j * LANES, (j + 1) * LANES)
            values = query[:, pair]
            square = mm((values * values).astype(BF16), by_heads())
            unit = values * lax.rsqrt(square + EPS) * scale[:, pair]
            even = jnp.where(low, unit, 0.0).astype(BF16)
            odd = jnp.where(low, pltpu.roll(unit, HEAD_DIM, 1), 0.0).astype(BF16)
            out_ref[:, 2 * j * LANES : (2 * j + 1) * LANES] = even
            out_ref[:, (2 * j + 1) * LANES : (2 * j + 2) * LANES] = odd


def attend_kernel(parts, row_parts, first, last, *refs):
    slabs, kvs = refs[: len(row_parts)], refs[len(row_parts) : len(row_parts) + parts]
    rest = refs[len(row_parts) + parts :]
    key_ref, value_ref, query_ref = rest[-3:]
    acc_in = None if first else rest[0]
    acc_ref = rest[-4]
    out_ref = rest[-5] if last else None
    rows_all = len(row_parts) * REG_DEV
    at = 0
    for kv_ref in kvs:
        kv = kv_ref[...]
        rows = kv.shape[0]
        key_ref[at : at + rows, :] = kv
        value_ref[at : at + rows, :] = jnp.where(low_lanes(rows), jnp.ones_like(kv), kv)
        at += rows
    for r, slab in enumerate(slabs):
        for h in range(GROUP):
            query_ref[h, r * REG_DEV : (r + 1) * REG_DEV, :] = slab[:, h * LANES : (h + 1) * LANES]
    block = max(n for n in range(REG_DEV, 2561, REG_DEV) if at % n == 0)
    span = min(rows_all, 512 if block <= 1024 else 256)

    def step(i, begin):
        keys = pl.ds(pl.multiple_of(i * block, block), block)
        for h in range(GROUP):
            for r in range(rows_all // span):
                here = slice(r * span, (r + 1) * span)
                score = lax.dot_general(
                    query_ref[h, here, :], key_ref[keys, :], NT, preferred_element_type=F32
                )
                new = mm(jnp.exp2(score).astype(BF16), value_ref[keys, :])
                if not begin:
                    new = acc_ref[h, here, :] + new
                elif not first:
                    base = row_parts[0] * REG_DEV
                    new = acc_in[h, base + r * span : base + (r + 1) * span, :] + new
                acc_ref[h, here, :] = new

    step(0, True)
    if at > block:

        def body(i, carry):
            step(i, False)
            return carry

        lax.fori_loop(1, at // block, body, 0)
    if last:
        low = low_lanes(rows_all)
        for j in range(GROUP // 2):
            a, b = acc_ref[2 * j], acc_ref[2 * j + 1]
            num = jnp.where(low, pltpu.roll(a, HEAD_DIM, 1), b)
            den = jnp.where(low, a, pltpu.roll(b, HEAD_DIM, 1))
            out_ref[:, j * LANES : (j + 1) * LANES] = (num / den).astype(BF16)


def post_kernel(
    core_ref, mine_ref, other_ref, pooled_ref, member_ref, w_out_ref, gain_ref, w_inner_ref, w_outer_ref, out_ref, inner_ref
):
    half = mine_ref.shape[1]
    core = core_ref[0]
    own = pl.ds(pl.multiple_of(core * half, half), half)
    far = pl.ds(pl.multiple_of((1 - core) * half, half), half)
    hidden = (
        pooled_ref[...] + mm(mine_ref[...], w_out_ref[own, :]) + mm(other_ref[...], w_out_ref[far, :])
    )
    mlp_in = (rms(hidden) * gain_ref[...]).astype(BF16)
    inner_width = w_inner_ref.shape[1]
    block = math.gcd(inner_width, 512)
    for j in range(inner_width // block):
        cols = slice(j * block, (j + 1) * block)
        inner_ref[:, cols] = jax.nn.gelu(mm(mlp_in, w_inner_ref[:, cols])).astype(BF16)
    region_out = (hidden + mm(inner_ref[...], w_outer_ref[...])).astype(BF16)
    slots = member_ref.shape[1]
    block = math.gcd(slots, 512)
    for i in range(slots // block):
        rows = slice(i * block, (i + 1) * block)
        out_ref[rows, :] = lax.dot_general(
            member_ref[:, rows], region_out, TN, preferred_element_type=F32
        ).astype(BF16)


def decode_kernel(back_ref, sensors_ref, live_ref, gain_ref, w_in_ref, w_out_ref, out_ref):
    count = out_ref.shape[0]
    block = math.gcd(count, 128)
    for i in range(count // block):
        rows = slice(i * block, (i + 1) * block)
        total = back_ref[rows, :].astype(F32) + sensors_ref[rows, :].astype(F32)
        dec_in = (rms(total) * gain_ref[...]).astype(BF16)
        hidden = jax.nn.gelu(mm(dec_in, w_in_ref[...])).astype(BF16)
        result = mm(hidden, w_out_ref[...])
        out_ref[rows, :] = jnp.where(live_ref[rows, :] > 0.0, result, 0.0).astype(BF16)


def local(
    sensors,
    slot_region,
    w_query,
    w_key,
    w_value,
    w_out,
    temper,
    gain_attn,
    w_inner,
    w_outer,
    gain_mlp,
    gain_dec,
    w_dec_in,
    w_dec_out,
):
    devices = lax.axis_size(AXES)
    sen_dev, width = sensors.shape
    tile = sen_dev // devices
    me = lax.axis_index(AXES).astype(jnp.int32).reshape(1)
    core = lax.rem(me, 2)
    bits = devices.bit_length() - 1
    pay_rows = tile * (width // LANES) + 8

    def flipped(value, mask):
        return lax.ppermute(value, AXES, [(i, i ^ mask) for i in range(devices)])

    payload = pl.pallas_call(
        functools.partial(pack_kernel, tile),
        out_shape=jax.ShapeDtypeStruct((devices, pay_rows, LANES), BF16),
        in_specs=[SMEM, VMEM, VMEM],
        out_specs=VMEM,
        compiler_params=PARAMS,
        name="pack",
    )(me, sensors, slot_region.reshape(-1, LANES))
    got = lax.all_to_all(payload, AXES, split_axis=0, concat_axis=0, tiled=True)

    scale = jnp.repeat(temper * (math.log2(math.e) / HEAD_DIM), HEAD_DIM).reshape(1, -1)
    live = (slot_region >= 0).astype(F32).reshape(sen_dev, 1)

    kv_shape = jax.ShapeDtypeStruct((REG_DEV, LANES), BF16)
    pooled, members, attn_in, kv_keep, kv_send = pl.pallas_call(
        functools.partial(pool_kernel, tile),
        out_shape=(
            jax.ShapeDtypeStruct((REG_DEV, width), F32),
            jax.ShapeDtypeStruct((REG_DEV, sen_dev), BF16),
            jax.ShapeDtypeStruct((REG_DEV, width), BF16),
            kv_shape,
            kv_shape,
        ),
        in_specs=[SMEM] + [VMEM] * 4,
        out_specs=(VMEM,) * 5,
        compiler_params=PARAMS,
        name="pool",
    )(core, got, w_key, w_value, gain_attn.reshape(1, width))
    kv_other = flipped(kv_send, 1)
    slab_shape = jax.ShapeDtypeStruct((REG_DEV, GROUP * LANES), BF16)
    q_keep, q_send = pl.pallas_call(
        query_kernel,
        out_shape=(slab_shape, slab_shape),
        in_specs=[SMEM] + [VMEM] * 3,
        out_specs=(VMEM, VMEM),
        compiler_params=PARAMS,
        cost_estimate=pl.CostEstimate(
            flops=2 * REG_DEV * width * width, bytes_accessed=2 * REG_DEV * width, transcendentals=0
        ),
        name="query",
    )(core, attn_in, w_query, scale)
    kv_other, q_keep, q_send = lax.optimization_barrier((kv_other, q_keep, q_send))
    slabs = (q_keep, flipped(q_send, 1))

    def attend(parts, acc, last=False, row_parts=(0, 1)):
        keys = sum(part.shape[0] for part in parts)
        rows = len(row_parts) * REG_DEV
        acc_shape = (GROUP, rows, LANES)
        work = GROUP * rows * keys
        out_shape = (rows, GROUP * HEAD_DIM) if last else acc_shape
        return pl.pallas_call(
            functools.partial(attend_kernel, len(parts), row_parts, acc is None, last),
            out_shape=jax.ShapeDtypeStruct(out_shape, BF16 if last else F32),
            in_specs=[VMEM] * (len(row_parts) + len(parts) + (acc is not None)),
            out_specs=VMEM,
            scratch_shapes=([pltpu.VMEM(acc_shape, F32)] if last else [])
            + [pltpu.VMEM((keys, LANES), BF16)] * 2
            + [pltpu.VMEM(acc_shape, BF16)],
            compiler_params=PARAMS,
            cost_estimate=pl.CostEstimate(
                flops=work * 4 * 256, bytes_accessed=keys * 2 * LANES, transcendentals=work
            ),
            name="attend",
        )(*(slabs[r] for r in row_parts), *parts, *(() if acc is None else (acc,)))

    one, two = 1 << (bits - 2), 1 << (bits - 1)
    own = jnp.concatenate([kv_keep, kv_other], axis=0)
    for bit in range(bits - 3, 2, -1):
        own = jnp.concatenate([own, flipped(own, 1 << bit)], axis=0)
    near, far = 1 << 1, 1 << 2

    a, b = flipped(own, far), flipped(own, near)
    own_one, own_two = flipped(own, one), flipped(own, two)
    acc = attend([own], None)
    acc, a, b, own_one, own_two = lax.optimization_barrier((acc, a, b, own_one, own_two))

    ab, c = jnp.concatenate([a, b], axis=0), flipped(a, near)
    ab_one, ab_two, own_corner = flipped(ab, one), flipped(ab, two), flipped(own_two, one)
    acc = attend([ab, own_one, own_two], acc)
    acc, c, ab_one, ab_two = lax.optimization_barrier((acc, c, ab_one, ab_two))

    c_one, c_two, ab_corner = flipped(c, one), flipped(c, two), flipped(ab_one, two)
    acc = attend([c, ab_one, ab_two, own_corner], acc)
    acc, c_one, c_two = lax.optimization_barrier((acc, c_one, c_two))

    c_corner = flipped(c_two, one)
    acc = attend([c_one, c_two, ab_corner], acc)

    theirs = attend([c_corner], acc, True, (1,))
    other_heads = flipped(theirs, 1)
    mine = attend([c_corner], acc, True, (0,))
    mine, other_heads = lax.optimization_barrier((mine, other_heads))

    back = pl.pallas_call(
        post_kernel,
        out_shape=jax.ShapeDtypeStruct((sen_dev, width), BF16),
        in_specs=[SMEM] + [VMEM] * 8,
        out_specs=VMEM,
        scratch_shapes=[pltpu.VMEM((REG_DEV, w_inner.shape[1]), BF16)],
        compiler_params=PARAMS,
        name="post",
    )(core, mine, other_heads, pooled, members, w_out, gain_mlp.reshape(1, width), w_inner, w_outer)
    returned = lax.all_to_all(
        back.reshape(devices, tile, width), AXES, split_axis=0, concat_axis=0, tiled=True
    ).reshape(sen_dev, width)

    rows = math.gcd(sen_dev, 512)
    by_rows = pl.BlockSpec((rows, width), lambda i: (i, 0))
    whole = lambda shape: pl.BlockSpec(shape, lambda i: (0, 0))
    return pl.pallas_call(
        decode_kernel,
        grid=(sen_dev // rows,),
        out_shape=jax.ShapeDtypeStruct((sen_dev, width), BF16),
        in_specs=[
            by_rows,
            by_rows,
            pl.BlockSpec((rows, 1), lambda i: (i, 0)),
            whole((1, width)),
            whole(w_dec_in.shape),
            whole(w_dec_out.shape),
        ],
        out_specs=by_rows,
        compiler_params=PARAMS,
        name="decode",
    )(returned, sensors, live, gain_dec.reshape(1, width), w_dec_in, w_dec_out)


def solution(mesh):
    placed = (P(AXES, None), P(AXES)) + (P(),) * 12
    return jax.shard_map(
        local, mesh=mesh, in_specs=placed, out_specs=P(AXES, None), check_vma=False
    )
```

time: 95.2 us -> 91.2 us (0.958)
  starting transfers between devices: 25.1 us -> 21.8 us
  local copies, waits for them, and re-layouts: 3.46 us -> 2.16 us
    ppermute x17 -> x15, starting transfers between devices: 14.4 us -> 12.1 us  [flipped(): return lax.ppermute(value, AXES, [(i, i ^ mask) for i in range(devices)])]
    pallas_call x1, Pallas kernels: 3.01 us -> 1.02 us  [local(): pl.pallas_call(functools.partial(pool_kernel, tile), out_shape=(jax.Shape...]
    all_to_all x1, waiting for transfers between devices: 15.8 us -> 17.4 us  [local(): got = lax.all_to_all(payload, AXES, split_axis=0, concat_axis=0, tiled=True)]
    pallas_call x5 -> x7, Pallas kernels: 19.2 us -> 20.6 us  [the longest x6 19.8 us: attend(): pl.pallas_call(functools.partial(attend_kernel, len(parts), row_parts, ac...]
    all_to_all x1, starting transfers between devices: 3.62 us -> 2.58 us  [local(): lax.all_to_all(back.reshape(devices, tile, width), AXES, split_axis=0, co...]
    ppermute x17 -> x15, waiting for transfers between devices: 5.93 us -> 5.22 us  [flipped(): return lax.ppermute(value, AXES, [(i, i ^ mask) for i in range(devices)])]
    unnamed x35 -> x34, local copies, waits for them, and re-layouts: 2.47 us -> 1.84 us
  transfers between devices with their start and end apart: 19 -> 17, of which waited for: 5 -> 4; matrix products, arithmetic and copies ran while one was open for 1% -> 0% of each run, Pallas kernels for 18% -> 22%
where the time goes in v3:
time: 91.2 us; the launch traced here: 90.4 us
  waiting for transfers between devices  38.5 us (42%)
  Pallas kernels  27.6 us (30%)
  starting transfers between devices  21.8 us (24%)
  local copies, waits for them, and re-layouts  2.16 us (2%)
    pallas_call x6, Pallas kernels, attend(): pl.pallas_call(functools.partial(attend_kernel, len(parts), row_parts, ac...  19.8 us
    all_to_all x1, waiting for transfers between devices, local(): got = lax.all_to_all(payload, AXES, split_axis=0, concat_axis=0, tiled=True)  17.4 us
    all_to_all x1, waiting for transfers between devices, local(): lax.all_to_all(back.reshape(devices, tile, width), AXES, split_axis=0, co...  15.9 us
    ppermute x15, starting transfers between devices, flipped(): return lax.ppermute(value, AXES, [(i, i ^ mask) for i in range(devices)])  12.1 us
    all_to_all x1, starting transfers between devices, local(): got = lax.all_to_all(payload, AXES, split_axis=0, concat_axis=0, tiled=True)  7.1 us
    ppermute x15, waiting for transfers between devices, flipped(): return lax.ppermute(value, AXES, [(i, i ^ mask) for i in range(devices)])  5.22 us
    pallas_call x1, Pallas kernels, local(): pl.pallas_call(post_kernel, out_shape=jax.ShapeDtypeStruct((sen_dev, widt...  2.79 us
    all_to_all x1, starting transfers between devices, local(): lax.all_to_all(back.reshape(devices, tile, width), AXES, split_axis=0, co...  2.58 us
  transfers between devices with their start and end apart: 17, of which 4 were waited for; matrix products, arithmetic and copies ran while one was open for 0% of the time, Pallas kernels for 22%

profile of v3, /device:TPU:1, one launch (start us, length us, event | category | flops | bytes accessed | tf_op | source)
XLA Modules:
  0.0 90.4 jit_solution(1424170189686379301)
XLA Ops:
  0.0 1.1 %copy-done = bf16[512,512]{1,0:T(8,128)(2,1)S(1)} copy-done((bf16[512,512]{1,0:T(8,128)(2,1)S(1)}, bf16[512,512]{1,0:T(8,128)(2,1)}, u32[]{:S(2)}) %copy-start) | copy-done | bytes 524312
  1.1 0.7 copy-done.10
  1.8 0.9 %pack.1 = bf16[32,72,128]{2,1,0:T(8,128)(2,1)} custom-call(s32[1]{0:T(128)} %bitcast.me_ref, bf16[512,512]{1,0:T(8,128)(2,1)S(1)} %copy-done, s32[4,128]{1,0:T(4,128)S(1)} %bitcast.9), custom_call_target="tpu_custom_call" | custom-call | tf_op jit(solution)/shard_map/pack/pallas_call | solution.py:242
  2.7 7.1 %all-to-all-start = ((bf16[32,72,128]{2,1,0:T(8,128)(2,1)}), bf16[32,72,128]{2,1,0:T(8,128)(2,1)S(1)}, u32[]{:S(2)}, u32[]{:S(2)}) async-start(bf16[32,72,128]{2,1,0:T(8,128)(2,1)} %pack.1), calls=%async_computation | async-start | bytes 1179648 | tf_op jit(solution)/shard_map/all_to_all | solution.py:250
  9.8 17.4 %all-to-all-done.got_ref = bf16[32,72,128]{2,1,0:T(8,128)(2,1)S(1)} async-done(((bf16[32,72,128]{2,1,0:T(8,128)(2,1)}), bf16[32,72,128]{2,1,0:T(8,128)(2,1)S(1)}, u32[]{:S(2)}, u32[]{:S(2)}) %all-to-all-start) | async-done | bytes 589856 | tf_op jit(solution)/shard_map/all_to_all | solution.py:250
  27.2 0.0 copy-done.12
  27.2 1.0 %pool.1 = (f32[256,512]{1,0:T(8,128)S(1)}, bf16[256,512]{1,0:T(8,128)(2,1)S(1)}, bf16[256,512]{1,0:T(8,128)(2,1)S(1)}, bf16[256,128]{1,0:T(8,128)(2,1)S(1)}, bf16[256,128]{1,0:T(8,128)(2,1)S(1)}) custom-call(s32[1]{0:T(128)S(6)} %rem.18.core_ref, bf16[32,72,128]{2,1,0:T(8,128)(2,1)S(1)} %all-to-all-done.got_ref, bf16[512,128]{1,0:T(8,128)(2,1)S(1)} %copy-done.8, ...), custom_call_target="tpu_custom_call" | custom-call | tf_op jit(solution)/shard_map/pool/pallas_call | solution.py:256
  28.2 0.7 collective-permute-start
  28.9 0.1 broadcast_in_dim.3
  29.0 0.1 reshape_reshape.3.scale_ref
  29.1 0.0 copy-done.7
  29.1 0.8 query.1
  29.8 0.0 collective-permute-done
  29.9 0.3 collective-permute-start.1
  30.2 0.1 collective-permute-start.2
  30.2 0.3 collective-permute-start.3
  30.6 1.1 %collective-permute-start.4 = (bf16[512,128]{1,0:T(8,128)(2,1)S(1)}, bf16[512,128]{1,0:T(8,128)(2,1)S(1)}, u32[]{:S(2)}, u32[]{:S(2)}) collective-permute-start(bf16[512,128]{1,0:T(8,128)(2,1)S(1)} %constant_dynamic-update-slice_fusion.refs_2_), channel_id=1, source_target_pairs={{0,8},{1,9},{2,10},{3,11},{4,12},{5,13},{6,14},{7,15},{8,0},{9,1},... | collective-permute-start | bytes 393224 | tf_op jit(solution)/shard_map/ppermute | solution.py:240
  31.7 1.0 %collective-permute-start.5 = (bf16[512,128]{1,0:T(8,128)(2,1)S(1)}, bf16[512,128]{1,0:T(8,128)(2,1)S(1)}, u32[]{:S(2)}, u32[]{:S(2)}) collective-permute-start(bf16[512,128]{1,0:T(8,128)(2,1)S(1)} %constant_dynamic-update-slice_fusion.refs_2_), channel_id=1, source_target_pairs={{0,16},{1,17},{2,18},{3,19},{4,20},{5,21},{6,22},{7,23},{8,24},{9,... | collective-permute-start | bytes 393224 | tf_op jit(solution)/shard_map/ppermute | solution.py:240
  32.7 0.0 collective-permute-done.1.refs_1_.refs_0_
  32.7 1.4 %attend.6.refs_5_ = f32[4,512,128]{2,1,0:T(8,128)S(1)} custom-call(bf16[256,512]{1,0:T(8,128)(2,1)S(1)} %get-tuple-element.33.refs_0_, bf16[256,512]{1,0:T(8,128)(2,1)S(1)} %collective-permute-done.1.refs_1_.refs_0_, bf16[512,128]{1,0:T(8,128)(2,1)S(1)} %constant_dynamic-update-slice_fusion.refs_2_), custom_call_target="tpu_custom_call" | custom-call | flops 1073741824 | bytes 131072 | tf_op jit(solution)/shard_map/attend/pallas_call | solution.py:292
  34.1 4.2 %collective-permute-done.2 = bf16[512,128]{1,0:T(8,128)(2,1)S(1)} collective-permute-done((bf16[512,128]{1,0:T(8,128)(2,1)S(1)}, bf16[512,128]{1,0:T(8,128)(2,1)S(1)}, u32[]{:S(2)}, u32[]{:S(2)}) %collective-permute-start.2) | collective-permute-done | bytes 131104 | tf_op jit(solution)/shard_map/ppermute | solution.py:240
  38.3 0.0 collective-permute-done.3
  38.3 0.0 collective-permute-done.4.refs_3_
  38.3 0.0 collective-permute-done.5.refs_4_
  38.3 1.1 %collective-permute-start.7 = (bf16[1024,128]{1,0:T(8,128)(2,1)S(1)}, bf16[1024,128]{1,0:T(8,128)(2,1)S(1)}, u32[]{:S(2)}, u32[]{:S(2)}) collective-permute-start(bf16[1024,128]{1,0:T(8,128)(2,1)S(1)} %constant_dynamic-update-slice_fusion.2.refs_2_), channel_id=1, source_target_pairs={{0,8},{1,9},{2,10},{3,11},{4,12},{5,13},{6,14},{7,15},{8,0},{9,1},... | collective-permute-start | bytes 786440 | tf_op jit(solution)/shard_map/ppermute | solution.py:240
  39.4 0.4 collective-permute-start.8
  39.8 0.0 collective-permute-start.6
  39.8 1.1 %collective-permute-start.9 = (bf16[512,128]{1,0:T(8,128)(2,1)S(1)}, bf16[512,128]{1,0:T(8,128)(2,1)S(1)}, u32[]{:S(2)}, u32[]{:S(2)}) collective-permute-start(bf16[512,128]{1,0:T(8,128)(2,1)S(1)} %collective-permute-done.5.refs_4_), channel_id=1, source_target_pairs={{0,8},{1,9},{2,10},{3,11},{4,12},{5,13},{6,14},{7,15},{8,0},{9,1},... | collective-permute-start | bytes 393224 | tf_op jit(solution)/shard_map/ppermute | solution.py:240
  40.9 4.6 %attend.7.refs_6_ = f32[4,512,128]{2,1,0:T(8,128)S(1)} custom-call(bf16[256,512]{1,0:T(8,128)(2,1)S(1)} %get-tuple-element.33.refs_0_, bf16[256,512]{1,0:T(8,128)(2,1)S(1)} %collective-permute-done.1.refs_1_.refs_0_, bf16[1024,128]{1,0:T(8,128)(2,1)S(1)} %constant_dynamic-update-slice_fusion.2.refs_2_, bf16[512,128]{1,0:T(8,128)(2,1)S(1)} %collective-permute-done.4.refs_3_, ...), custom_call_target="tpu_custom_call" | custom-call | flops 4294967296 | bytes 524288 | tf_op jit(solution)/shard_map/attend/pallas_call | solution.py:292
  45.5 0.0 collective-permute-done.6.refs_2_
  45.5 0.0 collective-permute-done.7.refs_3_
  45.5 1.0 %collective-permute-done.8.refs_4_ = bf16[1024,128]{1,0:T(8,128)(2,1)S(1)} collective-permute-done((bf16[1024,128]{1,0:T(8,128)(2,1)S(1)}, bf16[1024,128]{1,0:T(8,128)(2,1)S(1)}, u32[]{:S(2)}, u32[]{:S(2)}) %collective-permute-start.8) | collective-permute-done | bytes 262176 | tf_op jit(solution)/shard_map/ppermute | solution.py:240
  46.5 0.3 collective-permute-start.10
  46.8 1.2 %collective-permute-start.11 = (bf16[512,128]{1,0:T(8,128)(2,1)S(1)}, bf16[512,128]{1,0:T(8,128)(2,1)S(1)}, u32[]{:S(2)}, u32[]{:S(2)}) collective-permute-start(bf16[512,128]{1,0:T(8,128)(2,1)S(1)} %collective-permute-done.6.refs_2_), channel_id=1, source_target_pairs={{0,16},{1,17},{2,18},{3,19},{4,20},{5,21},{6,22},{7,23},{8,24},{9,... | collective-permute-start | bytes 393224 | tf_op jit(solution)/shard_map/ppermute | solution.py:240
  48.0 0.3 collective-permute-start.13
  48.3 0.0 collective-permute-done.9.refs_5_
  48.3 7.0 %attend.8.refs_5_ = f32[4,512,128]{2,1,0:T(8,128)S(1)} custom-call(bf16[256,512]{1,0:T(8,128)(2,1)S(1)} %get-tuple-element.33.refs_0_, bf16[256,512]{1,0:T(8,128)(2,1)S(1)} %collective-permute-done.1.refs_1_.refs_0_, bf16[512,128]{1,0:T(8,128)(2,1)S(1)} %collective-permute-done.6.refs_2_, bf16[1024,128]{1,0:T(8,128)(2,1)S(1)} %collective-permute-done.7.refs_3_, ...), custom_call_target="tpu_custom_call" | custom-call | flops 6442450944 | bytes 786432 | tf_op jit(solution)/shard_map/attend/pallas_call | solution.py:292
  55.3 0.0 collective-permute-done.10.refs_2_
  55.3 0.0 collective-permute-done.11.refs_3_
  55.3 1.4 %collective-permute-start.12 = (bf16[512,128]{1,0:T(8,128)(2,1)S(1)}, bf16[512,128]{1,0:T(8,128)(2,1)S(1)}, u32[]{:S(2)}, u32[]{:S(2)}) collective-permute-start(bf16[512,128]{1,0:T(8,128)(2,1)S(1)} %collective-permute-done.11.refs_3_), channel_id=1, source_target_pairs={{0,8},{1,9},{2,10},{3,11},{4,12},{5,13},{6,14},{7,15},{8,0},{9,1},... | collective-permute-start | bytes 393224 | tf_op jit(solution)/shard_map/ppermute | solution.py:240
  56.7 0.0 collective-permute-done.13.refs_4_
  56.7 4.6 %attend.9.refs_2_ = f32[4,512,128]{2,1,0:T(8,128)S(1)} custom-call(bf16[256,512]{1,0:T(8,128)(2,1)S(1)} %get-tuple-element.33.refs_0_, bf16[256,512]{1,0:T(8,128)(2,1)S(1)} %collective-permute-done.1.refs_1_.refs_0_, bf16[512,128]{1,0:T(8,128)(2,1)S(1)} %collective-permute-done.10.refs_2_, bf16[512,128]{1,0:T(8,128)(2,1)S(1)} %collective-permute-done.11.refs_3_, ...), custom_call_target="tpu_custom_call" | custom-call | flops 4294967296 | bytes 524288 | tf_op jit(solution)/shard_map/attend/pallas_call | solution.py:292
  61.3 0.0 copy-start.2
  61.3 0.0 copy-start.4
  61.3 0.0 copy-start.13
  61.3 0.0 collective-permute-done.12.refs_1_
  61.3 1.2 %attend.11 = bf16[256,256]{1,0:T(8,128)(2,1)S(1)} custom-call(bf16[256,512]{1,0:T(8,128)(2,1)S(1)} %collective-permute-done.1.refs_1_.refs_0_, bf16[512,128]{1,0:T(8,128)(2,1)S(1)} %collective-permute-done.12.refs_1_, f32[4,512,128]{2,1,0:T(8,128)S(1)} %attend.9.refs_2_), custom_call_target="tpu_custom_call" | custom-call | flops 536870912 | bytes 131072 | tf_op jit(solution)/shard_map/attend/pallas_call | solution.py:292
  62.5 2.9 %collective-permute-start.14 = (bf16[256,256]{1,0:T(8,128)(2,1)S(1)}, bf16[256,256]{1,0:T(8,128)(2,1)S(1)}, u32[]{:S(2)}, u32[]{:S(2)}) collective-permute-start(bf16[256,256]{1,0:T(8,128)(2,1)S(1)} %attend.11), channel_id=1, source_target_pairs={{0,1},{1,0},{2,3},{3,2},{4,5},{5,4},{6,7},{7,6},{8,9},{9,8},{10,11... | collective-permute-start | bytes 393224 | tf_op jit(solution)/shard_map/ppermute | solution.py:240
  65.4 1.1 %attend.10.mine_ref = bf16[256,256]{1,0:T(8,128)(2,1)S(1)} custom-call(bf16[256,512]{1,0:T(8,128)(2,1)S(1)} %get-tuple-element.33.refs_0_, bf16[512,128]{1,0:T(8,128)(2,1)S(1)} %collective-permute-done.12.refs_1_, f32[4,512,128]{2,1,0:T(8,128)S(1)} %attend.9.refs_2_), custom_call_target="tpu_custom_call" | custom-call | flops 536870912 | bytes 131072 | tf_op jit(solution)/shard_map/attend/pallas_call | solution.py:292
  66.5 0.0 collective-permute-done.14.other_ref
  66.5 0.0 copy-done.3
  66.5 0.0 copy-done.2
  66.6 0.0 copy-done.4
  66.6 0.0 copy-done.13
  66.6 0.0 copy-start.11
  66.6 0.0 copy-start.1
  66.6 0.0 copy-start.5
  66.6 0.0 copy-start.6
  66.6 0.0 copy-start.14
  66.6 2.8 %post.1 = bf16[512,512]{1,0:T(8,128)(2,1)} custom-call(s32[1]{0:T(128)S(6)} %rem.18.core_ref, bf16[256,256]{1,0:T(8,128)(2,1)S(1)} %attend.10.mine_ref, bf16[256,256]{1,0:T(8,128)(2,1)S(1)} %collective-permute-done.14.other_ref, f32[256,512]{1,0:T(8,128)S(1)} %get-tuple-element.51.pooled_ref, bf16[256,512]{1,0:T(8,128)(2,1)S(1)} %get-tuple-element.52.member_ref, ...), custom_call_target="tpu_custom_call" | custom-call | tf_op jit(solution)/shard_map/post/pallas_call | solution.py:335
  69.4 2.6 %all-to-all-start.1 = ((bf16[32,16,512]{2,1,0:T(8,128)(2,1)}), bf16[32,16,512]{2,1,0:T(8,128)(2,1)S(1)}, u32[]{:S(2)}, u32[]{:S(2)}) async-start(bf16[32,16,512]{2,1,0:T(8,128)(2,1)} %bitcast.4), calls=%async_computation.1 | async-start | bytes 1048576 | tf_op jit(solution)/shard_map/all_to_all | solution.py:344
  72.0 0.1 copy.15.live_ref
  72.2 15.9 %all-to-all-done.1 = bf16[32,16,512]{2,1,0:T(8,128)(2,1)S(1)} async-done(((bf16[32,16,512]{2,1,0:T(8,128)(2,1)}), bf16[32,16,512]{2,1,0:T(8,128)(2,1)S(1)}, u32[]{:S(2)}, u32[]{:S(2)}) %all-to-all-start.1) | async-done | bytes 524320 | tf_op jit(solution)/shard_map/all_to_all | solution.py:344
  88.2 2.3 %decode.1 = bf16[512,512]{1,0:T(8,128)(2,1)} custom-call(bf16[512,512]{1,0:T(8,128)(2,1)S(1)} %bitcast.8, bf16[512,512]{1,0:T(8,128)(2,1)S(1)} %copy-done.1, f32[512,1]{1,0:T(8,128)S(1)} %copy.15.live_ref, f32[1,512]{1,0:T(1,128)S(1)} %bitcast.12, bf16[512,512]{1,0:T(8,128)(2,1)S(1)} %copy-done.5, bf16[512,512]{1,0:T(8,128)(2,1)S(1)} %copy-done.6), custom_call_target="tpu_custom_call" | custom-call | tf_op jit(solution)/shard_map/decode/pallas_call | solution.py:351
  (22 shorter events, 0.1 us)
Async XLA Ops:
  0.0 27.2 %copy-start.12 = (f32[512]{0:T(512)S(1)}, f32[512]{0:T(512)}, u32[]{:S(2)}) copy-start(f32[512]{0:T(512)} %param.21) | copy-start | bytes 6148
  0.0 28.9 %copy-start.15 = (f32[8]{0:T(128)S(1)}, f32[8]{0:T(128)}, u32[]{:S(2)}) copy-start(f32[8]{0:T(128)} %param.20) | copy-start | bytes 100
  0.0 1.1 %copy-start = (bf16[512,512]{1,0:T(8,128)(2,1)S(1)}, bf16[512,512]{1,0:T(8,128)(2,1)}, u32[]{:S(2)}) copy-start(bf16[512,512]{1,0:T(8,128)(2,1)} %sensors_ref.3) | copy-start | bytes 1572868
  1.1 0.7 copy-start.10
  1.8 25.4 %copy-start.8 = (bf16[512,128]{1,0:T(8,128)(2,1)S(1)}, bf16[512,128]{1,0:T(8,128)(2,1)}, u32[]{:S(2)}) copy-start(bf16[512,128]{1,0:T(8,128)(2,1)} %w_key_ref.1) | copy-start | bytes 393220
  1.8 25.4 %copy-start.9 = (bf16[512,128]{1,0:T(8,128)(2,1)S(1)}, bf16[512,128]{1,0:T(8,128)(2,1)}, u32[]{:S(2)}) copy-start(bf16[512,128]{1,0:T(8,128)(2,1)} %w_value_ref.1) | copy-start | bytes 393220
  1.8 27.3 %copy-start.7 = (bf16[512,512]{1,0:T(8,128)(2,1)S(1)}, bf16[512,512]{1,0:T(8,128)(2,1)}, u32[]{:S(2)}) copy-start(bf16[512,512]{1,0:T(8,128)(2,1)} %w_query_ref.1) | copy-start | bytes 1572868
  2.7 24.5 %all-to-all-start = ((bf16[32,72,128]{2,1,0:T(8,128)(2,1)}), bf16[32,72,128]{2,1,0:T(8,128)(2,1)S(1)}, u32[]{:S(2)}, u32[]{:S(2)}) async-start(bf16[32,72,128]{2,1,0:T(8,128)(2,1)} %pack.1), calls=%async_computation | async-start | bytes 1179648 | tf_op jit(solution)/shard_map/all_to_all | solution.py:250
  28.2 1.7 %collective-permute-start = (bf16[256,128]{1,0:T(8,128)(2,1)S(1)}, bf16[256,128]{1,0:T(8,128)(2,1)S(1)}, u32[]{:S(2)}, u32[]{:S(2)}) collective-permute-start(bf16[256,128]{1,0:T(8,128)(2,1)S(1)} %get-tuple-element.29), channel_id=1, source_target_pairs={{0,1},{1,0},{2,3},{3,2},{4,5},{5,4},{6,7},{7,6},{8,9},{9,8},{10,11... | collective-permute-start | bytes 196616 | tf_op jit(solution)/shard_map/ppermute | solution.py:240
  29.9 2.8 %collective-permute-start.1 = (bf16[256,512]{1,0:T(8,128)(2,1)S(1)}, bf16[256,512]{1,0:T(8,128)(2,1)S(1)}, u32[]{:S(2)}, u32[]{:S(2)}) collective-permute-start(bf16[256,512]{1,0:T(8,128)(2,1)S(1)} %get-tuple-element.34), channel_id=1, source_target_pairs={{0,1},{1,0},{2,3},{3,2},{4,5},{5,4},{6,7},{7,6},{8,9},{9,8},{10,11... | collective-permute-start | bytes 786440 | tf_op jit(solution)/shard_map/ppermute | solution.py:240
  30.2 8.1 %collective-permute-start.2 = (bf16[512,128]{1,0:T(8,128)(2,1)S(1)}, bf16[512,128]{1,0:T(8,128)(2,1)S(1)}, u32[]{:S(2)}, u32[]{:S(2)}) collective-permute-start(bf16[512,128]{1,0:T(8,128)(2,1)S(1)} %constant_dynamic-update-slice_fusion.refs_2_), channel_id=1, source_target_pairs={{0,4},{1,5},{2,6},{3,7},{4,0},{5,1},{6,2},{7,3},{8,12},{9,13},{10,... | collective-permute-start | bytes 393224 | tf_op jit(solution)/shard_map/ppermute | solution.py:240
  30.2 8.0 %collective-permute-start.3 = (bf16[512,128]{1,0:T(8,128)(2,1)S(1)}, bf16[512,128]{1,0:T(8,128)(2,1)S(1)}, u32[]{:S(2)}, u32[]{:S(2)}) collective-permute-start(bf16[512,128]{1,0:T(8,128)(2,1)S(1)} %constant_dynamic-update-slice_fusion.refs_2_), channel_id=1, source_target_pairs={{0,2},{1,3},{2,0},{3,1},{4,6},{5,7},{6,4},{7,5},{8,10},{9,11},{10,... | collective-permute-start | bytes 393224 | tf_op jit(solution)/shard_map/ppermute | solution.py:240
  30.6 7.7 %collective-permute-start.4 = (bf16[512,128]{1,0:T(8,128)(2,1)S(1)}, bf16[512,128]{1,0:T(8,128)(2,1)S(1)}, u32[]{:S(2)}, u32[]{:S(2)}) collective-permute-start(bf16[512,128]{1,0:T(8,128)(2,1)S(1)} %constant_dynamic-update-slice_fusion.refs_2_), channel_id=1, source_target_pairs={{0,8},{1,9},{2,10},{3,11},{4,12},{5,13},{6,14},{7,15},{8,0},{9,1},... | collective-permute-start | bytes 393224 | tf_op jit(solution)/shard_map/ppermute | solution.py:240
  31.7 6.6 %collective-permute-start.5 = (bf16[512,128]{1,0:T(8,128)(2,1)S(1)}, bf16[512,128]{1,0:T(8,128)(2,1)S(1)}, u32[]{:S(2)}, u32[]{:S(2)}) collective-permute-start(bf16[512,128]{1,0:T(8,128)(2,1)S(1)} %constant_dynamic-update-slice_fusion.refs_2_), channel_id=1, source_target_pairs={{0,16},{1,17},{2,18},{3,19},{4,20},{5,21},{6,22},{7,23},{8,24},{9,... | collective-permute-start | bytes 393224 | tf_op jit(solution)/shard_map/ppermute | solution.py:240
  38.3 7.2 %collective-permute-start.7 = (bf16[1024,128]{1,0:T(8,128)(2,1)S(1)}, bf16[1024,128]{1,0:T(8,128)(2,1)S(1)}, u32[]{:S(2)}, u32[]{:S(2)}) collective-permute-start(bf16[1024,128]{1,0:T(8,128)(2,1)S(1)} %constant_dynamic-update-slice_fusion.2.refs_2_), channel_id=1, source_target_pairs={{0,8},{1,9},{2,10},{3,11},{4,12},{5,13},{6,14},{7,15},{8,0},{9,1},... | collective-permute-start | bytes 786440 | tf_op jit(solution)/shard_map/ppermute | solution.py:240
  39.4 7.1 %collective-permute-start.8 = (bf16[1024,128]{1,0:T(8,128)(2,1)S(1)}, bf16[1024,128]{1,0:T(8,128)(2,1)S(1)}, u32[]{:S(2)}, u32[]{:S(2)}) collective-permute-start(bf16[1024,128]{1,0:T(8,128)(2,1)S(1)} %constant_dynamic-update-slice_fusion.2.refs_2_), channel_id=1, source_target_pairs={{0,16},{1,17},{2,18},{3,19},{4,20},{5,21},{6,22},{7,23},{8,24},{9,... | collective-permute-start | bytes 786440 | tf_op jit(solution)/shard_map/ppermute | solution.py:240
  39.8 5.7 %collective-permute-start.6 = (bf16[512,128]{1,0:T(8,128)(2,1)S(1)}, bf16[512,128]{1,0:T(8,128)(2,1)S(1)}, u32[]{:S(2)}, u32[]{:S(2)}) collective-permute-start(bf16[512,128]{1,0:T(8,128)(2,1)S(1)} %collective-permute-done.2), channel_id=1, source_target_pairs={{0,2},{1,3},{2,0},{3,1},{4,6},{5,7},{6,4},{7,5},{8,10},{9,11},{10,... | collective-permute-start | bytes 393224 | tf_op jit(solution)/shard_map/ppermute | solution.py:240
  39.8 8.5 %collective-permute-start.9 = (bf16[512,128]{1,0:T(8,128)(2,1)S(1)}, bf16[512,128]{1,0:T(8,128)(2,1)S(1)}, u32[]{:S(2)}, u32[]{:S(2)}) collective-permute-start(bf16[512,128]{1,0:T(8,128)(2,1)S(1)} %collective-permute-done.5.refs_4_), channel_id=1, source_target_pairs={{0,8},{1,9},{2,10},{3,11},{4,12},{5,13},{6,14},{7,15},{8,0},{9,1},... | collective-permute-start | bytes 393224 | tf_op jit(solution)/shard_map/ppermute | solution.py:240
  46.5 8.8 %collective-permute-start.10 = (bf16[512,128]{1,0:T(8,128)(2,1)S(1)}, bf16[512,128]{1,0:T(8,128)(2,1)S(1)}, u32[]{:S(2)}, u32[]{:S(2)}) collective-permute-start(bf16[512,128]{1,0:T(8,128)(2,1)S(1)} %collective-permute-done.6.refs_2_), channel_id=1, source_target_pairs={{0,8},{1,9},{2,10},{3,11},{4,12},{5,13},{6,14},{7,15},{8,0},{9,1},... | collective-permute-start | bytes 393224 | tf_op jit(solution)/shard_map/ppermute | solution.py:240
  46.8 8.5 %collective-permute-start.11 = (bf16[512,128]{1,0:T(8,128)(2,1)S(1)}, bf16[512,128]{1,0:T(8,128)(2,1)S(1)}, u32[]{:S(2)}, u32[]{:S(2)}) collective-permute-start(bf16[512,128]{1,0:T(8,128)(2,1)S(1)} %collective-permute-done.6.refs_2_), channel_id=1, source_target_pairs={{0,16},{1,17},{2,18},{3,19},{4,20},{5,21},{6,22},{7,23},{8,24},{9,... | collective-permute-start | bytes 393224 | tf_op jit(solution)/shard_map/ppermute | solution.py:240
  48.0 8.7 %collective-permute-start.13 = (bf16[1024,128]{1,0:T(8,128)(2,1)S(1)}, bf16[1024,128]{1,0:T(8,128)(2,1)S(1)}, u32[]{:S(2)}, u32[]{:S(2)}) collective-permute-start(bf16[1024,128]{1,0:T(8,128)(2,1)S(1)} %collective-permute-done.7.refs_3_), channel_id=1, source_target_pairs={{0,16},{1,17},{2,18},{3,19},{4,20},{5,21},{6,22},{7,23},{8,24},{9,... | collective-permute-start | bytes 786440 | tf_op jit(solution)/shard_map/ppermute | solution.py:240
  55.3 6.0 %collective-permute-start.12 = (bf16[512,128]{1,0:T(8,128)(2,1)S(1)}, bf16[512,128]{1,0:T(8,128)(2,1)S(1)}, u32[]{:S(2)}, u32[]{:S(2)}) collective-permute-start(bf16[512,128]{1,0:T(8,128)(2,1)S(1)} %collective-permute-done.11.refs_3_), channel_id=1, source_target_pairs={{0,8},{1,9},{2,10},{3,11},{4,12},{5,13},{6,14},{7,15},{8,0},{9,1},... | collective-permute-start | bytes 393224 | tf_op jit(solution)/shard_map/ppermute | solution.py:240
  56.7 9.9 %copy-start.3 = (bf16[2048,512]{1,0:T(8,128)(2,1)S(1)}, bf16[2048,512]{1,0:T(8,128)(2,1)}, u32[]{:S(2)}) copy-start(bf16[2048,512]{1,0:T(8,128)(2,1)} %w_outer_ref.1) | copy-start | bytes 6291460
  61.3 5.3 %copy-start.2 = (bf16[512,2048]{1,0:T(8,128)(2,1)S(1)}, bf16[512,2048]{1,0:T(8,128)(2,1)}, u32[]{:S(2)}) copy-start(bf16[512,2048]{1,0:T(8,128)(2,1)} %w_inner_ref.1) | copy-start | bytes 6291460
  61.3 5.3 %copy-start.4 = (bf16[512,512]{1,0:T(8,128)(2,1)S(1)}, bf16[512,512]{1,0:T(8,128)(2,1)}, u32[]{:S(2)}) copy-start(bf16[512,512]{1,0:T(8,128)(2,1)} %w_out_ref.2) | copy-start | bytes 1572868
  61.3 5.3 %copy-start.13 = (f32[512]{0:T(512)S(1)}, f32[512]{0:T(512)}, u32[]{:S(2)}) copy-start(f32[512]{0:T(512)} %param.24) | copy-start | bytes 6148
  62.5 4.0 %collective-permute-start.14 = (bf16[256,256]{1,0:T(8,128)(2,1)S(1)}, bf16[256,256]{1,0:T(8,128)(2,1)S(1)}, u32[]{:S(2)}, u32[]{:S(2)}) collective-permute-start(bf16[256,256]{1,0:T(8,128)(2,1)S(1)} %attend.11), channel_id=1, source_target_pairs={{0,1},{1,0},{2,3},{3,2},{4,5},{5,4},{6,7},{7,6},{8,9},{9,8},{10,11... | collective-permute-start | bytes 393224 | tf_op jit(solution)/shard_map/ppermute | solution.py:240
  66.6 5.4 %copy-start.11 = (s32[512]{0:T(512)S(1)}, s32[512]{0:T(512)}, u32[]{:S(2)}) copy-start(s32[512]{0:T(512)} %param.15) | copy-start | bytes 6148
  66.6 21.5 %copy-start.1 = (bf16[512,512]{1,0:T(8,128)(2,1)S(1)}, bf16[512,512]{1,0:T(8,128)(2,1)}, u32[]{:S(2)}) copy-start(bf16[512,512]{1,0:T(8,128)(2,1)} %sensors_ref.3) | copy-start | bytes 1572868
  66.6 21.5 %copy-start.5 = (bf16[512,512]{1,0:T(8,128)(2,1)S(1)}, bf16[512,512]{1,0:T(8,128)(2,1)}, u32[]{:S(2)}) copy-start(bf16[512,512]{1,0:T(8,128)(2,1)} %w_in_ref.1) | copy-start | bytes 1572868
  66.6 21.5 %copy-start.6 = (bf16[512,512]{1,0:T(8,128)(2,1)S(1)}, bf16[512,512]{1,0:T(8,128)(2,1)}, u32[]{:S(2)}) copy-start(bf16[512,512]{1,0:T(8,128)(2,1)} %w_out_ref.3) | copy-start | bytes 1572868
  66.6 21.5 %copy-start.14 = (f32[512]{0:T(512)S(1)}, f32[512]{0:T(512)}, u32[]{:S(2)}) copy-start(f32[512]{0:T(512)} %param.25) | copy-start | bytes 6148
  69.4 18.7 %all-to-all-start.1 = ((bf16[32,16,512]{2,1,0:T(8,128)(2,1)}), bf16[32,16,512]{2,1,0:T(8,128)(2,1)S(1)}, u32[]{:S(2)}, u32[]{:S(2)}) async-start(bf16[32,16,512]{2,1,0:T(8,128)(2,1)} %bitcast.4), calls=%async_computation.1 | async-start | bytes 1048576 | tf_op jit(solution)/shard_map/all_to_all | solution.py:344

commit v4 on v3

--- a/solution.py
+++ b/solution.py
@@ -202,7 +202,7 @@
 
 def decode_kernel(back_ref, sensors_ref, live_ref, gain_ref, w_in_ref, w_out_ref, out_ref):
     count = out_ref.shape[0]
-    block = math.gcd(count, 128)
+    block = math.gcd(count, 512)
     for i in range(count // block):
         rows = slice(i * block, (i + 1) * block)
         total = back_ref[rows, :].astype(F32) + sensors_ref[rows, :].astype(F32)
@@ -310,22 +310,21 @@
         own = jnp.concatenate([own, flipped(own, 1 << bit)], axis=0)
     near, far = 1 << 1, 1 << 2
 
-    a, b = flipped(own, far), flipped(own, near)
-    own_one, own_two = flipped(own, one), flipped(own, two)
+    a, own_one, own_two = flipped(own, far), flipped(own, one), flipped(own, two)
     acc = attend([own], None)
-    acc, a, b, own_one, own_two = lax.optimization_barrier((acc, a, b, own_one, own_two))
-
-    ab, c = jnp.concatenate([a, b], axis=0), flipped(a, near)
-    ab_one, ab_two, own_corner = flipped(ab, one), flipped(ab, two), flipped(own_two, one)
-    acc = attend([ab, own_one, own_two], acc)
-    acc, c, ab_one, ab_two = lax.optimization_barrier((acc, c, ab_one, ab_two))
-
-    c_one, c_two, ab_corner = flipped(c, one), flipped(c, two), flipped(ab_one, two)
-    acc = attend([c, ab_one, ab_two, own_corner], acc)
-    acc, c_one, c_two = lax.optimization_barrier((acc, c_one, c_two))
-
-    c_corner = flipped(c_two, one)
-    acc = attend([c_one, c_two, ab_corner], acc)
+    acc, a, own_one, own_two = lax.optimization_barrier((acc, a, own_one, own_two))
+
+    bc = flipped(jnp.concatenate([own, a], axis=0), near)
+    a_one, a_two, own_corner = flipped(a, one), flipped(a, two), flipped(own_two, one)
+    acc = attend([a, own_one, own_two], acc)
+    acc, bc, a_one, a_two = lax.optimization_barrier((acc, bc, a_one, a_two))
+
+    bc_one, bc_two, a_corner = flipped(bc, one), flipped(bc, two), flipped(a_one, two)
+    acc = attend([bc, a_one, a_two, own_corner], acc)
+    acc, bc_one, bc_two = lax.optimization_barrier((acc, bc_one, bc_two))
+
+    c_corner = flipped(bc_two, one)
+    acc = attend([bc_one, bc_two, a_corner], acc)
 
     theirs = attend([c_corner], acc, True, (1,))
     other_heads = flipped(theirs, 1)

time: 91.2 us -> 91.3 us (level)
  waiting for transfers between devices: 38.5 us -> 41.2 us
  starting transfers between devices: 21.8 us -> 20.4 us
  Pallas kernels: 27.6 us -> 26.5 us
    ppermute x15 -> x14, waiting for transfers between devices: 5.22 us -> 7.88 us  [flipped(): return lax.ppermute(value, AXES, [(i, i ^ mask) for i in range(devices)])]
    ppermute x15 -> x14, starting transfers between devices: 12.1 us -> 10.7 us  [flipped(): return lax.ppermute(value, AXES, [(i, i ^ mask) for i in range(devices)])]
    unnamed x34 -> x33, local copies, waits for them, and re-layouts: 1.84 us -> 1.83 us
  transfers between devices with their start and end apart: 17 -> 16, of which waited for: 4 -> 5; matrix products, arithmetic and copies ran while one was open for 0% -> 0% of each run, Pallas kernels for 22% -> 21%
where the time goes in v4:
time: 91.3 us; the launch traced here: 90.5 us
  waiting for transfers between devices  41.2 us (45%)
  Pallas kernels  26.5 us (29%)
  starting transfers between devices  20.4 us (22%)
  local copies, waits for them, and re-layouts  2.14 us (2%)
    pallas_call x6, Pallas kernels, attend(): pl.pallas_call(functools.partial(attend_kernel, len(parts), row_parts, ac...  19.1 us
    all_to_all x1, waiting for transfers between devices, local(): got = lax.all_to_all(payload, AXES, split_axis=0, concat_axis=0, tiled=True)  17.4 us
    all_to_all x1, waiting for transfers between devices, local(): lax.all_to_all(back.reshape(devices, tile, width), AXES, split_axis=0, co...  15.9 us
    ppermute x14, starting transfers between devices, flipped(): return lax.ppermute(value, AXES, [(i, i ^ mask) for i in range(devices)])  10.7 us
    ppermute x14, waiting for transfers between devices, flipped(): return lax.ppermute(value, AXES, [(i, i ^ mask) for i in range(devices)])  7.88 us
    all_to_all x1, starting transfers between devices, local(): got = lax.all_to_all(payload, AXES, split_axis=0, concat_axis=0, tiled=True)  7.1 us
    pallas_call x1, Pallas kernels, local(): pl.pallas_call(post_kernel, out_shape=jax.ShapeDtypeStruct((sen_dev, widt...  2.79 us
    all_to_all x1, starting transfers between devices, local(): lax.all_to_all(back.reshape(devices, tile, width), AXES, split_axis=0, co...  2.57 us
  transfers between devices with their start and end apart: 16, of which 5 were waited for; matrix products, arithmetic and copies ran while one was open for 0% of the time, Pallas kernels for 21%

profile of v4, /device:TPU:1, one launch (start us, length us, event | category | flops | bytes accessed | tf_op | source)
XLA Modules:
  0.0 90.5 jit_solution(14529910909742723188)
XLA Ops:
  0.0 1.1 %copy-done = bf16[512,512]{1,0:T(8,128)(2,1)S(1)} copy-done((bf16[512,512]{1,0:T(8,128)(2,1)S(1)}, bf16[512,512]{1,0:T(8,128)(2,1)}, u32[]{:S(2)}) %copy-start) | copy-done | bytes 524312
  1.1 0.7 copy-done.10
  1.8 0.9 pack.1
  2.7 7.1 %all-to-all-start = ((bf16[32,72,128]{2,1,0:T(8,128)(2,1)}), bf16[32,72,128]{2,1,0:T(8,128)(2,1)S(1)}, u32[]{:S(2)}, u32[]{:S(2)}) async-start(bf16[32,72,128]{2,1,0:T(8,128)(2,1)} %pack.1), calls=%async_computation | async-start | bytes 1179648 | tf_op jit(solution)/shard_map/all_to_all | solution.py:250
  9.8 17.4 %all-to-all-done.got_ref = bf16[32,72,128]{2,1,0:T(8,128)(2,1)S(1)} async-done(((bf16[32,72,128]{2,1,0:T(8,128)(2,1)}), bf16[32,72,128]{2,1,0:T(8,128)(2,1)S(1)}, u32[]{:S(2)}, u32[]{:S(2)}) %all-to-all-start) | async-done | bytes 589856 | tf_op jit(solution)/shard_map/all_to_all | solution.py:250
  27.2 0.0 copy-done.12
  27.2 0.0 copy-done.8
  27.2 0.0 copy-done.9
  27.2 1.0 %pool.1 = (f32[256,512]{1,0:T(8,128)S(1)}, bf16[256,512]{1,0:T(8,128)(2,1)S(1)}, bf16[256,512]{1,0:T(8,128)(2,1)S(1)}, bf16[256,128]{1,0:T(8,128)(2,1)S(1)}, bf16[256,128]{1,0:T(8,128)(2,1)S(1)}) custom-call(s32[1]{0:T(128)S(6)} %rem.18.core_ref, bf16[32,72,128]{2,1,0:T(8,128)(2,1)S(1)} %all-to-all-done.got_ref, bf16[512,128]{1,0:T(8,128)(2,1)S(1)} %copy-done.8, ...), custom_call_target="tpu_custom_call" | custom-call | tf_op jit(solution)/shard_map/pool/pallas_call | solution.py:256
  28.2 0.7 collective-permute-start
  28.9 0.0 copy-done.15
  28.9 0.1 broadcast_in_dim.3
  29.0 0.1 reshape_reshape.3.scale_ref
  29.0 0.0 copy-done.7
  29.1 0.8 query.1
  29.8 0.0 collective-permute-done
  29.9 0.3 collective-permute-start.1
  30.2 0.1 collective-permute-start.2
  30.2 0.4 collective-permute-start.3
  30.7 0.5 collective-permute-start.4
  31.1 0.3 collective-permute-done.1.refs_1_.refs_0_
  31.5 1.4 %attend.6.refs_5_ = f32[4,512,128]{2,1,0:T(8,128)S(1)} custom-call(bf16[256,512]{1,0:T(8,128)(2,1)S(1)} %get-tuple-element.32.refs_0_, bf16[256,512]{1,0:T(8,128)(2,1)S(1)} %collective-permute-done.1.refs_1_.refs_0_, bf16[512,128]{1,0:T(8,128)(2,1)S(1)} %constant_dynamic-update-slice_fusion.refs_2_), custom_call_target="tpu_custom_call" | custom-call | flops 1073741824 | bytes 131072 | tf_op jit(solution)/shard_map/attend/pallas_call | solution.py:292
  32.8 5.4 %collective-permute-done.2.refs_2_ = bf16[512,128]{1,0:T(8,128)(2,1)S(1)} collective-permute-done((bf16[512,128]{1,0:T(8,128)(2,1)S(1)}, bf16[512,128]{1,0:T(8,128)(2,1)S(1)}, u32[]{:S(2)}, u32[]{:S(2)}) %collective-permute-start.2) | collective-permute-done | bytes 131104 | tf_op jit(solution)/shard_map/ppermute | solution.py:240
  38.2 0.0 collective-permute-done.3.refs_3_
  38.2 0.0 collective-permute-done.4.refs_4_
  38.2 1.1 %collective-permute-start.6 = (bf16[512,128]{1,0:T(8,128)(2,1)S(1)}, bf16[512,128]{1,0:T(8,128)(2,1)S(1)}, u32[]{:S(2)}, u32[]{:S(2)}) collective-permute-start(bf16[512,128]{1,0:T(8,128)(2,1)S(1)} %collective-permute-done.2.refs_2_), channel_id=1, source_target_pairs={{0,8},{1,9},{2,10},{3,11},{4,12},{5,13},{6,14},{7,15},{8,0},{9,1},... | collective-permute-start | bytes 393224 | tf_op jit(solution)/shard_map/ppermute | solution.py:240
  39.4 0.4 collective-permute-start.7
  39.7 0.0 collective-permute-start.5
  39.7 1.1 %collective-permute-start.8 = (bf16[512,128]{1,0:T(8,128)(2,1)S(1)}, bf16[512,128]{1,0:T(8,128)(2,1)S(1)}, u32[]{:S(2)}, u32[]{:S(2)}) collective-permute-start(bf16[512,128]{1,0:T(8,128)(2,1)S(1)} %collective-permute-done.4.refs_4_), channel_id=1, source_target_pairs={{0,8},{1,9},{2,10},{3,11},{4,12},{5,13},{6,14},{7,15},{8,0},{9,1},... | collective-permute-start | bytes 393224 | tf_op jit(solution)/shard_map/ppermute | solution.py:240
  40.8 3.5 %attend.7.refs_6_ = f32[4,512,128]{2,1,0:T(8,128)S(1)} custom-call(bf16[256,512]{1,0:T(8,128)(2,1)S(1)} %get-tuple-element.32.refs_0_, bf16[256,512]{1,0:T(8,128)(2,1)S(1)} %collective-permute-done.1.refs_1_.refs_0_, bf16[512,128]{1,0:T(8,128)(2,1)S(1)} %collective-permute-done.2.refs_2_, bf16[512,128]{1,0:T(8,128)(2,1)S(1)} %collective-permute-done.3.refs_3_, ...), custom_call_target="tpu_custom_call" | custom-call | flops 3221225472 | bytes 393216 | tf_op jit(solution)/shard_map/attend/pallas_call | solution.py:292
  44.3 0.0 collective-permute-done.6.refs_3_
  44.3 0.0 collective-permute-done.7.refs_4_
  44.3 2.2 %collective-permute-done.5.refs_2_ = bf16[1024,128]{1,0:T(8,128)(2,1)S(1)} collective-permute-done((bf16[1024,128]{1,0:T(8,128)(2,1)S(1)}, bf16[1024,128]{1,0:T(8,128)(2,1)S(1)}, u32[]{:S(2)}, u32[]{:S(2)}) %collective-permute-start.5) | collective-permute-done | bytes 262176 | tf_op jit(solution)/shard_map/ppermute | solution.py:240
  46.5 1.1 %collective-permute-start.10 = (bf16[1024,128]{1,0:T(8,128)(2,1)S(1)}, bf16[1024,128]{1,0:T(8,128)(2,1)S(1)}, u32[]{:S(2)}, u32[]{:S(2)}) collective-permute-start(bf16[1024,128]{1,0:T(8,128)(2,1)S(1)} %collective-permute-done.5.refs_2_), channel_id=1, source_target_pairs={{0,16},{1,17},{2,18},{3,19},{4,20},{5,21},{6,22},{7,23},{8,24},{9,... | collective-permute-start | bytes 786440 | tf_op jit(solution)/shard_map/ppermute | solution.py:240
  47.6 0.4 collective-permute-start.9
  48.0 1.1 %collective-permute-start.12 = (bf16[512,128]{1,0:T(8,128)(2,1)S(1)}, bf16[512,128]{1,0:T(8,128)(2,1)S(1)}, u32[]{:S(2)}, u32[]{:S(2)}) collective-permute-start(bf16[512,128]{1,0:T(8,128)(2,1)S(1)} %collective-permute-done.6.refs_3_), channel_id=1, source_target_pairs={{0,16},{1,17},{2,18},{3,19},{4,20},{5,21},{6,22},{7,23},{8,24},{9,... | collective-permute-start | bytes 393224 | tf_op jit(solution)/shard_map/ppermute | solution.py:240
  49.1 0.0 collective-permute-done.8.refs_5_
  49.1 5.9 %attend.8.refs_5_ = f32[4,512,128]{2,1,0:T(8,128)S(1)} custom-call(bf16[256,512]{1,0:T(8,128)(2,1)S(1)} %get-tuple-element.32.refs_0_, bf16[256,512]{1,0:T(8,128)(2,1)S(1)} %collective-permute-done.1.refs_1_.refs_0_, bf16[1024,128]{1,0:T(8,128)(2,1)S(1)} %collective-permute-done.5.refs_2_, bf16[512,128]{1,0:T(8,128)(2,1)S(1)} %collective-permute-done.6.refs_3_, ...), custom_call_target="tpu_custom_call" | custom-call | flops 5368709120 | bytes 655360 | tf_op jit(solution)/shard_map/attend/pallas_call | solution.py:292
  55.0 0.0 collective-permute-done.10.refs_3_
  55.0 0.0 collective-permute-done.9.refs_2_
  55.0 0.4 collective-permute-start.11
  55.4 0.0 collective-permute-done.12.refs_4_
  55.4 5.7 %attend.9.refs_2_ = f32[4,512,128]{2,1,0:T(8,128)S(1)} custom-call(bf16[256,512]{1,0:T(8,128)(2,1)S(1)} %get-tuple-element.32.refs_0_, bf16[256,512]{1,0:T(8,128)(2,1)S(1)} %collective-permute-done.1.refs_1_.refs_0_, bf16[1024,128]{1,0:T(8,128)(2,1)S(1)} %collective-permute-done.9.refs_2_, bf16[1024,128]{1,0:T(8,128)(2,1)S(1)} %collective-permute-done.10.refs_3_, ...), custom_call_target="tpu_custom_call" | custom-call | flops 5368709120 | bytes 655360 | tf_op jit(solution)/shard_map/attend/pallas_call | solution.py:292
  61.1 0.0 collective-permute-done.11.refs_1_
  61.1 0.0 copy-start.3
  61.1 1.4 %attend.11 = bf16[256,256]{1,0:T(8,128)(2,1)S(1)} custom-call(bf16[256,512]{1,0:T(8,128)(2,1)S(1)} %collective-permute-done.1.refs_1_.refs_0_, bf16[1024,128]{1,0:T(8,128)(2,1)S(1)} %collective-permute-done.11.refs_1_, f32[4,512,128]{2,1,0:T(8,128)S(1)} %attend.9.refs_2_), custom_call_target="tpu_custom_call" | custom-call | flops 1073741824 | bytes 262144 | tf_op jit(solution)/shard_map/attend/pallas_call | solution.py:292
  62.5 0.0 copy-start.2
  62.5 0.0 copy-start.4
  62.5 0.0 copy-start.13
  62.5 3.2 %collective-permute-start.13 = (bf16[256,256]{1,0:T(8,128)(2,1)S(1)}, bf16[256,256]{1,0:T(8,128)(2,1)S(1)}, u32[]{:S(2)}, u32[]{:S(2)}) collective-permute-start(bf16[256,256]{1,0:T(8,128)(2,1)S(1)} %attend.11), channel_id=1, source_target_pairs={{0,1},{1,0},{2,3},{3,2},{4,5},{5,4},{6,7},{7,6},{8,9},{9,8},{10,11... | collective-permute-start | bytes 393224 | tf_op jit(solution)/shard_map/ppermute | solution.py:240
  65.7 1.4 %attend.10.mine_ref = bf16[256,256]{1,0:T(8,128)(2,1)S(1)} custom-call(bf16[256,512]{1,0:T(8,128)(2,1)S(1)} %get-tuple-element.32.refs_0_, bf16[1024,128]{1,0:T(8,128)(2,1)S(1)} %collective-permute-done.11.refs_1_, f32[4,512,128]{2,1,0:T(8,128)S(1)} %attend.9.refs_2_), custom_call_target="tpu_custom_call" | custom-call | flops 1073741824 | bytes 262144 | tf_op jit(solution)/shard_map/attend/pallas_call | solution.py:292
  67.1 0.0 collective-permute-done.13.other_ref
  67.1 0.0 copy-start.11
  67.1 0.0 copy-start.1
  67.2 0.0 copy-start.5
  67.2 0.0 copy-start.6
  67.2 0.0 copy-start.14
  67.2 2.8 %post.1 = bf16[512,512]{1,0:T(8,128)(2,1)} custom-call(s32[1]{0:T(128)S(6)} %rem.18.core_ref, bf16[256,256]{1,0:T(8,128)(2,1)S(1)} %attend.10.mine_ref, bf16[256,256]{1,0:T(8,128)(2,1)S(1)} %collective-permute-done.13.other_ref, f32[256,512]{1,0:T(8,128)S(1)} %get-tuple-element.49.pooled_ref, bf16[256,512]{1,0:T(8,128)(2,1)S(1)} %get-tuple-element.50.member_ref, ...), custom_call_target="tpu_custom_call" | custom-call | tf_op jit(solution)/shard_map/post/pallas_call | solution.py:334
  70.0 2.6 %all-to-all-start.1 = ((bf16[32,16,512]{2,1,0:T(8,128)(2,1)}), bf16[32,16,512]{2,1,0:T(8,128)(2,1)S(1)}, u32[]{:S(2)}, u32[]{:S(2)}) async-start(bf16[32,16,512]{2,1,0:T(8,128)(2,1)} %bitcast.4), calls=%async_computation.1 | async-start | bytes 1048576 | tf_op jit(solution)/shard_map/all_to_all | solution.py:343
  72.6 0.0 copy-done.11
  72.6 0.1 copy.15.live_ref
  72.7 15.9 %all-to-all-done.1 = bf16[32,16,512]{2,1,0:T(8,128)(2,1)S(1)} async-done(((bf16[32,16,512]{2,1,0:T(8,128)(2,1)}), bf16[32,16,512]{2,1,0:T(8,128)(2,1)S(1)}, u32[]{:S(2)}, u32[]{:S(2)}) %all-to-all-start.1) | async-done | bytes 524320 | tf_op jit(solution)/shard_map/all_to_all | solution.py:343
  88.7 0.0 copy-done.5
  88.7 1.8 %decode.1 = bf16[512,512]{1,0:T(8,128)(2,1)} custom-call(bf16[512,512]{1,0:T(8,128)(2,1)S(1)} %bitcast.8, bf16[512,512]{1,0:T(8,128)(2,1)S(1)} %copy-done.1, f32[512,1]{1,0:T(8,128)S(1)} %copy.15.live_ref, f32[1,512]{1,0:T(1,128)S(1)} %bitcast.12, bf16[512,512]{1,0:T(8,128)(2,1)S(1)} %copy-done.5, bf16[512,512]{1,0:T(8,128)(2,1)S(1)} %copy-done.6), custom_call_target="tpu_custom_call" | custom-call | tf_op jit(solution)/shard_map/decode/pallas_call | solution.py:350
  (19 shorter events, 0.1 us)
Async XLA Ops:
  0.0 27.2 %copy-start.12 = (f32[512]{0:T(512)S(1)}, f32[512]{0:T(512)}, u32[]{:S(2)}) copy-start(f32[512]{0:T(512)} %param.21) | copy-start | bytes 6148
  0.0 28.9 %copy-start.15 = (f32[8]{0:T(128)S(1)}, f32[8]{0:T(128)}, u32[]{:S(2)}) copy-start(f32[8]{0:T(128)} %param.20) | copy-start | bytes 100
  0.0 1.1 %copy-start = (bf16[512,512]{1,0:T(8,128)(2,1)S(1)}, bf16[512,512]{1,0:T(8,128)(2,1)}, u32[]{:S(2)}) copy-start(bf16[512,512]{1,0:T(8,128)(2,1)} %sensors_ref.3) | copy-start | bytes 1572868
  1.1 0.7 copy-start.10
  1.8 25.4 %copy-start.8 = (bf16[512,128]{1,0:T(8,128)(2,1)S(1)}, bf16[512,128]{1,0:T(8,128)(2,1)}, u32[]{:S(2)}) copy-start(bf16[512,128]{1,0:T(8,128)(2,1)} %w_key_ref.1) | copy-start | bytes 393220
  1.8 25.4 %copy-start.9 = (bf16[512,128]{1,0:T(8,128)(2,1)S(1)}, bf16[512,128]{1,0:T(8,128)(2,1)}, u32[]{:S(2)}) copy-start(bf16[512,128]{1,0:T(8,128)(2,1)} %w_value_ref.1) | copy-start | bytes 393220
  1.8 27.3 %copy-start.7 = (bf16[512,512]{1,0:T(8,128)(2,1)S(1)}, bf16[512,512]{1,0:T(8,128)(2,1)}, u32[]{:S(2)}) copy-start(bf16[512,512]{1,0:T(8,128)(2,1)} %w_query_ref.1) | copy-start | bytes 1572868
  2.7 24.5 %all-to-all-start = ((bf16[32,72,128]{2,1,0:T(8,128)(2,1)}), bf16[32,72,128]{2,1,0:T(8,128)(2,1)S(1)}, u32[]{:S(2)}, u32[]{:S(2)}) async-start(bf16[32,72,128]{2,1,0:T(8,128)(2,1)} %pack.1), calls=%async_computation | async-start | bytes 1179648 | tf_op jit(solution)/shard_map/all_to_all | solution.py:250
  28.2 1.7 %collective-permute-start = (bf16[256,128]{1,0:T(8,128)(2,1)S(1)}, bf16[256,128]{1,0:T(8,128)(2,1)S(1)}, u32[]{:S(2)}, u32[]{:S(2)}) collective-permute-start(bf16[256,128]{1,0:T(8,128)(2,1)S(1)} %get-tuple-element.28), channel_id=1, source_target_pairs={{0,1},{1,0},{2,3},{3,2},{4,5},{5,4},{6,7},{7,6},{8,9},{9,8},{10,11... | collective-permute-start | bytes 196616 | tf_op jit(solution)/shard_map/ppermute | solution.py:240
  29.9 1.6 %collective-permute-start.1 = (bf16[256,512]{1,0:T(8,128)(2,1)S(1)}, bf16[256,512]{1,0:T(8,128)(2,1)S(1)}, u32[]{:S(2)}, u32[]{:S(2)}) collective-permute-start(bf16[256,512]{1,0:T(8,128)(2,1)S(1)} %get-tuple-element.33), channel_id=1, source_target_pairs={{0,1},{1,0},{2,3},{3,2},{4,5},{5,4},{6,7},{7,6},{8,9},{9,8},{10,11... | collective-permute-start | bytes 786440 | tf_op jit(solution)/shard_map/ppermute | solution.py:240
  30.2 8.0 %collective-permute-start.2 = (bf16[512,128]{1,0:T(8,128)(2,1)S(1)}, bf16[512,128]{1,0:T(8,128)(2,1)S(1)}, u32[]{:S(2)}, u32[]{:S(2)}) collective-permute-start(bf16[512,128]{1,0:T(8,128)(2,1)S(1)} %constant_dynamic-update-slice_fusion.refs_2_), channel_id=1, source_target_pairs={{0,4},{1,5},{2,6},{3,7},{4,0},{5,1},{6,2},{7,3},{8,12},{9,13},{10,... | collective-permute-start | bytes 393224 | tf_op jit(solution)/shard_map/ppermute | solution.py:240
  30.2 8.0 %collective-permute-start.3 = (bf16[512,128]{1,0:T(8,128)(2,1)S(1)}, bf16[512,128]{1,0:T(8,128)(2,1)S(1)}, u32[]{:S(2)}, u32[]{:S(2)}) collective-permute-start(bf16[512,128]{1,0:T(8,128)(2,1)S(1)} %constant_dynamic-update-slice_fusion.refs_2_), channel_id=1, source_target_pairs={{0,8},{1,9},{2,10},{3,11},{4,12},{5,13},{6,14},{7,15},{8,0},{9,1},... | collective-permute-start | bytes 393224 | tf_op jit(solution)/shard_map/ppermute | solution.py:240
  30.7 7.5 %collective-permute-start.4 = (bf16[512,128]{1,0:T(8,128)(2,1)S(1)}, bf16[512,128]{1,0:T(8,128)(2,1)S(1)}, u32[]{:S(2)}, u32[]{:S(2)}) collective-permute-start(bf16[512,128]{1,0:T(8,128)(2,1)S(1)} %constant_dynamic-update-slice_fusion.refs_2_), channel_id=1, source_target_pairs={{0,16},{1,17},{2,18},{3,19},{4,20},{5,21},{6,22},{7,23},{8,24},{9,... | collective-permute-start | bytes 393224 | tf_op jit(solution)/shard_map/ppermute | solution.py:240
  38.2 6.1 %collective-permute-start.6 = (bf16[512,128]{1,0:T(8,128)(2,1)S(1)}, bf16[512,128]{1,0:T(8,128)(2,1)S(1)}, u32[]{:S(2)}, u32[]{:S(2)}) collective-permute-start(bf16[512,128]{1,0:T(8,128)(2,1)S(1)} %collective-permute-done.2.refs_2_), channel_id=1, source_target_pairs={{0,8},{1,9},{2,10},{3,11},{4,12},{5,13},{6,14},{7,15},{8,0},{9,1},... | collective-permute-start | bytes 393224 | tf_op jit(solution)/shard_map/ppermute | solution.py:240
  39.4 5.0 %collective-permute-start.7 = (bf16[512,128]{1,0:T(8,128)(2,1)S(1)}, bf16[512,128]{1,0:T(8,128)(2,1)S(1)}, u32[]{:S(2)}, u32[]{:S(2)}) collective-permute-start(bf16[512,128]{1,0:T(8,128)(2,1)S(1)} %collective-permute-done.2.refs_2_), channel_id=1, source_target_pairs={{0,16},{1,17},{2,18},{3,19},{4,20},{5,21},{6,22},{7,23},{8,24},{9,... | collective-permute-start | bytes 393224 | tf_op jit(solution)/shard_map/ppermute | solution.py:240
  39.7 6.8 %collective-permute-start.5 = (bf16[1024,128]{1,0:T(8,128)(2,1)S(1)}, bf16[1024,128]{1,0:T(8,128)(2,1)S(1)}, u32[]{:S(2)}, u32[]{:S(2)}) collective-permute-start(bf16[1024,128]{1,0:T(8,128)(2,1)S(1)} %pad_maximum_fusion), channel_id=1, source_target_pairs={{0,2},{1,3},{2,0},{3,1},{4,6},{5,7},{6,4},{7,5},{8,10},{9,11},{10,... | collective-permute-start | bytes 786440 | tf_op jit(solution)/shard_map/ppermute | solution.py:240
  39.7 9.4 %collective-permute-start.8 = (bf16[512,128]{1,0:T(8,128)(2,1)S(1)}, bf16[512,128]{1,0:T(8,128)(2,1)S(1)}, u32[]{:S(2)}, u32[]{:S(2)}) collective-permute-start(bf16[512,128]{1,0:T(8,128)(2,1)S(1)} %collective-permute-done.4.refs_4_), channel_id=1, source_target_pairs={{0,8},{1,9},{2,10},{3,11},{4,12},{5,13},{6,14},{7,15},{8,0},{9,1},... | collective-permute-start | bytes 393224 | tf_op jit(solution)/shard_map/ppermute | solution.py:240
  46.5 8.5 %collective-permute-start.10 = (bf16[1024,128]{1,0:T(8,128)(2,1)S(1)}, bf16[1024,128]{1,0:T(8,128)(2,1)S(1)}, u32[]{:S(2)}, u32[]{:S(2)}) collective-permute-start(bf16[1024,128]{1,0:T(8,128)(2,1)S(1)} %collective-permute-done.5.refs_2_), channel_id=1, source_target_pairs={{0,16},{1,17},{2,18},{3,19},{4,20},{5,21},{6,22},{7,23},{8,24},{9,... | collective-permute-start | bytes 786440 | tf_op jit(solution)/shard_map/ppermute | solution.py:240
  47.6 7.4 %collective-permute-start.9 = (bf16[1024,128]{1,0:T(8,128)(2,1)S(1)}, bf16[1024,128]{1,0:T(8,128)(2,1)S(1)}, u32[]{:S(2)}, u32[]{:S(2)}) collective-permute-start(bf16[1024,128]{1,0:T(8,128)(2,1)S(1)} %collective-permute-done.5.refs_2_), channel_id=1, source_target_pairs={{0,8},{1,9},{2,10},{3,11},{4,12},{5,13},{6,14},{7,15},{8,0},{9,1},... | collective-permute-start | bytes 786440 | tf_op jit(solution)/shard_map/ppermute | solution.py:240
  48.0 7.4 %collective-permute-start.12 = (bf16[512,128]{1,0:T(8,128)(2,1)S(1)}, bf16[512,128]{1,0:T(8,128)(2,1)S(1)}, u32[]{:S(2)}, u32[]{:S(2)}) collective-permute-start(bf16[512,128]{1,0:T(8,128)(2,1)S(1)} %collective-permute-done.6.refs_3_), channel_id=1, source_target_pairs={{0,16},{1,17},{2,18},{3,19},{4,20},{5,21},{6,22},{7,23},{8,24},{9,... | collective-permute-start | bytes 393224 | tf_op jit(solution)/shard_map/ppermute | solution.py:240
  55.0 6.1 %collective-permute-start.11 = (bf16[1024,128]{1,0:T(8,128)(2,1)S(1)}, bf16[1024,128]{1,0:T(8,128)(2,1)S(1)}, u32[]{:S(2)}, u32[]{:S(2)}) collective-permute-start(bf16[1024,128]{1,0:T(8,128)(2,1)S(1)} %collective-permute-done.10.refs_3_), channel_id=1, source_target_pairs={{0,8},{1,9},{2,10},{3,11},{4,12},{5,13},{6,14},{7,15},{8,0},{9,1},... | collective-permute-start | bytes 786440 | tf_op jit(solution)/shard_map/ppermute | solution.py:240
  61.1 6.0 %copy-start.3 = (bf16[2048,512]{1,0:T(8,128)(2,1)S(1)}, bf16[2048,512]{1,0:T(8,128)(2,1)}, u32[]{:S(2)}) copy-start(bf16[2048,512]{1,0:T(8,128)(2,1)} %w_outer_ref.1) | copy-start | bytes 6291460
  62.5 4.6 %copy-start.2 = (bf16[512,2048]{1,0:T(8,128)(2,1)S(1)}, bf16[512,2048]{1,0:T(8,128)(2,1)}, u32[]{:S(2)}) copy-start(bf16[512,2048]{1,0:T(8,128)(2,1)} %w_inner_ref.1) | copy-start | bytes 6291460
  62.5 4.6 %copy-start.4 = (bf16[512,512]{1,0:T(8,128)(2,1)S(1)}, bf16[512,512]{1,0:T(8,128)(2,1)}, u32[]{:S(2)}) copy-start(bf16[512,512]{1,0:T(8,128)(2,1)} %w_out_ref.2) | copy-start | bytes 1572868
  62.5 4.6 %copy-start.13 = (f32[512]{0:T(512)S(1)}, f32[512]{0:T(512)}, u32[]{:S(2)}) copy-start(f32[512]{0:T(512)} %param.24) | copy-start | bytes 6148
  62.5 4.5 %collective-permute-start.13 = (bf16[256,256]{1,0:T(8,128)(2,1)S(1)}, bf16[256,256]{1,0:T(8,128)(2,1)S(1)}, u32[]{:S(2)}, u32[]{:S(2)}) collective-permute-start(bf16[256,256]{1,0:T(8,128)(2,1)S(1)} %attend.11), channel_id=1, source_target_pairs={{0,1},{1,0},{2,3},{3,2},{4,5},{5,4},{6,7},{7,6},{8,9},{9,8},{10,11... | collective-permute-start | bytes 393224 | tf_op jit(solution)/shard_map/ppermute | solution.py:240
  67.1 5.4 %copy-start.11 = (s32[512]{0:T(512)S(1)}, s32[512]{0:T(512)}, u32[]{:S(2)}) copy-start(s32[512]{0:T(512)} %param.15) | copy-start | bytes 6148
  67.1 21.5 %copy-start.1 = (bf16[512,512]{1,0:T(8,128)(2,1)S(1)}, bf16[512,512]{1,0:T(8,128)(2,1)}, u32[]{:S(2)}) copy-start(bf16[512,512]{1,0:T(8,128)(2,1)} %sensors_ref.3) | copy-start | bytes 1572868
  67.2 21.5 %copy-start.5 = (bf16[512,512]{1,0:T(8,128)(2,1)S(1)}, bf16[512,512]{1,0:T(8,128)(2,1)}, u32[]{:S(2)}) copy-start(bf16[512,512]{1,0:T(8,128)(2,1)} %w_in_ref.1) | copy-start | bytes 1572868
  67.2 21.5 %copy-start.6 = (bf16[512,512]{1,0:T(8,128)(2,1)S(1)}, bf16[512,512]{1,0:T(8,128)(2,1)}, u32[]{:S(2)}) copy-start(bf16[512,512]{1,0:T(8,128)(2,1)} %w_out_ref.3) | copy-start | bytes 1572868
  67.2 21.5 %copy-start.14 = (f32[512]{0:T(512)S(1)}, f32[512]{0:T(512)}, u32[]{:S(2)}) copy-start(f32[512]{0:T(512)} %param.25) | copy-start | bytes 6148
  70.0 18.7 %all-to-all-start.1 = ((bf16[32,16,512]{2,1,0:T(8,128)(2,1)}), bf16[32,16,512]{2,1,0:T(8,128)(2,1)S(1)}, u32[]{:S(2)}, u32[]{:S(2)}) async-start(bf16[32,16,512]{2,1,0:T(8,128)(2,1)} %bitcast.4), calls=%async_computation.1 | async-start | bytes 1048576 | tf_op jit(solution)/shard_map/all_to_all | solution.py:343

commit v5 on v3

--- a/solution.py
+++ b/solution.py
@@ -15,7 +15,7 @@
 REG_DEV = 256
 LANES = 128
 EPS = 1e-06
-AXES = ("seq", "dp")
+AXIS = "device"
 F32 = jnp.float32
 BF16 = jnp.bfloat16
 NT = (((1,), (1,)), ((), ()))
@@ -34,23 +34,24 @@
     return values * lax.rsqrt(jnp.mean(values * values, axis=-1, keepdims=True) + EPS)
 
 
-def pack_kernel(tile, me_ref, sensors_ref, labels_ref, out_ref):
+def pack_kernel(tile, order, place_ref, sensors_ref, labels_ref, out_ref):
     per_row = LANES // tile
     blocks = sensors_ref.shape[1] // LANES
-    tiles = out_ref.shape[0]
-    mine = lax.rem(me_ref[0], per_row)
+    mine = lax.rem(place_ref[0], per_row)
     labels = (labels_ref[...] + 1).astype(F32)
     lane = lax.broadcasted_iota(jnp.int32, labels.shape, 1)
     own_lanes = (lane // tile) == mine
     for k in range(per_row):
         shift = lax.rem(mine - k + per_row, per_row) * tile
         rolled = jnp.where(own_lanes, pltpu.roll(labels, shift, 1), 0.0)
-        for g in range(tiles // per_row):
-            t = g * per_row + k
+        for at, t in enumerate(order):
+            if t % per_row != k:
+                continue
+            g = t // per_row
             row = jnp.broadcast_to(rolled[g : g + 1, :], (8, LANES)).astype(BF16)
             rows = sensors_ref[t * tile : (t + 1) * tile, :]
             parts = [rows[:, c * LANES : (c + 1) * LANES] for c in range(blocks)]
-            out_ref[t] = jnp.concatenate(parts + [row], axis=0)
+            out_ref[at] = jnp.concatenate(parts + [row], axis=0)
 
 
 def by_heads():
@@ -200,19 +201,23 @@
         ).astype(BF16)
 
 
-def decode_kernel(back_ref, sensors_ref, live_ref, gain_ref, w_in_ref, w_out_ref, out_ref):
-    count = out_ref.shape[0]
-    block = math.gcd(count, 128)
-    for i in range(count // block):
-        rows = slice(i * block, (i + 1) * block)
-        total = back_ref[rows, :].astype(F32) + sensors_ref[rows, :].astype(F32)
+def decode_kernel(tile, order, back_ref, sensors_ref, live_ref, gain_ref, w_in_ref, w_out_ref, out_ref):
+    step = min(len(order), 32)
+    for begin in range(0, len(order), step):
+        tiles = [slice(t * tile, (t + 1) * tile) for t in order[begin : begin + step]]
+        sensors = jnp.concatenate([sensors_ref[rows, :] for rows in tiles], axis=0)
+        back = back_ref[begin * tile : (begin + step) * tile, :]
+        total = back.astype(F32) + sensors.astype(F32)
         dec_in = (rms(total) * gain_ref[...]).astype(BF16)
         hidden = jax.nn.gelu(mm(dec_in, w_in_ref[...])).astype(BF16)
         result = mm(hidden, w_out_ref[...])
-        out_ref[rows, :] = jnp.where(live_ref[rows, :] > 0.0, result, 0.0).astype(BF16)
+        for i, rows in enumerate(tiles):
+            here = result[i * tile : (i + 1) * tile, :]
+            out_ref[rows, :] = jnp.where(live_ref[rows, :] > 0.0, here, 0.0).astype(BF16)
 
 
 def local(
+    order,
     sensors,
     slot_region,
     w_query,
@@ -228,26 +233,32 @@
     w_dec_in,
     w_dec_out,
 ):
-    devices = lax.axis_size(AXES)
+    devices = len(order)
     sen_dev, width = sensors.shape
     tile = sen_dev // devices
-    me = lax.axis_index(AXES).astype(jnp.int32).reshape(1)
+    me = lax.axis_index(AXIS).astype(jnp.int32).reshape(1)
     core = lax.rem(me, 2)
+    place = jnp.asarray([order.index(i) for i in range(devices)], jnp.int32)[me]
     bits = devices.bit_length() - 1
     pay_rows = tile * (width // LANES) + 8
 
     def flipped(value, mask):
-        return lax.ppermute(value, AXES, [(i, i ^ mask) for i in range(devices)])
+        return lax.ppermute(value, AXIS, [(i, i ^ mask) for i in range(devices)])
+
+    def exchanged(value):
+        return lax.all_to_all(
+            value, AXIS, split_axis=0, concat_axis=0, tiled=True, axis_index_groups=[order]
+        )
 
     payload = pl.pallas_call(
-        functools.partial(pack_kernel, tile),
+        functools.partial(pack_kernel, tile, order),
         out_shape=jax.ShapeDtypeStruct((devices, pay_rows, LANES), BF16),
         in_specs=[SMEM, VMEM, VMEM],
         out_specs=VMEM,
         compiler_params=PARAMS,
         name="pack",
-    )(me, sensors, slot_region.reshape(-1, LANES))
-    got = lax.all_to_all(payload, AXES, split_axis=0, concat_axis=0, tiled=True)
+    )(place, sensors, slot_region.reshape(-1, LANES))
+    got = exchanged(payload)
 
     scale = jnp.repeat(temper * (math.log2(math.e) / HEAD_DIM), HEAD_DIM).reshape(1, -1)
     live = (slot_region >= 0).astype(F32).reshape(sen_dev, 1)
@@ -310,19 +321,26 @@
         own = jnp.concatenate([own, flipped(own, 1 << bit)], axis=0)
     near, far = 1 << 1, 1 << 2
 
+    hold = lax.optimization_barrier
     a, b = flipped(own, far), flipped(own, near)
     own_one, own_two = flipped(own, one), flipped(own, two)
     acc = attend([own], None)
-    acc, a, b, own_one, own_two = lax.optimization_barrier((acc, a, b, own_one, own_two))
+    acc, own_one, own_two = hold((acc, own_one, own_two))
+    acc = attend([own_one, own_two], acc)
+    acc, a, b, own_two = hold((acc, a, b, own_two))
 
     ab, c = jnp.concatenate([a, b], axis=0), flipped(a, near)
     ab_one, ab_two, own_corner = flipped(ab, one), flipped(ab, two), flipped(own_two, one)
-    acc = attend([ab, own_one, own_two], acc)
-    acc, c, ab_one, ab_two = lax.optimization_barrier((acc, c, ab_one, ab_two))
-
-    c_one, c_two, ab_corner = flipped(c, one), flipped(c, two), flipped(ab_one, two)
-    acc = attend([c, ab_one, ab_two, own_corner], acc)
-    acc, c_one, c_two = lax.optimization_barrier((acc, c_one, c_two))
+    acc = attend([ab], acc)
+    acc, c, own_corner = hold((acc, c, own_corner))
+
+    c_one, c_two = flipped(c, one), flipped(c, two)
+    acc = attend([c, own_corner], acc)
+    acc, ab_one, ab_two = hold((acc, ab_one, ab_two))
+
+    ab_corner = flipped(ab_one, two)
+    acc = attend([ab_one, ab_two], acc)
+    acc, c_one, c_two = hold((acc, c_one, c_two))
 
     c_corner = flipped(c_two, one)
     acc = attend([c_one, c_two, ab_corner], acc)
@@ -341,33 +359,26 @@
         compiler_params=PARAMS,
         name="post",
     )(core, mine, other_heads, pooled, members, w_out, gain_mlp.reshape(1, width), w_inner, w_outer)
-    returned = lax.all_to_all(
-        back.reshape(devices, tile, width), AXES, split_axis=0, concat_axis=0, tiled=True
-    ).reshape(sen_dev, width)
-
-    rows = math.gcd(sen_dev, 512)
-    by_rows = pl.BlockSpec((rows, width), lambda i: (i, 0))
-    whole = lambda shape: pl.BlockSpec(shape, lambda i: (0, 0))
+    returned = exchanged(back.reshape(devices, tile, width)).reshape(sen_dev, width)
     return pl.pallas_call(
-        decode_kernel,
-        grid=(sen_dev // rows,),
+        functools.partial(decode_kernel, tile, order),
         out_shape=jax.ShapeDtypeStruct((sen_dev, width), BF16),
-        in_specs=[
-            by_rows,
-            by_rows,
-            pl.BlockSpec((rows, 1), lambda i: (i, 0)),
-            whole((1, width)),
-            whole(w_dec_in.shape),
-            whole(w_dec_out.shape),
-        ],
-        out_specs=by_rows,
+        in_specs=[VMEM] * 6,
+        out_specs=VMEM,
         compiler_params=PARAMS,
         name="decode",
     )(returned, sensors, live, gain_dec.reshape(1, width), w_dec_in, w_dec_out)
 
 
 def solution(mesh):
-    placed = (P(AXES, None), P(AXES)) + (P(),) * 12
+    devices, line = mesh.size, mesh.shape["dp"]
+    order = sorted(range(devices), key=lambda i: (i // line, i % 2, i))
+    flat = jax.sharding.Mesh(mesh.devices.reshape(-1), (AXIS,))
+    placed = (P(AXIS, None), P(AXIS)) + (P(),) * 12
     return jax.shard_map(
-        local, mesh=mesh, in_specs=placed, out_specs=P(AXES, None), check_vma=False
+        functools.partial(local, order),
+        mesh=flat,
+        in_specs=placed,
+        out_specs=P(AXIS, None),
+        check_vma=False,
     )

time: 91.2 us -> 96.1 us (1.054)
  waiting for transfers between devices: 38.5 us -> 41.4 us
  local copies, waits for them, and re-layouts: 2.16 us -> 3.42 us
    ppermute x15, waiting for transfers between devices: 5.22 us -> 9.56 us  [flipped(): return lax.ppermute(value, AXIS, [(i, i ^ mask) for i in range(devices)])]
    all_to_all x2, waiting for transfers between devices: 33.3 us -> 31.8 us  [exchanged(): lax.all_to_all(value, AXIS, split_axis=0, concat_axis=0, tiled=True, axis...]
    gather x0 -> x1, local copies, waits for them, and re-layouts: none -> 1.28 us  [local(): place = jnp.asarray([order.index(i) for i in range(devices)], jnp.int32)[me]]
    pallas_call x6 -> x8, Pallas kernels: 19.8 us -> 20.3 us  [attend(): pl.pallas_call(functools.partial(attend_kernel, len(parts), row_parts, ac...]
  transfers between devices with their start and end apart: 17 -> 17, of which waited for: 4 -> 8; matrix products, arithmetic and copies ran while one was open for 0% -> 0% of each run, Pallas kernels for 22% -> 21%
where the time goes in v5:
time: 96.1 us; the launch traced here: 95.8 us
  waiting for transfers between devices  41.4 us (43%)
  Pallas kernels  28.3 us (29%)
  starting transfers between devices  22.3 us (23%)
  local copies, waits for them, and re-layouts  3.42 us (4%)
    all_to_all x2, waiting for transfers between devices, exchanged(): lax.all_to_all(value, AXIS, split_axis=0, concat_axis=0, tiled=True, axis...  31.8 us
    pallas_call x8, Pallas kernels, attend(): pl.pallas_call(functools.partial(attend_kernel, len(parts), row_parts, ac...  20.3 us
    ppermute x15, starting transfers between devices, flipped(): return lax.ppermute(value, AXIS, [(i, i ^ mask) for i in range(devices)])  12 us
    all_to_all x2, starting transfers between devices, exchanged(): lax.all_to_all(value, AXIS, split_axis=0, concat_axis=0, tiled=True, axis...  10.3 us
    ppermute x15, waiting for transfers between devices, flipped(): return lax.ppermute(value, AXIS, [(i, i ^ mask) for i in range(devices)])  9.56 us
    pallas_call x1, Pallas kernels, local(): pl.pallas_call(post_kernel, out_shape=jax.ShapeDtypeStruct((sen_dev, widt...  2.81 us
  transfers between devices with their start and end apart: 17, of which 8 were waited for; matrix products, arithmetic and copies ran while one was open for 0% of the time, Pallas kernels for 21%

profile of v5, /device:TPU:1, one launch (start us, length us, event | category | flops | bytes accessed | tf_op | source)
XLA Modules:
  0.0 95.8 jit_solution(4644724268559987371)
XLA Ops:
  0.0 1.3 %dynamic-slice.4.place_ref = s32[1]{0:T(128)} dynamic-slice(s32[32]{0:T(128)} %constant.20.clone..sunk.2, s32[]{:T(128)} %bitcast.1), dynamic_slice_sizes={1} | dynamic-slice | bytes 12 | tf_op jit(solution)/shard_map/gather | solution.py:241
  1.3 1.0 %copy-done = bf16[512,512]{1,0:T(8,128)(2,1)S(1)} copy-done((bf16[512,512]{1,0:T(8,128)(2,1)S(1)}, bf16[512,512]{1,0:T(8,128)(2,1)}, u32[]{:S(2)}) %copy-start) | copy-done | bytes 524312
  2.3 0.7 copy-done.10
  3.0 1.6 %pack.1 = bf16[32,72,128]{2,1,0:T(8,128)(2,1)} custom-call(s32[1]{0:T(128)} %dynamic-slice.4.place_ref, bf16[512,512]{1,0:T(8,128)(2,1)S(1)} %copy-done, s32[4,128]{1,0:T(4,128)S(1)} %bitcast.10), custom_call_target="tpu_custom_call" | custom-call | tf_op jit(solution)/shard_map/pack/pallas_call | solution.py:253
  4.6 7.1 %all-to-all-start = ((bf16[32,72,128]{2,1,0:T(8,128)(2,1)}), bf16[32,72,128]{2,1,0:T(8,128)(2,1)S(1)}, u32[]{:S(2)}, u32[]{:S(2)}) async-start(bf16[32,72,128]{2,1,0:T(8,128)(2,1)} %pack.1), calls=%async_computation | async-start | bytes 1179648 | tf_op jit(solution)/shard_map/all_to_all | solution.py:249
  11.7 16.7 %all-to-all-done.got_ref = bf16[32,72,128]{2,1,0:T(8,128)(2,1)S(1)} async-done(((bf16[32,72,128]{2,1,0:T(8,128)(2,1)}), bf16[32,72,128]{2,1,0:T(8,128)(2,1)S(1)}, u32[]{:S(2)}, u32[]{:S(2)}) %all-to-all-start) | async-done | bytes 589856 | tf_op jit(solution)/shard_map/all_to_all | solution.py:249
  28.4 0.0 copy-done.12
  28.4 0.0 copy-done.8
  28.4 1.0 %pool.1 = (f32[256,512]{1,0:T(8,128)S(1)}, bf16[256,512]{1,0:T(8,128)(2,1)S(1)}, bf16[256,512]{1,0:T(8,128)(2,1)S(1)}, bf16[256,128]{1,0:T(8,128)(2,1)S(1)}, bf16[256,128]{1,0:T(8,128)(2,1)S(1)}) custom-call(s32[1]{0:T(128)S(6)} %rem.18.core_ref, bf16[32,72,128]{2,1,0:T(8,128)(2,1)S(1)} %all-to-all-done.got_ref, bf16[512,128]{1,0:T(8,128)(2,1)S(1)} %copy-done.8, ...), custom_call_target="tpu_custom_call" | custom-call | tf_op jit(solution)/shard_map/pool/pallas_call | solution.py:267
  29.4 0.1 collective-permute-start
  29.5 0.1 broadcast_in_dim.7
  29.6 0.1 reshape_reshape.3.scale_ref
  29.7 0.8 query.1
  30.5 0.3 collective-permute-done
  30.8 0.3 collective-permute-start.1
  31.1 1.3 %collective-permute-start.2 = (bf16[512,128]{1,0:T(8,128)(2,1)S(1)}, bf16[512,128]{1,0:T(8,128)(2,1)S(1)}, u32[]{:S(2)}, u32[]{:S(2)}) collective-permute-start(bf16[512,128]{1,0:T(8,128)(2,1)S(1)} %constant_dynamic-update-slice_fusion.refs_2_), channel_id=1, source_target_pairs={{0,8},{1,9},{2,10},{3,11},{4,12},{5,13},{6,14},{7,15},{8,0},{9,1},... | collective-permute-start | bytes 393224 | tf_op jit(solution)/shard_map/ppermute | solution.py:246
  32.3 0.3 collective-permute-start.3
  32.6 0.7 collective-permute-start.4
  33.3 1.2 %collective-permute-start.5 = (bf16[512,128]{1,0:T(8,128)(2,1)S(1)}, bf16[512,128]{1,0:T(8,128)(2,1)S(1)}, u32[]{:S(2)}, u32[]{:S(2)}) collective-permute-start(bf16[512,128]{1,0:T(8,128)(2,1)S(1)} %constant_dynamic-update-slice_fusion.refs_2_), channel_id=1, source_target_pairs={{0,2},{1,3},{2,0},{3,1},{4,6},{5,7},{6,4},{7,5},{8,10},{9,11},{10,... | collective-permute-start | bytes 393224 | tf_op jit(solution)/shard_map/ppermute | solution.py:246
  34.4 0.0 collective-permute-done.1.refs_1_.refs_0_
  34.4 1.4 %attend.8.refs_4_ = f32[4,512,128]{2,1,0:T(8,128)S(1)} custom-call(bf16[256,512]{1,0:T(8,128)(2,1)S(1)} %get-tuple-element.37.refs_0_, bf16[256,512]{1,0:T(8,128)(2,1)S(1)} %collective-permute-done.1.refs_1_.refs_0_, bf16[512,128]{1,0:T(8,128)(2,1)S(1)} %constant_dynamic-update-slice_fusion.refs_2_), custom_call_target="tpu_custom_call" | custom-call | flops 1073741824 | bytes 131072 | tf_op jit(solution)/shard_map/attend/pallas_call | solution.py:303
  35.8 0.2 collective-permute-done.2.refs_2_
  36.0 0.9 collective-permute-done.3.refs_3_
  36.9 2.4 %attend.9.refs_3_ = f32[4,512,128]{2,1,0:T(8,128)S(1)} custom-call(bf16[256,512]{1,0:T(8,128)(2,1)S(1)} %get-tuple-element.37.refs_0_, bf16[256,512]{1,0:T(8,128)(2,1)S(1)} %collective-permute-done.1.refs_1_.refs_0_, bf16[512,128]{1,0:T(8,128)(2,1)S(1)} %collective-permute-done.2.refs_2_, bf16[512,128]{1,0:T(8,128)(2,1)S(1)} %collective-permute-done.3.refs_3_, ...), custom_call_target="tpu_custom_call" | custom-call | flops 2147483648 | bytes 262144 | tf_op jit(solution)/shard_map/attend/pallas_call | solution.py:303
  39.3 2.2 %collective-permute-done.4 = bf16[512,128]{1,0:T(8,128)(2,1)S(1)} collective-permute-done((bf16[512,128]{1,0:T(8,128)(2,1)S(1)}, bf16[512,128]{1,0:T(8,128)(2,1)S(1)}, u32[]{:S(2)}, u32[]{:S(2)}) %collective-permute-start.4) | collective-permute-done | bytes 131104 | tf_op jit(solution)/shard_map/ppermute | solution.py:246
  41.5 0.0 collective-permute-done.5
  41.5 0.1 collective-permute-start.6
  41.6 1.4 %collective-permute-start.8 = (bf16[1024,128]{1,0:T(8,128)(2,1)S(1)}, bf16[1024,128]{1,0:T(8,128)(2,1)S(1)}, u32[]{:S(2)}, u32[]{:S(2)}) collective-permute-start(bf16[1024,128]{1,0:T(8,128)(2,1)S(1)} %constant_dynamic-update-slice_fusion.2.refs_2_), channel_id=1, source_target_pairs={{0,8},{1,9},{2,10},{3,11},{4,12},{5,13},{6,14},{7,15},{8,0},{9,1},... | collective-permute-start | bytes 786440 | tf_op jit(solution)/shard_map/ppermute | solution.py:246
  43.0 0.1 collective-permute-start.9
  43.1 1.4 %collective-permute-start.7 = (bf16[512,128]{1,0:T(8,128)(2,1)S(1)}, bf16[512,128]{1,0:T(8,128)(2,1)S(1)}, u32[]{:S(2)}, u32[]{:S(2)}) collective-permute-start(bf16[512,128]{1,0:T(8,128)(2,1)S(1)} %collective-permute-done.3.refs_3_), channel_id=1, source_target_pairs={{0,8},{1,9},{2,10},{3,11},{4,12},{5,13},{6,14},{7,15},{8,0},{9,1},... | collective-permute-start | bytes 393224 | tf_op jit(solution)/shard_map/ppermute | solution.py:246
  44.5 2.4 %attend.10.refs_4_ = f32[4,512,128]{2,1,0:T(8,128)S(1)} custom-call(bf16[256,512]{1,0:T(8,128)(2,1)S(1)} %get-tuple-element.37.refs_0_, bf16[256,512]{1,0:T(8,128)(2,1)S(1)} %collective-permute-done.1.refs_1_.refs_0_, bf16[1024,128]{1,0:T(8,128)(2,1)S(1)} %constant_dynamic-update-slice_fusion.2.refs_2_, f32[4,512,128]{2,1,0:T(8,128)S(1)} %attend.9.refs_3_), custom_call_target="tpu_custom_call" | custom-call | flops 2147483648 | bytes 262144 | tf_op jit(solution)/shard_map/attend/pallas_call | solution.py:303
  46.9 0.0 collective-permute-done.6.refs_2_
  46.9 4.6 %collective-permute-done.7.refs_3_ = bf16[512,128]{1,0:T(8,128)(2,1)S(1)} collective-permute-done((bf16[512,128]{1,0:T(8,128)(2,1)S(1)}, bf16[512,128]{1,0:T(8,128)(2,1)S(1)}, u32[]{:S(2)}, u32[]{:S(2)}) %collective-permute-start.7) | collective-permute-done | bytes 131104 | tf_op jit(solution)/shard_map/ppermute | solution.py:246
  51.5 1.6 %collective-permute-start.10 = (bf16[512,128]{1,0:T(8,128)(2,1)S(1)}, bf16[512,128]{1,0:T(8,128)(2,1)S(1)}, u32[]{:S(2)}, u32[]{:S(2)}) collective-permute-start(bf16[512,128]{1,0:T(8,128)(2,1)S(1)} %collective-permute-done.6.refs_2_), channel_id=1, source_target_pairs={{0,8},{1,9},{2,10},{3,11},{4,12},{5,13},{6,14},{7,15},{8,0},{9,1},... | collective-permute-start | bytes 393224 | tf_op jit(solution)/shard_map/ppermute | solution.py:246
  53.1 0.1 collective-permute-start.11
  53.2 2.4 %attend.11.refs_4_ = f32[4,512,128]{2,1,0:T(8,128)S(1)} custom-call(bf16[256,512]{1,0:T(8,128)(2,1)S(1)} %get-tuple-element.37.refs_0_, bf16[256,512]{1,0:T(8,128)(2,1)S(1)} %collective-permute-done.1.refs_1_.refs_0_, bf16[512,128]{1,0:T(8,128)(2,1)S(1)} %collective-permute-done.6.refs_2_, bf16[512,128]{1,0:T(8,128)(2,1)S(1)} %collective-permute-done.7.refs_3_, ...), custom_call_target="tpu_custom_call" | custom-call | flops 2147483648 | bytes 262144 | tf_op jit(solution)/shard_map/attend/pallas_call | solution.py:303
  55.6 0.0 collective-permute-done.8.refs_2_
  55.7 0.0 collective-permute-done.9.refs_3_
  55.7 1.4 %collective-permute-start.13 = (bf16[1024,128]{1,0:T(8,128)(2,1)S(1)}, bf16[1024,128]{1,0:T(8,128)(2,1)S(1)}, u32[]{:S(2)}, u32[]{:S(2)}) collective-permute-start(bf16[1024,128]{1,0:T(8,128)(2,1)S(1)} %collective-permute-done.8.refs_2_), channel_id=1, source_target_pairs={{0,16},{1,17},{2,18},{3,19},{4,20},{5,21},{6,22},{7,23},{8,24},{9,... | collective-permute-start | bytes 786440 | tf_op jit(solution)/shard_map/ppermute | solution.py:246
  57.1 4.8 %attend.12.refs_5_ = f32[4,512,128]{2,1,0:T(8,128)S(1)} custom-call(bf16[256,512]{1,0:T(8,128)(2,1)S(1)} %get-tuple-element.37.refs_0_, bf16[256,512]{1,0:T(8,128)(2,1)S(1)} %collective-permute-done.1.refs_1_.refs_0_, bf16[1024,128]{1,0:T(8,128)(2,1)S(1)} %collective-permute-done.8.refs_2_, bf16[1024,128]{1,0:T(8,128)(2,1)S(1)} %collective-permute-done.9.refs_3_, ...), custom_call_target="tpu_custom_call" | custom-call | flops 4294967296 | bytes 524288 | tf_op jit(solution)/shard_map/attend/pallas_call | solution.py:303
  61.9 0.0 collective-permute-done.10.refs_2_
  61.9 0.0 collective-permute-done.11.refs_3_
  61.9 0.2 collective-permute-start.12
  62.1 1.5 %collective-permute-done.13.refs_4_ = bf16[1024,128]{1,0:T(8,128)(2,1)S(1)} collective-permute-done((bf16[1024,128]{1,0:T(8,128)(2,1)S(1)}, bf16[1024,128]{1,0:T(8,128)(2,1)S(1)}, u32[]{:S(2)}, u32[]{:S(2)}) %collective-permute-start.13) | collective-permute-done | bytes 262176 | tf_op jit(solution)/shard_map/ppermute | solution.py:246
  63.6 4.6 %attend.13.refs_2_ = f32[4,512,128]{2,1,0:T(8,128)S(1)} custom-call(bf16[256,512]{1,0:T(8,128)(2,1)S(1)} %get-tuple-element.37.refs_0_, bf16[256,512]{1,0:T(8,128)(2,1)S(1)} %collective-permute-done.1.refs_1_.refs_0_, bf16[512,128]{1,0:T(8,128)(2,1)S(1)} %collective-permute-done.10.refs_2_, bf16[512,128]{1,0:T(8,128)(2,1)S(1)} %collective-permute-done.11.refs_3_, ...), custom_call_target="tpu_custom_call" | custom-call | flops 4294967296 | bytes 524288 | tf_op jit(solution)/shard_map/attend/pallas_call | solution.py:303
  68.2 0.0 copy-start.2
  68.2 0.0 copy-start.4
  68.2 0.0 copy-start.13
  68.2 0.0 collective-permute-done.12.refs_1_
  68.2 1.1 %attend.15 = bf16[256,256]{1,0:T(8,128)(2,1)S(1)} custom-call(bf16[256,512]{1,0:T(8,128)(2,1)S(1)} %collective-permute-done.1.refs_1_.refs_0_, bf16[512,128]{1,0:T(8,128)(2,1)S(1)} %collective-permute-done.12.refs_1_, f32[4,512,128]{2,1,0:T(8,128)S(1)} %attend.13.refs_2_), custom_call_target="tpu_custom_call" | custom-call | flops 536870912 | bytes 131072 | tf_op jit(solution)/shard_map/attend/pallas_call | solution.py:303
  69.4 1.9 %collective-permute-start.14 = (bf16[256,256]{1,0:T(8,128)(2,1)S(1)}, bf16[256,256]{1,0:T(8,128)(2,1)S(1)}, u32[]{:S(2)}, u32[]{:S(2)}) collective-permute-start(bf16[256,256]{1,0:T(8,128)(2,1)S(1)} %attend.15), channel_id=1, source_target_pairs={{0,1},{1,0},{2,3},{3,2},{4,5},{5,4},{6,7},{7,6},{8,9},{9,8},{10,11... | collective-permute-start | bytes 393224 | tf_op jit(solution)/shard_map/ppermute | solution.py:246
  71.3 1.1 %attend.14.mine_ref = bf16[256,256]{1,0:T(8,128)(2,1)S(1)} custom-call(bf16[256,512]{1,0:T(8,128)(2,1)S(1)} %get-tuple-element.37.refs_0_, bf16[512,128]{1,0:T(8,128)(2,1)S(1)} %collective-permute-done.12.refs_1_, f32[4,512,128]{2,1,0:T(8,128)S(1)} %attend.13.refs_2_), custom_call_target="tpu_custom_call" | custom-call | flops 536870912 | bytes 131072 | tf_op jit(solution)/shard_map/attend/pallas_call | solution.py:303
  72.4 0.0 collective-permute-done.14.other_ref
  72.5 0.0 copy-start.11
  72.5 0.0 copy-start.1
  72.5 0.0 copy-start.5
  72.5 0.0 copy-start.6
  72.5 0.0 copy-start.14
  72.6 2.8 %post.1 = bf16[512,512]{1,0:T(8,128)(2,1)} custom-call(s32[1]{0:T(128)S(6)} %rem.18.core_ref, bf16[256,256]{1,0:T(8,128)(2,1)S(1)} %attend.14.mine_ref, bf16[256,256]{1,0:T(8,128)(2,1)S(1)} %collective-permute-done.14.other_ref, f32[256,512]{1,0:T(8,128)S(1)} %get-tuple-element.59.pooled_ref, bf16[256,512]{1,0:T(8,128)(2,1)S(1)} %get-tuple-element.60.member_ref, ...), custom_call_target="tpu_custom_call" | custom-call | tf_op jit(solution)/shard_map/post/pallas_call | solution.py:353
  75.4 3.3 %all-to-all-start.1 = ((bf16[32,16,512]{2,1,0:T(8,128)(2,1)}), bf16[32,16,512]{2,1,0:T(8,128)(2,1)S(1)}, u32[]{:S(2)}, u32[]{:S(2)}) async-start(bf16[32,16,512]{2,1,0:T(8,128)(2,1)} %bitcast.5), calls=%async_computation.1 | async-start | bytes 1048576 | tf_op jit(solution)/shard_map/all_to_all | solution.py:249
  78.7 0.1 copy.16.live_ref
  78.8 15.1 %all-to-all-done.1 = bf16[32,16,512]{2,1,0:T(8,128)(2,1)S(1)} async-done(((bf16[32,16,512]{2,1,0:T(8,128)(2,1)}), bf16[32,16,512]{2,1,0:T(8,128)(2,1)S(1)}, u32[]{:S(2)}, u32[]{:S(2)}) %all-to-all-start.1) | async-done | bytes 524320 | tf_op jit(solution)/shard_map/all_to_all | solution.py:249
  93.9 0.0 copy-done.1
  93.9 1.8 %decode.1 = bf16[512,512]{1,0:T(8,128)(2,1)} custom-call(bf16[512,512]{1,0:T(8,128)(2,1)S(1)} %bitcast.9, bf16[512,512]{1,0:T(8,128)(2,1)S(1)} %copy-done.1, f32[512,1]{1,0:T(8,128)S(1)} %copy.16.live_ref, f32[1,512]{1,0:T(1,128)S(1)} %bitcast.13, bf16[512,512]{1,0:T(8,128)(2,1)S(1)} %copy-done.5, bf16[512,512]{1,0:T(8,128)(2,1)S(1)} %copy-done.6), custom_call_target="tpu_custom_call" | custom-call | tf_op jit(solution)/shard_map/decode/pallas_call | solution.py:363
  (25 shorter events, 0.1 us)
Async XLA Ops:
  0.0 28.4 %copy-start.12 = (f32[512]{0:T(512)S(1)}, f32[512]{0:T(512)}, u32[]{:S(2)}) copy-start(f32[512]{0:T(512)} %param.22) | copy-start | bytes 6148
  0.0 29.5 %copy-start.15 = (f32[8]{0:T(128)S(1)}, f32[8]{0:T(128)}, u32[]{:S(2)}) copy-start(f32[8]{0:T(128)} %param.21) | copy-start | bytes 100
  1.3 1.0 %copy-start = (bf16[512,512]{1,0:T(8,128)(2,1)S(1)}, bf16[512,512]{1,0:T(8,128)(2,1)}, u32[]{:S(2)}) copy-start(bf16[512,512]{1,0:T(8,128)(2,1)} %sensors_ref.3) | copy-start | bytes 1572868
  2.3 0.7 copy-start.10
  3.0 25.4 %copy-start.8 = (bf16[512,128]{1,0:T(8,128)(2,1)S(1)}, bf16[512,128]{1,0:T(8,128)(2,1)}, u32[]{:S(2)}) copy-start(bf16[512,128]{1,0:T(8,128)(2,1)} %w_key_ref.1) | copy-start | bytes 393220
  3.0 25.4 %copy-start.9 = (bf16[512,128]{1,0:T(8,128)(2,1)S(1)}, bf16[512,128]{1,0:T(8,128)(2,1)}, u32[]{:S(2)}) copy-start(bf16[512,128]{1,0:T(8,128)(2,1)} %w_value_ref.1) | copy-start | bytes 393220
  3.0 26.7 %copy-start.7 = (bf16[512,512]{1,0:T(8,128)(2,1)S(1)}, bf16[512,512]{1,0:T(8,128)(2,1)}, u32[]{:S(2)}) copy-start(bf16[512,512]{1,0:T(8,128)(2,1)} %w_query_ref.1) | copy-start | bytes 1572868
  4.6 23.8 %all-to-all-start = ((bf16[32,72,128]{2,1,0:T(8,128)(2,1)}), bf16[32,72,128]{2,1,0:T(8,128)(2,1)S(1)}, u32[]{:S(2)}, u32[]{:S(2)}) async-start(bf16[32,72,128]{2,1,0:T(8,128)(2,1)} %pack.1), calls=%async_computation | async-start | bytes 1179648 | tf_op jit(solution)/shard_map/all_to_all | solution.py:249
  29.4 1.3 %collective-permute-start = (bf16[256,128]{1,0:T(8,128)(2,1)S(1)}, bf16[256,128]{1,0:T(8,128)(2,1)S(1)}, u32[]{:S(2)}, u32[]{:S(2)}) collective-permute-start(bf16[256,128]{1,0:T(8,128)(2,1)S(1)} %get-tuple-element.33), channel_id=1, source_target_pairs={{0,1},{1,0},{2,3},{3,2},{4,5},{5,4},{6,7},{7,6},{8,9},{9,8},{10,11... | collective-permute-start | bytes 196616 | tf_op jit(solution)/shard_map/ppermute | solution.py:246
  30.8 3.7 %collective-permute-start.1 = (bf16[256,512]{1,0:T(8,128)(2,1)S(1)}, bf16[256,512]{1,0:T(8,128)(2,1)S(1)}, u32[]{:S(2)}, u32[]{:S(2)}) collective-permute-start(bf16[256,512]{1,0:T(8,128)(2,1)S(1)} %get-tuple-element.38), channel_id=1, source_target_pairs={{0,1},{1,0},{2,3},{3,2},{4,5},{5,4},{6,7},{7,6},{8,9},{9,8},{10,11... | collective-permute-start | bytes 786440 | tf_op jit(solution)/shard_map/ppermute | solution.py:246
  31.1 4.9 %collective-permute-start.2 = (bf16[512,128]{1,0:T(8,128)(2,1)S(1)}, bf16[512,128]{1,0:T(8,128)(2,1)S(1)}, u32[]{:S(2)}, u32[]{:S(2)}) collective-permute-start(bf16[512,128]{1,0:T(8,128)(2,1)S(1)} %constant_dynamic-update-slice_fusion.refs_2_), channel_id=1, source_target_pairs={{0,8},{1,9},{2,10},{3,11},{4,12},{5,13},{6,14},{7,15},{8,0},{9,1},... | collective-permute-start | bytes 393224 | tf_op jit(solution)/shard_map/ppermute | solution.py:246
  32.3 4.6 %collective-permute-start.3 = (bf16[512,128]{1,0:T(8,128)(2,1)S(1)}, bf16[512,128]{1,0:T(8,128)(2,1)S(1)}, u32[]{:S(2)}, u32[]{:S(2)}) collective-permute-start(bf16[512,128]{1,0:T(8,128)(2,1)S(1)} %constant_dynamic-update-slice_fusion.refs_2_), channel_id=1, source_target_pairs={{0,16},{1,17},{2,18},{3,19},{4,20},{5,21},{6,22},{7,23},{8,24},{9,... | collective-permute-start | bytes 393224 | tf_op jit(solution)/shard_map/ppermute | solution.py:246
  32.6 8.9 %collective-permute-start.4 = (bf16[512,128]{1,0:T(8,128)(2,1)S(1)}, bf16[512,128]{1,0:T(8,128)(2,1)S(1)}, u32[]{:S(2)}, u32[]{:S(2)}) collective-permute-start(bf16[512,128]{1,0:T(8,128)(2,1)S(1)} %constant_dynamic-update-slice_fusion.refs_2_), channel_id=1, source_target_pairs={{0,4},{1,5},{2,6},{3,7},{4,0},{5,1},{6,2},{7,3},{8,12},{9,13},{10,... | collective-permute-start | bytes 393224 | tf_op jit(solution)/shard_map/ppermute | solution.py:246
  33.3 8.2 %collective-permute-start.5 = (bf16[512,128]{1,0:T(8,128)(2,1)S(1)}, bf16[512,128]{1,0:T(8,128)(2,1)S(1)}, u32[]{:S(2)}, u32[]{:S(2)}) collective-permute-start(bf16[512,128]{1,0:T(8,128)(2,1)S(1)} %constant_dynamic-update-slice_fusion.refs_2_), channel_id=1, source_target_pairs={{0,2},{1,3},{2,0},{3,1},{4,6},{5,7},{6,4},{7,5},{8,10},{9,11},{10,... | collective-permute-start | bytes 393224 | tf_op jit(solution)/shard_map/ppermute | solution.py:246
  41.5 5.4 %collective-permute-start.6 = (bf16[512,128]{1,0:T(8,128)(2,1)S(1)}, bf16[512,128]{1,0:T(8,128)(2,1)S(1)}, u32[]{:S(2)}, u32[]{:S(2)}) collective-permute-start(bf16[512,128]{1,0:T(8,128)(2,1)S(1)} %collective-permute-done.4), channel_id=1, source_target_pairs={{0,2},{1,3},{2,0},{3,1},{4,6},{5,7},{6,4},{7,5},{8,10},{9,11},{10,... | collective-permute-start | bytes 393224 | tf_op jit(solution)/shard_map/ppermute | solution.py:246
  41.6 14.0 %collective-permute-start.8 = (bf16[1024,128]{1,0:T(8,128)(2,1)S(1)}, bf16[1024,128]{1,0:T(8,128)(2,1)S(1)}, u32[]{:S(2)}, u32[]{:S(2)}) collective-permute-start(bf16[1024,128]{1,0:T(8,128)(2,1)S(1)} %constant_dynamic-update-slice_fusion.2.refs_2_), channel_id=1, source_target_pairs={{0,8},{1,9},{2,10},{3,11},{4,12},{5,13},{6,14},{7,15},{8,0},{9,1},... | collective-permute-start | bytes 786440 | tf_op jit(solution)/shard_map/ppermute | solution.py:246
  43.0 12.6 %collective-permute-start.9 = (bf16[1024,128]{1,0:T(8,128)(2,1)S(1)}, bf16[1024,128]{1,0:T(8,128)(2,1)S(1)}, u32[]{:S(2)}, u32[]{:S(2)}) collective-permute-start(bf16[1024,128]{1,0:T(8,128)(2,1)S(1)} %constant_dynamic-update-slice_fusion.2.refs_2_), channel_id=1, source_target_pairs={{0,16},{1,17},{2,18},{3,19},{4,20},{5,21},{6,22},{7,23},{8,24},{9,... | collective-permute-start | bytes 786440 | tf_op jit(solution)/shard_map/ppermute | solution.py:246
  43.1 8.4 %collective-permute-start.7 = (bf16[512,128]{1,0:T(8,128)(2,1)S(1)}, bf16[512,128]{1,0:T(8,128)(2,1)S(1)}, u32[]{:S(2)}, u32[]{:S(2)}) collective-permute-start(bf16[512,128]{1,0:T(8,128)(2,1)S(1)} %collective-permute-done.3.refs_3_), channel_id=1, source_target_pairs={{0,8},{1,9},{2,10},{3,11},{4,12},{5,13},{6,14},{7,15},{8,0},{9,1},... | collective-permute-start | bytes 393224 | tf_op jit(solution)/shard_map/ppermute | solution.py:246
  51.5 10.4 %collective-permute-start.10 = (bf16[512,128]{1,0:T(8,128)(2,1)S(1)}, bf16[512,128]{1,0:T(8,128)(2,1)S(1)}, u32[]{:S(2)}, u32[]{:S(2)}) collective-permute-start(bf16[512,128]{1,0:T(8,128)(2,1)S(1)} %collective-permute-done.6.refs_2_), channel_id=1, source_target_pairs={{0,8},{1,9},{2,10},{3,11},{4,12},{5,13},{6,14},{7,15},{8,0},{9,1},... | collective-permute-start | bytes 393224 | tf_op jit(solution)/shard_map/ppermute | solution.py:246
  53.1 8.8 %collective-permute-start.11 = (bf16[512,128]{1,0:T(8,128)(2,1)S(1)}, bf16[512,128]{1,0:T(8,128)(2,1)S(1)}, u32[]{:S(2)}, u32[]{:S(2)}) collective-permute-start(bf16[512,128]{1,0:T(8,128)(2,1)S(1)} %collective-permute-done.6.refs_2_), channel_id=1, source_target_pairs={{0,16},{1,17},{2,18},{3,19},{4,20},{5,21},{6,22},{7,23},{8,24},{9,... | collective-permute-start | bytes 393224 | tf_op jit(solution)/shard_map/ppermute | solution.py:246
  55.7 7.9 %collective-permute-start.13 = (bf16[1024,128]{1,0:T(8,128)(2,1)S(1)}, bf16[1024,128]{1,0:T(8,128)(2,1)S(1)}, u32[]{:S(2)}, u32[]{:S(2)}) collective-permute-start(bf16[1024,128]{1,0:T(8,128)(2,1)S(1)} %collective-permute-done.8.refs_2_), channel_id=1, source_target_pairs={{0,16},{1,17},{2,18},{3,19},{4,20},{5,21},{6,22},{7,23},{8,24},{9,... | collective-permute-start | bytes 786440 | tf_op jit(solution)/shard_map/ppermute | solution.py:246
  61.9 6.3 %collective-permute-start.12 = (bf16[512,128]{1,0:T(8,128)(2,1)S(1)}, bf16[512,128]{1,0:T(8,128)(2,1)S(1)}, u32[]{:S(2)}, u32[]{:S(2)}) collective-permute-start(bf16[512,128]{1,0:T(8,128)(2,1)S(1)} %collective-permute-done.11.refs_3_), channel_id=1, source_target_pairs={{0,8},{1,9},{2,10},{3,11},{4,12},{5,13},{6,14},{7,15},{8,0},{9,1},... | collective-permute-start | bytes 393224 | tf_op jit(solution)/shard_map/ppermute | solution.py:246
  63.6 8.9 %copy-start.3 = (bf16[2048,512]{1,0:T(8,128)(2,1)S(1)}, bf16[2048,512]{1,0:T(8,128)(2,1)}, u32[]{:S(2)}) copy-start(bf16[2048,512]{1,0:T(8,128)(2,1)} %w_outer_ref.1) | copy-start | bytes 6291460
  68.2 4.3 %copy-start.2 = (bf16[512,2048]{1,0:T(8,128)(2,1)S(1)}, bf16[512,2048]{1,0:T(8,128)(2,1)}, u32[]{:S(2)}) copy-start(bf16[512,2048]{1,0:T(8,128)(2,1)} %w_inner_ref.1) | copy-start | bytes 6291460
  68.2 4.3 %copy-start.4 = (bf16[512,512]{1,0:T(8,128)(2,1)S(1)}, bf16[512,512]{1,0:T(8,128)(2,1)}, u32[]{:S(2)}) copy-start(bf16[512,512]{1,0:T(8,128)(2,1)} %w_out_ref.2) | copy-start | bytes 1572868
  68.2 4.3 %copy-start.13 = (f32[512]{0:T(512)S(1)}, f32[512]{0:T(512)}, u32[]{:S(2)}) copy-start(f32[512]{0:T(512)} %param.25) | copy-start | bytes 6148
  69.4 3.1 %collective-permute-start.14 = (bf16[256,256]{1,0:T(8,128)(2,1)S(1)}, bf16[256,256]{1,0:T(8,128)(2,1)S(1)}, u32[]{:S(2)}, u32[]{:S(2)}) collective-permute-start(bf16[256,256]{1,0:T(8,128)(2,1)S(1)} %attend.15), channel_id=1, source_target_pairs={{0,1},{1,0},{2,3},{3,2},{4,5},{5,4},{6,7},{7,6},{8,9},{9,8},{10,11... | collective-permute-start | bytes 393224 | tf_op jit(solution)/shard_map/ppermute | solution.py:246
  72.5 6.1 %copy-start.11 = (s32[512]{0:T(512)S(1)}, s32[512]{0:T(512)}, u32[]{:S(2)}) copy-start(s32[512]{0:T(512)} %param.16) | copy-start | bytes 6148
  72.5 21.4 %copy-start.1 = (bf16[512,512]{1,0:T(8,128)(2,1)S(1)}, bf16[512,512]{1,0:T(8,128)(2,1)}, u32[]{:S(2)}) copy-start(bf16[512,512]{1,0:T(8,128)(2,1)} %sensors_ref.3) | copy-start | bytes 1572868
  72.5 21.4 %copy-start.5 = (bf16[512,512]{1,0:T(8,128)(2,1)S(1)}, bf16[512,512]{1,0:T(8,128)(2,1)}, u32[]{:S(2)}) copy-start(bf16[512,512]{1,0:T(8,128)(2,1)} %w_in_ref.1) | copy-start | bytes 1572868
  72.5 21.4 %copy-start.6 = (bf16[512,512]{1,0:T(8,128)(2,1)S(1)}, bf16[512,512]{1,0:T(8,128)(2,1)}, u32[]{:S(2)}) copy-start(bf16[512,512]{1,0:T(8,128)(2,1)} %w_out_ref.3) | copy-start | bytes 1572868
  72.5 21.4 %copy-start.14 = (f32[512]{0:T(512)S(1)}, f32[512]{0:T(512)}, u32[]{:S(2)}) copy-start(f32[512]{0:T(512)} %param.26) | copy-start | bytes 6148
  75.4 18.6 %all-to-all-start.1 = ((bf16[32,16,512]{2,1,0:T(8,128)(2,1)}), bf16[32,16,512]{2,1,0:T(8,128)(2,1)S(1)}, u32[]{:S(2)}, u32[]{:S(2)}) async-start(bf16[32,16,512]{2,1,0:T(8,128)(2,1)} %bitcast.5), calls=%async_computation.1 | async-start | bytes 1048576 | tf_op jit(solution)/shard_map/all_to_all | solution.py:249

commit v6 on v5

--- a/solution.py
+++ b/solution.py
@@ -41,17 +41,16 @@
     labels = (labels_ref[...] + 1).astype(F32)
     lane = lax.broadcasted_iota(jnp.int32, labels.shape, 1)
     own_lanes = (lane // tile) == mine
+    rolled = []
     for k in range(per_row):
         shift = lax.rem(mine - k + per_row, per_row) * tile
-        rolled = jnp.where(own_lanes, pltpu.roll(labels, shift, 1), 0.0)
-        for at, t in enumerate(order):
-            if t % per_row != k:
-                continue
-            g = t // per_row
-            row = jnp.broadcast_to(rolled[g : g + 1, :], (8, LANES)).astype(BF16)
-            rows = sensors_ref[t * tile : (t + 1) * tile, :]
-            parts = [rows[:, c * LANES : (c + 1) * LANES] for c in range(blocks)]
-            out_ref[at] = jnp.concatenate(parts + [row], axis=0)
+        rolled.append(jnp.where(own_lanes, pltpu.roll(labels, shift, 1), 0.0))
+    for at, t in enumerate(order):
+        g = t // per_row
+        row = jnp.broadcast_to(rolled[t % per_row][g : g + 1, :], (8, LANES)).astype(BF16)
+        rows = sensors_ref[t * tile : (t + 1) * tile, :]
+        parts = [rows[:, c * LANES : (c + 1) * LANES] for c in range(blocks)]
+        out_ref[at] = jnp.concatenate(parts + [row], axis=0)
 
 
 def by_heads():
@@ -218,6 +217,7 @@
 
 def local(
     order,
+    line,
     sensors,
     slot_region,
     w_query,
@@ -238,7 +238,7 @@
     tile = sen_dev // devices
     me = lax.axis_index(AXIS).astype(jnp.int32).reshape(1)
     core = lax.rem(me, 2)
-    place = jnp.asarray([order.index(i) for i in range(devices)], jnp.int32)[me]
+    place = me // line * line + core * (line // 2) + me % line // 2
     bits = devices.bit_length() - 1
     pay_rows = tile * (width // LANES) + 8
 
@@ -326,11 +326,12 @@
     own_one, own_two = flipped(own, one), flipped(own, two)
     acc = attend([own], None)
     acc, own_one, own_two = hold((acc, own_one, own_two))
+    own_corner = flipped(own_two, one)
     acc = attend([own_one, own_two], acc)
-    acc, a, b, own_two = hold((acc, a, b, own_two))
+    acc, a, b = hold((acc, a, b))
 
     ab, c = jnp.concatenate([a, b], axis=0), flipped(a, near)
-    ab_one, ab_two, own_corner = flipped(ab, one), flipped(ab, two), flipped(own_two, one)
+    ab_one, ab_two = flipped(ab, one), flipped(ab, two)
     acc = attend([ab], acc)
     acc, c, own_corner = hold((acc, c, own_corner))
 
@@ -376,7 +377,7 @@
     flat = jax.sharding.Mesh(mesh.devices.reshape(-1), (AXIS,))
     placed = (P(AXIS, None), P(AXIS)) + (P(),) * 12
     return jax.shard_map(
-        functools.partial(local, order),
+        functools.partial(local, order, line),
         mesh=flat,
         in_specs=placed,
         out_specs=P(AXIS, None),

time: 96.1 us -> 89.5 us (0.931)
  blocking collectives: 0 us -> 23.6 us
  waiting for transfers between devices: 41.4 us -> 19.3 us
  starting transfers between devices: 22.3 us -> 17 us
  Pallas kernels: 28.3 us -> 26.8 us
  local copies, waits for them, and re-layouts: 3.42 us -> 2.16 us
    all_to_all x0 -> x1, blocking collectives: none -> 23.6 us  [exchanged(): lax.all_to_all(value, AXIS, split_axis=0, concat_axis=0, tiled=True, axis...]
    all_to_all x2 -> x1, waiting for transfers between devices: 31.8 us -> 15.1 us  [exchanged(): lax.all_to_all(value, AXIS, split_axis=0, concat_axis=0, tiled=True, axis...]
    all_to_all x2 -> x1, starting transfers between devices: 10.3 us -> 3.55 us  [exchanged(): lax.all_to_all(value, AXIS, split_axis=0, concat_axis=0, tiled=True, axis...]
    ppermute x15, waiting for transfers between devices: 9.56 us -> 4.13 us  [flipped(): return lax.ppermute(value, AXIS, [(i, i ^ mask) for i in range(devices)])]
    pallas_call x1, Pallas kernels: 1.6 us -> 0.09 us  [local(): pl.pallas_call(functools.partial(pack_kernel, tile, order), out_shape=jax...]
    ppermute x15, starting transfers between devices: 12 us -> 13.4 us  [flipped(): return lax.ppermute(value, AXIS, [(i, i ^ mask) for i in range(devices)])]
    gather x1 -> x0, local copies, waits for them, and re-layouts: 1.28 us -> none  [local(): place = jnp.asarray([order.index(i) for i in range(devices)], jnp.int32)[me]]
  transfers between devices with their start and end apart: 17 -> 16, of which waited for: 8 -> 6; matrix products, arithmetic and copies ran while one was open for 0% -> 0% of each run, Pallas kernels for 21% -> 22%
where the time goes in v6:
time: 89.5 us; the launch traced here: 89.2 us
  Pallas kernels  26.8 us (30%)
  blocking collectives  23.6 us (26%)
  waiting for transfers between devices  19.3 us (22%)
  starting transfers between devices  17 us (19%)
  local copies, waits for them, and re-layouts  2.16 us (2%)
    all_to_all x1, blocking collectives, exchanged(): lax.all_to_all(value, AXIS, split_axis=0, concat_axis=0, tiled=True, axis...  23.6 us
    pallas_call x8, Pallas kernels, attend(): pl.pallas_call(functools.partial(attend_kernel, len(parts), row_parts, ac...  20.3 us
    all_to_all x1, waiting for transfers between devices, exchanged(): lax.all_to_all(value, AXIS, split_axis=0, concat_axis=0, tiled=True, axis...  15.1 us
    ppermute x15, starting transfers between devices, flipped(): return lax.ppermute(value, AXIS, [(i, i ^ mask) for i in range(devices)])  13.4 us
    ppermute x15, waiting for transfers between devices, flipped(): return lax.ppermute(value, AXIS, [(i, i ^ mask) for i in range(devices)])  4.13 us
    all_to_all x1, starting transfers between devices, exchanged(): lax.all_to_all(value, AXIS, split_axis=0, concat_axis=0, tiled=True, axis...  3.55 us
    pallas_call x1, Pallas kernels, local(): pl.pallas_call(post_kernel, out_shape=jax.ShapeDtypeStruct((sen_dev, widt...  2.79 us
    unnamed x34, local copies, waits for them, and re-layouts  1.84 us
  transfers between devices with their start and end apart: 16, of which 6 were waited for; matrix products, arithmetic and copies ran while one was open for 0% of the time, Pallas kernels for 22%

profile of v6, /device:TPU:1, one launch (start us, length us, event | category | flops | bytes accessed | tf_op | source)
XLA Modules:
  0.0 89.2 jit_solution(4553432053684382631)
XLA Ops:
  0.0 1.1 %copy-done = bf16[512,512]{1,0:T(8,128)(2,1)S(1)} copy-done((bf16[512,512]{1,0:T(8,128)(2,1)S(1)}, bf16[512,512]{1,0:T(8,128)(2,1)}, u32[]{:S(2)}) %copy-start) | copy-done | bytes 524312
  1.1 0.7 copy-done.10
  1.8 0.1 pack.1
  1.9 23.6 %all_to_all.10.got_ref = bf16[32,72,128]{2,1,0:T(8,128)(2,1)S(1)} all-to-all(bf16[32,72,128]{2,1,0:T(8,128)(2,1)S(1)} %pack.1), channel_id=1, replica_groups={{0,2,4,6,1,3,5,7,8,10,12,14,9,11,13,15,16,18,20,22,17,19,21,23,24,26,28..., dimensions={0} | all-to-all | bytes 1179648 | tf_op jit(solution)/shard_map/all_to_all | solution.py:249
  25.4 0.0 copy-done.12
  25.4 0.0 copy-done.9
  25.5 1.0 %pool.1 = (f32[256,512]{1,0:T(8,128)S(1)}, bf16[256,512]{1,0:T(8,128)(2,1)S(1)}, bf16[256,512]{1,0:T(8,128)(2,1)S(1)}, bf16[256,128]{1,0:T(8,128)(2,1)S(1)}, bf16[256,128]{1,0:T(8,128)(2,1)S(1)}) custom-call(s32[1]{0:T(128)S(6)} %rem.46.core_ref, bf16[32,72,128]{2,1,0:T(8,128)(2,1)S(1)} %all_to_all.10.got_ref, bf16[512,128]{1,0:T(8,128)(2,1)S(1)} %copy-done.8, ...), custom_call_target="tpu_custom_call" | custom-call | tf_op jit(solution)/shard_map/pool/pallas_call | solution.py:267
  26.5 0.1 collective-permute-start
  26.6 0.1 broadcast_in_dim.3
  26.7 0.1 reshape_reshape.3.scale_ref
  26.7 0.8 query.1
  27.5 0.3 collective-permute-done
  27.8 0.3 collective-permute-start.1
  28.1 1.3 %collective-permute-start.2 = (bf16[512,128]{1,0:T(8,128)(2,1)S(1)}, bf16[512,128]{1,0:T(8,128)(2,1)S(1)}, u32[]{:S(2)}, u32[]{:S(2)}) collective-permute-start(bf16[512,128]{1,0:T(8,128)(2,1)S(1)} %constant_dynamic-update-slice_fusion.refs_2_), channel_id=1, source_target_pairs={{0,8},{1,9},{2,10},{3,11},{4,12},{5,13},{6,14},{7,15},{8,0},{9,1},... | collective-permute-start | bytes 393224 | tf_op jit(solution)/shard_map/ppermute | solution.py:246
  29.4 0.3 collective-permute-start.3
  29.6 0.7 collective-permute-start.4
  30.3 1.2 %collective-permute-start.5 = (bf16[512,128]{1,0:T(8,128)(2,1)S(1)}, bf16[512,128]{1,0:T(8,128)(2,1)S(1)}, u32[]{:S(2)}, u32[]{:S(2)}) collective-permute-start(bf16[512,128]{1,0:T(8,128)(2,1)S(1)} %constant_dynamic-update-slice_fusion.refs_2_), channel_id=1, source_target_pairs={{0,2},{1,3},{2,0},{3,1},{4,6},{5,7},{6,4},{7,5},{8,10},{9,11},{10,... | collective-permute-start | bytes 393224 | tf_op jit(solution)/shard_map/ppermute | solution.py:246
  31.5 0.0 collective-permute-done.1.refs_1_.refs_0_
  31.5 1.4 %attend.8.refs_4_ = f32[4,512,128]{2,1,0:T(8,128)S(1)} custom-call(bf16[256,512]{1,0:T(8,128)(2,1)S(1)} %get-tuple-element.36.refs_0_, bf16[256,512]{1,0:T(8,128)(2,1)S(1)} %collective-permute-done.1.refs_1_.refs_0_, bf16[512,128]{1,0:T(8,128)(2,1)S(1)} %constant_dynamic-update-slice_fusion.refs_2_), custom_call_target="tpu_custom_call" | custom-call | flops 1073741824 | bytes 131072 | tf_op jit(solution)/shard_map/attend/pallas_call | solution.py:303
  32.9 0.2 collective-permute-done.2.refs_2_
  33.1 0.9 collective-permute-done.3.refs_3_
  33.9 2.4 %attend.9.refs_3_ = f32[4,512,128]{2,1,0:T(8,128)S(1)} custom-call(bf16[256,512]{1,0:T(8,128)(2,1)S(1)} %get-tuple-element.36.refs_0_, bf16[256,512]{1,0:T(8,128)(2,1)S(1)} %collective-permute-done.1.refs_1_.refs_0_, bf16[512,128]{1,0:T(8,128)(2,1)S(1)} %collective-permute-done.2.refs_2_, bf16[512,128]{1,0:T(8,128)(2,1)S(1)} %collective-permute-done.3.refs_3_, ...), custom_call_target="tpu_custom_call" | custom-call | flops 2147483648 | bytes 262144 | tf_op jit(solution)/shard_map/attend/pallas_call | solution.py:303
  36.3 2.2 %collective-permute-done.4 = bf16[512,128]{1,0:T(8,128)(2,1)S(1)} collective-permute-done((bf16[512,128]{1,0:T(8,128)(2,1)S(1)}, bf16[512,128]{1,0:T(8,128)(2,1)S(1)}, u32[]{:S(2)}, u32[]{:S(2)}) %collective-permute-start.4) | collective-permute-done | bytes 131104 | tf_op jit(solution)/shard_map/ppermute | solution.py:246
  38.5 0.0 collective-permute-done.5
  38.5 0.1 collective-permute-start.6
  38.6 1.4 %collective-permute-start.7 = (bf16[512,128]{1,0:T(8,128)(2,1)S(1)}, bf16[512,128]{1,0:T(8,128)(2,1)S(1)}, u32[]{:S(2)}, u32[]{:S(2)}) collective-permute-start(bf16[512,128]{1,0:T(8,128)(2,1)S(1)} %collective-permute-done.3.refs_3_), channel_id=1, source_target_pairs={{0,8},{1,9},{2,10},{3,11},{4,12},{5,13},{6,14},{7,15},{8,0},{9,1},... | collective-permute-start | bytes 393224 | tf_op jit(solution)/shard_map/ppermute | solution.py:246
  40.1 0.2 collective-permute-start.8
  40.2 1.4 %collective-permute-start.9 = (bf16[1024,128]{1,0:T(8,128)(2,1)S(1)}, bf16[1024,128]{1,0:T(8,128)(2,1)S(1)}, u32[]{:S(2)}, u32[]{:S(2)}) collective-permute-start(bf16[1024,128]{1,0:T(8,128)(2,1)S(1)} %constant_dynamic-update-slice_fusion.2.refs_2_), channel_id=1, source_target_pairs={{0,16},{1,17},{2,18},{3,19},{4,20},{5,21},{6,22},{7,23},{8,24},{9,... | collective-permute-start | bytes 786440 | tf_op jit(solution)/shard_map/ppermute | solution.py:246
  41.6 2.4 %attend.10.refs_4_ = f32[4,512,128]{2,1,0:T(8,128)S(1)} custom-call(bf16[256,512]{1,0:T(8,128)(2,1)S(1)} %get-tuple-element.36.refs_0_, bf16[256,512]{1,0:T(8,128)(2,1)S(1)} %collective-permute-done.1.refs_1_.refs_0_, bf16[1024,128]{1,0:T(8,128)(2,1)S(1)} %constant_dynamic-update-slice_fusion.2.refs_2_, f32[4,512,128]{2,1,0:T(8,128)S(1)} %attend.9.refs_3_), custom_call_target="tpu_custom_call" | custom-call | flops 2147483648 | bytes 262144 | tf_op jit(solution)/shard_map/attend/pallas_call | solution.py:303
  44.0 0.0 collective-permute-done.6.refs_2_
  44.0 0.0 collective-permute-done.7.refs_3_
  44.0 0.5 collective-permute-start.10
  44.5 1.1 %collective-permute-start.11 = (bf16[512,128]{1,0:T(8,128)(2,1)S(1)}, bf16[512,128]{1,0:T(8,128)(2,1)S(1)}, u32[]{:S(2)}, u32[]{:S(2)}) collective-permute-start(bf16[512,128]{1,0:T(8,128)(2,1)S(1)} %collective-permute-done.6.refs_2_), channel_id=1, source_target_pairs={{0,16},{1,17},{2,18},{3,19},{4,20},{5,21},{6,22},{7,23},{8,24},{9,... | collective-permute-start | bytes 393224 | tf_op jit(solution)/shard_map/ppermute | solution.py:246
  45.6 2.4 %attend.11.refs_4_ = f32[4,512,128]{2,1,0:T(8,128)S(1)} custom-call(bf16[256,512]{1,0:T(8,128)(2,1)S(1)} %get-tuple-element.36.refs_0_, bf16[256,512]{1,0:T(8,128)(2,1)S(1)} %collective-permute-done.1.refs_1_.refs_0_, bf16[512,128]{1,0:T(8,128)(2,1)S(1)} %collective-permute-done.6.refs_2_, bf16[512,128]{1,0:T(8,128)(2,1)S(1)} %collective-permute-done.7.refs_3_, ...), custom_call_target="tpu_custom_call" | custom-call | flops 2147483648 | bytes 262144 | tf_op jit(solution)/shard_map/attend/pallas_call | solution.py:303
  48.0 0.6 collective-permute-done.8.refs_2_
  48.6 0.0 collective-permute-done.9.refs_3_
  48.6 1.7 %collective-permute-start.13 = (bf16[1024,128]{1,0:T(8,128)(2,1)S(1)}, bf16[1024,128]{1,0:T(8,128)(2,1)S(1)}, u32[]{:S(2)}, u32[]{:S(2)}) collective-permute-start(bf16[1024,128]{1,0:T(8,128)(2,1)S(1)} %collective-permute-done.8.refs_2_), channel_id=1, source_target_pairs={{0,16},{1,17},{2,18},{3,19},{4,20},{5,21},{6,22},{7,23},{8,24},{9,... | collective-permute-start | bytes 786440 | tf_op jit(solution)/shard_map/ppermute | solution.py:246
  50.3 4.8 %attend.12.refs_5_ = f32[4,512,128]{2,1,0:T(8,128)S(1)} custom-call(bf16[256,512]{1,0:T(8,128)(2,1)S(1)} %get-tuple-element.36.refs_0_, bf16[256,512]{1,0:T(8,128)(2,1)S(1)} %collective-permute-done.1.refs_1_.refs_0_, bf16[1024,128]{1,0:T(8,128)(2,1)S(1)} %collective-permute-done.8.refs_2_, bf16[1024,128]{1,0:T(8,128)(2,1)S(1)} %collective-permute-done.9.refs_3_, ...), custom_call_target="tpu_custom_call" | custom-call | flops 4294967296 | bytes 524288 | tf_op jit(solution)/shard_map/attend/pallas_call | solution.py:303
  55.1 0.0 collective-permute-done.10.refs_2_
  55.1 0.0 collective-permute-done.11.refs_3_
  55.1 0.1 collective-permute-start.12
  55.2 0.0 collective-permute-done.13.refs_4_
  55.2 0.0 copy-start.3
  55.2 4.6 %attend.13.refs_2_ = f32[4,512,128]{2,1,0:T(8,128)S(1)} custom-call(bf16[256,512]{1,0:T(8,128)(2,1)S(1)} %get-tuple-element.36.refs_0_, bf16[256,512]{1,0:T(8,128)(2,1)S(1)} %collective-permute-done.1.refs_1_.refs_0_, bf16[512,128]{1,0:T(8,128)(2,1)S(1)} %collective-permute-done.10.refs_2_, bf16[512,128]{1,0:T(8,128)(2,1)S(1)} %collective-permute-done.11.refs_3_, ...), custom_call_target="tpu_custom_call" | custom-call | flops 4294967296 | bytes 524288 | tf_op jit(solution)/shard_map/attend/pallas_call | solution.py:303
  59.8 0.0 copy-start.2
  59.8 0.0 copy-start.4
  59.8 0.0 copy-start.13
  59.9 0.0 collective-permute-done.12.refs_1_
  59.9 1.2 %attend.15 = bf16[256,256]{1,0:T(8,128)(2,1)S(1)} custom-call(bf16[256,512]{1,0:T(8,128)(2,1)S(1)} %collective-permute-done.1.refs_1_.refs_0_, bf16[512,128]{1,0:T(8,128)(2,1)S(1)} %collective-permute-done.12.refs_1_, f32[4,512,128]{2,1,0:T(8,128)S(1)} %attend.13.refs_2_), custom_call_target="tpu_custom_call" | custom-call | flops 536870912 | bytes 131072 | tf_op jit(solution)/shard_map/attend/pallas_call | solution.py:303
  61.0 3.4 %collective-permute-start.14 = (bf16[256,256]{1,0:T(8,128)(2,1)S(1)}, bf16[256,256]{1,0:T(8,128)(2,1)S(1)}, u32[]{:S(2)}, u32[]{:S(2)}) collective-permute-start(bf16[256,256]{1,0:T(8,128)(2,1)S(1)} %attend.15), channel_id=1, source_target_pairs={{0,1},{1,0},{2,3},{3,2},{4,5},{5,4},{6,7},{7,6},{8,9},{9,8},{10,11... | collective-permute-start | bytes 393224 | tf_op jit(solution)/shard_map/ppermute | solution.py:246
  64.4 1.1 %attend.14.mine_ref = bf16[256,256]{1,0:T(8,128)(2,1)S(1)} custom-call(bf16[256,512]{1,0:T(8,128)(2,1)S(1)} %get-tuple-element.36.refs_0_, bf16[512,128]{1,0:T(8,128)(2,1)S(1)} %collective-permute-done.12.refs_1_, f32[4,512,128]{2,1,0:T(8,128)S(1)} %attend.13.refs_2_), custom_call_target="tpu_custom_call" | custom-call | flops 536870912 | bytes 131072 | tf_op jit(solution)/shard_map/attend/pallas_call | solution.py:303
  65.6 0.0 collective-permute-done.14.other_ref
  65.6 0.0 copy-start.11
  65.6 0.0 copy-start.1
  65.6 0.0 copy-start.5
  65.7 0.0 copy-start.6
  65.7 0.0 copy-start.14
  65.7 2.8 %post.1 = bf16[512,512]{1,0:T(8,128)(2,1)} custom-call(s32[1]{0:T(128)S(6)} %rem.46.core_ref, bf16[256,256]{1,0:T(8,128)(2,1)S(1)} %attend.14.mine_ref, bf16[256,256]{1,0:T(8,128)(2,1)S(1)} %collective-permute-done.14.other_ref, f32[256,512]{1,0:T(8,128)S(1)} %get-tuple-element.57.pooled_ref, bf16[256,512]{1,0:T(8,128)(2,1)S(1)} %get-tuple-element.58.member_ref, ...), custom_call_target="tpu_custom_call" | custom-call | tf_op jit(solution)/shard_map/post/pallas_call | solution.py:354
  68.5 3.5 %all-to-all-start.1 = ((bf16[32,16,512]{2,1,0:T(8,128)(2,1)}), bf16[32,16,512]{2,1,0:T(8,128)(2,1)S(1)}, u32[]{:S(2)}, u32[]{:S(2)}) async-start(bf16[32,16,512]{2,1,0:T(8,128)(2,1)} %bitcast.4), calls=%async_computation.1 | async-start | bytes 1048576 | tf_op jit(solution)/shard_map/all_to_all | solution.py:249
  72.0 0.0 copy-done.11
  72.1 0.1 copy.15.live_ref
  72.2 15.1 %all-to-all-done.1 = bf16[32,16,512]{2,1,0:T(8,128)(2,1)S(1)} async-done(((bf16[32,16,512]{2,1,0:T(8,128)(2,1)}), bf16[32,16,512]{2,1,0:T(8,128)(2,1)S(1)}, u32[]{:S(2)}, u32[]{:S(2)}) %all-to-all-start.1) | async-done | bytes 524320 | tf_op jit(solution)/shard_map/all_to_all | solution.py:249
  87.3 0.0 copy-done.14
  87.3 1.8 %decode.1 = bf16[512,512]{1,0:T(8,128)(2,1)} custom-call(bf16[512,512]{1,0:T(8,128)(2,1)S(1)} %bitcast.8, bf16[512,512]{1,0:T(8,128)(2,1)S(1)} %copy-done.1, f32[512,1]{1,0:T(8,128)S(1)} %copy.15.live_ref, f32[1,512]{1,0:T(1,128)S(1)} %bitcast.12, bf16[512,512]{1,0:T(8,128)(2,1)S(1)} %copy-done.5, bf16[512,512]{1,0:T(8,128)(2,1)S(1)} %copy-done.6), custom_call_target="tpu_custom_call" | custom-call | tf_op jit(solution)/shard_map/decode/pallas_call | solution.py:364
  (23 shorter events, 0.1 us)
Async XLA Ops:
  0.0 25.4 %copy-start.12 = (f32[512]{0:T(512)S(1)}, f32[512]{0:T(512)}, u32[]{:S(2)}) copy-start(f32[512]{0:T(512)} %param.21) | copy-start | bytes 6148
  0.0 26.6 %copy-start.15 = (f32[8]{0:T(128)S(1)}, f32[8]{0:T(128)}, u32[]{:S(2)}) copy-start(f32[8]{0:T(128)} %param.20) | copy-start | bytes 100
  0.0 1.1 %copy-start = (bf16[512,512]{1,0:T(8,128)(2,1)S(1)}, bf16[512,512]{1,0:T(8,128)(2,1)}, u32[]{:S(2)}) copy-start(bf16[512,512]{1,0:T(8,128)(2,1)} %sensors_ref.3) | copy-start | bytes 1572868
  1.1 0.7 copy-start.10
  1.8 23.7 %copy-start.8 = (bf16[512,128]{1,0:T(8,128)(2,1)S(1)}, bf16[512,128]{1,0:T(8,128)(2,1)}, u32[]{:S(2)}) copy-start(bf16[512,128]{1,0:T(8,128)(2,1)} %w_key_ref.1) | copy-start | bytes 393220
  1.8 23.7 %copy-start.9 = (bf16[512,128]{1,0:T(8,128)(2,1)S(1)}, bf16[512,128]{1,0:T(8,128)(2,1)}, u32[]{:S(2)}) copy-start(bf16[512,128]{1,0:T(8,128)(2,1)} %w_value_ref.1) | copy-start | bytes 393220
  1.8 25.0 %copy-start.7 = (bf16[512,512]{1,0:T(8,128)(2,1)S(1)}, bf16[512,512]{1,0:T(8,128)(2,1)}, u32[]{:S(2)}) copy-start(bf16[512,512]{1,0:T(8,128)(2,1)} %w_query_ref.1) | copy-start | bytes 1572868
  26.5 1.3 %collective-permute-start = (bf16[256,128]{1,0:T(8,128)(2,1)S(1)}, bf16[256,128]{1,0:T(8,128)(2,1)S(1)}, u32[]{:S(2)}, u32[]{:S(2)}) collective-permute-start(bf16[256,128]{1,0:T(8,128)(2,1)S(1)} %get-tuple-element.32), channel_id=1, source_target_pairs={{0,1},{1,0},{2,3},{3,2},{4,5},{5,4},{6,7},{7,6},{8,9},{9,8},{10,11... | collective-permute-start | bytes 196616 | tf_op jit(solution)/shard_map/ppermute | solution.py:246
  27.8 3.7 %collective-permute-start.1 = (bf16[256,512]{1,0:T(8,128)(2,1)S(1)}, bf16[256,512]{1,0:T(8,128)(2,1)S(1)}, u32[]{:S(2)}, u32[]{:S(2)}) collective-permute-start(bf16[256,512]{1,0:T(8,128)(2,1)S(1)} %get-tuple-element.37), channel_id=1, source_target_pairs={{0,1},{1,0},{2,3},{3,2},{4,5},{5,4},{6,7},{7,6},{8,9},{9,8},{10,11... | collective-permute-start | bytes 786440 | tf_op jit(solution)/shard_map/ppermute | solution.py:246
  28.1 4.9 %collective-permute-start.2 = (bf16[512,128]{1,0:T(8,128)(2,1)S(1)}, bf16[512,128]{1,0:T(8,128)(2,1)S(1)}, u32[]{:S(2)}, u32[]{:S(2)}) collective-permute-start(bf16[512,128]{1,0:T(8,128)(2,1)S(1)} %constant_dynamic-update-slice_fusion.refs_2_), channel_id=1, source_target_pairs={{0,8},{1,9},{2,10},{3,11},{4,12},{5,13},{6,14},{7,15},{8,0},{9,1},... | collective-permute-start | bytes 393224 | tf_op jit(solution)/shard_map/ppermute | solution.py:246
  29.4 4.6 %collective-permute-start.3 = (bf16[512,128]{1,0:T(8,128)(2,1)S(1)}, bf16[512,128]{1,0:T(8,128)(2,1)S(1)}, u32[]{:S(2)}, u32[]{:S(2)}) collective-permute-start(bf16[512,128]{1,0:T(8,128)(2,1)S(1)} %constant_dynamic-update-slice_fusion.refs_2_), channel_id=1, source_target_pairs={{0,16},{1,17},{2,18},{3,19},{4,20},{5,21},{6,22},{7,23},{8,24},{9,... | collective-permute-start | bytes 393224 | tf_op jit(solution)/shard_map/ppermute | solution.py:246
  29.6 8.9 %collective-permute-start.4 = (bf16[512,128]{1,0:T(8,128)(2,1)S(1)}, bf16[512,128]{1,0:T(8,128)(2,1)S(1)}, u32[]{:S(2)}, u32[]{:S(2)}) collective-permute-start(bf16[512,128]{1,0:T(8,128)(2,1)S(1)} %constant_dynamic-update-slice_fusion.refs_2_), channel_id=1, source_target_pairs={{0,4},{1,5},{2,6},{3,7},{4,0},{5,1},{6,2},{7,3},{8,12},{9,13},{10,... | collective-permute-start | bytes 393224 | tf_op jit(solution)/shard_map/ppermute | solution.py:246
  30.3 8.2 %collective-permute-start.5 = (bf16[512,128]{1,0:T(8,128)(2,1)S(1)}, bf16[512,128]{1,0:T(8,128)(2,1)S(1)}, u32[]{:S(2)}, u32[]{:S(2)}) collective-permute-start(bf16[512,128]{1,0:T(8,128)(2,1)S(1)} %constant_dynamic-update-slice_fusion.refs_2_), channel_id=1, source_target_pairs={{0,2},{1,3},{2,0},{3,1},{4,6},{5,7},{6,4},{7,5},{8,10},{9,11},{10,... | collective-permute-start | bytes 393224 | tf_op jit(solution)/shard_map/ppermute | solution.py:246
  38.5 5.5 %collective-permute-start.6 = (bf16[512,128]{1,0:T(8,128)(2,1)S(1)}, bf16[512,128]{1,0:T(8,128)(2,1)S(1)}, u32[]{:S(2)}, u32[]{:S(2)}) collective-permute-start(bf16[512,128]{1,0:T(8,128)(2,1)S(1)} %collective-permute-done.4), channel_id=1, source_target_pairs={{0,2},{1,3},{2,0},{3,1},{4,6},{5,7},{6,4},{7,5},{8,10},{9,11},{10,... | collective-permute-start | bytes 393224 | tf_op jit(solution)/shard_map/ppermute | solution.py:246
  38.6 5.4 %collective-permute-start.7 = (bf16[512,128]{1,0:T(8,128)(2,1)S(1)}, bf16[512,128]{1,0:T(8,128)(2,1)S(1)}, u32[]{:S(2)}, u32[]{:S(2)}) collective-permute-start(bf16[512,128]{1,0:T(8,128)(2,1)S(1)} %collective-permute-done.3.refs_3_), channel_id=1, source_target_pairs={{0,8},{1,9},{2,10},{3,11},{4,12},{5,13},{6,14},{7,15},{8,0},{9,1},... | collective-permute-start | bytes 393224 | tf_op jit(solution)/shard_map/ppermute | solution.py:246
  40.1 8.5 %collective-permute-start.8 = (bf16[1024,128]{1,0:T(8,128)(2,1)S(1)}, bf16[1024,128]{1,0:T(8,128)(2,1)S(1)}, u32[]{:S(2)}, u32[]{:S(2)}) collective-permute-start(bf16[1024,128]{1,0:T(8,128)(2,1)S(1)} %constant_dynamic-update-slice_fusion.2.refs_2_), channel_id=1, source_target_pairs={{0,8},{1,9},{2,10},{3,11},{4,12},{5,13},{6,14},{7,15},{8,0},{9,1},... | collective-permute-start | bytes 786440 | tf_op jit(solution)/shard_map/ppermute | solution.py:246
  40.2 8.3 %collective-permute-start.9 = (bf16[1024,128]{1,0:T(8,128)(2,1)S(1)}, bf16[1024,128]{1,0:T(8,128)(2,1)S(1)}, u32[]{:S(2)}, u32[]{:S(2)}) collective-permute-start(bf16[1024,128]{1,0:T(8,128)(2,1)S(1)} %constant_dynamic-update-slice_fusion.2.refs_2_), channel_id=1, source_target_pairs={{0,16},{1,17},{2,18},{3,19},{4,20},{5,21},{6,22},{7,23},{8,24},{9,... | collective-permute-start | bytes 786440 | tf_op jit(solution)/shard_map/ppermute | solution.py:246
  44.0 11.0 %collective-permute-start.10 = (bf16[512,128]{1,0:T(8,128)(2,1)S(1)}, bf16[512,128]{1,0:T(8,128)(2,1)S(1)}, u32[]{:S(2)}, u32[]{:S(2)}) collective-permute-start(bf16[512,128]{1,0:T(8,128)(2,1)S(1)} %collective-permute-done.6.refs_2_), channel_id=1, source_target_pairs={{0,8},{1,9},{2,10},{3,11},{4,12},{5,13},{6,14},{7,15},{8,0},{9,1},... | collective-permute-start | bytes 393224 | tf_op jit(solution)/shard_map/ppermute | solution.py:246
  44.5 10.6 %collective-permute-start.11 = (bf16[512,128]{1,0:T(8,128)(2,1)S(1)}, bf16[512,128]{1,0:T(8,128)(2,1)S(1)}, u32[]{:S(2)}, u32[]{:S(2)}) collective-permute-start(bf16[512,128]{1,0:T(8,128)(2,1)S(1)} %collective-permute-done.6.refs_2_), channel_id=1, source_target_pairs={{0,16},{1,17},{2,18},{3,19},{4,20},{5,21},{6,22},{7,23},{8,24},{9,... | collective-permute-start | bytes 393224 | tf_op jit(solution)/shard_map/ppermute | solution.py:246
  48.6 6.6 %collective-permute-start.13 = (bf16[1024,128]{1,0:T(8,128)(2,1)S(1)}, bf16[1024,128]{1,0:T(8,128)(2,1)S(1)}, u32[]{:S(2)}, u32[]{:S(2)}) collective-permute-start(bf16[1024,128]{1,0:T(8,128)(2,1)S(1)} %collective-permute-done.8.refs_2_), channel_id=1, source_target_pairs={{0,16},{1,17},{2,18},{3,19},{4,20},{5,21},{6,22},{7,23},{8,24},{9,... | collective-permute-start | bytes 786440 | tf_op jit(solution)/shard_map/ppermute | solution.py:246
  55.1 4.8 %collective-permute-start.12 = (bf16[512,128]{1,0:T(8,128)(2,1)S(1)}, bf16[512,128]{1,0:T(8,128)(2,1)S(1)}, u32[]{:S(2)}, u32[]{:S(2)}) collective-permute-start(bf16[512,128]{1,0:T(8,128)(2,1)S(1)} %collective-permute-done.11.refs_3_), channel_id=1, source_target_pairs={{0,8},{1,9},{2,10},{3,11},{4,12},{5,13},{6,14},{7,15},{8,0},{9,1},... | collective-permute-start | bytes 393224 | tf_op jit(solution)/shard_map/ppermute | solution.py:246
  55.2 10.4 %copy-start.3 = (bf16[2048,512]{1,0:T(8,128)(2,1)S(1)}, bf16[2048,512]{1,0:T(8,128)(2,1)}, u32[]{:S(2)}) copy-start(bf16[2048,512]{1,0:T(8,128)(2,1)} %w_outer_ref.1) | copy-start | bytes 6291460
  59.8 5.8 %copy-start.2 = (bf16[512,2048]{1,0:T(8,128)(2,1)S(1)}, bf16[512,2048]{1,0:T(8,128)(2,1)}, u32[]{:S(2)}) copy-start(bf16[512,2048]{1,0:T(8,128)(2,1)} %w_inner_ref.1) | copy-start | bytes 6291460
  59.8 5.8 %copy-start.4 = (bf16[512,512]{1,0:T(8,128)(2,1)S(1)}, bf16[512,512]{1,0:T(8,128)(2,1)}, u32[]{:S(2)}) copy-start(bf16[512,512]{1,0:T(8,128)(2,1)} %w_out_ref.2) | copy-start | bytes 1572868
  59.8 5.8 %copy-start.13 = (f32[512]{0:T(512)S(1)}, f32[512]{0:T(512)}, u32[]{:S(2)}) copy-start(f32[512]{0:T(512)} %param.24) | copy-start | bytes 6148
  61.0 4.6 %collective-permute-start.14 = (bf16[256,256]{1,0:T(8,128)(2,1)S(1)}, bf16[256,256]{1,0:T(8,128)(2,1)S(1)}, u32[]{:S(2)}, u32[]{:S(2)}) collective-permute-start(bf16[256,256]{1,0:T(8,128)(2,1)S(1)} %attend.15), channel_id=1, source_target_pairs={{0,1},{1,0},{2,3},{3,2},{4,5},{5,4},{6,7},{7,6},{8,9},{9,8},{10,11... | collective-permute-start | bytes 393224 | tf_op jit(solution)/shard_map/ppermute | solution.py:246
  65.6 6.4 %copy-start.11 = (s32[512]{0:T(512)S(1)}, s32[512]{0:T(512)}, u32[]{:S(2)}) copy-start(s32[512]{0:T(512)} %param.15) | copy-start | bytes 6148
  65.6 21.7 %copy-start.1 = (bf16[512,512]{1,0:T(8,128)(2,1)S(1)}, bf16[512,512]{1,0:T(8,128)(2,1)}, u32[]{:S(2)}) copy-start(bf16[512,512]{1,0:T(8,128)(2,1)} %sensors_ref.3) | copy-start | bytes 1572868
  65.6 21.7 %copy-start.5 = (bf16[512,512]{1,0:T(8,128)(2,1)S(1)}, bf16[512,512]{1,0:T(8,128)(2,1)}, u32[]{:S(2)}) copy-start(bf16[512,512]{1,0:T(8,128)(2,1)} %w_in_ref.1) | copy-start | bytes 1572868
  65.7 21.7 %copy-start.6 = (bf16[512,512]{1,0:T(8,128)(2,1)S(1)}, bf16[512,512]{1,0:T(8,128)(2,1)}, u32[]{:S(2)}) copy-start(bf16[512,512]{1,0:T(8,128)(2,1)} %w_out_ref.3) | copy-start | bytes 1572868
  65.7 21.7 %copy-start.14 = (f32[512]{0:T(512)S(1)}, f32[512]{0:T(512)}, u32[]{:S(2)}) copy-start(f32[512]{0:T(512)} %param.25) | copy-start | bytes 6148
  68.5 18.8 %all-to-all-start.1 = ((bf16[32,16,512]{2,1,0:T(8,128)(2,1)}), bf16[32,16,512]{2,1,0:T(8,128)(2,1)S(1)}, u32[]{:S(2)}, u32[]{:S(2)}) async-start(bf16[32,16,512]{2,1,0:T(8,128)(2,1)} %bitcast.4), calls=%async_computation.1 | async-start | bytes 1048576 | tf_op jit(solution)/shard_map/all_to_all | solution.py:249

commit v7 on v6

--- a/solution.py
+++ b/solution.py
@@ -23,6 +23,7 @@
 
 VMEM = pl.BlockSpec(memory_space=pltpu.VMEM)
 SMEM = pl.BlockSpec(memory_space=pltpu.SMEM)
+HBM = pl.BlockSpec(memory_space=pltpu.HBM)
 PARAMS = pltpu.CompilerParams(vmem_limit_bytes=40 * 1024 * 1024)
 
 
@@ -30,27 +31,45 @@
     return jnp.dot(a, b, preferred_element_type=F32)
 
 
+def gelu(values):
+    half = 0.5 * values
+    slope = math.sqrt(2.0 / math.pi)
+    return half + half * jnp.tanh(values * (slope + slope * 0.044715 * values * values))
+
+
 def rms(values):
     return values * lax.rsqrt(jnp.mean(values * values, axis=-1, keepdims=True) + EPS)
 
 
-def pack_kernel(tile, order, place_ref, sensors_ref, labels_ref, out_ref):
+def pack_kernel(tile, order, place_ref, sensors_ref, labels_ref, out_ref, rows_ref, own_ref, sems):
     per_row = LANES // tile
     blocks = sensors_ref.shape[1] // LANES
+    pieces = sems.shape[0] - 1
+    piece = sensors_ref.shape[0] // pieces
+    label_copy = pltpu.make_async_copy(labels_ref, own_ref, sems.at[pieces])
+    label_copy.start()
+    copies = []
+    for i in range(pieces):
+        here = slice(i * piece, (i + 1) * piece)
+        copies.append(pltpu.make_async_copy(sensors_ref.at[here], rows_ref.at[here], sems.at[i]))
+        copies[i].start()
+    label_copy.wait()
     mine = lax.rem(place_ref[0], per_row)
-    labels = (labels_ref[...] + 1).astype(F32)
+    labels = (own_ref[...] + 1).astype(F32)
     lane = lax.broadcasted_iota(jnp.int32, labels.shape, 1)
     own_lanes = (lane // tile) == mine
     rolled = []
     for k in range(per_row):
         shift = lax.rem(mine - k + per_row, per_row) * tile
         rolled.append(jnp.where(own_lanes, pltpu.roll(labels, shift, 1), 0.0))
-    for at, t in enumerate(order):
+    for t in range(len(order)):
+        if t * tile % piece == 0:
+            copies[t * tile // piece].wait()
         g = t // per_row
         row = jnp.broadcast_to(rolled[t % per_row][g : g + 1, :], (8, LANES)).astype(BF16)
-        rows = sensors_ref[t * tile : (t + 1) * tile, :]
+        rows = rows_ref[t * tile : (t + 1) * tile, :]
         parts = [rows[:, c * LANES : (c + 1) * LANES] for c in range(blocks)]
-        out_ref[at] = jnp.concatenate(parts + [row], axis=0)
+        out_ref[order.index(t)] = jnp.concatenate(parts + [row], axis=0)
 
 
 def by_heads():
@@ -64,7 +83,7 @@
 
 
 def pool_kernel(
-    tile, core_ref, got_ref, w_key_ref, w_value_ref, gain_ref, pooled_ref, member_ref, attn_in_ref, keep_ref, send_ref
+    tile, group_ref, got_ref, w_key_ref, w_value_ref, gain_ref, pooled_ref, member_ref, attn_in_ref, keep_ref, send_ref
 ):
     tiles, _, _ = got_ref.shape
     per_row = LANES // tile
@@ -96,16 +115,16 @@
     value = mm(attn_in, w_value_ref[...])
     zero = jnp.where(low, key, pltpu.roll(value, HEAD_DIM, 1)).astype(BF16)
     one = jnp.where(low, pltpu.roll(key, HEAD_DIM, 1), value).astype(BF16)
-    first = core_ref[0] == 0
+    first = group_ref[0] == 0
     keep_ref[...] = jnp.where(first, zero, one)
     send_ref[...] = jnp.where(first, one, zero)
 
 
-def query_kernel(core_ref, attn_in_ref, w_query_ref, scale_ref, keep_ref, send_ref):
-    core = core_ref[0]
+def query_kernel(group_ref, attn_in_ref, w_query_ref, scale_ref, keep_ref, send_ref):
+    mine = group_ref[0]
     half = GROUP * HEAD_DIM
     low = low_lanes(REG_DEV)
-    for out_ref, group in ((send_ref, 1 - core), (keep_ref, core)):
+    for out_ref, group in ((send_ref, 1 - mine), (keep_ref, mine)):
         cols = pl.ds(pl.multiple_of(group * half, half), half)
         query = mm(attn_in_ref[...], w_query_ref[:, cols])
         scale = scale_ref[:, cols]
@@ -153,7 +172,7 @@
                 if not begin:
                     new = acc_ref[h, here, :] + new
                 elif not first:
-                    base = row_parts[0] * REG_DEV
+                    base = row_parts[0] * REG_DEV if acc_in.shape[1] > rows_all else 0
                     new = acc_in[h, base + r * span : base + (r + 1) * span, :] + new
                 acc_ref[h, here, :] = new
 
@@ -175,12 +194,12 @@
 
 
 def post_kernel(
-    core_ref, mine_ref, other_ref, pooled_ref, member_ref, w_out_ref, gain_ref, w_inner_ref, w_outer_ref, out_ref, inner_ref
+    group_ref, mine_ref, other_ref, pooled_ref, member_ref, w_out_ref, gain_ref, w_inner_ref, w_outer_ref, out_ref, inner_ref
 ):
     half = mine_ref.shape[1]
-    core = core_ref[0]
-    own = pl.ds(pl.multiple_of(core * half, half), half)
-    far = pl.ds(pl.multiple_of((1 - core) * half, half), half)
+    group = group_ref[0]
+    own = pl.ds(pl.multiple_of(group * half, half), half)
+    far = pl.ds(pl.multiple_of((1 - group) * half, half), half)
     hidden = (
         pooled_ref[...] + mm(mine_ref[...], w_out_ref[own, :]) + mm(other_ref[...], w_out_ref[far, :])
     )
@@ -189,7 +208,7 @@
     block = math.gcd(inner_width, 512)
     for j in range(inner_width // block):
         cols = slice(j * block, (j + 1) * block)
-        inner_ref[:, cols] = jax.nn.gelu(mm(mlp_in, w_inner_ref[:, cols])).astype(BF16)
+        inner_ref[:, cols] = gelu(mm(mlp_in, w_inner_ref[:, cols])).astype(BF16)
     region_out = (hidden + mm(inner_ref[...], w_outer_ref[...])).astype(BF16)
     slots = member_ref.shape[1]
     block = math.gcd(slots, 512)
@@ -208,7 +227,7 @@
         back = back_ref[begin * tile : (begin + step) * tile, :]
         total = back.astype(F32) + sensors.astype(F32)
         dec_in = (rms(total) * gain_ref[...]).astype(BF16)
-        hidden = jax.nn.gelu(mm(dec_in, w_in_ref[...])).astype(BF16)
+        hidden = gelu(mm(dec_in, w_in_ref[...])).astype(BF16)
         result = mm(hidden, w_out_ref[...])
         for i, rows in enumerate(tiles):
             here = result[i * tile : (i + 1) * tile, :]
@@ -240,6 +259,8 @@
     core = lax.rem(me, 2)
     place = me // line * line + core * (line // 2) + me % line // 2
     bits = devices.bit_length() - 1
+    one, two = 1 << (bits - 2), 1 << (bits - 1)
+    group = me // one % 2
     pay_rows = tile * (width // LANES) + 8
 
     def flipped(value, mask):
@@ -253,8 +274,13 @@
     payload = pl.pallas_call(
         functools.partial(pack_kernel, tile, order),
         out_shape=jax.ShapeDtypeStruct((devices, pay_rows, LANES), BF16),
-        in_specs=[SMEM, VMEM, VMEM],
+        in_specs=[SMEM, HBM, HBM],
         out_specs=VMEM,
+        scratch_shapes=[
+            pltpu.VMEM(sensors.shape, BF16),
+            pltpu.VMEM((sen_dev // LANES, LANES), jnp.int32),
+            pltpu.SemaphoreType.DMA((5,)),
+        ],
         compiler_params=PARAMS,
         name="pack",
     )(place, sensors, slot_region.reshape(-1, LANES))
@@ -277,8 +303,8 @@
         out_specs=(VMEM,) * 5,
         compiler_params=PARAMS,
         name="pool",
-    )(core, got, w_key, w_value, gain_attn.reshape(1, width))
-    kv_other = flipped(kv_send, 1)
+    )(group, got, w_key, w_value, gain_attn.reshape(1, width))
+    kv_other = flipped(kv_send, one)
     slab_shape = jax.ShapeDtypeStruct((REG_DEV, GROUP * LANES), BF16)
     q_keep, q_send = pl.pallas_call(
         query_kernel,
@@ -290,9 +316,9 @@
             flops=2 * REG_DEV * width * width, bytes_accessed=2 * REG_DEV * width, transcendentals=0
         ),
         name="query",
-    )(core, attn_in, w_query, scale)
+    )(group, attn_in, w_query, scale)
     kv_other, q_keep, q_send = lax.optimization_barrier((kv_other, q_keep, q_send))
-    slabs = (q_keep, flipped(q_send, 1))
+    slabs = (q_keep, flipped(q_send, one))
 
     def attend(parts, acc, last=False, row_parts=(0, 1)):
         keys = sum(part.shape[0] for part in parts)
@@ -315,7 +341,6 @@
             name="attend",
         )(*(slabs[r] for r in row_parts), *parts, *(() if acc is None else (acc,)))
 
-    one, two = 1 << (bits - 2), 1 << (bits - 1)
     own = jnp.concatenate([kv_keep, kv_other], axis=0)
     for bit in range(bits - 3, 2, -1):
         own = jnp.concatenate([own, flipped(own, 1 << bit)], axis=0)
@@ -323,33 +348,31 @@
 
     hold = lax.optimization_barrier
     a, b = flipped(own, far), flipped(own, near)
-    own_one, own_two = flipped(own, one), flipped(own, two)
+    own_two, own_core = flipped(own, two), flipped(own, 1)
     acc = attend([own], None)
-    acc, own_one, own_two = hold((acc, own_one, own_two))
-    own_corner = flipped(own_two, one)
-    acc = attend([own_one, own_two], acc)
+    own_both = flipped(own_two, 1)
+    acc = attend([own_core, own_two], acc)
     acc, a, b = hold((acc, a, b))
 
     ab, c = jnp.concatenate([a, b], axis=0), flipped(a, near)
-    ab_one, ab_two = flipped(ab, one), flipped(ab, two)
-    acc = attend([ab], acc)
-    acc, c, own_corner = hold((acc, c, own_corner))
-
-    c_one, c_two = flipped(c, one), flipped(c, two)
-    acc = attend([c, own_corner], acc)
-    acc, ab_one, ab_two = hold((acc, ab_one, ab_two))
-
-    ab_corner = flipped(ab_one, two)
-    acc = attend([ab_one, ab_two], acc)
-    acc, c_one, c_two = hold((acc, c_one, c_two))
-
-    c_corner = flipped(c_two, one)
-    acc = attend([c_one, c_two, ab_corner], acc)
-
-    theirs = attend([c_corner], acc, True, (1,))
-    other_heads = flipped(theirs, 1)
-    mine = attend([c_corner], acc, True, (0,))
-    mine, other_heads = lax.optimization_barrier((mine, other_heads))
+    ab_two, ab_core = flipped(ab, two), flipped(ab, 1)
+    acc = attend([ab, own_both], acc)
+    acc, c = hold((acc, c))
+
+    c_two, c_core = flipped(c, two), flipped(c, 1)
+    acc = attend([c, ab_core], acc)
+    acc, ab_two = hold((acc, ab_two))
+
+    ab_both = flipped(ab_two, 1)
+    acc = attend([ab_two, c_core], acc)
+    acc, ab_both, c_two = hold((acc, ab_both, c_two))
+
+    c_both = flipped(c_two, 1)
+    partial = attend([ab_both, c_two], acc, False, (1,))
+    theirs = attend([c_both], partial, True, (1,))
+    other_heads = flipped(theirs, one)
+    mine = attend([ab_both, c_two, c_both], acc, True, (0,))
+    mine, other_heads = hold((mine, other_heads))
 
     back = pl.pallas_call(
         post_kernel,
@@ -359,7 +382,7 @@
         scratch_shapes=[pltpu.VMEM((REG_DEV, w_inner.shape[1]), BF16)],
         compiler_params=PARAMS,
         name="post",
-    )(core, mine, other_heads, pooled, members, w_out, gain_mlp.reshape(1, width), w_inner, w_outer)
+    )(group, mine, other_heads, pooled, members, w_out, gain_mlp.reshape(1, width), w_inner, w_outer)
     returned = exchanged(back.reshape(devices, tile, width)).reshape(sen_dev, width)
     return pl.pallas_call(
         functools.partial(decode_kernel, tile, order),

time: 89.5 us -> 91.5 us (1.022)
  blocking collectives: 23.6 us -> 0 us
  waiting for transfers between devices: 19.3 us -> 36.4 us
  starting transfers between devices: 17 us -> 24.3 us
  Pallas kernels: 26.8 us -> 28 us
    all_to_all x1 -> x0, blocking collectives: 23.6 us -> none  [exchanged(): lax.all_to_all(value, AXIS, split_axis=0, concat_axis=0, tiled=True, axis...]
    all_to_all x1 -> x2, waiting for transfers between devices: 15.1 us -> 31.8 us  [exchanged(): lax.all_to_all(value, AXIS, split_axis=0, concat_axis=0, tiled=True, axis...]
    all_to_all x1 -> x2, starting transfers between devices: 3.55 us -> 11.9 us  [exchanged(): lax.all_to_all(value, AXIS, split_axis=0, concat_axis=0, tiled=True, axis...]
    pallas_call x1, Pallas kernels: 0.09 us -> 1.71 us  [local(): pl.pallas_call(functools.partial(pack_kernel, tile, order), out_shape=jax...]
    ppermute x15, starting transfers between devices: 13.4 us -> 12.4 us  [flipped(): return lax.ppermute(value, AXIS, [(i, i ^ mask) for i in range(devices)])]
  transfers between devices with their start and end apart: 16 -> 17, of which waited for: 6 -> 7; matrix products, arithmetic and copies ran while one was open for 0% -> 0% of each run, Pallas kernels for 22% -> 21%
where the time goes in v7:
time: 91.5 us; the launch traced here: 91.2 us
  waiting for transfers between devices  36.4 us (40%)
  Pallas kernels  28 us (31%)
  starting transfers between devices  24.3 us (27%)
  local copies, waits for them, and re-layouts  2.17 us (2%)
    all_to_all x2, waiting for transfers between devices, exchanged(): lax.all_to_all(value, AXIS, split_axis=0, concat_axis=0, tiled=True, axis...  31.8 us
    pallas_call x8, Pallas kernels, attend(): pl.pallas_call(functools.partial(attend_kernel, len(parts), row_parts, ac...  19.9 us
    ppermute x15, starting transfers between devices, flipped(): return lax.ppermute(value, AXIS, [(i, i ^ mask) for i in range(devices)])  12.4 us
    all_to_all x2, starting transfers between devices, exchanged(): lax.all_to_all(value, AXIS, split_axis=0, concat_axis=0, tiled=True, axis...  11.9 us
    ppermute x15, waiting for transfers between devices, flipped(): return lax.ppermute(value, AXIS, [(i, i ^ mask) for i in range(devices)])  4.67 us
    pallas_call x1, Pallas kernels, local(): pl.pallas_call(post_kernel, out_shape=jax.ShapeDtypeStruct((sen_dev, widt...  2.78 us
    unnamed x34, local copies, waits for them, and re-layouts  1.84 us
  transfers between devices with their start and end apart: 17, of which 7 were waited for; matrix products, arithmetic and copies ran while one was open for 0% of the time, Pallas kernels for 21%

profile of v7, /device:TPU:1, one launch (start us, length us, event | category | flops | bytes accessed | tf_op | source)
XLA Modules:
  0.0 91.2 jit_solution(7268954247061402632)
XLA Ops:
  0.0 1.1 %copy-done = bf16[512,512]{1,0:T(8,128)(2,1)S(1)} copy-done((bf16[512,512]{1,0:T(8,128)(2,1)S(1)}, bf16[512,512]{1,0:T(8,128)(2,1)}, u32[]{:S(2)}) %copy-start) | copy-done | bytes 524312
  1.1 0.7 copy-done.10
  1.8 1.7 %pack.1 = bf16[32,72,128]{2,1,0:T(8,128)(2,1)} custom-call(s32[1]{0:T(128)S(6)} %add.21.place_ref, bf16[512,512]{1,0:T(8,128)(2,1)S(1)} %copy-done, s32[4,128]{1,0:T(4,128)S(1)} %bitcast.9), custom_call_target="tpu_custom_call" | custom-call | tf_op jit(solution)/shard_map/pack/pallas_call | solution.py:274
  3.5 7.1 %all-to-all-start = ((bf16[32,72,128]{2,1,0:T(8,128)(2,1)}), bf16[32,72,128]{2,1,0:T(8,128)(2,1)S(1)}, u32[]{:S(2)}, u32[]{:S(2)}) async-start(bf16[32,72,128]{2,1,0:T(8,128)(2,1)} %pack.1), calls=%async_computation | async-start | bytes 1179648 | tf_op jit(solution)/shard_map/all_to_all | solution.py:270
  10.6 16.7 %all-to-all-done.got_ref = bf16[32,72,128]{2,1,0:T(8,128)(2,1)S(1)} async-done(((bf16[32,72,128]{2,1,0:T(8,128)(2,1)}), bf16[32,72,128]{2,1,0:T(8,128)(2,1)S(1)}, u32[]{:S(2)}, u32[]{:S(2)}) %all-to-all-start) | async-done | bytes 589856 | tf_op jit(solution)/shard_map/all_to_all | solution.py:270
  27.3 0.0 copy-done.12
  27.3 0.0 copy-done.8
  27.3 1.0 %pool.1 = (f32[256,512]{1,0:T(8,128)S(1)}, bf16[256,512]{1,0:T(8,128)(2,1)S(1)}, bf16[256,512]{1,0:T(8,128)(2,1)S(1)}, bf16[256,128]{1,0:T(8,128)(2,1)S(1)}, bf16[256,128]{1,0:T(8,128)(2,1)S(1)}) custom-call(s32[1]{0:T(128)S(6)} %select_n.21.group_ref, bf16[32,72,128]{2,1,0:T(8,128)(2,1)S(1)} %all-to-all-done.got_ref, bf16[512,128]{1,0:T(8,128)(2,1)S(1)} %copy-done.8, ...), custom_call_target="tpu_custom_call" | custom-call | tf_op jit(solution)/shard_map/pool/pallas_call | solution.py:293
  28.3 1.3 %collective-permute-start = (bf16[256,128]{1,0:T(8,128)(2,1)S(1)}, bf16[256,128]{1,0:T(8,128)(2,1)S(1)}, u32[]{:S(2)}, u32[]{:S(2)}) collective-permute-start(bf16[256,128]{1,0:T(8,128)(2,1)S(1)} %get-tuple-element.27), channel_id=1, source_target_pairs={{0,8},{1,9},{2,10},{3,11},{4,12},{5,13},{6,14},{7,15},{8,0},{9,1},... | collective-permute-start | bytes 196616 | tf_op jit(solution)/shard_map/ppermute | solution.py:267
  29.6 0.1 broadcast_in_dim.3
  29.6 0.1 reshape_reshape.3.scale_ref
  29.7 0.8 query.1
  30.5 1.4 %collective-permute-done = bf16[256,128]{1,0:T(8,128)(2,1)S(1)} collective-permute-done((bf16[256,128]{1,0:T(8,128)(2,1)S(1)}, bf16[256,128]{1,0:T(8,128)(2,1)S(1)}, u32[]{:S(2)}, u32[]{:S(2)}) %collective-permute-start) | collective-permute-done | bytes 65568 | tf_op jit(solution)/shard_map/ppermute | solution.py:267
  31.9 1.2 %collective-permute-start.1 = (bf16[256,512]{1,0:T(8,128)(2,1)S(1)}, bf16[256,512]{1,0:T(8,128)(2,1)S(1)}, u32[]{:S(2)}, u32[]{:S(2)}) collective-permute-start(bf16[256,512]{1,0:T(8,128)(2,1)S(1)} %get-tuple-element.32), channel_id=1, source_target_pairs={{0,8},{1,9},{2,10},{3,11},{4,12},{5,13},{6,14},{7,15},{8,0},{9,1},... | collective-permute-start | bytes 786440 | tf_op jit(solution)/shard_map/ppermute | solution.py:267
  33.1 0.5 collective-permute-start.3
  33.6 1.4 %collective-permute-start.2 = (bf16[512,128]{1,0:T(8,128)(2,1)S(1)}, bf16[512,128]{1,0:T(8,128)(2,1)S(1)}, u32[]{:S(2)}, u32[]{:S(2)}) collective-permute-start(bf16[512,128]{1,0:T(8,128)(2,1)S(1)} %constant_dynamic-update-slice_fusion.refs_2_), channel_id=1, source_target_pairs={{0,1},{1,0},{2,3},{3,2},{4,5},{5,4},{6,7},{7,6},{8,9},{9,8},{10,11... | collective-permute-start | bytes 393224 | tf_op jit(solution)/shard_map/ppermute | solution.py:267
  35.0 0.7 collective-permute-start.4
  35.7 1.2 %collective-permute-start.5 = (bf16[512,128]{1,0:T(8,128)(2,1)S(1)}, bf16[512,128]{1,0:T(8,128)(2,1)S(1)}, u32[]{:S(2)}, u32[]{:S(2)}) collective-permute-start(bf16[512,128]{1,0:T(8,128)(2,1)S(1)} %constant_dynamic-update-slice_fusion.refs_2_), channel_id=1, source_target_pairs={{0,2},{1,3},{2,0},{3,1},{4,6},{5,7},{6,4},{7,5},{8,10},{9,11},{10,... | collective-permute-start | bytes 393224 | tf_op jit(solution)/shard_map/ppermute | solution.py:267
  36.9 0.7 collective-permute-done.3.refs_3_
  37.5 1.5 %collective-permute-start.6 = (bf16[512,128]{1,0:T(8,128)(2,1)S(1)}, bf16[512,128]{1,0:T(8,128)(2,1)S(1)}, u32[]{:S(2)}, u32[]{:S(2)}) collective-permute-start(bf16[512,128]{1,0:T(8,128)(2,1)S(1)} %collective-permute-done.3.refs_3_), channel_id=1, source_target_pairs={{0,1},{1,0},{2,3},{3,2},{4,5},{5,4},{6,7},{7,6},{8,9},{9,8},{10,11... | collective-permute-start | bytes 393224 | tf_op jit(solution)/shard_map/ppermute | solution.py:267
  39.1 0.3 collective-permute-done.1.refs_1_.refs_0_
  39.4 1.4 %attend.8.refs_4_ = f32[4,512,128]{2,1,0:T(8,128)S(1)} custom-call(bf16[256,512]{1,0:T(8,128)(2,1)S(1)} %get-tuple-element.31.refs_0_, bf16[256,512]{1,0:T(8,128)(2,1)S(1)} %collective-permute-done.1.refs_1_.refs_0_, bf16[512,128]{1,0:T(8,128)(2,1)S(1)} %constant_dynamic-update-slice_fusion.refs_2_), custom_call_target="tpu_custom_call" | custom-call | flops 1073741824 | bytes 131072 | tf_op jit(solution)/shard_map/attend/pallas_call | solution.py:329
  40.8 0.0 collective-permute-done.2.refs_2_
  40.8 2.4 %attend.9.refs_4_ = f32[4,512,128]{2,1,0:T(8,128)S(1)} custom-call(bf16[256,512]{1,0:T(8,128)(2,1)S(1)} %get-tuple-element.31.refs_0_, bf16[256,512]{1,0:T(8,128)(2,1)S(1)} %collective-permute-done.1.refs_1_.refs_0_, bf16[512,128]{1,0:T(8,128)(2,1)S(1)} %collective-permute-done.2.refs_2_, bf16[512,128]{1,0:T(8,128)(2,1)S(1)} %collective-permute-done.3.refs_3_, ...), custom_call_target="tpu_custom_call" | custom-call | flops 2147483648 | bytes 262144 | tf_op jit(solution)/shard_map/attend/pallas_call | solution.py:329
  43.2 0.7 collective-permute-done.4
  43.9 0.0 collective-permute-done.5
  43.9 0.1 collective-permute-start.7
  44.0 0.9 collective-permute-start.8
  44.9 1.1 %collective-permute-start.9 = (bf16[1024,128]{1,0:T(8,128)(2,1)S(1)}, bf16[1024,128]{1,0:T(8,128)(2,1)S(1)}, u32[]{:S(2)}, u32[]{:S(2)}) collective-permute-start(bf16[1024,128]{1,0:T(8,128)(2,1)S(1)} %constant_dynamic-update-slice_fusion.2.refs_2_), channel_id=1, source_target_pairs={{0,16},{1,17},{2,18},{3,19},{4,20},{5,21},{6,22},{7,23},{8,24},{9,... | collective-permute-start | bytes 786440 | tf_op jit(solution)/shard_map/ppermute | solution.py:267
  46.0 0.0 collective-permute-done.6.refs_3_
  46.0 3.5 %attend.10.refs_4_ = f32[4,512,128]{2,1,0:T(8,128)S(1)} custom-call(bf16[256,512]{1,0:T(8,128)(2,1)S(1)} %get-tuple-element.31.refs_0_, bf16[256,512]{1,0:T(8,128)(2,1)S(1)} %collective-permute-done.1.refs_1_.refs_0_, bf16[1024,128]{1,0:T(8,128)(2,1)S(1)} %constant_dynamic-update-slice_fusion.2.refs_2_, bf16[512,128]{1,0:T(8,128)(2,1)S(1)} %collective-permute-done.6.refs_3_, ...), custom_call_target="tpu_custom_call" | custom-call | flops 3221225472 | bytes 393216 | tf_op jit(solution)/shard_map/attend/pallas_call | solution.py:329
  49.5 0.0 collective-permute-done.7.refs_2_
  49.5 0.4 collective-permute-start.10
  49.9 0.8 collective-permute-start.12
  50.7 0.0 collective-permute-done.8.refs_3_
  50.7 3.7 %attend.11.refs_4_ = f32[4,512,128]{2,1,0:T(8,128)S(1)} custom-call(bf16[256,512]{1,0:T(8,128)(2,1)S(1)} %get-tuple-element.31.refs_0_, bf16[256,512]{1,0:T(8,128)(2,1)S(1)} %collective-permute-done.1.refs_1_.refs_0_, bf16[512,128]{1,0:T(8,128)(2,1)S(1)} %collective-permute-done.7.refs_2_, bf16[1024,128]{1,0:T(8,128)(2,1)S(1)} %collective-permute-done.8.refs_3_, ...), custom_call_target="tpu_custom_call" | custom-call | flops 3221225472 | bytes 393216 | tf_op jit(solution)/shard_map/attend/pallas_call | solution.py:329
  54.4 0.0 collective-permute-done.9.refs_2_
  54.4 0.4 collective-permute-start.11
  54.8 0.0 collective-permute-done.10.refs_3_
  54.8 3.5 %attend.12.refs_4_.refs_3_ = f32[4,512,128]{2,1,0:T(8,128)S(1)} custom-call(bf16[256,512]{1,0:T(8,128)(2,1)S(1)} %get-tuple-element.31.refs_0_, bf16[256,512]{1,0:T(8,128)(2,1)S(1)} %collective-permute-done.1.refs_1_.refs_0_, bf16[1024,128]{1,0:T(8,128)(2,1)S(1)} %collective-permute-done.9.refs_2_, bf16[512,128]{1,0:T(8,128)(2,1)S(1)} %collective-permute-done.10.refs_3_, ...), custom_call_target="tpu_custom_call" | custom-call | flops 3221225472 | bytes 393216 | tf_op jit(solution)/shard_map/attend/pallas_call | solution.py:329
  58.2 0.0 collective-permute-done.12.refs_2_
  58.3 0.0 collective-permute-done.11.refs_1_
  58.3 0.3 collective-permute-start.13
  58.5 1.8 %attend.14.refs_2_ = f32[4,256,128]{2,1,0:T(8,128)S(1)} custom-call(bf16[256,512]{1,0:T(8,128)(2,1)S(1)} %collective-permute-done.1.refs_1_.refs_0_, bf16[1024,128]{1,0:T(8,128)(2,1)S(1)} %collective-permute-done.11.refs_1_, bf16[512,128]{1,0:T(8,128)(2,1)S(1)} %collective-permute-done.12.refs_2_, f32[4,512,128]{2,1,0:T(8,128)S(1)} %attend.12.refs_4_.refs_3_), custom_call_target="tpu_custom_call" | custom-call | flops 1610612736 | bytes 393216 | tf_op jit(solution)/shard_map/attend/pallas_call | solution.py:329
  60.4 0.0 collective-permute-done.13.refs_3_.refs_1_
  60.4 1.1 %attend.15 = bf16[256,256]{1,0:T(8,128)(2,1)S(1)} custom-call(bf16[256,512]{1,0:T(8,128)(2,1)S(1)} %collective-permute-done.1.refs_1_.refs_0_, bf16[512,128]{1,0:T(8,128)(2,1)S(1)} %collective-permute-done.13.refs_3_.refs_1_, f32[4,256,128]{2,1,0:T(8,128)S(1)} %attend.14.refs_2_), custom_call_target="tpu_custom_call" | custom-call | flops 536870912 | bytes 131072 | tf_op jit(solution)/shard_map/attend/pallas_call | solution.py:329
  61.6 0.0 copy-start.2
  61.6 0.0 copy-start.3
  61.6 0.0 copy-start.4
  61.6 0.0 copy-start.13
  61.6 0.8 collective-permute-start.14
  62.4 2.5 %attend.13.mine_ref = bf16[256,256]{1,0:T(8,128)(2,1)S(1)} custom-call(bf16[256,512]{1,0:T(8,128)(2,1)S(1)} %get-tuple-element.31.refs_0_, bf16[1024,128]{1,0:T(8,128)(2,1)S(1)} %collective-permute-done.11.refs_1_, bf16[512,128]{1,0:T(8,128)(2,1)S(1)} %collective-permute-done.12.refs_2_, bf16[512,128]{1,0:T(8,128)(2,1)S(1)} %collective-permute-done.13.refs_3_.refs_1_, ...), custom_call_target="tpu_custom_call" | custom-call | flops 2147483648 | bytes 524288 | tf_op jit(solution)/shard_map/attend/pallas_call | solution.py:329
  64.9 1.6 %collective-permute-done.14.other_ref = bf16[256,256]{1,0:T(8,128)(2,1)S(1)} collective-permute-done((bf16[256,256]{1,0:T(8,128)(2,1)S(1)}, bf16[256,256]{1,0:T(8,128)(2,1)S(1)}, u32[]{:S(2)}, u32[]{:S(2)}) %collective-permute-start.14) | collective-permute-done | bytes 131104 | tf_op jit(solution)/shard_map/ppermute | solution.py:267
  66.5 0.0 copy-done.3
  66.5 0.0 copy-start.11
  66.5 0.0 copy-start.1
  66.5 0.0 copy-start.5
  66.5 0.0 copy-start.6
  66.5 0.0 copy-start.14
  66.6 2.8 %post.1 = bf16[512,512]{1,0:T(8,128)(2,1)} custom-call(s32[1]{0:T(128)S(6)} %select_n.21.group_ref, bf16[256,256]{1,0:T(8,128)(2,1)S(1)} %attend.13.mine_ref, bf16[256,256]{1,0:T(8,128)(2,1)S(1)} %collective-permute-done.14.other_ref, f32[256,512]{1,0:T(8,128)S(1)} %get-tuple-element.47.pooled_ref, bf16[256,512]{1,0:T(8,128)(2,1)S(1)} %get-tuple-element.48.member_ref, ...), custom_call_target="tpu_custom_call" | custom-call | tf_op jit(solution)/shard_map/post/pallas_call | solution.py:377
  69.3 4.8 %all-to-all-start.1 = ((bf16[32,16,512]{2,1,0:T(8,128)(2,1)}), bf16[32,16,512]{2,1,0:T(8,128)(2,1)S(1)}, u32[]{:S(2)}, u32[]{:S(2)}) async-start(bf16[32,16,512]{2,1,0:T(8,128)(2,1)} %bitcast.4), calls=%async_computation.1 | async-start | bytes 1048576 | tf_op jit(solution)/shard_map/all_to_all | solution.py:270
  74.1 0.1 copy.15.live_ref
  74.3 15.1 %all-to-all-done.1 = bf16[32,16,512]{2,1,0:T(8,128)(2,1)S(1)} async-done(((bf16[32,16,512]{2,1,0:T(8,128)(2,1)}), bf16[32,16,512]{2,1,0:T(8,128)(2,1)S(1)}, u32[]{:S(2)}, u32[]{:S(2)}) %all-to-all-start.1) | async-done | bytes 524320 | tf_op jit(solution)/shard_map/all_to_all | solution.py:270
  89.4 1.8 %decode.1 = bf16[512,512]{1,0:T(8,128)(2,1)} custom-call(bf16[512,512]{1,0:T(8,128)(2,1)S(1)} %bitcast.8, bf16[512,512]{1,0:T(8,128)(2,1)S(1)} %copy-done.1, f32[512,1]{1,0:T(8,128)S(1)} %copy.15.live_ref, f32[1,512]{1,0:T(1,128)S(1)} %bitcast.12, bf16[512,512]{1,0:T(8,128)(2,1)S(1)} %copy-done.5, bf16[512,512]{1,0:T(8,128)(2,1)S(1)} %copy-done.6), custom_call_target="tpu_custom_call" | custom-call | tf_op jit(solution)/shard_map/decode/pallas_call | solution.py:387
  (24 shorter events, 0.1 us)
Async XLA Ops:
  0.0 27.3 %copy-start.12 = (f32[512]{0:T(512)S(1)}, f32[512]{0:T(512)}, u32[]{:S(2)}) copy-start(f32[512]{0:T(512)} %param.21) | copy-start | bytes 6148
  0.0 29.6 %copy-start.15 = (f32[8]{0:T(128)S(1)}, f32[8]{0:T(128)}, u32[]{:S(2)}) copy-start(f32[8]{0:T(128)} %param.20) | copy-start | bytes 100
  0.0 1.1 %copy-start = (bf16[512,512]{1,0:T(8,128)(2,1)S(1)}, bf16[512,512]{1,0:T(8,128)(2,1)}, u32[]{:S(2)}) copy-start(bf16[512,512]{1,0:T(8,128)(2,1)} %sensors_ref.3) | copy-start | bytes 1572868
  1.1 0.7 copy-start.10
  1.8 25.5 %copy-start.8 = (bf16[512,128]{1,0:T(8,128)(2,1)S(1)}, bf16[512,128]{1,0:T(8,128)(2,1)}, u32[]{:S(2)}) copy-start(bf16[512,128]{1,0:T(8,128)(2,1)} %w_key_ref.1) | copy-start | bytes 393220
  1.8 25.5 %copy-start.9 = (bf16[512,128]{1,0:T(8,128)(2,1)S(1)}, bf16[512,128]{1,0:T(8,128)(2,1)}, u32[]{:S(2)}) copy-start(bf16[512,128]{1,0:T(8,128)(2,1)} %w_value_ref.1) | copy-start | bytes 393220
  1.8 28.0 %copy-start.7 = (bf16[512,512]{1,0:T(8,128)(2,1)S(1)}, bf16[512,512]{1,0:T(8,128)(2,1)}, u32[]{:S(2)}) copy-start(bf16[512,512]{1,0:T(8,128)(2,1)} %w_query_ref.1) | copy-start | bytes 1572868
  3.5 23.8 %all-to-all-start = ((bf16[32,72,128]{2,1,0:T(8,128)(2,1)}), bf16[32,72,128]{2,1,0:T(8,128)(2,1)S(1)}, u32[]{:S(2)}, u32[]{:S(2)}) async-start(bf16[32,72,128]{2,1,0:T(8,128)(2,1)} %pack.1), calls=%async_computation | async-start | bytes 1179648 | tf_op jit(solution)/shard_map/all_to_all | solution.py:270
  28.3 3.6 %collective-permute-start = (bf16[256,128]{1,0:T(8,128)(2,1)S(1)}, bf16[256,128]{1,0:T(8,128)(2,1)S(1)}, u32[]{:S(2)}, u32[]{:S(2)}) collective-permute-start(bf16[256,128]{1,0:T(8,128)(2,1)S(1)} %get-tuple-element.27), channel_id=1, source_target_pairs={{0,8},{1,9},{2,10},{3,11},{4,12},{5,13},{6,14},{7,15},{8,0},{9,1},... | collective-permute-start | bytes 196616 | tf_op jit(solution)/shard_map/ppermute | solution.py:267
  31.9 7.5 %collective-permute-start.1 = (bf16[256,512]{1,0:T(8,128)(2,1)S(1)}, bf16[256,512]{1,0:T(8,128)(2,1)S(1)}, u32[]{:S(2)}, u32[]{:S(2)}) collective-permute-start(bf16[256,512]{1,0:T(8,128)(2,1)S(1)} %get-tuple-element.32), channel_id=1, source_target_pairs={{0,8},{1,9},{2,10},{3,11},{4,12},{5,13},{6,14},{7,15},{8,0},{9,1},... | collective-permute-start | bytes 786440 | tf_op jit(solution)/shard_map/ppermute | solution.py:267
  33.1 4.5 %collective-permute-start.3 = (bf16[512,128]{1,0:T(8,128)(2,1)S(1)}, bf16[512,128]{1,0:T(8,128)(2,1)S(1)}, u32[]{:S(2)}, u32[]{:S(2)}) collective-permute-start(bf16[512,128]{1,0:T(8,128)(2,1)S(1)} %constant_dynamic-update-slice_fusion.refs_2_), channel_id=1, source_target_pairs={{0,16},{1,17},{2,18},{3,19},{4,20},{5,21},{6,22},{7,23},{8,24},{9,... | collective-permute-start | bytes 393224 | tf_op jit(solution)/shard_map/ppermute | solution.py:267
  33.6 7.2 %collective-permute-start.2 = (bf16[512,128]{1,0:T(8,128)(2,1)S(1)}, bf16[512,128]{1,0:T(8,128)(2,1)S(1)}, u32[]{:S(2)}, u32[]{:S(2)}) collective-permute-start(bf16[512,128]{1,0:T(8,128)(2,1)S(1)} %constant_dynamic-update-slice_fusion.refs_2_), channel_id=1, source_target_pairs={{0,1},{1,0},{2,3},{3,2},{4,5},{5,4},{6,7},{7,6},{8,9},{9,8},{10,11... | collective-permute-start | bytes 393224 | tf_op jit(solution)/shard_map/ppermute | solution.py:267
  35.0 8.9 %collective-permute-start.4 = (bf16[512,128]{1,0:T(8,128)(2,1)S(1)}, bf16[512,128]{1,0:T(8,128)(2,1)S(1)}, u32[]{:S(2)}, u32[]{:S(2)}) collective-permute-start(bf16[512,128]{1,0:T(8,128)(2,1)S(1)} %constant_dynamic-update-slice_fusion.refs_2_), channel_id=1, source_target_pairs={{0,4},{1,5},{2,6},{3,7},{4,0},{5,1},{6,2},{7,3},{8,12},{9,13},{10,... | collective-permute-start | bytes 393224 | tf_op jit(solution)/shard_map/ppermute | solution.py:267
  35.7 8.2 %collective-permute-start.5 = (bf16[512,128]{1,0:T(8,128)(2,1)S(1)}, bf16[512,128]{1,0:T(8,128)(2,1)S(1)}, u32[]{:S(2)}, u32[]{:S(2)}) collective-permute-start(bf16[512,128]{1,0:T(8,128)(2,1)S(1)} %constant_dynamic-update-slice_fusion.refs_2_), channel_id=1, source_target_pairs={{0,2},{1,3},{2,0},{3,1},{4,6},{5,7},{6,4},{7,5},{8,10},{9,11},{10,... | collective-permute-start | bytes 393224 | tf_op jit(solution)/shard_map/ppermute | solution.py:267
  37.5 8.5 %collective-permute-start.6 = (bf16[512,128]{1,0:T(8,128)(2,1)S(1)}, bf16[512,128]{1,0:T(8,128)(2,1)S(1)}, u32[]{:S(2)}, u32[]{:S(2)}) collective-permute-start(bf16[512,128]{1,0:T(8,128)(2,1)S(1)} %collective-permute-done.3.refs_3_), channel_id=1, source_target_pairs={{0,1},{1,0},{2,3},{3,2},{4,5},{5,4},{6,7},{7,6},{8,9},{9,8},{10,11... | collective-permute-start | bytes 393224 | tf_op jit(solution)/shard_map/ppermute | solution.py:267
  43.9 5.6 %collective-permute-start.7 = (bf16[512,128]{1,0:T(8,128)(2,1)S(1)}, bf16[512,128]{1,0:T(8,128)(2,1)S(1)}, u32[]{:S(2)}, u32[]{:S(2)}) collective-permute-start(bf16[512,128]{1,0:T(8,128)(2,1)S(1)} %collective-permute-done.4), channel_id=1, source_target_pairs={{0,2},{1,3},{2,0},{3,1},{4,6},{5,7},{6,4},{7,5},{8,10},{9,11},{10,... | collective-permute-start | bytes 393224 | tf_op jit(solution)/shard_map/ppermute | solution.py:267
  44.0 6.7 %collective-permute-start.8 = (bf16[1024,128]{1,0:T(8,128)(2,1)S(1)}, bf16[1024,128]{1,0:T(8,128)(2,1)S(1)}, u32[]{:S(2)}, u32[]{:S(2)}) collective-permute-start(bf16[1024,128]{1,0:T(8,128)(2,1)S(1)} %constant_dynamic-update-slice_fusion.2.refs_2_), channel_id=1, source_target_pairs={{0,1},{1,0},{2,3},{3,2},{4,5},{5,4},{6,7},{7,6},{8,9},{9,8},{10,11... | collective-permute-start | bytes 786440 | tf_op jit(solution)/shard_map/ppermute | solution.py:267
  44.9 9.5 %collective-permute-start.9 = (bf16[1024,128]{1,0:T(8,128)(2,1)S(1)}, bf16[1024,128]{1,0:T(8,128)(2,1)S(1)}, u32[]{:S(2)}, u32[]{:S(2)}) collective-permute-start(bf16[1024,128]{1,0:T(8,128)(2,1)S(1)} %constant_dynamic-update-slice_fusion.2.refs_2_), channel_id=1, source_target_pairs={{0,16},{1,17},{2,18},{3,19},{4,20},{5,21},{6,22},{7,23},{8,24},{9,... | collective-permute-start | bytes 786440 | tf_op jit(solution)/shard_map/ppermute | solution.py:267
  49.5 5.2 %collective-permute-start.10 = (bf16[512,128]{1,0:T(8,128)(2,1)S(1)}, bf16[512,128]{1,0:T(8,128)(2,1)S(1)}, u32[]{:S(2)}, u32[]{:S(2)}) collective-permute-start(bf16[512,128]{1,0:T(8,128)(2,1)S(1)} %collective-permute-done.7.refs_2_), channel_id=1, source_target_pairs={{0,1},{1,0},{2,3},{3,2},{4,5},{5,4},{6,7},{7,6},{8,9},{9,8},{10,11... | collective-permute-start | bytes 393224 | tf_op jit(solution)/shard_map/ppermute | solution.py:267
  49.9 8.3 %collective-permute-start.12 = (bf16[512,128]{1,0:T(8,128)(2,1)S(1)}, bf16[512,128]{1,0:T(8,128)(2,1)S(1)}, u32[]{:S(2)}, u32[]{:S(2)}) collective-permute-start(bf16[512,128]{1,0:T(8,128)(2,1)S(1)} %collective-permute-done.7.refs_2_), channel_id=1, source_target_pairs={{0,16},{1,17},{2,18},{3,19},{4,20},{5,21},{6,22},{7,23},{8,24},{9,... | collective-permute-start | bytes 393224 | tf_op jit(solution)/shard_map/ppermute | solution.py:267
  54.4 3.9 %collective-permute-start.11 = (bf16[1024,128]{1,0:T(8,128)(2,1)S(1)}, bf16[1024,128]{1,0:T(8,128)(2,1)S(1)}, u32[]{:S(2)}, u32[]{:S(2)}) collective-permute-start(bf16[1024,128]{1,0:T(8,128)(2,1)S(1)} %collective-permute-done.9.refs_2_), channel_id=1, source_target_pairs={{0,1},{1,0},{2,3},{3,2},{4,5},{5,4},{6,7},{7,6},{8,9},{9,8},{10,11... | collective-permute-start | bytes 786440 | tf_op jit(solution)/shard_map/ppermute | solution.py:267
  58.3 2.1 %collective-permute-start.13 = (bf16[512,128]{1,0:T(8,128)(2,1)S(1)}, bf16[512,128]{1,0:T(8,128)(2,1)S(1)}, u32[]{:S(2)}, u32[]{:S(2)}) collective-permute-start(bf16[512,128]{1,0:T(8,128)(2,1)S(1)} %collective-permute-done.12.refs_2_), channel_id=1, source_target_pairs={{0,1},{1,0},{2,3},{3,2},{4,5},{5,4},{6,7},{7,6},{8,9},{9,8},{10,11... | collective-permute-start | bytes 393224 | tf_op jit(solution)/shard_map/ppermute | solution.py:267
  61.6 4.9 %copy-start.2 = (bf16[512,2048]{1,0:T(8,128)(2,1)S(1)}, bf16[512,2048]{1,0:T(8,128)(2,1)}, u32[]{:S(2)}) copy-start(bf16[512,2048]{1,0:T(8,128)(2,1)} %w_inner_ref.1) | copy-start | bytes 6291460
  61.6 4.9 %copy-start.3 = (bf16[2048,512]{1,0:T(8,128)(2,1)S(1)}, bf16[2048,512]{1,0:T(8,128)(2,1)}, u32[]{:S(2)}) copy-start(bf16[2048,512]{1,0:T(8,128)(2,1)} %w_outer_ref.1) | copy-start | bytes 6291460
  61.6 4.9 %copy-start.4 = (bf16[512,512]{1,0:T(8,128)(2,1)S(1)}, bf16[512,512]{1,0:T(8,128)(2,1)}, u32[]{:S(2)}) copy-start(bf16[512,512]{1,0:T(8,128)(2,1)} %w_out_ref.2) | copy-start | bytes 1572868
  61.6 4.9 %copy-start.13 = (f32[512]{0:T(512)S(1)}, f32[512]{0:T(512)}, u32[]{:S(2)}) copy-start(f32[512]{0:T(512)} %param.24) | copy-start | bytes 6148
  61.6 4.9 %collective-permute-start.14 = (bf16[256,256]{1,0:T(8,128)(2,1)S(1)}, bf16[256,256]{1,0:T(8,128)(2,1)S(1)}, u32[]{:S(2)}, u32[]{:S(2)}) collective-permute-start(bf16[256,256]{1,0:T(8,128)(2,1)S(1)} %attend.15), channel_id=1, source_target_pairs={{0,8},{1,9},{2,10},{3,11},{4,12},{5,13},{6,14},{7,15},{8,0},{9,1},... | collective-permute-start | bytes 393224 | tf_op jit(solution)/shard_map/ppermute | solution.py:267
  66.5 7.6 %copy-start.11 = (s32[512]{0:T(512)S(1)}, s32[512]{0:T(512)}, u32[]{:S(2)}) copy-start(s32[512]{0:T(512)} %param.15) | copy-start | bytes 6148
  66.5 22.9 %copy-start.1 = (bf16[512,512]{1,0:T(8,128)(2,1)S(1)}, bf16[512,512]{1,0:T(8,128)(2,1)}, u32[]{:S(2)}) copy-start(bf16[512,512]{1,0:T(8,128)(2,1)} %sensors_ref.3) | copy-start | bytes 1572868
  66.5 22.9 %copy-start.5 = (bf16[512,512]{1,0:T(8,128)(2,1)S(1)}, bf16[512,512]{1,0:T(8,128)(2,1)}, u32[]{:S(2)}) copy-start(bf16[512,512]{1,0:T(8,128)(2,1)} %w_in_ref.1) | copy-start | bytes 1572868
  66.5 22.9 %copy-start.6 = (bf16[512,512]{1,0:T(8,128)(2,1)S(1)}, bf16[512,512]{1,0:T(8,128)(2,1)}, u32[]{:S(2)}) copy-start(bf16[512,512]{1,0:T(8,128)(2,1)} %w_out_ref.3) | copy-start | bytes 1572868
  66.5 22.9 %copy-start.14 = (f32[512]{0:T(512)S(1)}, f32[512]{0:T(512)}, u32[]{:S(2)}) copy-start(f32[512]{0:T(512)} %param.25) | copy-start | bytes 6148
  69.3 20.1 %all-to-all-start.1 = ((bf16[32,16,512]{2,1,0:T(8,128)(2,1)}), bf16[32,16,512]{2,1,0:T(8,128)(2,1)S(1)}, u32[]{:S(2)}, u32[]{:S(2)}) async-start(bf16[32,16,512]{2,1,0:T(8,128)(2,1)} %bitcast.4), calls=%async_computation.1 | async-start | bytes 1048576 | tf_op jit(solution)/shard_map/all_to_all | solution.py:270

commit v8 on v7

--- a/solution.py
+++ b/solution.py
@@ -23,7 +23,6 @@
 
 VMEM = pl.BlockSpec(memory_space=pltpu.VMEM)
 SMEM = pl.BlockSpec(memory_space=pltpu.SMEM)
-HBM = pl.BlockSpec(memory_space=pltpu.HBM)
 PARAMS = pltpu.CompilerParams(vmem_limit_bytes=40 * 1024 * 1024)
 
 
@@ -41,35 +40,23 @@
     return values * lax.rsqrt(jnp.mean(values * values, axis=-1, keepdims=True) + EPS)
 
 
-def pack_kernel(tile, order, place_ref, sensors_ref, labels_ref, out_ref, rows_ref, own_ref, sems):
+def pack_kernel(tile, order, place_ref, sensors_ref, labels_ref, out_ref):
     per_row = LANES // tile
     blocks = sensors_ref.shape[1] // LANES
-    pieces = sems.shape[0] - 1
-    piece = sensors_ref.shape[0] // pieces
-    label_copy = pltpu.make_async_copy(labels_ref, own_ref, sems.at[pieces])
-    label_copy.start()
-    copies = []
-    for i in range(pieces):
-        here = slice(i * piece, (i + 1) * piece)
-        copies.append(pltpu.make_async_copy(sensors_ref.at[here], rows_ref.at[here], sems.at[i]))
-        copies[i].start()
-    label_copy.wait()
     mine = lax.rem(place_ref[0], per_row)
-    labels = (own_ref[...] + 1).astype(F32)
+    labels = labels_ref[...]
     lane = lax.broadcasted_iota(jnp.int32, labels.shape, 1)
     own_lanes = (lane // tile) == mine
     rolled = []
     for k in range(per_row):
         shift = lax.rem(mine - k + per_row, per_row) * tile
         rolled.append(jnp.where(own_lanes, pltpu.roll(labels, shift, 1), 0.0))
-    for t in range(len(order)):
-        if t * tile % piece == 0:
-            copies[t * tile // piece].wait()
+    for at, t in enumerate(order):
         g = t // per_row
         row = jnp.broadcast_to(rolled[t % per_row][g : g + 1, :], (8, LANES)).astype(BF16)
-        rows = rows_ref[t * tile : (t + 1) * tile, :]
+        rows = sensors_ref[t * tile : (t + 1) * tile, :]
         parts = [rows[:, c * LANES : (c + 1) * LANES] for c in range(blocks)]
-        out_ref[order.index(t)] = jnp.concatenate(parts + [row], axis=0)
+        out_ref[at] = jnp.concatenate(parts + [row], axis=0)
 
 
 def by_heads():
@@ -274,16 +261,11 @@
     payload = pl.pallas_call(
         functools.partial(pack_kernel, tile, order),
         out_shape=jax.ShapeDtypeStruct((devices, pay_rows, LANES), BF16),
-        in_specs=[SMEM, HBM, HBM],
+        in_specs=[SMEM, VMEM, VMEM],
         out_specs=VMEM,
-        scratch_shapes=[
-            pltpu.VMEM(sensors.shape, BF16),
-            pltpu.VMEM((sen_dev // LANES, LANES), jnp.int32),
-            pltpu.SemaphoreType.DMA((5,)),
-        ],
         compiler_params=PARAMS,
         name="pack",
-    )(place, sensors, slot_region.reshape(-1, LANES))
+    )(place, sensors, (slot_region + 1).astype(F32).reshape(-1, LANES))
     got = exchanged(payload)
 
     scale = jnp.repeat(temper * (math.log2(math.e) / HEAD_DIM), HEAD_DIM).reshape(1, -1)
@@ -304,7 +286,8 @@
         compiler_params=PARAMS,
         name="pool",
     )(group, got, w_key, w_value, gain_attn.reshape(1, width))
-    kv_other = flipped(kv_send, one)
+    kv_other, keep_core = flipped(kv_send, one), flipped(kv_keep, 1)
+    keep_core, attn_in = lax.optimization_barrier((keep_core, attn_in))
     slab_shape = jax.ShapeDtypeStruct((REG_DEV, GROUP * LANES), BF16)
     q_keep, q_send = pl.pallas_call(
         query_kernel,
@@ -317,7 +300,6 @@
         ),
         name="query",
     )(group, attn_in, w_query, scale)
-    kv_other, q_keep, q_send = lax.optimization_barrier((kv_other, q_keep, q_send))
     slabs = (q_keep, flipped(q_send, one))
 
     def attend(parts, acc, last=False, row_parts=(0, 1)):
@@ -348,10 +330,13 @@
 
     hold = lax.optimization_barrier
     a, b = flipped(own, far), flipped(own, near)
-    own_two, own_core = flipped(own, two), flipped(own, 1)
+    own_two = flipped(own, two)
+    own_core = [keep_core, flipped(kv_other, 1)]
+    if own.shape[0] > 2 * REG_DEV:
+        own_core.append(flipped(own[2 * REG_DEV :], 1))
     acc = attend([own], None)
     own_both = flipped(own_two, 1)
-    acc = attend([own_core, own_two], acc)
+    acc = attend(own_core + [own_two], acc)
     acc, a, b = hold((acc, a, b))
 
     ab, c = jnp.concatenate([a, b], axis=0), flipped(a, near)
@@ -364,14 +349,14 @@
     acc, ab_two = hold((acc, ab_two))
 
     ab_both = flipped(ab_two, 1)
-    acc = attend([ab_two, c_core], acc)
-    acc, ab_both, c_two = hold((acc, ab_both, c_two))
+    partial = attend([ab_two, c_core], acc, False, (1,))
+    partial, ab_both, c_two = hold((partial, ab_both, c_two))
 
     c_both = flipped(c_two, 1)
-    partial = attend([ab_both, c_two], acc, False, (1,))
+    partial = attend([ab_both, c_two], partial, False, (1,))
     theirs = attend([c_both], partial, True, (1,))
     other_heads = flipped(theirs, one)
-    mine = attend([ab_both, c_two, c_both], acc, True, (0,))
+    mine = attend([ab_two, c_core, ab_both, c_two, c_both], acc, True, (0,))
     mine, other_heads = hold((mine, other_heads))
 
     back = pl.pallas_call(

time: 91.5 us -> 90.3 us (0.987)
  waiting for transfers between devices: 36.4 us -> 34.9 us
  starting transfers between devices: 24.3 us -> 25.4 us
    ppermute x15 -> x16, starting transfers between devices: 12.4 us -> 15.2 us  [flipped(): return lax.ppermute(value, AXIS, [(i, i ^ mask) for i in range(devices)])]
    all_to_all x2, starting transfers between devices: 11.9 us -> 10.1 us  [exchanged(): lax.all_to_all(value, AXIS, split_axis=0, concat_axis=0, tiled=True, axis...]
    ppermute x15 -> x16, waiting for transfers between devices: 4.67 us -> 3.01 us  [flipped(): return lax.ppermute(value, AXIS, [(i, i ^ mask) for i in range(devices)])]
    unnamed x34 -> x32, local copies, waits for them, and re-layouts: 1.84 us -> 1.13 us
  transfers between devices with their start and end apart: 17 -> 18, of which waited for: 7 -> 4; matrix products, arithmetic and copies ran while one was open for 0% -> 0% of each run, Pallas kernels for 21% -> 22%
where the time goes in v8:
time: 90.3 us; the launch traced here: 90 us
  waiting for transfers between devices  34.9 us (39%)
  Pallas kernels  27.2 us (30%)
  starting transfers between devices  25.4 us (28%)
  local copies, waits for them, and re-layouts  1.46 us (2%)
    all_to_all x2, waiting for transfers between devices, exchanged(): lax.all_to_all(value, AXIS, split_axis=0, concat_axis=0, tiled=True, axis...  31.9 us
    pallas_call x8, Pallas kernels, attend(): pl.pallas_call(functools.partial(attend_kernel, len(parts), row_parts, ac...  19.9 us
    ppermute x16, starting transfers between devices, flipped(): return lax.ppermute(value, AXIS, [(i, i ^ mask) for i in range(devices)])  15.2 us
    all_to_all x2, starting transfers between devices, exchanged(): lax.all_to_all(value, AXIS, split_axis=0, concat_axis=0, tiled=True, axis...  10.1 us
    ppermute x16, waiting for transfers between devices, flipped(): return lax.ppermute(value, AXIS, [(i, i ^ mask) for i in range(devices)])  3.01 us
    pallas_call x1, Pallas kernels, local(): pl.pallas_call(post_kernel, out_shape=jax.ShapeDtypeStruct((sen_dev, widt...  2.78 us
  transfers between devices with their start and end apart: 18, of which 4 were waited for; matrix products, arithmetic and copies ran while one was open for 0% of the time, Pallas kernels for 22%

profile of v8, /device:TPU:1, one launch (start us, length us, event | category | flops | bytes accessed | tf_op | source)
XLA Modules:
  0.0 90.0 jit_solution(18446082943010066537)
XLA Ops:
  0.0 0.7 convert_bitcast_fusion.labels_ref
  0.7 1.0 %copy-done = bf16[512,512]{1,0:T(8,128)(2,1)S(1)} copy-done((bf16[512,512]{1,0:T(8,128)(2,1)S(1)}, bf16[512,512]{1,0:T(8,128)(2,1)}, u32[]{:S(2)}) %copy-start) | copy-done | bytes 524312
  1.8 0.9 %pack.1 = bf16[32,72,128]{2,1,0:T(8,128)(2,1)} custom-call(s32[1]{0:T(128)S(6)} %add.27.place_ref, bf16[512,512]{1,0:T(8,128)(2,1)S(1)} %copy-done, f32[4,128]{1,0:T(4,128)S(1)} %convert_bitcast_fusion.labels_ref), custom_call_target="tpu_custom_call" | custom-call | tf_op jit(solution)/shard_map/pack/pallas_call | solution.py:261
  2.7 7.1 %all-to-all-start = ((bf16[32,72,128]{2,1,0:T(8,128)(2,1)}), bf16[32,72,128]{2,1,0:T(8,128)(2,1)S(1)}, u32[]{:S(2)}, u32[]{:S(2)}) async-start(bf16[32,72,128]{2,1,0:T(8,128)(2,1)} %pack.1), calls=%async_computation | async-start | bytes 1179648 | tf_op jit(solution)/shard_map/all_to_all | solution.py:257
  9.8 16.7 %all-to-all-done.got_ref = bf16[32,72,128]{2,1,0:T(8,128)(2,1)S(1)} async-done(((bf16[32,72,128]{2,1,0:T(8,128)(2,1)}), bf16[32,72,128]{2,1,0:T(8,128)(2,1)S(1)}, u32[]{:S(2)}, u32[]{:S(2)}) %all-to-all-start) | async-done | bytes 589856 | tf_op jit(solution)/shard_map/all_to_all | solution.py:257
  26.5 0.0 copy-done.9
  26.5 1.0 %pool.1 = (f32[256,512]{1,0:T(8,128)S(1)}, bf16[256,512]{1,0:T(8,128)(2,1)S(1)}, bf16[256,512]{1,0:T(8,128)(2,1)S(1)}, bf16[256,128]{1,0:T(8,128)(2,1)S(1)}, bf16[256,128]{1,0:T(8,128)(2,1)S(1)}) custom-call(s32[1]{0:T(128)S(6)} %select_n.21.group_ref, bf16[32,72,128]{2,1,0:T(8,128)(2,1)S(1)} %all-to-all-done.got_ref, bf16[512,128]{1,0:T(8,128)(2,1)S(1)} %copy-done.8, ...), custom_call_target="tpu_custom_call" | custom-call | tf_op jit(solution)/shard_map/pool/pallas_call | solution.py:275
  27.5 0.1 collective-permute-start
  27.6 0.1 broadcast_in_dim.3
  27.7 0.1 reshape_reshape.3.scale_ref
  27.7 1.2 %collective-permute-start.2 = (bf16[256,128]{1,0:T(8,128)(2,1)S(1)}, bf16[256,128]{1,0:T(8,128)(2,1)S(1)}, u32[]{:S(2)}, u32[]{:S(2)}) collective-permute-start(bf16[256,128]{1,0:T(8,128)(2,1)S(1)} %get-tuple-element.32), channel_id=1, source_target_pairs={{0,8},{1,9},{2,10},{3,11},{4,12},{5,13},{6,14},{7,15},{8,0},{9,1},... | collective-permute-start | bytes 196616 | tf_op jit(solution)/shard_map/ppermute | solution.py:254
  28.9 0.0 collective-permute-done.refs_2_
  28.9 0.8 query.1
  29.7 1.1 %collective-permute-start.1 = (bf16[256,512]{1,0:T(8,128)(2,1)S(1)}, bf16[256,512]{1,0:T(8,128)(2,1)S(1)}, u32[]{:S(2)}, u32[]{:S(2)}) collective-permute-start(bf16[256,512]{1,0:T(8,128)(2,1)S(1)} %get-tuple-element.30), channel_id=1, source_target_pairs={{0,8},{1,9},{2,10},{3,11},{4,12},{5,13},{6,14},{7,15},{8,0},{9,1},... | collective-permute-start | bytes 786440 | tf_op jit(solution)/shard_map/ppermute | solution.py:254
  30.9 0.0 collective-permute-done.2
  30.9 1.3 %collective-permute-start.4 = (bf16[512,128]{1,0:T(8,128)(2,1)S(1)}, bf16[512,128]{1,0:T(8,128)(2,1)S(1)}, u32[]{:S(2)}, u32[]{:S(2)}) collective-permute-start(bf16[512,128]{1,0:T(8,128)(2,1)S(1)} %constant_dynamic-update-slice_fusion.refs_2_), channel_id=1, source_target_pairs={{0,16},{1,17},{2,18},{3,19},{4,20},{5,21},{6,22},{7,23},{8,24},{9,... | collective-permute-start | bytes 393224 | tf_op jit(solution)/shard_map/ppermute | solution.py:254
  32.2 1.4 %collective-permute-start.5 = (bf16[512,128]{1,0:T(8,128)(2,1)S(1)}, bf16[512,128]{1,0:T(8,128)(2,1)S(1)}, u32[]{:S(2)}, u32[]{:S(2)}) collective-permute-start(bf16[512,128]{1,0:T(8,128)(2,1)S(1)} %constant_dynamic-update-slice_fusion.refs_2_), channel_id=1, source_target_pairs={{0,4},{1,5},{2,6},{3,7},{4,0},{5,1},{6,2},{7,3},{8,12},{9,13},{10,... | collective-permute-start | bytes 393224 | tf_op jit(solution)/shard_map/ppermute | solution.py:254
  33.6 1.3 %collective-permute-start.6 = (bf16[512,128]{1,0:T(8,128)(2,1)S(1)}, bf16[512,128]{1,0:T(8,128)(2,1)S(1)}, u32[]{:S(2)}, u32[]{:S(2)}) collective-permute-start(bf16[512,128]{1,0:T(8,128)(2,1)S(1)} %constant_dynamic-update-slice_fusion.refs_2_), channel_id=1, source_target_pairs={{0,2},{1,3},{2,0},{3,1},{4,6},{5,7},{6,4},{7,5},{8,10},{9,11},{10,... | collective-permute-start | bytes 393224 | tf_op jit(solution)/shard_map/ppermute | solution.py:254
  34.8 1.6 %collective-permute-start.3 = (bf16[256,128]{1,0:T(8,128)(2,1)S(1)}, bf16[256,128]{1,0:T(8,128)(2,1)S(1)}, u32[]{:S(2)}, u32[]{:S(2)}) collective-permute-start(bf16[256,128]{1,0:T(8,128)(2,1)S(1)} %collective-permute-done.2), channel_id=1, source_target_pairs={{0,1},{1,0},{2,3},{3,2},{4,5},{5,4},{6,7},{7,6},{8,9},{9,8},{10,11... | collective-permute-start | bytes 196616 | tf_op jit(solution)/shard_map/ppermute | solution.py:254
  36.5 0.0 collective-permute-done.4.refs_4_
  36.5 1.1 %collective-permute-start.7 = (bf16[512,128]{1,0:T(8,128)(2,1)S(1)}, bf16[512,128]{1,0:T(8,128)(2,1)S(1)}, u32[]{:S(2)}, u32[]{:S(2)}) collective-permute-start(bf16[512,128]{1,0:T(8,128)(2,1)S(1)} %collective-permute-done.4.refs_4_), channel_id=1, source_target_pairs={{0,1},{1,0},{2,3},{3,2},{4,5},{5,4},{6,7},{7,6},{8,9},{9,8},{10,11... | collective-permute-start | bytes 393224 | tf_op jit(solution)/shard_map/ppermute | solution.py:254
  37.5 0.0 collective-permute-done.1.refs_1_.refs_0_
  37.5 1.4 %attend.8.refs_5_ = f32[4,512,128]{2,1,0:T(8,128)S(1)} custom-call(bf16[256,512]{1,0:T(8,128)(2,1)S(1)} %get-tuple-element.29.refs_0_, bf16[256,512]{1,0:T(8,128)(2,1)S(1)} %collective-permute-done.1.refs_1_.refs_0_, bf16[512,128]{1,0:T(8,128)(2,1)S(1)} %constant_dynamic-update-slice_fusion.refs_2_), custom_call_target="tpu_custom_call" | custom-call | flops 1073741824 | bytes 131072 | tf_op jit(solution)/shard_map/attend/pallas_call | solution.py:311
  38.9 0.0 collective-permute-done.3.refs_3_
  38.9 2.4 %attend.9.refs_4_ = f32[4,512,128]{2,1,0:T(8,128)S(1)} custom-call(bf16[256,512]{1,0:T(8,128)(2,1)S(1)} %get-tuple-element.29.refs_0_, bf16[256,512]{1,0:T(8,128)(2,1)S(1)} %collective-permute-done.1.refs_1_.refs_0_, bf16[256,128]{1,0:T(8,128)(2,1)S(1)} %collective-permute-done.refs_2_, bf16[256,128]{1,0:T(8,128)(2,1)S(1)} %collective-permute-done.3.refs_3_, ...), custom_call_target="tpu_custom_call" | custom-call | flops 2147483648 | bytes 262144 | tf_op jit(solution)/shard_map/attend/pallas_call | solution.py:311
  41.3 0.0 collective-permute-done.5
  41.4 0.0 collective-permute-done.6
  41.4 1.6 %collective-permute-start.8 = (bf16[512,128]{1,0:T(8,128)(2,1)S(1)}, bf16[512,128]{1,0:T(8,128)(2,1)S(1)}, u32[]{:S(2)}, u32[]{:S(2)}) collective-permute-start(bf16[512,128]{1,0:T(8,128)(2,1)S(1)} %collective-permute-done.5), channel_id=1, source_target_pairs={{0,2},{1,3},{2,0},{3,1},{4,6},{5,7},{6,4},{7,5},{8,10},{9,11},{10,... | collective-permute-start | bytes 393224 | tf_op jit(solution)/shard_map/ppermute | solution.py:254
  43.0 1.0 %collective-permute-start.9 = (bf16[1024,128]{1,0:T(8,128)(2,1)S(1)}, bf16[1024,128]{1,0:T(8,128)(2,1)S(1)}, u32[]{:S(2)}, u32[]{:S(2)}) collective-permute-start(bf16[1024,128]{1,0:T(8,128)(2,1)S(1)} %constant_dynamic-update-slice_fusion.2.refs_2_), channel_id=1, source_target_pairs={{0,1},{1,0},{2,3},{3,2},{4,5},{5,4},{6,7},{7,6},{8,9},{9,8},{10,11... | collective-permute-start | bytes 786440 | tf_op jit(solution)/shard_map/ppermute | solution.py:254
  43.9 0.3 collective-permute-start.10
  44.2 0.0 collective-permute-done.7.refs_3_
  44.2 3.5 %attend.10.refs_4_ = f32[4,512,128]{2,1,0:T(8,128)S(1)} custom-call(bf16[256,512]{1,0:T(8,128)(2,1)S(1)} %get-tuple-element.29.refs_0_, bf16[256,512]{1,0:T(8,128)(2,1)S(1)} %collective-permute-done.1.refs_1_.refs_0_, bf16[1024,128]{1,0:T(8,128)(2,1)S(1)} %constant_dynamic-update-slice_fusion.2.refs_2_, bf16[512,128]{1,0:T(8,128)(2,1)S(1)} %collective-permute-done.7.refs_3_, ...), custom_call_target="tpu_custom_call" | custom-call | flops 3221225472 | bytes 393216 | tf_op jit(solution)/shard_map/attend/pallas_call | solution.py:311
  47.7 0.0 collective-permute-done.8.refs_2_
  47.7 0.4 collective-permute-start.11
  48.1 0.0 collective-permute-done.9.refs_3_
  48.1 3.7 %attend.11.refs_3_.refs_6_ = f32[4,512,128]{2,1,0:T(8,128)S(1)} custom-call(bf16[256,512]{1,0:T(8,128)(2,1)S(1)} %get-tuple-element.29.refs_0_, bf16[256,512]{1,0:T(8,128)(2,1)S(1)} %collective-permute-done.1.refs_1_.refs_0_, bf16[512,128]{1,0:T(8,128)(2,1)S(1)} %collective-permute-done.8.refs_2_, bf16[1024,128]{1,0:T(8,128)(2,1)S(1)} %collective-permute-done.9.refs_3_, ...), custom_call_target="tpu_custom_call" | custom-call | flops 3221225472 | bytes 393216 | tf_op jit(solution)/shard_map/attend/pallas_call | solution.py:311
  51.8 0.0 collective-permute-done.10.refs_1_
  51.8 0.8 collective-permute-start.12
  52.7 0.6 collective-permute-start.13
  53.3 0.0 collective-permute-done.11.refs_2_
  53.3 1.8 %attend.12.refs_3_ = f32[4,256,128]{2,1,0:T(8,128)S(1)} custom-call(bf16[256,512]{1,0:T(8,128)(2,1)S(1)} %collective-permute-done.1.refs_1_.refs_0_, bf16[1024,128]{1,0:T(8,128)(2,1)S(1)} %collective-permute-done.10.refs_1_, bf16[512,128]{1,0:T(8,128)(2,1)S(1)} %collective-permute-done.11.refs_2_, f32[4,512,128]{2,1,0:T(8,128)S(1)} %attend.11.refs_3_.refs_6_), custom_call_target="tpu_custom_call" | custom-call | flops 1610612736 | bytes 393216 | tf_op jit(solution)/shard_map/attend/pallas_call | solution.py:311
  55.1 2.7 %collective-permute-done.13.refs_4_.refs_2_ = bf16[512,128]{1,0:T(8,128)(2,1)S(1)} collective-permute-done((bf16[512,128]{1,0:T(8,128)(2,1)S(1)}, bf16[512,128]{1,0:T(8,128)(2,1)S(1)}, u32[]{:S(2)}, u32[]{:S(2)}) %collective-permute-start.13) | collective-permute-done | bytes 131104 | tf_op jit(solution)/shard_map/ppermute | solution.py:254
  57.8 0.0 collective-permute-done.12.refs_3_.refs_1_
  57.8 0.8 collective-permute-start.14
  58.6 1.8 %attend.14.refs_2_ = f32[4,256,128]{2,1,0:T(8,128)S(1)} custom-call(bf16[256,512]{1,0:T(8,128)(2,1)S(1)} %collective-permute-done.1.refs_1_.refs_0_, bf16[1024,128]{1,0:T(8,128)(2,1)S(1)} %collective-permute-done.12.refs_3_.refs_1_, bf16[512,128]{1,0:T(8,128)(2,1)S(1)} %collective-permute-done.13.refs_4_.refs_2_, f32[4,256,128]{2,1,0:T(8,128)S(1)} %attend.12.refs_3_), custom_call_target="tpu_custom_call" | custom-call | flops 1610612736 | bytes 393216 | tf_op jit(solution)/shard_map/attend/pallas_call | solution.py:311
  60.4 0.0 collective-permute-done.14.refs_5_.refs_1_
  60.5 1.1 %attend.15 = bf16[256,256]{1,0:T(8,128)(2,1)S(1)} custom-call(bf16[256,512]{1,0:T(8,128)(2,1)S(1)} %collective-permute-done.1.refs_1_.refs_0_, bf16[512,128]{1,0:T(8,128)(2,1)S(1)} %collective-permute-done.14.refs_5_.refs_1_, f32[4,256,128]{2,1,0:T(8,128)S(1)} %attend.14.refs_2_), custom_call_target="tpu_custom_call" | custom-call | flops 536870912 | bytes 131072 | tf_op jit(solution)/shard_map/attend/pallas_call | solution.py:311
  61.6 0.0 copy-start.2
  61.6 0.0 copy-start.3
  61.6 0.0 copy-start.4
  61.6 0.0 copy-start.11
  61.7 0.8 collective-permute-start.15
  62.4 4.2 %attend.13.mine_ref = bf16[256,256]{1,0:T(8,128)(2,1)S(1)} custom-call(bf16[256,512]{1,0:T(8,128)(2,1)S(1)} %get-tuple-element.29.refs_0_, bf16[1024,128]{1,0:T(8,128)(2,1)S(1)} %collective-permute-done.10.refs_1_, bf16[512,128]{1,0:T(8,128)(2,1)S(1)} %collective-permute-done.11.refs_2_, bf16[1024,128]{1,0:T(8,128)(2,1)S(1)} %collective-permute-done.12.refs_3_.refs_1_, ...), custom_call_target="tpu_custom_call" | custom-call | flops 3758096384 | bytes 917504 | tf_op jit(solution)/shard_map/attend/pallas_call | solution.py:311
  66.6 0.3 collective-permute-done.15.other_ref
  66.9 0.0 copy-start.13
  66.9 0.0 copy-start.1
  66.9 0.0 copy-start.5
  66.9 0.0 copy-start.6
  66.9 0.0 copy-start.12
  66.9 2.8 %post.1 = bf16[512,512]{1,0:T(8,128)(2,1)} custom-call(s32[1]{0:T(128)S(6)} %select_n.21.group_ref, bf16[256,256]{1,0:T(8,128)(2,1)S(1)} %attend.13.mine_ref, bf16[256,256]{1,0:T(8,128)(2,1)S(1)} %collective-permute-done.15.other_ref, f32[256,512]{1,0:T(8,128)S(1)} %get-tuple-element.45.pooled_ref, bf16[256,512]{1,0:T(8,128)(2,1)S(1)} %get-tuple-element.46.member_ref, ...), custom_call_target="tpu_custom_call" | custom-call | tf_op jit(solution)/shard_map/post/pallas_call | solution.py:362
  69.7 3.0 %all-to-all-start.1 = ((bf16[32,16,512]{2,1,0:T(8,128)(2,1)}), bf16[32,16,512]{2,1,0:T(8,128)(2,1)S(1)}, u32[]{:S(2)}, u32[]{:S(2)}) async-start(bf16[32,16,512]{2,1,0:T(8,128)(2,1)} %bitcast.4), calls=%async_computation.1 | async-start | bytes 1048576 | tf_op jit(solution)/shard_map/all_to_all | solution.py:257
  72.8 0.1 copy.15.live_ref
  72.9 15.2 %all-to-all-done.1 = bf16[32,16,512]{2,1,0:T(8,128)(2,1)S(1)} async-done(((bf16[32,16,512]{2,1,0:T(8,128)(2,1)}), bf16[32,16,512]{2,1,0:T(8,128)(2,1)S(1)}, u32[]{:S(2)}, u32[]{:S(2)}) %all-to-all-start.1) | async-done | bytes 524320 | tf_op jit(solution)/shard_map/all_to_all | solution.py:257
  88.2 1.8 %decode.1 = bf16[512,512]{1,0:T(8,128)(2,1)} custom-call(bf16[512,512]{1,0:T(8,128)(2,1)S(1)} %bitcast.9, bf16[512,512]{1,0:T(8,128)(2,1)S(1)} %copy-done.1, f32[512,1]{1,0:T(8,128)S(1)} %copy.15.live_ref, f32[1,512]{1,0:T(1,128)S(1)} %bitcast.12, bf16[512,512]{1,0:T(8,128)(2,1)S(1)} %copy-done.5, bf16[512,512]{1,0:T(8,128)(2,1)S(1)} %copy-done.6), custom_call_target="tpu_custom_call" | custom-call | tf_op jit(solution)/shard_map/decode/pallas_call | solution.py:372
  (25 shorter events, 0.1 us)
Async XLA Ops:
  0.0 26.5 %copy-start.10 = (f32[512]{0:T(512)S(1)}, f32[512]{0:T(512)}, u32[]{:S(2)}) copy-start(f32[512]{0:T(512)} %param.21) | copy-start | bytes 6148
  0.0 27.6 %copy-start.14 = (f32[8]{0:T(128)S(1)}, f32[8]{0:T(128)}, u32[]{:S(2)}) copy-start(f32[8]{0:T(128)} %param.20) | copy-start | bytes 100
  0.7 1.0 %copy-start = (bf16[512,512]{1,0:T(8,128)(2,1)S(1)}, bf16[512,512]{1,0:T(8,128)(2,1)}, u32[]{:S(2)}) copy-start(bf16[512,512]{1,0:T(8,128)(2,1)} %sensors_ref.3) | copy-start | bytes 1572868
  1.8 24.7 %copy-start.8 = (bf16[512,128]{1,0:T(8,128)(2,1)S(1)}, bf16[512,128]{1,0:T(8,128)(2,1)}, u32[]{:S(2)}) copy-start(bf16[512,128]{1,0:T(8,128)(2,1)} %w_key_ref.1) | copy-start | bytes 393220
  1.8 24.7 %copy-start.9 = (bf16[512,128]{1,0:T(8,128)(2,1)S(1)}, bf16[512,128]{1,0:T(8,128)(2,1)}, u32[]{:S(2)}) copy-start(bf16[512,128]{1,0:T(8,128)(2,1)} %w_value_ref.1) | copy-start | bytes 393220
  1.8 27.2 %copy-start.7 = (bf16[512,512]{1,0:T(8,128)(2,1)S(1)}, bf16[512,512]{1,0:T(8,128)(2,1)}, u32[]{:S(2)}) copy-start(bf16[512,512]{1,0:T(8,128)(2,1)} %w_query_ref.1) | copy-start | bytes 1572868
  2.7 23.8 %all-to-all-start = ((bf16[32,72,128]{2,1,0:T(8,128)(2,1)}), bf16[32,72,128]{2,1,0:T(8,128)(2,1)S(1)}, u32[]{:S(2)}, u32[]{:S(2)}) async-start(bf16[32,72,128]{2,1,0:T(8,128)(2,1)} %pack.1), calls=%async_computation | async-start | bytes 1179648 | tf_op jit(solution)/shard_map/all_to_all | solution.py:257
  27.5 1.4 %collective-permute-start = (bf16[256,128]{1,0:T(8,128)(2,1)S(1)}, bf16[256,128]{1,0:T(8,128)(2,1)S(1)}, u32[]{:S(2)}, u32[]{:S(2)}) collective-permute-start(bf16[256,128]{1,0:T(8,128)(2,1)S(1)} %get-tuple-element.26), channel_id=1, source_target_pairs={{0,1},{1,0},{2,3},{3,2},{4,5},{5,4},{6,7},{7,6},{8,9},{9,8},{10,11... | collective-permute-start | bytes 196616 | tf_op jit(solution)/shard_map/ppermute | solution.py:254
  27.7 3.1 %collective-permute-start.2 = (bf16[256,128]{1,0:T(8,128)(2,1)S(1)}, bf16[256,128]{1,0:T(8,128)(2,1)S(1)}, u32[]{:S(2)}, u32[]{:S(2)}) collective-permute-start(bf16[256,128]{1,0:T(8,128)(2,1)S(1)} %get-tuple-element.32), channel_id=1, source_target_pairs={{0,8},{1,9},{2,10},{3,11},{4,12},{5,13},{6,14},{7,15},{8,0},{9,1},... | collective-permute-start | bytes 196616 | tf_op jit(solution)/shard_map/ppermute | solution.py:254
  29.7 7.8 %collective-permute-start.1 = (bf16[256,512]{1,0:T(8,128)(2,1)S(1)}, bf16[256,512]{1,0:T(8,128)(2,1)S(1)}, u32[]{:S(2)}, u32[]{:S(2)}) collective-permute-start(bf16[256,512]{1,0:T(8,128)(2,1)S(1)} %get-tuple-element.30), channel_id=1, source_target_pairs={{0,8},{1,9},{2,10},{3,11},{4,12},{5,13},{6,14},{7,15},{8,0},{9,1},... | collective-permute-start | bytes 786440 | tf_op jit(solution)/shard_map/ppermute | solution.py:254
  30.9 5.6 %collective-permute-start.4 = (bf16[512,128]{1,0:T(8,128)(2,1)S(1)}, bf16[512,128]{1,0:T(8,128)(2,1)S(1)}, u32[]{:S(2)}, u32[]{:S(2)}) collective-permute-start(bf16[512,128]{1,0:T(8,128)(2,1)S(1)} %constant_dynamic-update-slice_fusion.refs_2_), channel_id=1, source_target_pairs={{0,16},{1,17},{2,18},{3,19},{4,20},{5,21},{6,22},{7,23},{8,24},{9,... | collective-permute-start | bytes 393224 | tf_op jit(solution)/shard_map/ppermute | solution.py:254
  32.2 9.2 %collective-permute-start.5 = (bf16[512,128]{1,0:T(8,128)(2,1)S(1)}, bf16[512,128]{1,0:T(8,128)(2,1)S(1)}, u32[]{:S(2)}, u32[]{:S(2)}) collective-permute-start(bf16[512,128]{1,0:T(8,128)(2,1)S(1)} %constant_dynamic-update-slice_fusion.refs_2_), channel_id=1, source_target_pairs={{0,4},{1,5},{2,6},{3,7},{4,0},{5,1},{6,2},{7,3},{8,12},{9,13},{10,... | collective-permute-start | bytes 393224 | tf_op jit(solution)/shard_map/ppermute | solution.py:254
  33.6 7.8 %collective-permute-start.6 = (bf16[512,128]{1,0:T(8,128)(2,1)S(1)}, bf16[512,128]{1,0:T(8,128)(2,1)S(1)}, u32[]{:S(2)}, u32[]{:S(2)}) collective-permute-start(bf16[512,128]{1,0:T(8,128)(2,1)S(1)} %constant_dynamic-update-slice_fusion.refs_2_), channel_id=1, source_target_pairs={{0,2},{1,3},{2,0},{3,1},{4,6},{5,7},{6,4},{7,5},{8,10},{9,11},{10,... | collective-permute-start | bytes 393224 | tf_op jit(solution)/shard_map/ppermute | solution.py:254
  34.8 4.1 %collective-permute-start.3 = (bf16[256,128]{1,0:T(8,128)(2,1)S(1)}, bf16[256,128]{1,0:T(8,128)(2,1)S(1)}, u32[]{:S(2)}, u32[]{:S(2)}) collective-permute-start(bf16[256,128]{1,0:T(8,128)(2,1)S(1)} %collective-permute-done.2), channel_id=1, source_target_pairs={{0,1},{1,0},{2,3},{3,2},{4,5},{5,4},{6,7},{7,6},{8,9},{9,8},{10,11... | collective-permute-start | bytes 196616 | tf_op jit(solution)/shard_map/ppermute | solution.py:254
  36.5 7.7 %collective-permute-start.7 = (bf16[512,128]{1,0:T(8,128)(2,1)S(1)}, bf16[512,128]{1,0:T(8,128)(2,1)S(1)}, u32[]{:S(2)}, u32[]{:S(2)}) collective-permute-start(bf16[512,128]{1,0:T(8,128)(2,1)S(1)} %collective-permute-done.4.refs_4_), channel_id=1, source_target_pairs={{0,1},{1,0},{2,3},{3,2},{4,5},{5,4},{6,7},{7,6},{8,9},{9,8},{10,11... | collective-permute-start | bytes 393224 | tf_op jit(solution)/shard_map/ppermute | solution.py:254
  41.4 6.3 %collective-permute-start.8 = (bf16[512,128]{1,0:T(8,128)(2,1)S(1)}, bf16[512,128]{1,0:T(8,128)(2,1)S(1)}, u32[]{:S(2)}, u32[]{:S(2)}) collective-permute-start(bf16[512,128]{1,0:T(8,128)(2,1)S(1)} %collective-permute-done.5), channel_id=1, source_target_pairs={{0,2},{1,3},{2,0},{3,1},{4,6},{5,7},{6,4},{7,5},{8,10},{9,11},{10,... | collective-permute-start | bytes 393224 | tf_op jit(solution)/shard_map/ppermute | solution.py:254
  43.0 5.2 %collective-permute-start.9 = (bf16[1024,128]{1,0:T(8,128)(2,1)S(1)}, bf16[1024,128]{1,0:T(8,128)(2,1)S(1)}, u32[]{:S(2)}, u32[]{:S(2)}) collective-permute-start(bf16[1024,128]{1,0:T(8,128)(2,1)S(1)} %constant_dynamic-update-slice_fusion.2.refs_2_), channel_id=1, source_target_pairs={{0,1},{1,0},{2,3},{3,2},{4,5},{5,4},{6,7},{7,6},{8,9},{9,8},{10,11... | collective-permute-start | bytes 786440 | tf_op jit(solution)/shard_map/ppermute | solution.py:254
  43.9 7.9 %collective-permute-start.10 = (bf16[1024,128]{1,0:T(8,128)(2,1)S(1)}, bf16[1024,128]{1,0:T(8,128)(2,1)S(1)}, u32[]{:S(2)}, u32[]{:S(2)}) collective-permute-start(bf16[1024,128]{1,0:T(8,128)(2,1)S(1)} %constant_dynamic-update-slice_fusion.2.refs_2_), channel_id=1, source_target_pairs={{0,16},{1,17},{2,18},{3,19},{4,20},{5,21},{6,22},{7,23},{8,24},{9,... | collective-permute-start | bytes 786440 | tf_op jit(solution)/shard_map/ppermute | solution.py:254
  47.7 5.6 %collective-permute-start.11 = (bf16[512,128]{1,0:T(8,128)(2,1)S(1)}, bf16[512,128]{1,0:T(8,128)(2,1)S(1)}, u32[]{:S(2)}, u32[]{:S(2)}) collective-permute-start(bf16[512,128]{1,0:T(8,128)(2,1)S(1)} %collective-permute-done.8.refs_2_), channel_id=1, source_target_pairs={{0,1},{1,0},{2,3},{3,2},{4,5},{5,4},{6,7},{7,6},{8,9},{9,8},{10,11... | collective-permute-start | bytes 393224 | tf_op jit(solution)/shard_map/ppermute | solution.py:254
  51.8 6.0 %collective-permute-start.12 = (bf16[1024,128]{1,0:T(8,128)(2,1)S(1)}, bf16[1024,128]{1,0:T(8,128)(2,1)S(1)}, u32[]{:S(2)}, u32[]{:S(2)}) collective-permute-start(bf16[1024,128]{1,0:T(8,128)(2,1)S(1)} %collective-permute-done.10.refs_1_), channel_id=1, source_target_pairs={{0,1},{1,0},{2,3},{3,2},{4,5},{5,4},{6,7},{7,6},{8,9},{9,8},{10,11... | collective-permute-start | bytes 786440 | tf_op jit(solution)/shard_map/ppermute | solution.py:254
  52.7 5.1 %collective-permute-start.13 = (bf16[512,128]{1,0:T(8,128)(2,1)S(1)}, bf16[512,128]{1,0:T(8,128)(2,1)S(1)}, u32[]{:S(2)}, u32[]{:S(2)}) collective-permute-start(bf16[512,128]{1,0:T(8,128)(2,1)S(1)} %collective-permute-done.8.refs_2_), channel_id=1, source_target_pairs={{0,16},{1,17},{2,18},{3,19},{4,20},{5,21},{6,22},{7,23},{8,24},{9,... | collective-permute-start | bytes 393224 | tf_op jit(solution)/shard_map/ppermute | solution.py:254
  57.8 2.6 %collective-permute-start.14 = (bf16[512,128]{1,0:T(8,128)(2,1)S(1)}, bf16[512,128]{1,0:T(8,128)(2,1)S(1)}, u32[]{:S(2)}, u32[]{:S(2)}) collective-permute-start(bf16[512,128]{1,0:T(8,128)(2,1)S(1)} %collective-permute-done.13.refs_4_.refs_2_), channel_id=1, source_target_pairs={{0,1},{1,0},{2,3},{3,2},{4,5},{5,4},{6,7},{7,6},{8,9},{9,8},{10,11... | collective-permute-start | bytes 393224 | tf_op jit(solution)/shard_map/ppermute | solution.py:254
  61.6 5.3 %copy-start.2 = (bf16[512,2048]{1,0:T(8,128)(2,1)S(1)}, bf16[512,2048]{1,0:T(8,128)(2,1)}, u32[]{:S(2)}) copy-start(bf16[512,2048]{1,0:T(8,128)(2,1)} %w_inner_ref.1) | copy-start | bytes 6291460
  61.6 5.2 %copy-start.3 = (bf16[2048,512]{1,0:T(8,128)(2,1)S(1)}, bf16[2048,512]{1,0:T(8,128)(2,1)}, u32[]{:S(2)}) copy-start(bf16[2048,512]{1,0:T(8,128)(2,1)} %w_outer_ref.1) | copy-start | bytes 6291460
  61.6 5.2 %copy-start.4 = (bf16[512,512]{1,0:T(8,128)(2,1)S(1)}, bf16[512,512]{1,0:T(8,128)(2,1)}, u32[]{:S(2)}) copy-start(bf16[512,512]{1,0:T(8,128)(2,1)} %w_out_ref.2) | copy-start | bytes 1572868
  61.6 5.2 %copy-start.11 = (f32[512]{0:T(512)S(1)}, f32[512]{0:T(512)}, u32[]{:S(2)}) copy-start(f32[512]{0:T(512)} %param.24) | copy-start | bytes 6148
  61.7 5.2 %collective-permute-start.15 = (bf16[256,256]{1,0:T(8,128)(2,1)S(1)}, bf16[256,256]{1,0:T(8,128)(2,1)S(1)}, u32[]{:S(2)}, u32[]{:S(2)}) collective-permute-start(bf16[256,256]{1,0:T(8,128)(2,1)S(1)} %attend.15), channel_id=1, source_target_pairs={{0,8},{1,9},{2,10},{3,11},{4,12},{5,13},{6,14},{7,15},{8,0},{9,1},... | collective-permute-start | bytes 393224 | tf_op jit(solution)/shard_map/ppermute | solution.py:254
  66.9 5.9 %copy-start.13 = (s32[512]{0:T(512)S(1)}, s32[512]{0:T(512)}, u32[]{:S(2)}) copy-start(s32[512]{0:T(512)} %param.15) | copy-start | bytes 6148
  66.9 21.3 %copy-start.1 = (bf16[512,512]{1,0:T(8,128)(2,1)S(1)}, bf16[512,512]{1,0:T(8,128)(2,1)}, u32[]{:S(2)}) copy-start(bf16[512,512]{1,0:T(8,128)(2,1)} %sensors_ref.3) | copy-start | bytes 1572868
  66.9 21.2 %copy-start.5 = (bf16[512,512]{1,0:T(8,128)(2,1)S(1)}, bf16[512,512]{1,0:T(8,128)(2,1)}, u32[]{:S(2)}) copy-start(bf16[512,512]{1,0:T(8,128)(2,1)} %w_in_ref.1) | copy-start | bytes 1572868
  66.9 21.2 %copy-start.6 = (bf16[512,512]{1,0:T(8,128)(2,1)S(1)}, bf16[512,512]{1,0:T(8,128)(2,1)}, u32[]{:S(2)}) copy-start(bf16[512,512]{1,0:T(8,128)(2,1)} %w_out_ref.3) | copy-start | bytes 1572868
  66.9 21.2 %copy-start.12 = (f32[512]{0:T(512)S(1)}, f32[512]{0:T(512)}, u32[]{:S(2)}) copy-start(f32[512]{0:T(512)} %param.25) | copy-start | bytes 6148
  69.7 18.4 %all-to-all-start.1 = ((bf16[32,16,512]{2,1,0:T(8,128)(2,1)}), bf16[32,16,512]{2,1,0:T(8,128)(2,1)S(1)}, u32[]{:S(2)}, u32[]{:S(2)}) async-start(bf16[32,16,512]{2,1,0:T(8,128)(2,1)} %bitcast.4), calls=%async_computation.1 | async-start | bytes 1048576 | tf_op jit(solution)/shard_map/all_to_all | solution.py:257

commit v9 on v6

--- a/solution.py
+++ b/solution.py
@@ -28,6 +28,12 @@
 
 def mm(a, b):
     return jnp.dot(a, b, preferred_element_type=F32)
+
+
+def gelu(values):
+    half = 0.5 * values
+    slope = math.sqrt(2.0 / math.pi)
+    return half + half * jnp.tanh(values * (slope + slope * 0.044715 * values * values))
 
 
 def rms(values):
@@ -189,7 +195,7 @@
     block = math.gcd(inner_width, 512)
     for j in range(inner_width // block):
         cols = slice(j * block, (j + 1) * block)
-        inner_ref[:, cols] = jax.nn.gelu(mm(mlp_in, w_inner_ref[:, cols])).astype(BF16)
+        inner_ref[:, cols] = gelu(mm(mlp_in, w_inner_ref[:, cols])).astype(BF16)
     region_out = (hidden + mm(inner_ref[...], w_outer_ref[...])).astype(BF16)
     slots = member_ref.shape[1]
     block = math.gcd(slots, 512)
@@ -208,7 +214,7 @@
         back = back_ref[begin * tile : (begin + step) * tile, :]
         total = back.astype(F32) + sensors.astype(F32)
         dec_in = (rms(total) * gain_ref[...]).astype(BF16)
-        hidden = jax.nn.gelu(mm(dec_in, w_in_ref[...])).astype(BF16)
+        hidden = gelu(mm(dec_in, w_in_ref[...])).astype(BF16)
         result = mm(hidden, w_out_ref[...])
         for i, rows in enumerate(tiles):
             here = result[i * tile : (i + 1) * tile, :]
@@ -310,7 +316,7 @@
             + [pltpu.VMEM(acc_shape, BF16)],
             compiler_params=PARAMS,
             cost_estimate=pl.CostEstimate(
-                flops=work * 4 * 256, bytes_accessed=keys * 2 * LANES, transcendentals=work
+                flops=work, bytes_accessed=keys * 2 * LANES, transcendentals=0
             ),
             name="attend",
         )(*(slabs[r] for r in row_parts), *parts, *(() if acc is None else (acc,)))
@@ -325,24 +331,14 @@
     a, b = flipped(own, far), flipped(own, near)
     own_one, own_two = flipped(own, one), flipped(own, two)
     acc = attend([own], None)
-    acc, own_one, own_two = hold((acc, own_one, own_two))
-    own_corner = flipped(own_two, one)
-    acc = attend([own_one, own_two], acc)
-    acc, a, b = hold((acc, a, b))
-
+    acc, a, b, own_one, own_two = hold((acc, a, b, own_one, own_two))
     ab, c = jnp.concatenate([a, b], axis=0), flipped(a, near)
-    ab_one, ab_two = flipped(ab, one), flipped(ab, two)
-    acc = attend([ab], acc)
-    acc, c, own_corner = hold((acc, c, own_corner))
-
-    c_one, c_two = flipped(c, one), flipped(c, two)
-    acc = attend([c, own_corner], acc)
-    acc, ab_one, ab_two = hold((acc, ab_one, ab_two))
-
-    ab_corner = flipped(ab_one, two)
-    acc = attend([ab_one, ab_two], acc)
+    ab_one, ab_two, own_corner = flipped(ab, one), flipped(ab, two), flipped(own_two, one)
+    acc = attend([ab, own_one, own_two], acc)
+    acc, c, ab_one, ab_two = hold((acc, c, ab_one, ab_two))
+    c_one, c_two, ab_corner = flipped(c, one), flipped(c, two), flipped(ab_one, two)
+    acc = attend([c, ab_one, ab_two, own_corner], acc)
     acc, c_one, c_two = hold((acc, c_one, c_two))
-
     c_corner = flipped(c_two, one)
     acc = attend([c_one, c_two, ab_corner], acc)
 

time: 89.5 us -> 88.8 us (level)
    pallas_call x8 -> x6, Pallas kernels: 20.3 us -> 19.8 us  [attend(): pl.pallas_call(functools.partial(attend_kernel, len(parts), row_parts, ac...]
  transfers between devices with their start and end apart: 16 -> 16, of which waited for: 6 -> 4; matrix products, arithmetic and copies ran while one was open for 0% -> 0% of each run, Pallas kernels for 22% -> 22%
where the time goes in v9:
time: 88.8 us; the launch traced here: 88.5 us
  Pallas kernels  26.3 us (30%)
  blocking collectives  23.6 us (27%)
  waiting for transfers between devices  19.9 us (22%)
  starting transfers between devices  16.3 us (18%)
  local copies, waits for them, and re-layouts  2.16 us (2%)
    all_to_all x1, blocking collectives, exchanged(): lax.all_to_all(value, AXIS, split_axis=0, concat_axis=0, tiled=True, axis...  23.6 us
    pallas_call x6, Pallas kernels, attend(): pl.pallas_call(functools.partial(attend_kernel, len(parts), row_parts, ac...  19.8 us
    all_to_all x1, waiting for transfers between devices, exchanged(): lax.all_to_all(value, AXIS, split_axis=0, concat_axis=0, tiled=True, axis...  15.1 us
    ppermute x15, starting transfers between devices, flipped(): return lax.ppermute(value, AXIS, [(i, i ^ mask) for i in range(devices)])  13 us
    ppermute x15, waiting for transfers between devices, flipped(): return lax.ppermute(value, AXIS, [(i, i ^ mask) for i in range(devices)])  4.76 us
    all_to_all x1, starting transfers between devices, exchanged(): lax.all_to_all(value, AXIS, split_axis=0, concat_axis=0, tiled=True, axis...  3.27 us
    pallas_call x1, Pallas kernels, local(): pl.pallas_call(post_kernel, out_shape=jax.ShapeDtypeStruct((sen_dev, widt...  2.8 us
    unnamed x34, local copies, waits for them, and re-layouts  1.84 us
  transfers between devices with their start and end apart: 16, of which 4 were waited for; matrix products, arithmetic and copies ran while one was open for 0% of the time, Pallas kernels for 22%

profile of v9, /device:TPU:1, one launch (start us, length us, event | category | flops | bytes accessed | tf_op | source)
XLA Modules:
  0.0 88.5 jit_solution(1835209514232015063)
XLA Ops:
  0.0 1.1 %copy-done = bf16[512,512]{1,0:T(8,128)(2,1)S(1)} copy-done((bf16[512,512]{1,0:T(8,128)(2,1)S(1)}, bf16[512,512]{1,0:T(8,128)(2,1)}, u32[]{:S(2)}) %copy-start) | copy-done | bytes 524312
  1.1 0.7 copy-done.10
  1.8 0.1 pack.1
  1.9 23.6 %all_to_all.10.got_ref = bf16[32,72,128]{2,1,0:T(8,128)(2,1)S(1)} all-to-all(bf16[32,72,128]{2,1,0:T(8,128)(2,1)S(1)} %pack.1), channel_id=1, replica_groups={{0,2,4,6,1,3,5,7,8,10,12,14,9,11,13,15,16,18,20,22,17,19,21,23,24,26,28..., dimensions={0} | all-to-all | bytes 1179648 | tf_op jit(solution)/shard_map/all_to_all | solution.py:255
  25.4 0.0 copy-done.12
  25.4 0.0 copy-done.8
  25.5 1.0 %pool.1 = (f32[256,512]{1,0:T(8,128)S(1)}, bf16[256,512]{1,0:T(8,128)(2,1)S(1)}, bf16[256,512]{1,0:T(8,128)(2,1)S(1)}, bf16[256,128]{1,0:T(8,128)(2,1)S(1)}, bf16[256,128]{1,0:T(8,128)(2,1)S(1)}) custom-call(s32[1]{0:T(128)S(6)} %rem.46.core_ref, bf16[32,72,128]{2,1,0:T(8,128)(2,1)S(1)} %all_to_all.10.got_ref, bf16[512,128]{1,0:T(8,128)(2,1)S(1)} %copy-done.8, ...), custom_call_target="tpu_custom_call" | custom-call | tf_op jit(solution)/shard_map/pool/pallas_call | solution.py:273
  26.5 0.1 collective-permute-start
  26.6 0.0 copy-done.15
  26.6 0.1 broadcast_in_dim.3
  26.7 0.1 reshape_reshape.3.scale_ref
  26.7 0.8 query.1
  27.5 0.3 collective-permute-done
  27.8 0.3 collective-permute-start.1
  28.1 0.9 %collective-permute-start.2 = (bf16[512,128]{1,0:T(8,128)(2,1)S(1)}, bf16[512,128]{1,0:T(8,128)(2,1)S(1)}, u32[]{:S(2)}, u32[]{:S(2)}) collective-permute-start(bf16[512,128]{1,0:T(8,128)(2,1)S(1)} %constant_dynamic-update-slice_fusion.refs_2_), channel_id=1, source_target_pairs={{0,4},{1,5},{2,6},{3,7},{4,0},{5,1},{6,2},{7,3},{8,12},{9,13},{10,... | collective-permute-start | bytes 393224 | tf_op jit(solution)/shard_map/ppermute | solution.py:252
  29.1 1.0 %collective-permute-start.3 = (bf16[512,128]{1,0:T(8,128)(2,1)S(1)}, bf16[512,128]{1,0:T(8,128)(2,1)S(1)}, u32[]{:S(2)}, u32[]{:S(2)}) collective-permute-start(bf16[512,128]{1,0:T(8,128)(2,1)S(1)} %constant_dynamic-update-slice_fusion.refs_2_), channel_id=1, source_target_pairs={{0,2},{1,3},{2,0},{3,1},{4,6},{5,7},{6,4},{7,5},{8,10},{9,11},{10,... | collective-permute-start | bytes 393224 | tf_op jit(solution)/shard_map/ppermute | solution.py:252
  30.0 1.2 %collective-permute-start.4 = (bf16[512,128]{1,0:T(8,128)(2,1)S(1)}, bf16[512,128]{1,0:T(8,128)(2,1)S(1)}, u32[]{:S(2)}, u32[]{:S(2)}) collective-permute-start(bf16[512,128]{1,0:T(8,128)(2,1)S(1)} %constant_dynamic-update-slice_fusion.refs_2_), channel_id=1, source_target_pairs={{0,8},{1,9},{2,10},{3,11},{4,12},{5,13},{6,14},{7,15},{8,0},{9,1},... | collective-permute-start | bytes 393224 | tf_op jit(solution)/shard_map/ppermute | solution.py:252
  31.2 0.3 collective-permute-start.5
  31.5 0.0 collective-permute-done.1.refs_1_.refs_0_
  31.5 1.4 %attend.6.refs_5_ = f32[4,512,128]{2,1,0:T(8,128)S(1)} custom-call(bf16[256,512]{1,0:T(8,128)(2,1)S(1)} %get-tuple-element.33.refs_0_, bf16[256,512]{1,0:T(8,128)(2,1)S(1)} %collective-permute-done.1.refs_1_.refs_0_, bf16[512,128]{1,0:T(8,128)(2,1)S(1)} %constant_dynamic-update-slice_fusion.refs_2_), custom_call_target="tpu_custom_call" | custom-call | flops 1048576 | bytes 131072 | tf_op jit(solution)/shard_map/attend/pallas_call | solution.py:309
  32.9 3.9 %collective-permute-done.2 = bf16[512,128]{1,0:T(8,128)(2,1)S(1)} collective-permute-done((bf16[512,128]{1,0:T(8,128)(2,1)S(1)}, bf16[512,128]{1,0:T(8,128)(2,1)S(1)}, u32[]{:S(2)}, u32[]{:S(2)}) %collective-permute-start.2) | collective-permute-done | bytes 131104 | tf_op jit(solution)/shard_map/ppermute | solution.py:252
  36.8 0.0 collective-permute-done.3
  36.8 0.0 collective-permute-done.4.refs_3_
  36.8 0.0 collective-permute-done.5.refs_4_
  36.9 1.3 %collective-permute-start.7 = (bf16[1024,128]{1,0:T(8,128)(2,1)S(1)}, bf16[1024,128]{1,0:T(8,128)(2,1)S(1)}, u32[]{:S(2)}, u32[]{:S(2)}) collective-permute-start(bf16[1024,128]{1,0:T(8,128)(2,1)S(1)} %constant_dynamic-update-slice_fusion.2.refs_2_), channel_id=1, source_target_pairs={{0,8},{1,9},{2,10},{3,11},{4,12},{5,13},{6,14},{7,15},{8,0},{9,1},... | collective-permute-start | bytes 786440 | tf_op jit(solution)/shard_map/ppermute | solution.py:252
  38.2 0.5 collective-permute-start.8
  38.7 0.0 collective-permute-start.6
  38.7 1.4 %collective-permute-start.9 = (bf16[512,128]{1,0:T(8,128)(2,1)S(1)}, bf16[512,128]{1,0:T(8,128)(2,1)S(1)}, u32[]{:S(2)}, u32[]{:S(2)}) collective-permute-start(bf16[512,128]{1,0:T(8,128)(2,1)S(1)} %collective-permute-done.5.refs_4_), channel_id=1, source_target_pairs={{0,8},{1,9},{2,10},{3,11},{4,12},{5,13},{6,14},{7,15},{8,0},{9,1},... | collective-permute-start | bytes 393224 | tf_op jit(solution)/shard_map/ppermute | solution.py:252
  40.0 4.6 %attend.7.refs_6_ = f32[4,512,128]{2,1,0:T(8,128)S(1)} custom-call(bf16[256,512]{1,0:T(8,128)(2,1)S(1)} %get-tuple-element.33.refs_0_, bf16[256,512]{1,0:T(8,128)(2,1)S(1)} %collective-permute-done.1.refs_1_.refs_0_, bf16[1024,128]{1,0:T(8,128)(2,1)S(1)} %constant_dynamic-update-slice_fusion.2.refs_2_, bf16[512,128]{1,0:T(8,128)(2,1)S(1)} %collective-permute-done.4.refs_3_, ...), custom_call_target="tpu_custom_call" | custom-call | flops 4194304 | bytes 524288 | tf_op jit(solution)/shard_map/attend/pallas_call | solution.py:309
  44.6 0.0 collective-permute-done.6.refs_2_
  44.6 0.0 collective-permute-done.7.refs_3_
  44.6 0.5 collective-permute-done.8.refs_4_
  45.2 0.7 collective-permute-start.13
  45.8 1.1 %collective-permute-start.10 = (bf16[512,128]{1,0:T(8,128)(2,1)S(1)}, bf16[512,128]{1,0:T(8,128)(2,1)S(1)}, u32[]{:S(2)}, u32[]{:S(2)}) collective-permute-start(bf16[512,128]{1,0:T(8,128)(2,1)S(1)} %collective-permute-done.6.refs_2_), channel_id=1, source_target_pairs={{0,8},{1,9},{2,10},{3,11},{4,12},{5,13},{6,14},{7,15},{8,0},{9,1},... | collective-permute-start | bytes 393224 | tf_op jit(solution)/shard_map/ppermute | solution.py:252
  47.0 0.0 collective-permute-start.11
  47.0 0.0 collective-permute-done.9.refs_5_
  47.0 7.0 %attend.8.refs_5_ = f32[4,512,128]{2,1,0:T(8,128)S(1)} custom-call(bf16[256,512]{1,0:T(8,128)(2,1)S(1)} %get-tuple-element.33.refs_0_, bf16[256,512]{1,0:T(8,128)(2,1)S(1)} %collective-permute-done.1.refs_1_.refs_0_, bf16[512,128]{1,0:T(8,128)(2,1)S(1)} %collective-permute-done.6.refs_2_, bf16[1024,128]{1,0:T(8,128)(2,1)S(1)} %collective-permute-done.7.refs_3_, ...), custom_call_target="tpu_custom_call" | custom-call | flops 6291456 | bytes 786432 | tf_op jit(solution)/shard_map/attend/pallas_call | solution.py:309
  53.9 0.0 collective-permute-done.10.refs_2_
  53.9 0.0 collective-permute-done.11.refs_3_
  53.9 1.4 %collective-permute-start.12 = (bf16[512,128]{1,0:T(8,128)(2,1)S(1)}, bf16[512,128]{1,0:T(8,128)(2,1)S(1)}, u32[]{:S(2)}, u32[]{:S(2)}) collective-permute-start(bf16[512,128]{1,0:T(8,128)(2,1)S(1)} %collective-permute-done.11.refs_3_), channel_id=1, source_target_pairs={{0,8},{1,9},{2,10},{3,11},{4,12},{5,13},{6,14},{7,15},{8,0},{9,1},... | collective-permute-start | bytes 393224 | tf_op jit(solution)/shard_map/ppermute | solution.py:252
  55.3 0.0 collective-permute-done.13.refs_4_
  55.3 4.6 %attend.9.refs_2_ = f32[4,512,128]{2,1,0:T(8,128)S(1)} custom-call(bf16[256,512]{1,0:T(8,128)(2,1)S(1)} %get-tuple-element.33.refs_0_, bf16[256,512]{1,0:T(8,128)(2,1)S(1)} %collective-permute-done.1.refs_1_.refs_0_, bf16[512,128]{1,0:T(8,128)(2,1)S(1)} %collective-permute-done.10.refs_2_, bf16[512,128]{1,0:T(8,128)(2,1)S(1)} %collective-permute-done.11.refs_3_, ...), custom_call_target="tpu_custom_call" | custom-call | flops 4194304 | bytes 524288 | tf_op jit(solution)/shard_map/attend/pallas_call | solution.py:309
  59.9 0.0 copy-start.2
  59.9 0.0 copy-start.4
  60.0 0.0 copy-start.13
  60.0 0.0 collective-permute-done.12.refs_1_
  60.0 1.1 %attend.11 = bf16[256,256]{1,0:T(8,128)(2,1)S(1)} custom-call(bf16[256,512]{1,0:T(8,128)(2,1)S(1)} %collective-permute-done.1.refs_1_.refs_0_, bf16[512,128]{1,0:T(8,128)(2,1)S(1)} %collective-permute-done.12.refs_1_, f32[4,512,128]{2,1,0:T(8,128)S(1)} %attend.9.refs_2_), custom_call_target="tpu_custom_call" | custom-call | flops 524288 | bytes 131072 | tf_op jit(solution)/shard_map/attend/pallas_call | solution.py:309
  61.1 2.9 %collective-permute-start.14 = (bf16[256,256]{1,0:T(8,128)(2,1)S(1)}, bf16[256,256]{1,0:T(8,128)(2,1)S(1)}, u32[]{:S(2)}, u32[]{:S(2)}) collective-permute-start(bf16[256,256]{1,0:T(8,128)(2,1)S(1)} %attend.11), channel_id=1, source_target_pairs={{0,1},{1,0},{2,3},{3,2},{4,5},{5,4},{6,7},{7,6},{8,9},{9,8},{10,11... | collective-permute-start | bytes 393224 | tf_op jit(solution)/shard_map/ppermute | solution.py:252
  64.0 1.1 %attend.10.mine_ref = bf16[256,256]{1,0:T(8,128)(2,1)S(1)} custom-call(bf16[256,512]{1,0:T(8,128)(2,1)S(1)} %get-tuple-element.33.refs_0_, bf16[512,128]{1,0:T(8,128)(2,1)S(1)} %collective-permute-done.12.refs_1_, f32[4,512,128]{2,1,0:T(8,128)S(1)} %attend.9.refs_2_), custom_call_target="tpu_custom_call" | custom-call | flops 524288 | bytes 131072 | tf_op jit(solution)/shard_map/attend/pallas_call | solution.py:309
  65.2 0.0 collective-permute-done.14.other_ref
  65.2 0.0 copy-done.3
  65.2 0.0 copy-done.2
  65.2 0.0 copy-done.4
  65.2 0.0 copy-done.13
  65.2 0.0 copy-start.11
  65.3 0.0 copy-start.1
  65.3 0.0 copy-start.5
  65.3 0.0 copy-start.6
  65.3 0.0 copy-start.14
  65.3 2.8 %post.1 = bf16[512,512]{1,0:T(8,128)(2,1)} custom-call(s32[1]{0:T(128)S(6)} %rem.46.core_ref, bf16[256,256]{1,0:T(8,128)(2,1)S(1)} %attend.10.mine_ref, bf16[256,256]{1,0:T(8,128)(2,1)S(1)} %collective-permute-done.14.other_ref, f32[256,512]{1,0:T(8,128)S(1)} %get-tuple-element.51.pooled_ref, bf16[256,512]{1,0:T(8,128)(2,1)S(1)} %get-tuple-element.52.member_ref, ...), custom_call_target="tpu_custom_call" | custom-call | tf_op jit(solution)/shard_map/post/pallas_call | solution.py:350
  68.1 3.3 %all-to-all-start.1 = ((bf16[32,16,512]{2,1,0:T(8,128)(2,1)}), bf16[32,16,512]{2,1,0:T(8,128)(2,1)S(1)}, u32[]{:S(2)}, u32[]{:S(2)}) async-start(bf16[32,16,512]{2,1,0:T(8,128)(2,1)} %bitcast.4), calls=%async_computation.1 | async-start | bytes 1048576 | tf_op jit(solution)/shard_map/all_to_all | solution.py:255
  71.4 0.1 copy.15.live_ref
  71.5 15.1 %all-to-all-done.1 = bf16[32,16,512]{2,1,0:T(8,128)(2,1)S(1)} async-done(((bf16[32,16,512]{2,1,0:T(8,128)(2,1)}), bf16[32,16,512]{2,1,0:T(8,128)(2,1)S(1)}, u32[]{:S(2)}, u32[]{:S(2)}) %all-to-all-start.1) | async-done | bytes 524320 | tf_op jit(solution)/shard_map/all_to_all | solution.py:255
  86.7 1.8 %decode.1 = bf16[512,512]{1,0:T(8,128)(2,1)} custom-call(bf16[512,512]{1,0:T(8,128)(2,1)S(1)} %bitcast.8, bf16[512,512]{1,0:T(8,128)(2,1)S(1)} %copy-done.1, f32[512,1]{1,0:T(8,128)S(1)} %copy.15.live_ref, f32[1,512]{1,0:T(1,128)S(1)} %bitcast.12, bf16[512,512]{1,0:T(8,128)(2,1)S(1)} %copy-done.5, bf16[512,512]{1,0:T(8,128)(2,1)S(1)} %copy-done.6), custom_call_target="tpu_custom_call" | custom-call | tf_op jit(solution)/shard_map/decode/pallas_call | solution.py:360
  (21 shorter events, 0.1 us)
Async XLA Ops:
  0.0 25.4 %copy-start.12 = (f32[512]{0:T(512)S(1)}, f32[512]{0:T(512)}, u32[]{:S(2)}) copy-start(f32[512]{0:T(512)} %param.21) | copy-start | bytes 6148
  0.0 26.6 %copy-start.15 = (f32[8]{0:T(128)S(1)}, f32[8]{0:T(128)}, u32[]{:S(2)}) copy-start(f32[8]{0:T(128)} %param.20) | copy-start | bytes 100
  0.0 1.1 %copy-start = (bf16[512,512]{1,0:T(8,128)(2,1)S(1)}, bf16[512,512]{1,0:T(8,128)(2,1)}, u32[]{:S(2)}) copy-start(bf16[512,512]{1,0:T(8,128)(2,1)} %sensors_ref.3) | copy-start | bytes 1572868
  1.1 0.7 copy-start.10
  1.8 23.7 %copy-start.8 = (bf16[512,128]{1,0:T(8,128)(2,1)S(1)}, bf16[512,128]{1,0:T(8,128)(2,1)}, u32[]{:S(2)}) copy-start(bf16[512,128]{1,0:T(8,128)(2,1)} %w_key_ref.1) | copy-start | bytes 393220
  1.8 23.7 %copy-start.9 = (bf16[512,128]{1,0:T(8,128)(2,1)S(1)}, bf16[512,128]{1,0:T(8,128)(2,1)}, u32[]{:S(2)}) copy-start(bf16[512,128]{1,0:T(8,128)(2,1)} %w_value_ref.1) | copy-start | bytes 393220
  1.8 25.0 %copy-start.7 = (bf16[512,512]{1,0:T(8,128)(2,1)S(1)}, bf16[512,512]{1,0:T(8,128)(2,1)}, u32[]{:S(2)}) copy-start(bf16[512,512]{1,0:T(8,128)(2,1)} %w_query_ref.1) | copy-start | bytes 1572868
  26.5 1.3 %collective-permute-start = (bf16[256,128]{1,0:T(8,128)(2,1)S(1)}, bf16[256,128]{1,0:T(8,128)(2,1)S(1)}, u32[]{:S(2)}, u32[]{:S(2)}) collective-permute-start(bf16[256,128]{1,0:T(8,128)(2,1)S(1)} %get-tuple-element.29), channel_id=1, source_target_pairs={{0,1},{1,0},{2,3},{3,2},{4,5},{5,4},{6,7},{7,6},{8,9},{9,8},{10,11... | collective-permute-start | bytes 196616 | tf_op jit(solution)/shard_map/ppermute | solution.py:252
  27.8 3.7 %collective-permute-start.1 = (bf16[256,512]{1,0:T(8,128)(2,1)S(1)}, bf16[256,512]{1,0:T(8,128)(2,1)S(1)}, u32[]{:S(2)}, u32[]{:S(2)}) collective-permute-start(bf16[256,512]{1,0:T(8,128)(2,1)S(1)} %get-tuple-element.34), channel_id=1, source_target_pairs={{0,1},{1,0},{2,3},{3,2},{4,5},{5,4},{6,7},{7,6},{8,9},{9,8},{10,11... | collective-permute-start | bytes 786440 | tf_op jit(solution)/shard_map/ppermute | solution.py:252
  28.1 8.7 %collective-permute-start.2 = (bf16[512,128]{1,0:T(8,128)(2,1)S(1)}, bf16[512,128]{1,0:T(8,128)(2,1)S(1)}, u32[]{:S(2)}, u32[]{:S(2)}) collective-permute-start(bf16[512,128]{1,0:T(8,128)(2,1)S(1)} %constant_dynamic-update-slice_fusion.refs_2_), channel_id=1, source_target_pairs={{0,4},{1,5},{2,6},{3,7},{4,0},{5,1},{6,2},{7,3},{8,12},{9,13},{10,... | collective-permute-start | bytes 393224 | tf_op jit(solution)/shard_map/ppermute | solution.py:252
  29.1 7.8 %collective-permute-start.3 = (bf16[512,128]{1,0:T(8,128)(2,1)S(1)}, bf16[512,128]{1,0:T(8,128)(2,1)S(1)}, u32[]{:S(2)}, u32[]{:S(2)}) collective-permute-start(bf16[512,128]{1,0:T(8,128)(2,1)S(1)} %constant_dynamic-update-slice_fusion.refs_2_), channel_id=1, source_target_pairs={{0,2},{1,3},{2,0},{3,1},{4,6},{5,7},{6,4},{7,5},{8,10},{9,11},{10,... | collective-permute-start | bytes 393224 | tf_op jit(solution)/shard_map/ppermute | solution.py:252
  30.0 6.8 %collective-permute-start.4 = (bf16[512,128]{1,0:T(8,128)(2,1)S(1)}, bf16[512,128]{1,0:T(8,128)(2,1)S(1)}, u32[]{:S(2)}, u32[]{:S(2)}) collective-permute-start(bf16[512,128]{1,0:T(8,128)(2,1)S(1)} %constant_dynamic-update-slice_fusion.refs_2_), channel_id=1, source_target_pairs={{0,8},{1,9},{2,10},{3,11},{4,12},{5,13},{6,14},{7,15},{8,0},{9,1},... | collective-permute-start | bytes 393224 | tf_op jit(solution)/shard_map/ppermute | solution.py:252
  31.2 5.6 %collective-permute-start.5 = (bf16[512,128]{1,0:T(8,128)(2,1)S(1)}, bf16[512,128]{1,0:T(8,128)(2,1)S(1)}, u32[]{:S(2)}, u32[]{:S(2)}) collective-permute-start(bf16[512,128]{1,0:T(8,128)(2,1)S(1)} %constant_dynamic-update-slice_fusion.refs_2_), channel_id=1, source_target_pairs={{0,16},{1,17},{2,18},{3,19},{4,20},{5,21},{6,22},{7,23},{8,24},{9,... | collective-permute-start | bytes 393224 | tf_op jit(solution)/shard_map/ppermute | solution.py:252
  36.9 7.7 %collective-permute-start.7 = (bf16[1024,128]{1,0:T(8,128)(2,1)S(1)}, bf16[1024,128]{1,0:T(8,128)(2,1)S(1)}, u32[]{:S(2)}, u32[]{:S(2)}) collective-permute-start(bf16[1024,128]{1,0:T(8,128)(2,1)S(1)} %constant_dynamic-update-slice_fusion.2.refs_2_), channel_id=1, source_target_pairs={{0,8},{1,9},{2,10},{3,11},{4,12},{5,13},{6,14},{7,15},{8,0},{9,1},... | collective-permute-start | bytes 786440 | tf_op jit(solution)/shard_map/ppermute | solution.py:252
  38.2 7.0 %collective-permute-start.8 = (bf16[1024,128]{1,0:T(8,128)(2,1)S(1)}, bf16[1024,128]{1,0:T(8,128)(2,1)S(1)}, u32[]{:S(2)}, u32[]{:S(2)}) collective-permute-start(bf16[1024,128]{1,0:T(8,128)(2,1)S(1)} %constant_dynamic-update-slice_fusion.2.refs_2_), channel_id=1, source_target_pairs={{0,16},{1,17},{2,18},{3,19},{4,20},{5,21},{6,22},{7,23},{8,24},{9,... | collective-permute-start | bytes 786440 | tf_op jit(solution)/shard_map/ppermute | solution.py:252
  38.7 6.0 %collective-permute-start.6 = (bf16[512,128]{1,0:T(8,128)(2,1)S(1)}, bf16[512,128]{1,0:T(8,128)(2,1)S(1)}, u32[]{:S(2)}, u32[]{:S(2)}) collective-permute-start(bf16[512,128]{1,0:T(8,128)(2,1)S(1)} %collective-permute-done.2), channel_id=1, source_target_pairs={{0,2},{1,3},{2,0},{3,1},{4,6},{5,7},{6,4},{7,5},{8,10},{9,11},{10,... | collective-permute-start | bytes 393224 | tf_op jit(solution)/shard_map/ppermute | solution.py:252
  38.7 8.3 %collective-permute-start.9 = (bf16[512,128]{1,0:T(8,128)(2,1)S(1)}, bf16[512,128]{1,0:T(8,128)(2,1)S(1)}, u32[]{:S(2)}, u32[]{:S(2)}) collective-permute-start(bf16[512,128]{1,0:T(8,128)(2,1)S(1)} %collective-permute-done.5.refs_4_), channel_id=1, source_target_pairs={{0,8},{1,9},{2,10},{3,11},{4,12},{5,13},{6,14},{7,15},{8,0},{9,1},... | collective-permute-start | bytes 393224 | tf_op jit(solution)/shard_map/ppermute | solution.py:252
  45.2 10.2 %collective-permute-start.13 = (bf16[1024,128]{1,0:T(8,128)(2,1)S(1)}, bf16[1024,128]{1,0:T(8,128)(2,1)S(1)}, u32[]{:S(2)}, u32[]{:S(2)}) collective-permute-start(bf16[1024,128]{1,0:T(8,128)(2,1)S(1)} %collective-permute-done.7.refs_3_), channel_id=1, source_target_pairs={{0,16},{1,17},{2,18},{3,19},{4,20},{5,21},{6,22},{7,23},{8,24},{9,... | collective-permute-start | bytes 786440 | tf_op jit(solution)/shard_map/ppermute | solution.py:252
  45.8 8.1 %collective-permute-start.10 = (bf16[512,128]{1,0:T(8,128)(2,1)S(1)}, bf16[512,128]{1,0:T(8,128)(2,1)S(1)}, u32[]{:S(2)}, u32[]{:S(2)}) collective-permute-start(bf16[512,128]{1,0:T(8,128)(2,1)S(1)} %collective-permute-done.6.refs_2_), channel_id=1, source_target_pairs={{0,8},{1,9},{2,10},{3,11},{4,12},{5,13},{6,14},{7,15},{8,0},{9,1},... | collective-permute-start | bytes 393224 | tf_op jit(solution)/shard_map/ppermute | solution.py:252
  47.0 7.0 %collective-permute-start.11 = (bf16[512,128]{1,0:T(8,128)(2,1)S(1)}, bf16[512,128]{1,0:T(8,128)(2,1)S(1)}, u32[]{:S(2)}, u32[]{:S(2)}) collective-permute-start(bf16[512,128]{1,0:T(8,128)(2,1)S(1)} %collective-permute-done.6.refs_2_), channel_id=1, source_target_pairs={{0,16},{1,17},{2,18},{3,19},{4,20},{5,21},{6,22},{7,23},{8,24},{9,... | collective-permute-start | bytes 393224 | tf_op jit(solution)/shard_map/ppermute | solution.py:252
  53.9 6.0 %collective-permute-start.12 = (bf16[512,128]{1,0:T(8,128)(2,1)S(1)}, bf16[512,128]{1,0:T(8,128)(2,1)S(1)}, u32[]{:S(2)}, u32[]{:S(2)}) collective-permute-start(bf16[512,128]{1,0:T(8,128)(2,1)S(1)} %collective-permute-done.11.refs_3_), channel_id=1, source_target_pairs={{0,8},{1,9},{2,10},{3,11},{4,12},{5,13},{6,14},{7,15},{8,0},{9,1},... | collective-permute-start | bytes 393224 | tf_op jit(solution)/shard_map/ppermute | solution.py:252
  55.3 9.9 %copy-start.3 = (bf16[2048,512]{1,0:T(8,128)(2,1)S(1)}, bf16[2048,512]{1,0:T(8,128)(2,1)}, u32[]{:S(2)}) copy-start(bf16[2048,512]{1,0:T(8,128)(2,1)} %w_outer_ref.1) | copy-start | bytes 6291460
  59.9 5.3 %copy-start.2 = (bf16[512,2048]{1,0:T(8,128)(2,1)S(1)}, bf16[512,2048]{1,0:T(8,128)(2,1)}, u32[]{:S(2)}) copy-start(bf16[512,2048]{1,0:T(8,128)(2,1)} %w_inner_ref.1) | copy-start | bytes 6291460
  59.9 5.3 %copy-start.4 = (bf16[512,512]{1,0:T(8,128)(2,1)S(1)}, bf16[512,512]{1,0:T(8,128)(2,1)}, u32[]{:S(2)}) copy-start(bf16[512,512]{1,0:T(8,128)(2,1)} %w_out_ref.2) | copy-start | bytes 1572868
  60.0 5.3 %copy-start.13 = (f32[512]{0:T(512)S(1)}, f32[512]{0:T(512)}, u32[]{:S(2)}) copy-start(f32[512]{0:T(512)} %param.24) | copy-start | bytes 6148
  61.1 4.1 %collective-permute-start.14 = (bf16[256,256]{1,0:T(8,128)(2,1)S(1)}, bf16[256,256]{1,0:T(8,128)(2,1)S(1)}, u32[]{:S(2)}, u32[]{:S(2)}) collective-permute-start(bf16[256,256]{1,0:T(8,128)(2,1)S(1)} %attend.11), channel_id=1, source_target_pairs={{0,1},{1,0},{2,3},{3,2},{4,5},{5,4},{6,7},{7,6},{8,9},{9,8},{10,11... | collective-permute-start | bytes 393224 | tf_op jit(solution)/shard_map/ppermute | solution.py:252
  65.2 6.1 %copy-start.11 = (s32[512]{0:T(512)S(1)}, s32[512]{0:T(512)}, u32[]{:S(2)}) copy-start(s32[512]{0:T(512)} %param.15) | copy-start | bytes 6148
  65.3 21.4 %copy-start.1 = (bf16[512,512]{1,0:T(8,128)(2,1)S(1)}, bf16[512,512]{1,0:T(8,128)(2,1)}, u32[]{:S(2)}) copy-start(bf16[512,512]{1,0:T(8,128)(2,1)} %sensors_ref.3) | copy-start | bytes 1572868
  65.3 21.4 %copy-start.5 = (bf16[512,512]{1,0:T(8,128)(2,1)S(1)}, bf16[512,512]{1,0:T(8,128)(2,1)}, u32[]{:S(2)}) copy-start(bf16[512,512]{1,0:T(8,128)(2,1)} %w_in_ref.1) | copy-start | bytes 1572868
  65.3 21.4 %copy-start.6 = (bf16[512,512]{1,0:T(8,128)(2,1)S(1)}, bf16[512,512]{1,0:T(8,128)(2,1)}, u32[]{:S(2)}) copy-start(bf16[512,512]{1,0:T(8,128)(2,1)} %w_out_ref.3) | copy-start | bytes 1572868
  65.3 21.4 %copy-start.14 = (f32[512]{0:T(512)S(1)}, f32[512]{0:T(512)}, u32[]{:S(2)}) copy-start(f32[512]{0:T(512)} %param.25) | copy-start | bytes 6148
  68.1 18.6 %all-to-all-start.1 = ((bf16[32,16,512]{2,1,0:T(8,128)(2,1)}), bf16[32,16,512]{2,1,0:T(8,128)(2,1)S(1)}, u32[]{:S(2)}, u32[]{:S(2)}) async-start(bf16[32,16,512]{2,1,0:T(8,128)(2,1)} %bitcast.4), calls=%async_computation.1 | async-start | bytes 1048576 | tf_op jit(solution)/shard_map/all_to_all | solution.py:255

commit v10 on v9

--- a/solution.py
+++ b/solution.py
@@ -16,6 +16,10 @@
 LANES = 128
 EPS = 1e-06
 AXIS = "device"
+ORDER = (
+    30, 6, 18, 15, 11, 23, 7, 13, 3, 14, 28, 12, 26, 5, 24, 21,
+    8, 0, 27, 16, 1, 4, 22, 17, 19, 9, 25, 29, 10, 31, 20, 2,
+)
 F32 = jnp.float32
 BF16 = jnp.bfloat16
 NT = (((1,), (1,)), ((), ()))
@@ -40,10 +44,12 @@
     return values * lax.rsqrt(jnp.mean(values * values, axis=-1, keepdims=True) + EPS)
 
 
-def pack_kernel(tile, order, place_ref, sensors_ref, labels_ref, out_ref):
+def pack_kernel(tile, order, me_ref, core_ref, sensors_ref, labels_ref, out_ref):
     per_row = LANES // tile
     blocks = sensors_ref.shape[1] // LANES
-    mine = lax.rem(place_ref[0], per_row)
+    me, mine = me_ref[0], jnp.int32(0)
+    for at, i in enumerate(order):
+        mine = jnp.where(me == i, at % per_row, mine)
     labels = (labels_ref[...] + 1).astype(F32)
     lane = lax.broadcasted_iota(jnp.int32, labels.shape, 1)
     own_lanes = (lane // tile) == mine
@@ -223,7 +229,6 @@
 
 def local(
     order,
-    line,
     sensors,
     slot_region,
     w_query,
@@ -244,7 +249,6 @@
     tile = sen_dev // devices
     me = lax.axis_index(AXIS).astype(jnp.int32).reshape(1)
     core = lax.rem(me, 2)
-    place = me // line * line + core * (line // 2) + me % line // 2
     bits = devices.bit_length() - 1
     pay_rows = tile * (width // LANES) + 8
 
@@ -259,11 +263,11 @@
     payload = pl.pallas_call(
         functools.partial(pack_kernel, tile, order),
         out_shape=jax.ShapeDtypeStruct((devices, pay_rows, LANES), BF16),
-        in_specs=[SMEM, VMEM, VMEM],
+        in_specs=[SMEM, SMEM, VMEM, VMEM],
         out_specs=VMEM,
         compiler_params=PARAMS,
         name="pack",
-    )(place, sensors, slot_region.reshape(-1, LANES))
+    )(me, core, sensors, slot_region.reshape(-1, LANES))
     got = exchanged(payload)
 
     scale = jnp.repeat(temper * (math.log2(math.e) / HEAD_DIM), HEAD_DIM).reshape(1, -1)
@@ -370,10 +374,12 @@
 def solution(mesh):
     devices, line = mesh.size, mesh.shape["dp"]
     order = sorted(range(devices), key=lambda i: (i // line, i % 2, i))
+    if devices == len(ORDER):
+        order = list(ORDER)
     flat = jax.sharding.Mesh(mesh.devices.reshape(-1), (AXIS,))
     placed = (P(AXIS, None), P(AXIS)) + (P(),) * 12
     return jax.shard_map(
-        functools.partial(local, order, line),
+        functools.partial(local, order),
         mesh=flat,
         in_specs=placed,
         out_specs=P(AXIS, None),

time: 88.8 us -> 88.3 us (level)
  starting transfers between devices: 16.3 us -> 17.5 us
  waiting for transfers between devices: 19.9 us -> 18.9 us
    ppermute x15, starting transfers between devices: 13 us -> 14 us  [flipped(): return lax.ppermute(value, AXIS, [(i, i ^ mask) for i in range(devices)])]
  transfers between devices with their start and end apart: 16 -> 16, of which waited for: 4 -> 5; matrix products, arithmetic and copies ran while one was open for 0% -> 0% of each run, Pallas kernels for 22% -> 22%
where the time goes in v10:
time: 88.3 us; the launch traced here: 88 us
  Pallas kernels  26.3 us (30%)
  blocking collectives  22.8 us (26%)
  waiting for transfers between devices  18.9 us (21%)
  starting transfers between devices  17.5 us (20%)
  local copies, waits for them, and re-layouts  2.16 us (2%)
    all_to_all x1, blocking collectives, exchanged(): lax.all_to_all(value, AXIS, split_axis=0, concat_axis=0, tiled=True, axis...  22.8 us
    pallas_call x6, Pallas kernels, attend(): pl.pallas_call(functools.partial(attend_kernel, len(parts), row_parts, ac...  19.8 us
    all_to_all x1, waiting for transfers between devices, exchanged(): lax.all_to_all(value, AXIS, split_axis=0, concat_axis=0, tiled=True, axis...  14.6 us
    ppermute x15, starting transfers between devices, flipped(): return lax.ppermute(value, AXIS, [(i, i ^ mask) for i in range(devices)])  14 us
    ppermute x15, waiting for transfers between devices, flipped(): return lax.ppermute(value, AXIS, [(i, i ^ mask) for i in range(devices)])  4.33 us
    all_to_all x1, starting transfers between devices, exchanged(): lax.all_to_all(value, AXIS, split_axis=0, concat_axis=0, tiled=True, axis...  3.49 us
    pallas_call x1, Pallas kernels, local(): pl.pallas_call(post_kernel, out_shape=jax.ShapeDtypeStruct((sen_dev, widt...  2.8 us
    unnamed x34, local copies, waits for them, and re-layouts  1.83 us
  transfers between devices with their start and end apart: 16, of which 5 were waited for; matrix products, arithmetic and copies ran while one was open for 0% of the time, Pallas kernels for 22%

profile of v10, /device:TPU:1, one launch (start us, length us, event | category | flops | bytes accessed | tf_op | source)
XLA Modules:
  0.0 88.0 jit_solution(17231053879182192682)
XLA Ops:
  0.0 1.1 %copy-done = bf16[512,512]{1,0:T(8,128)(2,1)S(1)} copy-done((bf16[512,512]{1,0:T(8,128)(2,1)S(1)}, bf16[512,512]{1,0:T(8,128)(2,1)}, u32[]{:S(2)}) %copy-start) | copy-done | bytes 524312
  1.1 0.7 copy-done.10
  1.8 0.1 pack.1
  1.9 22.8 %all_to_all.10.got_ref = bf16[32,72,128]{2,1,0:T(8,128)(2,1)S(1)} all-to-all(bf16[32,72,128]{2,1,0:T(8,128)(2,1)S(1)} %pack.1), channel_id=1, replica_groups={{30,6,18,15,11,23,7,13,3,14,28,12,26,5,24,21,8,0,27,16,1,4,22,17,19,9,2..., dimensions={0} | all-to-all | bytes 1179648 | tf_op jit(solution)/shard_map/all_to_all | solution.py:259
  24.7 0.0 copy-done.12
  24.7 0.0 copy-done.8
  24.7 0.0 copy-done.9
  24.7 1.0 %pool.1 = (f32[256,512]{1,0:T(8,128)S(1)}, bf16[256,512]{1,0:T(8,128)(2,1)S(1)}, bf16[256,512]{1,0:T(8,128)(2,1)S(1)}, bf16[256,128]{1,0:T(8,128)(2,1)S(1)}, bf16[256,128]{1,0:T(8,128)(2,1)S(1)}) custom-call(s32[1]{0:T(128)S(6)} %rem.18.core_ref, bf16[32,72,128]{2,1,0:T(8,128)(2,1)S(1)} %all_to_all.10.got_ref, bf16[512,128]{1,0:T(8,128)(2,1)S(1)} %copy-done.8, ...), custom_call_target="tpu_custom_call" | custom-call | tf_op jit(solution)/shard_map/pool/pallas_call | solution.py:277
  25.7 0.1 collective-permute-start
  25.8 0.0 copy-done.15
  25.8 0.1 broadcast_in_dim.3
  25.9 0.1 reshape_reshape.3.scale_ref
  26.0 0.0 copy-done.7
  26.0 0.8 query.1
  26.8 0.3 collective-permute-done
  27.0 0.3 collective-permute-start.1
  27.3 2.4 %collective-permute-start.2 = (bf16[512,128]{1,0:T(8,128)(2,1)S(1)}, bf16[512,128]{1,0:T(8,128)(2,1)S(1)}, u32[]{:S(2)}, u32[]{:S(2)}) collective-permute-start(bf16[512,128]{1,0:T(8,128)(2,1)S(1)} %constant_dynamic-update-slice_fusion.refs_2_), channel_id=1, source_target_pairs={{0,4},{1,5},{2,6},{3,7},{4,0},{5,1},{6,2},{7,3},{8,12},{9,13},{10,... | collective-permute-start | bytes 393224 | tf_op jit(solution)/shard_map/ppermute | solution.py:256
  29.8 1.2 %collective-permute-start.3 = (bf16[512,128]{1,0:T(8,128)(2,1)S(1)}, bf16[512,128]{1,0:T(8,128)(2,1)S(1)}, u32[]{:S(2)}, u32[]{:S(2)}) collective-permute-start(bf16[512,128]{1,0:T(8,128)(2,1)S(1)} %constant_dynamic-update-slice_fusion.refs_2_), channel_id=1, source_target_pairs={{0,2},{1,3},{2,0},{3,1},{4,6},{5,7},{6,4},{7,5},{8,10},{9,11},{10,... | collective-permute-start | bytes 393224 | tf_op jit(solution)/shard_map/ppermute | solution.py:256
  30.9 0.0 collective-permute-start.4
  30.9 0.5 collective-permute-start.5
  31.4 0.0 collective-permute-done.1.refs_1_.refs_0_
  31.4 1.4 %attend.6.refs_5_ = f32[4,512,128]{2,1,0:T(8,128)S(1)} custom-call(bf16[256,512]{1,0:T(8,128)(2,1)S(1)} %get-tuple-element.33.refs_0_, bf16[256,512]{1,0:T(8,128)(2,1)S(1)} %collective-permute-done.1.refs_1_.refs_0_, bf16[512,128]{1,0:T(8,128)(2,1)S(1)} %constant_dynamic-update-slice_fusion.refs_2_), custom_call_target="tpu_custom_call" | custom-call | flops 1048576 | bytes 131072 | tf_op jit(solution)/shard_map/attend/pallas_call | solution.py:313
  32.8 0.4 collective-permute-done.2
  33.2 2.9 %collective-permute-done.3 = bf16[512,128]{1,0:T(8,128)(2,1)S(1)} collective-permute-done((bf16[512,128]{1,0:T(8,128)(2,1)S(1)}, bf16[512,128]{1,0:T(8,128)(2,1)S(1)}, u32[]{:S(2)}, u32[]{:S(2)}) %collective-permute-start.3) | collective-permute-done | bytes 131104 | tf_op jit(solution)/shard_map/ppermute | solution.py:256
  36.1 0.0 collective-permute-done.4.refs_3_
  36.1 0.0 collective-permute-done.5.refs_4_
  36.2 2.0 %collective-permute-start.7 = (bf16[1024,128]{1,0:T(8,128)(2,1)S(1)}, bf16[1024,128]{1,0:T(8,128)(2,1)S(1)}, u32[]{:S(2)}, u32[]{:S(2)}) collective-permute-start(bf16[1024,128]{1,0:T(8,128)(2,1)S(1)} %constant_dynamic-update-slice_fusion.2.refs_2_), channel_id=1, source_target_pairs={{0,8},{1,9},{2,10},{3,11},{4,12},{5,13},{6,14},{7,15},{8,0},{9,1},... | collective-permute-start | bytes 786440 | tf_op jit(solution)/shard_map/ppermute | solution.py:256
  38.2 0.6 collective-permute-start.8
  38.8 0.0 collective-permute-start.6
  38.8 1.2 %collective-permute-start.9 = (bf16[512,128]{1,0:T(8,128)(2,1)S(1)}, bf16[512,128]{1,0:T(8,128)(2,1)S(1)}, u32[]{:S(2)}, u32[]{:S(2)}) collective-permute-start(bf16[512,128]{1,0:T(8,128)(2,1)S(1)} %collective-permute-done.5.refs_4_), channel_id=1, source_target_pairs={{0,8},{1,9},{2,10},{3,11},{4,12},{5,13},{6,14},{7,15},{8,0},{9,1},... | collective-permute-start | bytes 393224 | tf_op jit(solution)/shard_map/ppermute | solution.py:256
  39.9 4.6 %attend.7.refs_6_ = f32[4,512,128]{2,1,0:T(8,128)S(1)} custom-call(bf16[256,512]{1,0:T(8,128)(2,1)S(1)} %get-tuple-element.33.refs_0_, bf16[256,512]{1,0:T(8,128)(2,1)S(1)} %collective-permute-done.1.refs_1_.refs_0_, bf16[1024,128]{1,0:T(8,128)(2,1)S(1)} %constant_dynamic-update-slice_fusion.2.refs_2_, bf16[512,128]{1,0:T(8,128)(2,1)S(1)} %collective-permute-done.4.refs_3_, ...), custom_call_target="tpu_custom_call" | custom-call | flops 4194304 | bytes 524288 | tf_op jit(solution)/shard_map/attend/pallas_call | solution.py:313
  44.5 0.0 collective-permute-done.6.refs_2_
  44.5 0.0 collective-permute-done.7.refs_3_
  44.5 0.7 collective-permute-done.8.refs_4_
  45.3 0.6 collective-permute-start.13
  45.9 1.1 %collective-permute-start.10 = (bf16[512,128]{1,0:T(8,128)(2,1)S(1)}, bf16[512,128]{1,0:T(8,128)(2,1)S(1)}, u32[]{:S(2)}, u32[]{:S(2)}) collective-permute-start(bf16[512,128]{1,0:T(8,128)(2,1)S(1)} %collective-permute-done.6.refs_2_), channel_id=1, source_target_pairs={{0,8},{1,9},{2,10},{3,11},{4,12},{5,13},{6,14},{7,15},{8,0},{9,1},... | collective-permute-start | bytes 393224 | tf_op jit(solution)/shard_map/ppermute | solution.py:256
  47.0 0.3 collective-permute-start.11
  47.3 0.0 collective-permute-done.9.refs_5_
  47.3 7.0 %attend.8.refs_5_ = f32[4,512,128]{2,1,0:T(8,128)S(1)} custom-call(bf16[256,512]{1,0:T(8,128)(2,1)S(1)} %get-tuple-element.33.refs_0_, bf16[256,512]{1,0:T(8,128)(2,1)S(1)} %collective-permute-done.1.refs_1_.refs_0_, bf16[512,128]{1,0:T(8,128)(2,1)S(1)} %collective-permute-done.6.refs_2_, bf16[1024,128]{1,0:T(8,128)(2,1)S(1)} %collective-permute-done.7.refs_3_, ...), custom_call_target="tpu_custom_call" | custom-call | flops 6291456 | bytes 786432 | tf_op jit(solution)/shard_map/attend/pallas_call | solution.py:313
  54.3 0.0 collective-permute-done.10.refs_2_
  54.3 0.0 collective-permute-done.11.refs_3_
  54.3 1.1 %collective-permute-start.12 = (bf16[512,128]{1,0:T(8,128)(2,1)S(1)}, bf16[512,128]{1,0:T(8,128)(2,1)S(1)}, u32[]{:S(2)}, u32[]{:S(2)}) collective-permute-start(bf16[512,128]{1,0:T(8,128)(2,1)S(1)} %collective-permute-done.11.refs_3_), channel_id=1, source_target_pairs={{0,8},{1,9},{2,10},{3,11},{4,12},{5,13},{6,14},{7,15},{8,0},{9,1},... | collective-permute-start | bytes 393224 | tf_op jit(solution)/shard_map/ppermute | solution.py:256
  55.4 0.0 collective-permute-done.13.refs_4_
  55.4 4.6 %attend.9.refs_2_ = f32[4,512,128]{2,1,0:T(8,128)S(1)} custom-call(bf16[256,512]{1,0:T(8,128)(2,1)S(1)} %get-tuple-element.33.refs_0_, bf16[256,512]{1,0:T(8,128)(2,1)S(1)} %collective-permute-done.1.refs_1_.refs_0_, bf16[512,128]{1,0:T(8,128)(2,1)S(1)} %collective-permute-done.10.refs_2_, bf16[512,128]{1,0:T(8,128)(2,1)S(1)} %collective-permute-done.11.refs_3_, ...), custom_call_target="tpu_custom_call" | custom-call | flops 4194304 | bytes 524288 | tf_op jit(solution)/shard_map/attend/pallas_call | solution.py:313
  60.0 0.0 copy-start.2
  60.0 0.0 copy-start.4
  60.0 0.0 copy-start.13
  60.1 0.0 collective-permute-done.12.refs_1_
  60.1 1.1 %attend.11 = bf16[256,256]{1,0:T(8,128)(2,1)S(1)} custom-call(bf16[256,512]{1,0:T(8,128)(2,1)S(1)} %collective-permute-done.1.refs_1_.refs_0_, bf16[512,128]{1,0:T(8,128)(2,1)S(1)} %collective-permute-done.12.refs_1_, f32[4,512,128]{2,1,0:T(8,128)S(1)} %attend.9.refs_2_), custom_call_target="tpu_custom_call" | custom-call | flops 524288 | bytes 131072 | tf_op jit(solution)/shard_map/attend/pallas_call | solution.py:313
  61.2 2.6 %collective-permute-start.14 = (bf16[256,256]{1,0:T(8,128)(2,1)S(1)}, bf16[256,256]{1,0:T(8,128)(2,1)S(1)}, u32[]{:S(2)}, u32[]{:S(2)}) collective-permute-start(bf16[256,256]{1,0:T(8,128)(2,1)S(1)} %attend.11), channel_id=1, source_target_pairs={{0,1},{1,0},{2,3},{3,2},{4,5},{5,4},{6,7},{7,6},{8,9},{9,8},{10,11... | collective-permute-start | bytes 393224 | tf_op jit(solution)/shard_map/ppermute | solution.py:256
  63.9 1.1 %attend.10.mine_ref = bf16[256,256]{1,0:T(8,128)(2,1)S(1)} custom-call(bf16[256,512]{1,0:T(8,128)(2,1)S(1)} %get-tuple-element.33.refs_0_, bf16[512,128]{1,0:T(8,128)(2,1)S(1)} %collective-permute-done.12.refs_1_, f32[4,512,128]{2,1,0:T(8,128)S(1)} %attend.9.refs_2_), custom_call_target="tpu_custom_call" | custom-call | flops 524288 | bytes 131072 | tf_op jit(solution)/shard_map/attend/pallas_call | solution.py:313
  65.0 0.0 collective-permute-done.14.other_ref
  65.0 0.0 copy-done.3
  65.1 0.0 copy-start.11
  65.1 0.0 copy-start.1
  65.1 0.0 copy-start.5
  65.1 0.0 copy-start.6
  65.1 0.0 copy-start.14
  65.1 2.8 %post.1 = bf16[512,512]{1,0:T(8,128)(2,1)} custom-call(s32[1]{0:T(128)S(6)} %rem.18.core_ref, bf16[256,256]{1,0:T(8,128)(2,1)S(1)} %attend.10.mine_ref, bf16[256,256]{1,0:T(8,128)(2,1)S(1)} %collective-permute-done.14.other_ref, f32[256,512]{1,0:T(8,128)S(1)} %get-tuple-element.51.pooled_ref, bf16[256,512]{1,0:T(8,128)(2,1)S(1)} %get-tuple-element.52.member_ref, ...), custom_call_target="tpu_custom_call" | custom-call | tf_op jit(solution)/shard_map/post/pallas_call | solution.py:354
  67.9 3.5 %all-to-all-start.1 = ((bf16[32,16,512]{2,1,0:T(8,128)(2,1)}), bf16[32,16,512]{2,1,0:T(8,128)(2,1)S(1)}, u32[]{:S(2)}, u32[]{:S(2)}) async-start(bf16[32,16,512]{2,1,0:T(8,128)(2,1)} %bitcast.4), calls=%async_computation.1 | async-start | bytes 1048576 | tf_op jit(solution)/shard_map/all_to_all | solution.py:259
  71.4 0.1 copy.15.live_ref
  71.6 14.6 %all-to-all-done.1 = bf16[32,16,512]{2,1,0:T(8,128)(2,1)S(1)} async-done(((bf16[32,16,512]{2,1,0:T(8,128)(2,1)}), bf16[32,16,512]{2,1,0:T(8,128)(2,1)S(1)}, u32[]{:S(2)}, u32[]{:S(2)}) %all-to-all-start.1) | async-done | bytes 524320 | tf_op jit(solution)/shard_map/all_to_all | solution.py:259
  86.2 0.0 copy-done.5
  86.2 1.8 %decode.1 = bf16[512,512]{1,0:T(8,128)(2,1)} custom-call(bf16[512,512]{1,0:T(8,128)(2,1)S(1)} %bitcast.8, bf16[512,512]{1,0:T(8,128)(2,1)S(1)} %copy-done.1, f32[512,1]{1,0:T(8,128)S(1)} %copy.15.live_ref, f32[1,512]{1,0:T(1,128)S(1)} %bitcast.12, bf16[512,512]{1,0:T(8,128)(2,1)S(1)} %copy-done.5, bf16[512,512]{1,0:T(8,128)(2,1)S(1)} %copy-done.6), custom_call_target="tpu_custom_call" | custom-call | tf_op jit(solution)/shard_map/decode/pallas_call | solution.py:364
  (21 shorter events, 0.1 us)
Async XLA Ops:
  0.0 24.7 %copy-start.12 = (f32[512]{0:T(512)S(1)}, f32[512]{0:T(512)}, u32[]{:S(2)}) copy-start(f32[512]{0:T(512)} %param.21) | copy-start | bytes 6148
  0.0 25.8 %copy-start.15 = (f32[8]{0:T(128)S(1)}, f32[8]{0:T(128)}, u32[]{:S(2)}) copy-start(f32[8]{0:T(128)} %param.20) | copy-start | bytes 100
  0.0 1.1 %copy-start = (bf16[512,512]{1,0:T(8,128)(2,1)S(1)}, bf16[512,512]{1,0:T(8,128)(2,1)}, u32[]{:S(2)}) copy-start(bf16[512,512]{1,0:T(8,128)(2,1)} %sensors_ref.3) | copy-start | bytes 1572868
  1.1 0.7 copy-start.10
  1.8 22.9 %copy-start.8 = (bf16[512,128]{1,0:T(8,128)(2,1)S(1)}, bf16[512,128]{1,0:T(8,128)(2,1)}, u32[]{:S(2)}) copy-start(bf16[512,128]{1,0:T(8,128)(2,1)} %w_key_ref.1) | copy-start | bytes 393220
  1.8 22.9 %copy-start.9 = (bf16[512,128]{1,0:T(8,128)(2,1)S(1)}, bf16[512,128]{1,0:T(8,128)(2,1)}, u32[]{:S(2)}) copy-start(bf16[512,128]{1,0:T(8,128)(2,1)} %w_value_ref.1) | copy-start | bytes 393220
  1.8 24.2 %copy-start.7 = (bf16[512,512]{1,0:T(8,128)(2,1)S(1)}, bf16[512,512]{1,0:T(8,128)(2,1)}, u32[]{:S(2)}) copy-start(bf16[512,512]{1,0:T(8,128)(2,1)} %w_query_ref.1) | copy-start | bytes 1572868
  25.7 1.3 %collective-permute-start = (bf16[256,128]{1,0:T(8,128)(2,1)S(1)}, bf16[256,128]{1,0:T(8,128)(2,1)S(1)}, u32[]{:S(2)}, u32[]{:S(2)}) collective-permute-start(bf16[256,128]{1,0:T(8,128)(2,1)S(1)} %get-tuple-element.29), channel_id=1, source_target_pairs={{0,1},{1,0},{2,3},{3,2},{4,5},{5,4},{6,7},{7,6},{8,9},{9,8},{10,11... | collective-permute-start | bytes 196616 | tf_op jit(solution)/shard_map/ppermute | solution.py:256
  27.0 4.4 %collective-permute-start.1 = (bf16[256,512]{1,0:T(8,128)(2,1)S(1)}, bf16[256,512]{1,0:T(8,128)(2,1)S(1)}, u32[]{:S(2)}, u32[]{:S(2)}) collective-permute-start(bf16[256,512]{1,0:T(8,128)(2,1)S(1)} %get-tuple-element.34), channel_id=1, source_target_pairs={{0,1},{1,0},{2,3},{3,2},{4,5},{5,4},{6,7},{7,6},{8,9},{9,8},{10,11... | collective-permute-start | bytes 786440 | tf_op jit(solution)/shard_map/ppermute | solution.py:256
  27.3 5.9 %collective-permute-start.2 = (bf16[512,128]{1,0:T(8,128)(2,1)S(1)}, bf16[512,128]{1,0:T(8,128)(2,1)S(1)}, u32[]{:S(2)}, u32[]{:S(2)}) collective-permute-start(bf16[512,128]{1,0:T(8,128)(2,1)S(1)} %constant_dynamic-update-slice_fusion.refs_2_), channel_id=1, source_target_pairs={{0,4},{1,5},{2,6},{3,7},{4,0},{5,1},{6,2},{7,3},{8,12},{9,13},{10,... | collective-permute-start | bytes 393224 | tf_op jit(solution)/shard_map/ppermute | solution.py:256
  29.8 6.4 %collective-permute-start.3 = (bf16[512,128]{1,0:T(8,128)(2,1)S(1)}, bf16[512,128]{1,0:T(8,128)(2,1)S(1)}, u32[]{:S(2)}, u32[]{:S(2)}) collective-permute-start(bf16[512,128]{1,0:T(8,128)(2,1)S(1)} %constant_dynamic-update-slice_fusion.refs_2_), channel_id=1, source_target_pairs={{0,2},{1,3},{2,0},{3,1},{4,6},{5,7},{6,4},{7,5},{8,10},{9,11},{10,... | collective-permute-start | bytes 393224 | tf_op jit(solution)/shard_map/ppermute | solution.py:256
  30.9 5.2 %collective-permute-start.4 = (bf16[512,128]{1,0:T(8,128)(2,1)S(1)}, bf16[512,128]{1,0:T(8,128)(2,1)S(1)}, u32[]{:S(2)}, u32[]{:S(2)}) collective-permute-start(bf16[512,128]{1,0:T(8,128)(2,1)S(1)} %constant_dynamic-update-slice_fusion.refs_2_), channel_id=1, source_target_pairs={{0,8},{1,9},{2,10},{3,11},{4,12},{5,13},{6,14},{7,15},{8,0},{9,1},... | collective-permute-start | bytes 393224 | tf_op jit(solution)/shard_map/ppermute | solution.py:256
  30.9 5.2 %collective-permute-start.5 = (bf16[512,128]{1,0:T(8,128)(2,1)S(1)}, bf16[512,128]{1,0:T(8,128)(2,1)S(1)}, u32[]{:S(2)}, u32[]{:S(2)}) collective-permute-start(bf16[512,128]{1,0:T(8,128)(2,1)S(1)} %constant_dynamic-update-slice_fusion.refs_2_), channel_id=1, source_target_pairs={{0,16},{1,17},{2,18},{3,19},{4,20},{5,21},{6,22},{7,23},{8,24},{9,... | collective-permute-start | bytes 393224 | tf_op jit(solution)/shard_map/ppermute | solution.py:256
  36.2 8.3 %collective-permute-start.7 = (bf16[1024,128]{1,0:T(8,128)(2,1)S(1)}, bf16[1024,128]{1,0:T(8,128)(2,1)S(1)}, u32[]{:S(2)}, u32[]{:S(2)}) collective-permute-start(bf16[1024,128]{1,0:T(8,128)(2,1)S(1)} %constant_dynamic-update-slice_fusion.2.refs_2_), channel_id=1, source_target_pairs={{0,8},{1,9},{2,10},{3,11},{4,12},{5,13},{6,14},{7,15},{8,0},{9,1},... | collective-permute-start | bytes 786440 | tf_op jit(solution)/shard_map/ppermute | solution.py:256
  38.2 7.1 %collective-permute-start.8 = (bf16[1024,128]{1,0:T(8,128)(2,1)S(1)}, bf16[1024,128]{1,0:T(8,128)(2,1)S(1)}, u32[]{:S(2)}, u32[]{:S(2)}) collective-permute-start(bf16[1024,128]{1,0:T(8,128)(2,1)S(1)} %constant_dynamic-update-slice_fusion.2.refs_2_), channel_id=1, source_target_pairs={{0,16},{1,17},{2,18},{3,19},{4,20},{5,21},{6,22},{7,23},{8,24},{9,... | collective-permute-start | bytes 786440 | tf_op jit(solution)/shard_map/ppermute | solution.py:256
  38.8 5.7 %collective-permute-start.6 = (bf16[512,128]{1,0:T(8,128)(2,1)S(1)}, bf16[512,128]{1,0:T(8,128)(2,1)S(1)}, u32[]{:S(2)}, u32[]{:S(2)}) collective-permute-start(bf16[512,128]{1,0:T(8,128)(2,1)S(1)} %collective-permute-done.2), channel_id=1, source_target_pairs={{0,2},{1,3},{2,0},{3,1},{4,6},{5,7},{6,4},{7,5},{8,10},{9,11},{10,... | collective-permute-start | bytes 393224 | tf_op jit(solution)/shard_map/ppermute | solution.py:256
  38.8 8.6 %collective-permute-start.9 = (bf16[512,128]{1,0:T(8,128)(2,1)S(1)}, bf16[512,128]{1,0:T(8,128)(2,1)S(1)}, u32[]{:S(2)}, u32[]{:S(2)}) collective-permute-start(bf16[512,128]{1,0:T(8,128)(2,1)S(1)} %collective-permute-done.5.refs_4_), channel_id=1, source_target_pairs={{0,8},{1,9},{2,10},{3,11},{4,12},{5,13},{6,14},{7,15},{8,0},{9,1},... | collective-permute-start | bytes 393224 | tf_op jit(solution)/shard_map/ppermute | solution.py:256
  45.3 10.2 %collective-permute-start.13 = (bf16[1024,128]{1,0:T(8,128)(2,1)S(1)}, bf16[1024,128]{1,0:T(8,128)(2,1)S(1)}, u32[]{:S(2)}, u32[]{:S(2)}) collective-permute-start(bf16[1024,128]{1,0:T(8,128)(2,1)S(1)} %collective-permute-done.7.refs_3_), channel_id=1, source_target_pairs={{0,16},{1,17},{2,18},{3,19},{4,20},{5,21},{6,22},{7,23},{8,24},{9,... | collective-permute-start | bytes 786440 | tf_op jit(solution)/shard_map/ppermute | solution.py:256
  45.9 8.4 %collective-permute-start.10 = (bf16[512,128]{1,0:T(8,128)(2,1)S(1)}, bf16[512,128]{1,0:T(8,128)(2,1)S(1)}, u32[]{:S(2)}, u32[]{:S(2)}) collective-permute-start(bf16[512,128]{1,0:T(8,128)(2,1)S(1)} %collective-permute-done.6.refs_2_), channel_id=1, source_target_pairs={{0,8},{1,9},{2,10},{3,11},{4,12},{5,13},{6,14},{7,15},{8,0},{9,1},... | collective-permute-start | bytes 393224 | tf_op jit(solution)/shard_map/ppermute | solution.py:256
  47.0 7.3 %collective-permute-start.11 = (bf16[512,128]{1,0:T(8,128)(2,1)S(1)}, bf16[512,128]{1,0:T(8,128)(2,1)S(1)}, u32[]{:S(2)}, u32[]{:S(2)}) collective-permute-start(bf16[512,128]{1,0:T(8,128)(2,1)S(1)} %collective-permute-done.6.refs_2_), channel_id=1, source_target_pairs={{0,16},{1,17},{2,18},{3,19},{4,20},{5,21},{6,22},{7,23},{8,24},{9,... | collective-permute-start | bytes 393224 | tf_op jit(solution)/shard_map/ppermute | solution.py:256
  54.3 5.7 %collective-permute-start.12 = (bf16[512,128]{1,0:T(8,128)(2,1)S(1)}, bf16[512,128]{1,0:T(8,128)(2,1)S(1)}, u32[]{:S(2)}, u32[]{:S(2)}) collective-permute-start(bf16[512,128]{1,0:T(8,128)(2,1)S(1)} %collective-permute-done.11.refs_3_), channel_id=1, source_target_pairs={{0,8},{1,9},{2,10},{3,11},{4,12},{5,13},{6,14},{7,15},{8,0},{9,1},... | collective-permute-start | bytes 393224 | tf_op jit(solution)/shard_map/ppermute | solution.py:256
  55.4 9.6 %copy-start.3 = (bf16[2048,512]{1,0:T(8,128)(2,1)S(1)}, bf16[2048,512]{1,0:T(8,128)(2,1)}, u32[]{:S(2)}) copy-start(bf16[2048,512]{1,0:T(8,128)(2,1)} %w_outer_ref.1) | copy-start | bytes 6291460
  60.0 5.0 %copy-start.2 = (bf16[512,2048]{1,0:T(8,128)(2,1)S(1)}, bf16[512,2048]{1,0:T(8,128)(2,1)}, u32[]{:S(2)}) copy-start(bf16[512,2048]{1,0:T(8,128)(2,1)} %w_inner_ref.1) | copy-start | bytes 6291460
  60.0 5.0 %copy-start.4 = (bf16[512,512]{1,0:T(8,128)(2,1)S(1)}, bf16[512,512]{1,0:T(8,128)(2,1)}, u32[]{:S(2)}) copy-start(bf16[512,512]{1,0:T(8,128)(2,1)} %w_out_ref.2) | copy-start | bytes 1572868
  60.0 5.0 %copy-start.13 = (f32[512]{0:T(512)S(1)}, f32[512]{0:T(512)}, u32[]{:S(2)}) copy-start(f32[512]{0:T(512)} %param.24) | copy-start | bytes 6148
  61.2 3.8 %collective-permute-start.14 = (bf16[256,256]{1,0:T(8,128)(2,1)S(1)}, bf16[256,256]{1,0:T(8,128)(2,1)S(1)}, u32[]{:S(2)}, u32[]{:S(2)}) collective-permute-start(bf16[256,256]{1,0:T(8,128)(2,1)S(1)} %attend.11), channel_id=1, source_target_pairs={{0,1},{1,0},{2,3},{3,2},{4,5},{5,4},{6,7},{7,6},{8,9},{9,8},{10,11... | collective-permute-start | bytes 393224 | tf_op jit(solution)/shard_map/ppermute | solution.py:256
  65.1 6.4 %copy-start.11 = (s32[512]{0:T(512)S(1)}, s32[512]{0:T(512)}, u32[]{:S(2)}) copy-start(s32[512]{0:T(512)} %param.15) | copy-start | bytes 6148
  65.1 21.1 %copy-start.1 = (bf16[512,512]{1,0:T(8,128)(2,1)S(1)}, bf16[512,512]{1,0:T(8,128)(2,1)}, u32[]{:S(2)}) copy-start(bf16[512,512]{1,0:T(8,128)(2,1)} %sensors_ref.3) | copy-start | bytes 1572868
  65.1 21.1 %copy-start.5 = (bf16[512,512]{1,0:T(8,128)(2,1)S(1)}, bf16[512,512]{1,0:T(8,128)(2,1)}, u32[]{:S(2)}) copy-start(bf16[512,512]{1,0:T(8,128)(2,1)} %w_in_ref.1) | copy-start | bytes 1572868
  65.1 21.1 %copy-start.6 = (bf16[512,512]{1,0:T(8,128)(2,1)S(1)}, bf16[512,512]{1,0:T(8,128)(2,1)}, u32[]{:S(2)}) copy-start(bf16[512,512]{1,0:T(8,128)(2,1)} %w_out_ref.3) | copy-start | bytes 1572868
  65.1 21.1 %copy-start.14 = (f32[512]{0:T(512)S(1)}, f32[512]{0:T(512)}, u32[]{:S(2)}) copy-start(f32[512]{0:T(512)} %param.25) | copy-start | bytes 6148
  67.9 18.3 %all-to-all-start.1 = ((bf16[32,16,512]{2,1,0:T(8,128)(2,1)}), bf16[32,16,512]{2,1,0:T(8,128)(2,1)S(1)}, u32[]{:S(2)}, u32[]{:S(2)}) async-start(bf16[32,16,512]{2,1,0:T(8,128)(2,1)} %bitcast.4), calls=%async_computation.1 | async-start | bytes 1048576 | tf_op jit(solution)/shard_map/all_to_all | solution.py:259

commit v11 on v10

--- a/solution.py
+++ b/solution.py
@@ -150,7 +150,7 @@
     for r, slab in enumerate(slabs):
         for h in range(GROUP):
             query_ref[h, r * REG_DEV : (r + 1) * REG_DEV, :] = slab[:, h * LANES : (h + 1) * LANES]
-    block = max(n for n in range(REG_DEV, 2561, REG_DEV) if at % n == 0)
+    block = max(n for n in range(REG_DEV, 3073, REG_DEV) if at % n == 0)
     span = min(rows_all, 512 if block <= 1024 else 256)
 
     def step(i, begin):

time: 88.3 us -> 88.3 us (level)
  no operation moved by 1% of the time
where the time goes in v11:
time: 88.3 us; the launch traced here: 88 us
  Pallas kernels  26.3 us (30%)
  blocking collectives  22.8 us (26%)
  waiting for transfers between devices  18.9 us (21%)
  starting transfers between devices  17.5 us (20%)
  local copies, waits for them, and re-layouts  2.16 us (2%)
    all_to_all x1, blocking collectives, exchanged(): lax.all_to_all(value, AXIS, split_axis=0, concat_axis=0, tiled=True, axis...  22.8 us
    pallas_call x6, Pallas kernels, attend(): pl.pallas_call(functools.partial(attend_kernel, len(parts), row_parts, ac...  19.8 us
    all_to_all x1, waiting for transfers between devices, exchanged(): lax.all_to_all(value, AXIS, split_axis=0, concat_axis=0, tiled=True, axis...  14.6 us
    ppermute x15, starting transfers between devices, flipped(): return lax.ppermute(value, AXIS, [(i, i ^ mask) for i in range(devices)])  14 us
    ppermute x15, waiting for transfers between devices, flipped(): return lax.ppermute(value, AXIS, [(i, i ^ mask) for i in range(devices)])  4.33 us
    all_to_all x1, starting transfers between devices, exchanged(): lax.all_to_all(value, AXIS, split_axis=0, concat_axis=0, tiled=True, axis...  3.51 us
    pallas_call x1, Pallas kernels, local(): pl.pallas_call(post_kernel, out_shape=jax.ShapeDtypeStruct((sen_dev, widt...  2.8 us
    unnamed x34, local copies, waits for them, and re-layouts  1.83 us
  transfers between devices with their start and end apart: 16, of which 5 were waited for; matrix products, arithmetic and copies ran while one was open for 0% of the time, Pallas kernels for 22%

profile of v11, /device:TPU:1, one launch (start us, length us, event | category | flops | bytes accessed | tf_op | source)
XLA Modules:
  0.0 88.0 jit_solution(5996150290450367198)
XLA Ops:
  0.0 1.1 %copy-done = bf16[512,512]{1,0:T(8,128)(2,1)S(1)} copy-done((bf16[512,512]{1,0:T(8,128)(2,1)S(1)}, bf16[512,512]{1,0:T(8,128)(2,1)}, u32[]{:S(2)}) %copy-start) | copy-done | bytes 524312
  1.1 0.7 copy-done.10
  1.8 0.1 pack.1
  1.9 22.8 %all_to_all.10.got_ref = bf16[32,72,128]{2,1,0:T(8,128)(2,1)S(1)} all-to-all(bf16[32,72,128]{2,1,0:T(8,128)(2,1)S(1)} %pack.1), channel_id=1, replica_groups={{30,6,18,15,11,23,7,13,3,14,28,12,26,5,24,21,8,0,27,16,1,4,22,17,19,9,2..., dimensions={0} | all-to-all | bytes 1179648 | tf_op jit(solution)/shard_map/all_to_all | solution.py:259
  24.7 0.0 copy-done.12
  24.7 1.0 %pool.1 = (f32[256,512]{1,0:T(8,128)S(1)}, bf16[256,512]{1,0:T(8,128)(2,1)S(1)}, bf16[256,512]{1,0:T(8,128)(2,1)S(1)}, bf16[256,128]{1,0:T(8,128)(2,1)S(1)}, bf16[256,128]{1,0:T(8,128)(2,1)S(1)}) custom-call(s32[1]{0:T(128)S(6)} %rem.18.core_ref, bf16[32,72,128]{2,1,0:T(8,128)(2,1)S(1)} %all_to_all.10.got_ref, bf16[512,128]{1,0:T(8,128)(2,1)S(1)} %copy-done.8, ...), custom_call_target="tpu_custom_call" | custom-call | tf_op jit(solution)/shard_map/pool/pallas_call | solution.py:277
  25.7 0.1 collective-permute-start
  25.8 0.0 copy-done.15
  25.8 0.1 broadcast_in_dim.3
  25.9 0.1 reshape_reshape.3.scale_ref
  26.0 0.8 query.1
  26.8 0.3 collective-permute-done
  27.0 0.3 collective-permute-start.1
  27.3 2.4 %collective-permute-start.2 = (bf16[512,128]{1,0:T(8,128)(2,1)S(1)}, bf16[512,128]{1,0:T(8,128)(2,1)S(1)}, u32[]{:S(2)}, u32[]{:S(2)}) collective-permute-start(bf16[512,128]{1,0:T(8,128)(2,1)S(1)} %constant_dynamic-update-slice_fusion.refs_2_), channel_id=1, source_target_pairs={{0,4},{1,5},{2,6},{3,7},{4,0},{5,1},{6,2},{7,3},{8,12},{9,13},{10,... | collective-permute-start | bytes 393224 | tf_op jit(solution)/shard_map/ppermute | solution.py:256
  29.8 1.2 %collective-permute-start.3 = (bf16[512,128]{1,0:T(8,128)(2,1)S(1)}, bf16[512,128]{1,0:T(8,128)(2,1)S(1)}, u32[]{:S(2)}, u32[]{:S(2)}) collective-permute-start(bf16[512,128]{1,0:T(8,128)(2,1)S(1)} %constant_dynamic-update-slice_fusion.refs_2_), channel_id=1, source_target_pairs={{0,2},{1,3},{2,0},{3,1},{4,6},{5,7},{6,4},{7,5},{8,10},{9,11},{10,... | collective-permute-start | bytes 393224 | tf_op jit(solution)/shard_map/ppermute | solution.py:256
  30.9 0.0 collective-permute-start.4
  30.9 0.5 collective-permute-start.5
  31.4 0.0 collective-permute-done.1.refs_1_.refs_0_
  31.4 1.4 %attend.6.refs_5_ = f32[4,512,128]{2,1,0:T(8,128)S(1)} custom-call(bf16[256,512]{1,0:T(8,128)(2,1)S(1)} %get-tuple-element.33.refs_0_, bf16[256,512]{1,0:T(8,128)(2,1)S(1)} %collective-permute-done.1.refs_1_.refs_0_, bf16[512,128]{1,0:T(8,128)(2,1)S(1)} %constant_dynamic-update-slice_fusion.refs_2_), custom_call_target="tpu_custom_call" | custom-call | flops 1048576 | bytes 131072 | tf_op jit(solution)/shard_map/attend/pallas_call | solution.py:313
  32.8 0.4 collective-permute-done.2
  33.2 2.9 %collective-permute-done.3 = bf16[512,128]{1,0:T(8,128)(2,1)S(1)} collective-permute-done((bf16[512,128]{1,0:T(8,128)(2,1)S(1)}, bf16[512,128]{1,0:T(8,128)(2,1)S(1)}, u32[]{:S(2)}, u32[]{:S(2)}) %collective-permute-start.3) | collective-permute-done | bytes 131104 | tf_op jit(solution)/shard_map/ppermute | solution.py:256
  36.1 0.0 collective-permute-done.4.refs_3_
  36.1 0.0 collective-permute-done.5.refs_4_
  36.2 2.0 %collective-permute-start.7 = (bf16[1024,128]{1,0:T(8,128)(2,1)S(1)}, bf16[1024,128]{1,0:T(8,128)(2,1)S(1)}, u32[]{:S(2)}, u32[]{:S(2)}) collective-permute-start(bf16[1024,128]{1,0:T(8,128)(2,1)S(1)} %constant_dynamic-update-slice_fusion.2.refs_2_), channel_id=1, source_target_pairs={{0,8},{1,9},{2,10},{3,11},{4,12},{5,13},{6,14},{7,15},{8,0},{9,1},... | collective-permute-start | bytes 786440 | tf_op jit(solution)/shard_map/ppermute | solution.py:256
  38.2 0.6 collective-permute-start.8
  38.8 0.0 collective-permute-start.6
  38.8 1.2 %collective-permute-start.9 = (bf16[512,128]{1,0:T(8,128)(2,1)S(1)}, bf16[512,128]{1,0:T(8,128)(2,1)S(1)}, u32[]{:S(2)}, u32[]{:S(2)}) collective-permute-start(bf16[512,128]{1,0:T(8,128)(2,1)S(1)} %collective-permute-done.5.refs_4_), channel_id=1, source_target_pairs={{0,8},{1,9},{2,10},{3,11},{4,12},{5,13},{6,14},{7,15},{8,0},{9,1},... | collective-permute-start | bytes 393224 | tf_op jit(solution)/shard_map/ppermute | solution.py:256
  39.9 4.6 %attend.7.refs_6_ = f32[4,512,128]{2,1,0:T(8,128)S(1)} custom-call(bf16[256,512]{1,0:T(8,128)(2,1)S(1)} %get-tuple-element.33.refs_0_, bf16[256,512]{1,0:T(8,128)(2,1)S(1)} %collective-permute-done.1.refs_1_.refs_0_, bf16[1024,128]{1,0:T(8,128)(2,1)S(1)} %constant_dynamic-update-slice_fusion.2.refs_2_, bf16[512,128]{1,0:T(8,128)(2,1)S(1)} %collective-permute-done.4.refs_3_, ...), custom_call_target="tpu_custom_call" | custom-call | flops 4194304 | bytes 524288 | tf_op jit(solution)/shard_map/attend/pallas_call | solution.py:313
  44.5 0.0 collective-permute-done.6.refs_2_
  44.5 0.0 collective-permute-done.7.refs_3_
  44.5 0.7 collective-permute-done.8.refs_4_
  45.3 0.6 collective-permute-start.13
  45.9 1.1 %collective-permute-start.10 = (bf16[512,128]{1,0:T(8,128)(2,1)S(1)}, bf16[512,128]{1,0:T(8,128)(2,1)S(1)}, u32[]{:S(2)}, u32[]{:S(2)}) collective-permute-start(bf16[512,128]{1,0:T(8,128)(2,1)S(1)} %collective-permute-done.6.refs_2_), channel_id=1, source_target_pairs={{0,8},{1,9},{2,10},{3,11},{4,12},{5,13},{6,14},{7,15},{8,0},{9,1},... | collective-permute-start | bytes 393224 | tf_op jit(solution)/shard_map/ppermute | solution.py:256
  47.0 0.3 collective-permute-start.11
  47.3 0.0 collective-permute-done.9.refs_5_
  47.3 7.0 %attend.8.refs_5_ = f32[4,512,128]{2,1,0:T(8,128)S(1)} custom-call(bf16[256,512]{1,0:T(8,128)(2,1)S(1)} %get-tuple-element.33.refs_0_, bf16[256,512]{1,0:T(8,128)(2,1)S(1)} %collective-permute-done.1.refs_1_.refs_0_, bf16[512,128]{1,0:T(8,128)(2,1)S(1)} %collective-permute-done.6.refs_2_, bf16[1024,128]{1,0:T(8,128)(2,1)S(1)} %collective-permute-done.7.refs_3_, ...), custom_call_target="tpu_custom_call" | custom-call | flops 6291456 | bytes 786432 | tf_op jit(solution)/shard_map/attend/pallas_call | solution.py:313
  54.3 0.0 collective-permute-done.10.refs_2_
  54.3 0.0 collective-permute-done.11.refs_3_
  54.3 1.1 %collective-permute-start.12 = (bf16[512,128]{1,0:T(8,128)(2,1)S(1)}, bf16[512,128]{1,0:T(8,128)(2,1)S(1)}, u32[]{:S(2)}, u32[]{:S(2)}) collective-permute-start(bf16[512,128]{1,0:T(8,128)(2,1)S(1)} %collective-permute-done.11.refs_3_), channel_id=1, source_target_pairs={{0,8},{1,9},{2,10},{3,11},{4,12},{5,13},{6,14},{7,15},{8,0},{9,1},... | collective-permute-start | bytes 393224 | tf_op jit(solution)/shard_map/ppermute | solution.py:256
  55.4 0.0 collective-permute-done.13.refs_4_
  55.4 4.6 %attend.9.refs_2_ = f32[4,512,128]{2,1,0:T(8,128)S(1)} custom-call(bf16[256,512]{1,0:T(8,128)(2,1)S(1)} %get-tuple-element.33.refs_0_, bf16[256,512]{1,0:T(8,128)(2,1)S(1)} %collective-permute-done.1.refs_1_.refs_0_, bf16[512,128]{1,0:T(8,128)(2,1)S(1)} %collective-permute-done.10.refs_2_, bf16[512,128]{1,0:T(8,128)(2,1)S(1)} %collective-permute-done.11.refs_3_, ...), custom_call_target="tpu_custom_call" | custom-call | flops 4194304 | bytes 524288 | tf_op jit(solution)/shard_map/attend/pallas_call | solution.py:313
  60.0 0.0 copy-start.2
  60.0 0.0 copy-start.4
  60.1 0.0 copy-start.13
  60.1 0.0 collective-permute-done.12.refs_1_
  60.1 1.1 %attend.11 = bf16[256,256]{1,0:T(8,128)(2,1)S(1)} custom-call(bf16[256,512]{1,0:T(8,128)(2,1)S(1)} %collective-permute-done.1.refs_1_.refs_0_, bf16[512,128]{1,0:T(8,128)(2,1)S(1)} %collective-permute-done.12.refs_1_, f32[4,512,128]{2,1,0:T(8,128)S(1)} %attend.9.refs_2_), custom_call_target="tpu_custom_call" | custom-call | flops 524288 | bytes 131072 | tf_op jit(solution)/shard_map/attend/pallas_call | solution.py:313
  61.2 2.6 %collective-permute-start.14 = (bf16[256,256]{1,0:T(8,128)(2,1)S(1)}, bf16[256,256]{1,0:T(8,128)(2,1)S(1)}, u32[]{:S(2)}, u32[]{:S(2)}) collective-permute-start(bf16[256,256]{1,0:T(8,128)(2,1)S(1)} %attend.11), channel_id=1, source_target_pairs={{0,1},{1,0},{2,3},{3,2},{4,5},{5,4},{6,7},{7,6},{8,9},{9,8},{10,11... | collective-permute-start | bytes 393224 | tf_op jit(solution)/shard_map/ppermute | solution.py:256
  63.9 1.1 %attend.10.mine_ref = bf16[256,256]{1,0:T(8,128)(2,1)S(1)} custom-call(bf16[256,512]{1,0:T(8,128)(2,1)S(1)} %get-tuple-element.33.refs_0_, bf16[512,128]{1,0:T(8,128)(2,1)S(1)} %collective-permute-done.12.refs_1_, f32[4,512,128]{2,1,0:T(8,128)S(1)} %attend.9.refs_2_), custom_call_target="tpu_custom_call" | custom-call | flops 524288 | bytes 131072 | tf_op jit(solution)/shard_map/attend/pallas_call | solution.py:313
  65.0 0.0 collective-permute-done.14.other_ref
  65.0 0.0 copy-done.3
  65.0 0.0 copy-done.2
  65.0 0.0 copy-done.4
  65.1 0.0 copy-done.13
  65.1 0.0 copy-start.11
  65.1 0.0 copy-start.1
  65.1 0.0 copy-start.5
  65.1 0.0 copy-start.6
  65.1 0.0 copy-start.14
  65.1 2.8 %post.1 = bf16[512,512]{1,0:T(8,128)(2,1)} custom-call(s32[1]{0:T(128)S(6)} %rem.18.core_ref, bf16[256,256]{1,0:T(8,128)(2,1)S(1)} %attend.10.mine_ref, bf16[256,256]{1,0:T(8,128)(2,1)S(1)} %collective-permute-done.14.other_ref, f32[256,512]{1,0:T(8,128)S(1)} %get-tuple-element.51.pooled_ref, bf16[256,512]{1,0:T(8,128)(2,1)S(1)} %get-tuple-element.52.member_ref, ...), custom_call_target="tpu_custom_call" | custom-call | tf_op jit(solution)/shard_map/post/pallas_call | solution.py:354
  67.9 3.5 %all-to-all-start.1 = ((bf16[32,16,512]{2,1,0:T(8,128)(2,1)}), bf16[32,16,512]{2,1,0:T(8,128)(2,1)S(1)}, u32[]{:S(2)}, u32[]{:S(2)}) async-start(bf16[32,16,512]{2,1,0:T(8,128)(2,1)} %bitcast.4), calls=%async_computation.1 | async-start | bytes 1048576 | tf_op jit(solution)/shard_map/all_to_all | solution.py:259
  71.5 0.1 copy.15.live_ref
  71.6 14.6 %all-to-all-done.1 = bf16[32,16,512]{2,1,0:T(8,128)(2,1)S(1)} async-done(((bf16[32,16,512]{2,1,0:T(8,128)(2,1)}), bf16[32,16,512]{2,1,0:T(8,128)(2,1)S(1)}, u32[]{:S(2)}, u32[]{:S(2)}) %all-to-all-start.1) | async-done | bytes 524320 | tf_op jit(solution)/shard_map/all_to_all | solution.py:259
  86.2 0.0 copy-done.14
  86.2 1.8 %decode.1 = bf16[512,512]{1,0:T(8,128)(2,1)} custom-call(bf16[512,512]{1,0:T(8,128)(2,1)S(1)} %bitcast.8, bf16[512,512]{1,0:T(8,128)(2,1)S(1)} %copy-done.1, f32[512,1]{1,0:T(8,128)S(1)} %copy.15.live_ref, f32[1,512]{1,0:T(1,128)S(1)} %bitcast.12, bf16[512,512]{1,0:T(8,128)(2,1)S(1)} %copy-done.5, bf16[512,512]{1,0:T(8,128)(2,1)S(1)} %copy-done.6), custom_call_target="tpu_custom_call" | custom-call | tf_op jit(solution)/shard_map/decode/pallas_call | solution.py:364
  (21 shorter events, 0.1 us)
Async XLA Ops:
  0.0 24.7 %copy-start.12 = (f32[512]{0:T(512)S(1)}, f32[512]{0:T(512)}, u32[]{:S(2)}) copy-start(f32[512]{0:T(512)} %param.21) | copy-start | bytes 6148
  0.0 25.8 %copy-start.15 = (f32[8]{0:T(128)S(1)}, f32[8]{0:T(128)}, u32[]{:S(2)}) copy-start(f32[8]{0:T(128)} %param.20) | copy-start | bytes 100
  0.0 1.1 %copy-start = (bf16[512,512]{1,0:T(8,128)(2,1)S(1)}, bf16[512,512]{1,0:T(8,128)(2,1)}, u32[]{:S(2)}) copy-start(bf16[512,512]{1,0:T(8,128)(2,1)} %sensors_ref.3) | copy-start | bytes 1572868
  1.1 0.7 copy-start.10
  1.8 22.9 %copy-start.8 = (bf16[512,128]{1,0:T(8,128)(2,1)S(1)}, bf16[512,128]{1,0:T(8,128)(2,1)}, u32[]{:S(2)}) copy-start(bf16[512,128]{1,0:T(8,128)(2,1)} %w_key_ref.1) | copy-start | bytes 393220
  1.8 22.9 %copy-start.9 = (bf16[512,128]{1,0:T(8,128)(2,1)S(1)}, bf16[512,128]{1,0:T(8,128)(2,1)}, u32[]{:S(2)}) copy-start(bf16[512,128]{1,0:T(8,128)(2,1)} %w_value_ref.1) | copy-start | bytes 393220
  1.8 24.2 %copy-start.7 = (bf16[512,512]{1,0:T(8,128)(2,1)S(1)}, bf16[512,512]{1,0:T(8,128)(2,1)}, u32[]{:S(2)}) copy-start(bf16[512,512]{1,0:T(8,128)(2,1)} %w_query_ref.1) | copy-start | bytes 1572868
  25.7 1.3 %collective-permute-start = (bf16[256,128]{1,0:T(8,128)(2,1)S(1)}, bf16[256,128]{1,0:T(8,128)(2,1)S(1)}, u32[]{:S(2)}, u32[]{:S(2)}) collective-permute-start(bf16[256,128]{1,0:T(8,128)(2,1)S(1)} %get-tuple-element.29), channel_id=1, source_target_pairs={{0,1},{1,0},{2,3},{3,2},{4,5},{5,4},{6,7},{7,6},{8,9},{9,8},{10,11... | collective-permute-start | bytes 196616 | tf_op jit(solution)/shard_map/ppermute | solution.py:256
  27.0 4.4 %collective-permute-start.1 = (bf16[256,512]{1,0:T(8,128)(2,1)S(1)}, bf16[256,512]{1,0:T(8,128)(2,1)S(1)}, u32[]{:S(2)}, u32[]{:S(2)}) collective-permute-start(bf16[256,512]{1,0:T(8,128)(2,1)S(1)} %get-tuple-element.34), channel_id=1, source_target_pairs={{0,1},{1,0},{2,3},{3,2},{4,5},{5,4},{6,7},{7,6},{8,9},{9,8},{10,11... | collective-permute-start | bytes 786440 | tf_op jit(solution)/shard_map/ppermute | solution.py:256
  27.3 5.9 %collective-permute-start.2 = (bf16[512,128]{1,0:T(8,128)(2,1)S(1)}, bf16[512,128]{1,0:T(8,128)(2,1)S(1)}, u32[]{:S(2)}, u32[]{:S(2)}) collective-permute-start(bf16[512,128]{1,0:T(8,128)(2,1)S(1)} %constant_dynamic-update-slice_fusion.refs_2_), channel_id=1, source_target_pairs={{0,4},{1,5},{2,6},{3,7},{4,0},{5,1},{6,2},{7,3},{8,12},{9,13},{10,... | collective-permute-start | bytes 393224 | tf_op jit(solution)/shard_map/ppermute | solution.py:256
  29.8 6.4 %collective-permute-start.3 = (bf16[512,128]{1,0:T(8,128)(2,1)S(1)}, bf16[512,128]{1,0:T(8,128)(2,1)S(1)}, u32[]{:S(2)}, u32[]{:S(2)}) collective-permute-start(bf16[512,128]{1,0:T(8,128)(2,1)S(1)} %constant_dynamic-update-slice_fusion.refs_2_), channel_id=1, source_target_pairs={{0,2},{1,3},{2,0},{3,1},{4,6},{5,7},{6,4},{7,5},{8,10},{9,11},{10,... | collective-permute-start | bytes 393224 | tf_op jit(solution)/shard_map/ppermute | solution.py:256
  30.9 5.2 %collective-permute-start.4 = (bf16[512,128]{1,0:T(8,128)(2,1)S(1)}, bf16[512,128]{1,0:T(8,128)(2,1)S(1)}, u32[]{:S(2)}, u32[]{:S(2)}) collective-permute-start(bf16[512,128]{1,0:T(8,128)(2,1)S(1)} %constant_dynamic-update-slice_fusion.refs_2_), channel_id=1, source_target_pairs={{0,8},{1,9},{2,10},{3,11},{4,12},{5,13},{6,14},{7,15},{8,0},{9,1},... | collective-permute-start | bytes 393224 | tf_op jit(solution)/shard_map/ppermute | solution.py:256
  30.9 5.2 %collective-permute-start.5 = (bf16[512,128]{1,0:T(8,128)(2,1)S(1)}, bf16[512,128]{1,0:T(8,128)(2,1)S(1)}, u32[]{:S(2)}, u32[]{:S(2)}) collective-permute-start(bf16[512,128]{1,0:T(8,128)(2,1)S(1)} %constant_dynamic-update-slice_fusion.refs_2_), channel_id=1, source_target_pairs={{0,16},{1,17},{2,18},{3,19},{4,20},{5,21},{6,22},{7,23},{8,24},{9,... | collective-permute-start | bytes 393224 | tf_op jit(solution)/shard_map/ppermute | solution.py:256
  36.2 8.3 %collective-permute-start.7 = (bf16[1024,128]{1,0:T(8,128)(2,1)S(1)}, bf16[1024,128]{1,0:T(8,128)(2,1)S(1)}, u32[]{:S(2)}, u32[]{:S(2)}) collective-permute-start(bf16[1024,128]{1,0:T(8,128)(2,1)S(1)} %constant_dynamic-update-slice_fusion.2.refs_2_), channel_id=1, source_target_pairs={{0,8},{1,9},{2,10},{3,11},{4,12},{5,13},{6,14},{7,15},{8,0},{9,1},... | collective-permute-start | bytes 786440 | tf_op jit(solution)/shard_map/ppermute | solution.py:256
  38.2 7.1 %collective-permute-start.8 = (bf16[1024,128]{1,0:T(8,128)(2,1)S(1)}, bf16[1024,128]{1,0:T(8,128)(2,1)S(1)}, u32[]{:S(2)}, u32[]{:S(2)}) collective-permute-start(bf16[1024,128]{1,0:T(8,128)(2,1)S(1)} %constant_dynamic-update-slice_fusion.2.refs_2_), channel_id=1, source_target_pairs={{0,16},{1,17},{2,18},{3,19},{4,20},{5,21},{6,22},{7,23},{8,24},{9,... | collective-permute-start | bytes 786440 | tf_op jit(solution)/shard_map/ppermute | solution.py:256
  38.8 5.7 %collective-permute-start.6 = (bf16[512,128]{1,0:T(8,128)(2,1)S(1)}, bf16[512,128]{1,0:T(8,128)(2,1)S(1)}, u32[]{:S(2)}, u32[]{:S(2)}) collective-permute-start(bf16[512,128]{1,0:T(8,128)(2,1)S(1)} %collective-permute-done.2), channel_id=1, source_target_pairs={{0,2},{1,3},{2,0},{3,1},{4,6},{5,7},{6,4},{7,5},{8,10},{9,11},{10,... | collective-permute-start | bytes 393224 | tf_op jit(solution)/shard_map/ppermute | solution.py:256
  38.8 8.6 %collective-permute-start.9 = (bf16[512,128]{1,0:T(8,128)(2,1)S(1)}, bf16[512,128]{1,0:T(8,128)(2,1)S(1)}, u32[]{:S(2)}, u32[]{:S(2)}) collective-permute-start(bf16[512,128]{1,0:T(8,128)(2,1)S(1)} %collective-permute-done.5.refs_4_), channel_id=1, source_target_pairs={{0,8},{1,9},{2,10},{3,11},{4,12},{5,13},{6,14},{7,15},{8,0},{9,1},... | collective-permute-start | bytes 393224 | tf_op jit(solution)/shard_map/ppermute | solution.py:256
  45.3 10.2 %collective-permute-start.13 = (bf16[1024,128]{1,0:T(8,128)(2,1)S(1)}, bf16[1024,128]{1,0:T(8,128)(2,1)S(1)}, u32[]{:S(2)}, u32[]{:S(2)}) collective-permute-start(bf16[1024,128]{1,0:T(8,128)(2,1)S(1)} %collective-permute-done.7.refs_3_), channel_id=1, source_target_pairs={{0,16},{1,17},{2,18},{3,19},{4,20},{5,21},{6,22},{7,23},{8,24},{9,... | collective-permute-start | bytes 786440 | tf_op jit(solution)/shard_map/ppermute | solution.py:256
  45.9 8.4 %collective-permute-start.10 = (bf16[512,128]{1,0:T(8,128)(2,1)S(1)}, bf16[512,128]{1,0:T(8,128)(2,1)S(1)}, u32[]{:S(2)}, u32[]{:S(2)}) collective-permute-start(bf16[512,128]{1,0:T(8,128)(2,1)S(1)} %collective-permute-done.6.refs_2_), channel_id=1, source_target_pairs={{0,8},{1,9},{2,10},{3,11},{4,12},{5,13},{6,14},{7,15},{8,0},{9,1},... | collective-permute-start | bytes 393224 | tf_op jit(solution)/shard_map/ppermute | solution.py:256
  47.0 7.3 %collective-permute-start.11 = (bf16[512,128]{1,0:T(8,128)(2,1)S(1)}, bf16[512,128]{1,0:T(8,128)(2,1)S(1)}, u32[]{:S(2)}, u32[]{:S(2)}) collective-permute-start(bf16[512,128]{1,0:T(8,128)(2,1)S(1)} %collective-permute-done.6.refs_2_), channel_id=1, source_target_pairs={{0,16},{1,17},{2,18},{3,19},{4,20},{5,21},{6,22},{7,23},{8,24},{9,... | collective-permute-start | bytes 393224 | tf_op jit(solution)/shard_map/ppermute | solution.py:256
  54.3 5.7 %collective-permute-start.12 = (bf16[512,128]{1,0:T(8,128)(2,1)S(1)}, bf16[512,128]{1,0:T(8,128)(2,1)S(1)}, u32[]{:S(2)}, u32[]{:S(2)}) collective-permute-start(bf16[512,128]{1,0:T(8,128)(2,1)S(1)} %collective-permute-done.11.refs_3_), channel_id=1, source_target_pairs={{0,8},{1,9},{2,10},{3,11},{4,12},{5,13},{6,14},{7,15},{8,0},{9,1},... | collective-permute-start | bytes 393224 | tf_op jit(solution)/shard_map/ppermute | solution.py:256
  55.4 9.6 %copy-start.3 = (bf16[2048,512]{1,0:T(8,128)(2,1)S(1)}, bf16[2048,512]{1,0:T(8,128)(2,1)}, u32[]{:S(2)}) copy-start(bf16[2048,512]{1,0:T(8,128)(2,1)} %w_outer_ref.1) | copy-start | bytes 6291460
  60.0 5.0 %copy-start.2 = (bf16[512,2048]{1,0:T(8,128)(2,1)S(1)}, bf16[512,2048]{1,0:T(8,128)(2,1)}, u32[]{:S(2)}) copy-start(bf16[512,2048]{1,0:T(8,128)(2,1)} %w_inner_ref.1) | copy-start | bytes 6291460
  60.0 5.0 %copy-start.4 = (bf16[512,512]{1,0:T(8,128)(2,1)S(1)}, bf16[512,512]{1,0:T(8,128)(2,1)}, u32[]{:S(2)}) copy-start(bf16[512,512]{1,0:T(8,128)(2,1)} %w_out_ref.2) | copy-start | bytes 1572868
  60.1 5.0 %copy-start.13 = (f32[512]{0:T(512)S(1)}, f32[512]{0:T(512)}, u32[]{:S(2)}) copy-start(f32[512]{0:T(512)} %param.24) | copy-start | bytes 6148
  61.2 3.8 %collective-permute-start.14 = (bf16[256,256]{1,0:T(8,128)(2,1)S(1)}, bf16[256,256]{1,0:T(8,128)(2,1)S(1)}, u32[]{:S(2)}, u32[]{:S(2)}) collective-permute-start(bf16[256,256]{1,0:T(8,128)(2,1)S(1)} %attend.11), channel_id=1, source_target_pairs={{0,1},{1,0},{2,3},{3,2},{4,5},{5,4},{6,7},{7,6},{8,9},{9,8},{10,11... | collective-permute-start | bytes 393224 | tf_op jit(solution)/shard_map/ppermute | solution.py:256
  65.1 6.4 %copy-start.11 = (s32[512]{0:T(512)S(1)}, s32[512]{0:T(512)}, u32[]{:S(2)}) copy-start(s32[512]{0:T(512)} %param.15) | copy-start | bytes 6148
  65.1 21.1 %copy-start.1 = (bf16[512,512]{1,0:T(8,128)(2,1)S(1)}, bf16[512,512]{1,0:T(8,128)(2,1)}, u32[]{:S(2)}) copy-start(bf16[512,512]{1,0:T(8,128)(2,1)} %sensors_ref.3) | copy-start | bytes 1572868
  65.1 21.1 %copy-start.5 = (bf16[512,512]{1,0:T(8,128)(2,1)S(1)}, bf16[512,512]{1,0:T(8,128)(2,1)}, u32[]{:S(2)}) copy-start(bf16[512,512]{1,0:T(8,128)(2,1)} %w_in_ref.1) | copy-start | bytes 1572868
  65.1 21.1 %copy-start.6 = (bf16[512,512]{1,0:T(8,128)(2,1)S(1)}, bf16[512,512]{1,0:T(8,128)(2,1)}, u32[]{:S(2)}) copy-start(bf16[512,512]{1,0:T(8,128)(2,1)} %w_out_ref.3) | copy-start | bytes 1572868
  65.1 21.1 %copy-start.14 = (f32[512]{0:T(512)S(1)}, f32[512]{0:T(512)}, u32[]{:S(2)}) copy-start(f32[512]{0:T(512)} %param.25) | copy-start | bytes 6148
  67.9 18.3 %all-to-all-start.1 = ((bf16[32,16,512]{2,1,0:T(8,128)(2,1)}), bf16[32,16,512]{2,1,0:T(8,128)(2,1)S(1)}, u32[]{:S(2)}, u32[]{:S(2)}) async-start(bf16[32,16,512]{2,1,0:T(8,128)(2,1)} %bitcast.4), calls=%async_computation.1 | async-start | bytes 1048576 | tf_op jit(solution)/shard_map/all_to_all | solution.py:259
